TPU v7x, 512 devices: a whole 4x4x16 slice. The times are simulated.
512 devices in a mesh: tp: 8 (over z_lo, core), dp: 4 (over z_hi), draft: 16 (over x, y).
Axes of the slice: x: 4, y: 4, z: 16 (z_hi: 4, z_lo: 4; z = z_hi * 4 + z_lo), core: 2. Of those that a mesh axis runs over, the one named last changes fastest.
Arguments:
- features: bfloat16 [4096, 3, 8192], P(('dp', 'draft'), None, 'tp'), may hold values from -6 to 6
- fc_weight: bfloat16 [8192, 3, 8192], P('tp', None, 'draft'), may hold values from -0.0390625 to 0.0390625
- mix_gain: float32 [8192], P('draft'), may hold values from 0.3 to 1.5
- lengths: int32 [4], replicated, may hold values from 1 to 1024, 3072 in all
Outputs:
- fc_grad: bfloat16 [8192, 3, 8192], P(('tp', 'dp'), None, 'draft')
- mix_grad: float32 [8192], P('draft')
Inputs may be any that keep to these rules, and one draw needn't show every extreme that they name: `lengths`: valid tokens of each sequence; they sum to 3072.
All inputs are finite; a program needn't handle non-finite values.
Results may differ from a plain program's by a relative error of at most 0.025.
Values may be sent and summed in bfloat16 or wider, within the bound.
No kernel may reach another device: no remote copies, remote signals or barrier semaphores. Data moves between devices by JAX's collectives and lax.ppermute only.
A program may use at most 128 MiB of HBM per device.

v0:
```python
import jax
import jax.numpy as jnp
from jax import lax
from jax.sharding import PartitionSpec as P

LEVELS = 3
UNROLL = 3


loss_scale = 64.0


def broadcast(shard, axis, root):
    mine = lax.axis_index(axis) == root
    return lax.psum(jnp.where(mine, shard, jnp.zeros_like(shard)), axis)


def shifted_down(values, amount):
    padding = jnp.zeros((amount,) + values.shape[1:], values.dtype)
    return jnp.concatenate([padding, values[:-amount]], axis=0)


def shifted_up(values, amount):
    padding = jnp.zeros((amount,) + values.shape[1:], values.dtype)
    return jnp.concatenate([values[amount:], padding], axis=0)


def draft_loss(joined, mix_gain, high_rows, length, valid_count):
    positions = jnp.arange(joined.shape[0], dtype=jnp.int32)
    draft_state = jax.nn.silu(joined)
    running_total = jnp.zeros((), jnp.float32)
    for unroll in range(UNROLL):
        if unroll > 0:
            draft_state = jax.nn.silu(joined + mix_gain * shifted_down(draft_state, 1))
        target = shifted_up(high_rows, unroll + 1)
        valid_rows = (positions + unroll + 1 < length).astype(jnp.float32)
        residual_error = (draft_state - target) * valid_rows[:, None]
        running_total = running_total + jnp.sum(residual_error * residual_error)
    return running_total * (loss_scale / (2.0 * valid_count))


def chain_grads(joined, mix_gain, high_rows, length, valid_count):

    def loss_of(joined_in, mix_in):
        return draft_loss(joined_in, mix_in, high_rows, length, valid_count)

    loss_value, pullback = jax.vjp(loss_of, joined, mix_gain)
    return pullback(jnp.ones_like(loss_value))


def valid_total(lengths):
    running = jnp.zeros((), jnp.float32)
    for unroll in range(1, UNROLL + 1):
        running = running + jnp.sum(jnp.maximum(lengths - unroll, 0)).astype(jnp.float32)
    return running


def local(features, fc_weight, mix_gain, lengths):
    tp_count = lax.axis_size("tp")
    block_ratio = lax.axis_size("draft") // tp_count
    draft_index = lax.axis_index("draft")
    sequence_index = lax.axis_index("dp")
    block_width = fc_weight.shape[2]
    gathered = lax.all_gather(features, "draft", axis=0, tiled=True)
    partial_sums = jnp.einsum(
        "rlk,kln->rn", gathered, fc_weight, preferred_element_type=jnp.float32
    )
    offset = draft_index % block_ratio * block_width
    high_slice = lax.dynamic_slice_in_dim(gathered[:, LEVELS - 1, :], offset, block_width, 1)
    high_rows = broadcast(high_slice, "tp", draft_index // block_ratio)
    length = lengths[sequence_index]
    valid_count = valid_total(lengths)
    joined = lax.psum(partial_sums.astype(jnp.bfloat16), "tp").astype(jnp.float32)
    grad_joined, grad_mix = chain_grads(
        joined, mix_gain, high_rows.astype(jnp.float32), length, valid_count
    )
    joined_grad = grad_joined.astype(jnp.bfloat16)
    mix_total = lax.psum(grad_mix, "dp")
    fc_grad = lax.psum_scatter(
        jnp.einsum("rlk,rn->kln", gathered, joined_grad, preferred_element_type=jnp.float32).astype(
            jnp.bfloat16
        ),
        "dp",
        scatter_dimension=0,
        tiled=True,
    )
    return (fc_grad, mix_total)


def solution(mesh):
    placed = (P(("dp", "draft"), None, "tp"), P("tp", None, "draft"), P("draft"), P())
    return jax.shard_map(
        local,
        mesh=mesh,
        in_specs=placed,
        out_specs=(P(("tp", "dp"), None, "draft"), P("draft")),
        check_vma=False,
    )
```

profile of v0, /device:TPU:1, one launch (start us, length us, event | category | flops | bytes accessed | tf_op | source)
XLA Modules:
  0.0 347.7 jit_solution(7170375849602706044)
XLA Ops:
  7.2 0.0 copy-start
  7.2 0.0 all-gather.2.cloned.1.call-start
  7.2 0.7 all-gather.2.cloned.1.call-update
  7.9 0.0 all-reduce.10.cloned.1.call-start
  8.0 85.1 %all-gather.2.cloned.1.call-done = bf16[1024,3,1024]{2,0,1:T(8,128)(2,1)} async-done(((bf16[64,3,1024]{2,0,1:T(8,128)(2,1)}), bf16[1024,3,1024]{2,0,1:T(8,128)(2,1)}) %all-gather.2.cloned.1.call-update) | async-done | bytes 6291472 | tf_op jit(solution)/shard_map/all_gather | solution.py:64
  93.1 0.0 slice-start.2
  93.1 1.6 slice-done.2
  94.7 1.3 select_bitcast_fusion
  96.0 0.0 copy-done
  96.0 7.1 %bitcast_convert_fusion = bf16[1024,512]{1,0:T(8,128)(2,1)} fusion(bf16[1024,3,1024]{2,0,1:T(8,128)(2,1)} %all-gather.2.cloned.1.call-done, bf16[1024,3,512]{2,0,1:T(8,128)(2,1)S(1)} %copy-done), kind=kOutput, calls=%fused_computation.22 | convolution fusion | flops 3221749760 | bytes 10485760 | tf_op jit(solution)/shard_map/rlk,kln->rn/dot_general | solution.py:65
  103.1 0.0 copy-start.4
  103.1 0.0 all-reduce.10.cloned.1.call-update
  103.2 0.0 reduce-scatter.2.cloned.1.call-start
  103.2 0.6 copy-done.4
  103.8 0.6 dynamic_slice.7
  104.4 0.7 maximum_reduce_fusion
  107.1 0.6 fusion.23
  107.7 0.6 fusion.21
  108.3 83.9 %all-reduce.10.cloned.1.call-done = (bf16[1024,512]{1,0:T(8,128)(2,1)}, bf16[1024,512]{1,0:T(8,128)(2,1)}) async-done(((bf16[1024,512]{1,0:T(8,128)(2,1)}, bf16[1024,512]{1,0:T(8,128)(2,1)}), (bf16[1024,512]{1,0:T(8,128)(2,1)}, bf16[1024,512]{1,0:T(8,128)(2,1)})) %all-reduce.10.cloned.1.call-update) | async-done | bytes 2097168 | tf_op jit(solution)/shard_map/psum | solution.py:15
  192.3 0.0 copy-start.1
  192.3 1.6 slice.27
  193.9 0.0 copy-done.1
  193.9 0.3 slice.28
  194.2 0.0 copy-start.2
  194.2 0.3 slice.29
  194.6 0.0 copy-start.3
  194.6 0.9 copy-done.2
  195.4 0.6 convert_multiply_fusion.1
  196.0 0.0 copy-done.3
  196.0 0.7 fusion.16
  196.7 2.5 multiply_reduce_fusion.1
  199.2 0.0 slice-start
  199.2 0.3 slice_multiply_fusion.1
  199.5 0.0 slice-start.1
  199.5 2.7 multiply_reduce_fusion
  202.3 0.3 slice_multiply_fusion
  202.6 0.0 slice-done
  202.6 0.0 slice-done.1
  202.6 6.3 %convert_bitcast_fusion = bf16[1024,3,512]{0,2,1:T(8,128)(2,1)} fusion(bf16[1024,3,1024]{2,0,1:T(8,128)(2,1)S(1)} %bitcast.19, bf16[1024,512]{1,0:T(8,128)(2,1)S(1)} %copy-done.2, f32[1023,512]{1,0:T(8,128)S(1)} %slice.29, f32[1023,512]{1,0:T(8,128)S(1)} %slice_multiply_fusion, f32[1024,512]{1,0:T(8,128)S(1)} %get-tuple-element.12, ...), kind=kOutput, calls=%fused_computation.5 | convolution fusion | flops 3233284096 | bytes 18874372 | tf_op jit(solution)/shard_map/rlk,rn->kln/dot_general | solution.py:80
  208.9 0.0 reduce-scatter.2.cloned.1.call-update
  208.9 15.0 %psum.23 = f32[512]{0:T(512)} all-reduce(f32[512]{0:T(512)S(1)} %add_any.44), channel_id=1, replica_groups=mesh['tp'=8,'dp'=4,'draft'=16] {'dp'}, use_global_device_ids=true, to_apply=%region_8.9 | all-reduce | flops 512 | bytes 4096 | tf_op jit(solution)/shard_map/psum | solution.py:78
  223.9 114.9 %reduce-scatter.2.cloned.1.call-done = bf16[256,3,512]{0,2,1:T(8,128)(2,1)} async-done(((bf16[1024,3,512]{0,2,1:T(8,128)(2,1)}), bf16[256,3,512]{0,2,1:T(8,128)(2,1)}) %reduce-scatter.2.cloned.1.call-update) | async-done | bytes 786448 | tf_op jit(solution)/shard_map/reduce_scatter | solution.py:79
  338.8 2.3 copy.7
  (2 shorter events, 0.0 us)
Async XLA Ops:
  7.2 88.8 %copy-start = (bf16[1024,3,512]{2,0,1:T(8,128)(2,1)S(1)}, bf16[1024,3,512]{2,0,1:T(8,128)(2,1)}, u32[]{:S(2)}) copy-start(bf16[1024,3,512]{2,0,1:T(8,128)(2,1)} %param.5) | copy-start | bytes 9437188
  7.2 85.9 %all-gather.2.cloned.1.call-start = ((), (), s32[]{:S(2)}) async-start(), calls=%async_computation.1 | async-start | bytes 6684672 | tf_op jit(solution)/shard_map/all_gather | solution.py:64
  7.9 184.3 %all-reduce.10.cloned.1.call-start = ((), (), s32[]{:S(2)}) async-start(), calls=%async_computation.3 | async-start | bytes 4194304 | tf_op jit(solution)/shard_map/psum | solution.py:15
  93.1 1.6 slice-start.2
  103.1 0.7 copy-start.4
  103.2 235.7 %reduce-scatter.2.cloned.1.call-start = ((), (), s32[]{:S(2)}) async-start(), calls=%async_computation.2 | async-start | bytes 3932160 | tf_op jit(solution)/shard_map/reduce_scatter | solution.py:79
  192.3 1.6 copy-start.1
  194.2 1.2 copy-start.2
  194.6 1.4 copy-start.3
  199.2 3.3 slice-start
  199.5 3.0 slice-start.1
Sparse Core Ops, SparseCore 0:
  11.1 81.9 all-gather.1
  103.3 88.9 all-reduce.9
  209.0 129.7 reduce-scatter.1
where the time goes:
time: 348 us
  waiting for transfers between devices  285 us (82%)
  between operations  15.9 us (5%)
  blocking collectives  15 us (4%)
  matrix products  13.5 us (4%)
  other arithmetic  10.3 us (3%)
  local copies, waits for them, and re-layouts  8.23 us (2%)
    reduce_scatter x1, waiting for transfers between devices, local(): lax.psum_scatter(jnp.einsum('rlk,rn->kln', gathered, joined_grad, preferr...  115 us
    all_gather x1, waiting for transfers between devices, local(): gathered = lax.all_gather(features, 'draft', axis=0, tiled=True)  85.1 us
    psum x1, waiting for transfers between devices, broadcast(): return lax.psum(jnp.where(mine, shard, jnp.zeros_like(shard)), axis)  83.9 us
    psum x1, blocking collectives, local(): mix_total = lax.psum(grad_mix, 'dp')  15 us
    dot_general x1, matrix products, local(): jnp.einsum('rlk,kln->rn', gathered, fc_weight, preferred_element_type=jnp...  7.15 us
  transfers between devices with their start and end apart: 3, of which 3 were waited for; matrix products, arithmetic and copies ran while one was open for 1% of the time, Pallas kernels for 0%

commit v1 on v0

v1 whole, which is shorter than its diff:
```python
import jax
import jax.numpy as jnp
from jax import lax
from jax.experimental import pallas as pl
from jax.experimental.pallas import tpu as pltpu
from jax.sharding import PartitionSpec as P

LEVELS = 3
UNROLL = 3
LOSS_SCALE = 64.0
HALO = 8
TAIL = 16


def sigmoid(v):
    return 1.0 / (1.0 + jnp.exp(-v))


def chain_kernel(meta_ref, scale_ref, parts_ref, high_ref, gain_ref, grad_ref, mix_ref):
    rows = parts_ref.shape[1]
    own = rows - 2 * HALO
    joined = parts_ref[0].astype(jnp.float32)
    for member in range(1, parts_ref.shape[0]):
        joined = joined + parts_ref[member].astype(jnp.float32)
    high = high_ref[...].astype(jnp.float32)
    width = joined.shape[1]
    gain = gain_ref[...]
    scale = scale_ref[0]
    start, length = meta_ref[0], meta_ref[1]
    position = start - HALO + lax.broadcasted_iota(jnp.int32, (rows, width), 0)

    def down(values):
        return jnp.concatenate([jnp.zeros((1, width), jnp.float32), values[:-1]], axis=0)

    def up(values):
        return jnp.concatenate([values[1:], jnp.zeros((1, width), jnp.float32)], axis=0)

    def target(step):
        lead = jnp.zeros((HALO - step, width), jnp.float32)
        return jnp.concatenate([lead, high[: rows - HALO + step]], axis=0)

    def state_and_slope(v):
        gate = sigmoid(v)
        return v * gate, gate * (1.0 + v * (1.0 - gate))

    def residual(state, step):
        return jnp.where(position + step < length, scale * (state - target(step)), 0.0)

    state_1, slope_1 = state_and_slope(joined)
    before_1 = down(state_1)
    state_2, slope_2 = state_and_slope(joined + gain * before_1)
    before_2 = down(state_2)
    state_3, slope_3 = state_and_slope(joined + gain * before_2)
    delta_3 = residual(state_3, 3) * slope_3
    delta_2 = (residual(state_2, 2) + up(gain * delta_3)) * slope_2
    delta_1 = (residual(state_1, 1) + up(gain * delta_2)) * slope_1
    total = delta_1 + delta_2 + delta_3
    grad_ref[...] = total[HALO : HALO + own].astype(jnp.bfloat16)
    mix = (delta_2 * before_1 + delta_3 * before_2)[HALO : HALO + own]
    mix_ref[...] = jnp.sum(mix, axis=0, keepdims=True)


def chain(parts, high, gain, start, length, scale):
    members, rows, width = parts.shape
    own = rows - 2 * HALO
    vmem = pl.BlockSpec(memory_space=pltpu.VMEM)
    smem = pl.BlockSpec(memory_space=pltpu.SMEM)
    return pl.pallas_call(
        chain_kernel,
        out_shape=(
            jax.ShapeDtypeStruct((own, width), jnp.bfloat16),
            jax.ShapeDtypeStruct((1, width), jnp.float32),
        ),
        in_specs=[smem, smem, vmem, vmem, vmem],
        out_specs=(vmem, vmem),
        compiler_params=pltpu.CompilerParams(vmem_limit_bytes=32 << 20),
        cost_estimate=pl.CostEstimate(
            flops=60 * rows * width, bytes_accessed=2 * parts.size, transcendentals=3 * rows * width
        ),
        name="chain",
    )(jnp.stack([start, length]), scale.reshape(1), parts, high, gain.reshape(1, width))


def valid_total(lengths):
    running = jnp.zeros((), jnp.float32)
    for unroll in range(1, UNROLL + 1):
        running = running + jnp.sum(jnp.maximum(lengths - unroll, 0)).astype(jnp.float32)
    return running


def high_of(top, tp_count, draft_count, draft_index):
    width = top.shape[1] // 2
    even = draft_index % 2 == 0
    left, right = top[:, :width], top[:, width:]
    flat = lambda t, e: t * draft_count + e
    first, second = [], []
    for t in range(tp_count):
        for e in range(draft_count):
            first.append((flat(t, e), flat(e // 2, 2 * t + e % 2)))
            second.append((flat(t, e), flat(e // 2, 2 * t + 1 - e % 2)))
    axes = ("tp", "draft")
    one = lax.ppermute(jnp.where(even, left, right), axes, first)
    two = lax.ppermute(jnp.where(even, right, left), axes, second)
    rows = jnp.concatenate([jnp.where(even, one, two), jnp.where(even, two, one)], axis=0)
    following = lax.ppermute(rows[:TAIL], "tp", [(j, j - 1) for j in range(1, tp_count)])
    return jnp.concatenate([rows, following], axis=0)


def local(features, fc_weight, mix_gain, lengths):
    tp_count, dp_count = lax.axis_size("tp"), lax.axis_size("dp")
    draft_count = lax.axis_size("draft")
    tp_index, draft_index = lax.axis_index("tp"), lax.axis_index("draft")
    own_rows, _, depth = features.shape
    width = fc_weight.shape[2]
    rows = own_rows * draft_count
    piece = rows // tp_count
    part = depth // dp_count
    own = features.transpose(1, 0, 2)
    weight = fc_weight.transpose(1, 0, 2)

    gathered = lax.all_gather(own, "draft", axis=1, tiled=True)
    traded = lax.all_to_all(
        own.reshape(LEVELS, own_rows, dp_count, part), "dp", split_axis=2, concat_axis=0, tiled=False
    )
    high = high_of(own[LEVELS - 1], tp_count, draft_count, draft_index)

    gathered, traded = lax.optimization_barrier((gathered, traded))
    every = lax.all_gather(traded, "draft", axis=2, tiled=True)
    every = every.transpose(1, 0, 2, 3).reshape(LEVELS, dp_count * rows, part)

    partial = jnp.einsum("lrk,lkn->rn", gathered, weight, preferred_element_type=jnp.float32)
    middle = partial.astype(jnp.bfloat16).reshape(tp_count, piece, width)
    edge = jnp.zeros((1, HALO, width), jnp.bfloat16)
    before = jnp.concatenate([edge, middle[:-1, piece - HALO :]], axis=0)
    after = jnp.concatenate([middle[1:, :HALO], edge], axis=0)
    pieces = jnp.concatenate([before, middle, after], axis=1)
    parts = lax.all_to_all(pieces, "tp", split_axis=0, concat_axis=0, tiled=True)

    length = lengths[lax.axis_index("dp")]
    scale = LOSS_SCALE / valid_total(lengths)
    grad, mix = chain(parts, high, mix_gain, tp_index * piece, length, scale)
    grads = lax.all_gather(grad, ("dp", "tp"), axis=0, tiled=True)
    mix_total = lax.psum(mix[0], ("tp", "dp"))
    fc_grad = jnp.einsum("ltk,tn->lkn", every, grads, preferred_element_type=jnp.float32)
    return (fc_grad.astype(jnp.bfloat16).transpose(1, 0, 2), mix_total)


def solution(mesh):
    placed = (P(("dp", "draft"), None, "tp"), P("tp", None, "draft"), P("draft"), P())
    return jax.shard_map(
        local,
        mesh=mesh,
        in_specs=placed,
        out_specs=(P(("tp", "dp"), None, "draft"), P("draft")),
        check_vma=False,
    )
```

time: 348 us -> 269 us (0.77); the launches traced: 348 us -> 264 us
  waiting for transfers between devices: 285 us -> 74.1 us
  blocking collectives: 15 us -> 114 us
  local copies, waits for them, and re-layouts: 8.23 us -> 25.4 us
  starting transfers between devices: 0.12 us -> 15.3 us
  other arithmetic: 10.3 us -> 2.68 us
    reduce_scatter x1 -> x0, waiting for transfers between devices: 115 us -> none  [local(): lax.psum_scatter(jnp.einsum('rlk,rn->kln', gathered, joined_grad, preferr...]
    psum x1 -> x0, waiting for transfers between devices: 83.9 us -> none  [broadcast(): return lax.psum(jnp.where(mine, shard, jnp.zeros_like(shard)), axis)]
    psum x1, blocking collectives: 15 us -> 80.6 us  [local(): mix_total = lax.psum(mix[0], ('tp', 'dp'))]
    all_to_all x0 -> x1, blocking collectives: none -> 33.2 us  [local(): lax.all_to_all(own.reshape(LEVELS, own_rows, dp_count, part), 'dp', split...]
    all_gather x1 -> x3, waiting for transfers between devices: 85.1 us -> 53.4 us  [the longest x1 50.2 us: local(): gathered = lax.all_gather(own, 'draft', axis=1, tiled=True)]
    ppermute x0 -> x3, waiting for transfers between devices: none -> 19.9 us  [the longest x1 15.8 us: high_of(): lax.ppermute(rows[:TAIL], 'tp', [(j, j - 1) for j in range(1, tp_count)])]
    transpose x0 -> x1, local copies, waits for them, and re-layouts: none -> 11.3 us  [local(): every = every.transpose(1, 0, 2, 3).reshape(LEVELS, dp_count * rows, part)]
    reshape x0 -> x1, local copies, waits for them, and re-layouts: none -> 11.1 us  [local(): every = every.transpose(1, 0, 2, 3).reshape(LEVELS, dp_count * rows, part)]
  transfers between devices with their start and end apart: 3 -> 7, of which waited for: 3 -> 4; matrix products, arithmetic and copies ran while one was open for 1% -> 13% of each run, Pallas kernels for 0% -> 1%
where the time goes in v1:
time: 269 us; the launch traced here: 264 us
  blocking collectives  114 us (42%)
  waiting for transfers between devices  74.1 us (28%)
  local copies, waits for them, and re-layouts  25.4 us (9%)
  between operations  15.9 us (6%)
  starting transfers between devices  15.3 us (6%)
  matrix products  14.5 us (5%)
  Pallas kernels  2.81 us (1%)
    psum x1, blocking collectives, local(): mix_total = lax.psum(mix[0], ('tp', 'dp'))  80.6 us
    all_gather x1, waiting for transfers between devices, local(): gathered = lax.all_gather(own, 'draft', axis=1, tiled=True)  50.2 us
    all_to_all x1, blocking collectives, local(): lax.all_to_all(own.reshape(LEVELS, own_rows, dp_count, part), 'dp', split...  33.2 us
    ppermute x1, waiting for transfers between devices, high_of(): lax.ppermute(rows[:TAIL], 'tp', [(j, j - 1) for j in range(1, tp_count)])  15.8 us
    transpose x1, local copies, waits for them, and re-layouts, local(): every = every.transpose(1, 0, 2, 3).reshape(LEVELS, dp_count * rows, part)  11.3 us
    reshape x1, local copies, waits for them, and re-layouts, local(): every = every.transpose(1, 0, 2, 3).reshape(LEVELS, dp_count * rows, part)  11.1 us
    dot_general x1, matrix products, local(): jnp.einsum('ltk,tn->lkn', every, grads, preferred_element_type=jnp.float32)  8.29 us
    dot_general x1, matrix products, local(): jnp.einsum('lrk,lkn->rn', gathered, weight, preferred_element_type=jnp.fl...  6.19 us
  transfers between devices with their start and end apart: 7, of which 4 were waited for; matrix products, arithmetic and copies ran while one was open for 13% of the time, Pallas kernels for 1%

profile of v1, /device:TPU:1, one launch (start us, length us, event | category | flops | bytes accessed | tf_op | source)
XLA Modules:
  0.0 264.3 jit_solution(13984881240534338418)
XLA Ops:
  7.2 0.0 copy-start
  7.2 0.0 all-gather.4.cloned.1.call-start
  7.2 0.7 all-gather.4.cloned.1.call-update
  7.9 0.0 all-gather.6.cloned.1.call-start
  8.0 1.4 broadcast_in_dim_reshape.3
  9.5 33.2 %all_to_all.20 = bf16[1,3,64,4,256]{4,2,1,0,3:T(8,128)(2,1)} all-to-all(bf16[1,3,64,4,256]{4,2,1,0,3:T(8,128)(2,1)S(1)} %copy.7), channel_id=1, replica_groups=mesh['tp'=8,'dp'=4,'draft'=16] {'dp'}, dimensions={3} | all-to-all | bytes 786432 | tf_op jit(solution)/shard_map/all_to_all | solution.py:122
  42.7 50.2 %all-gather.4.cloned.1.call-done = bf16[3,1024,1024]{2,1,0:T(8,128)(2,1)} async-done(((bf16[3,64,1024]{2,1,0:T(8,128)(2,1)}), bf16[3,1024,1024]{2,1,0:T(8,128)(2,1)}) %all-gather.4.cloned.1.call-update) | async-done | bytes 6291472 | tf_op jit(solution)/shard_map/all_gather | solution.py:121
  92.8 0.0 all-gather.6.cloned.1.call-update
  92.9 0.0 copy-done
  92.9 6.2 %bitcast_convert_fusion = bf16[1024,512]{1,0:T(8,128)(2,1)S(1)} fusion(bf16[3,1024,1024]{2,1,0:T(8,128)(2,1)} %all-gather.4.cloned.1.call-done, bf16[1024,3,512]{2,0,1:T(8,128)(2,1)S(1)} %copy-done), kind=kOutput, calls=%fused_computation.8 | convolution fusion | flops 3221749760 | bytes 10485760 | tf_op jit(solution)/shard_map/lrk,lkn->rn/dot_general | solution.py:131
  99.1 0.0 copy-start.2
  99.1 1.2 fusion.14
  100.3 0.0 copy-start.1
  100.3 5.6 %all-to-all-start.1 = ((bf16[8,144,512]{2,1,0:T(8,128)(2,1)}), bf16[8,144,512]{2,1,0:T(8,128)(2,1)}, u32[]{:S(2)}, u32[]{:S(2)}) async-start(bf16[8,144,512]{2,1,0:T(8,128)(2,1)} %fusion.14), calls=%async_computation.1 | async-start | bytes 2359296 | tf_op jit(solution)/shard_map/all_to_all | solution.py:137
  105.9 0.0 all-gather.8.cloned.1.call-start
  105.9 0.9 slice_bitcast_fusion
  106.9 4.5 %collective-permute-start = (bf16[64,512]{1,0:T(8,128)(2,1)S(1)}, bf16[64,512]{1,0:T(8,128)(2,1)S(1)}, u32[]{:S(2)}, u32[]{:S(2)}) collective-permute-start(bf16[64,512]{1,0:T(8,128)(2,1)S(1)} %get-tuple-element.18), channel_id=1, source_target_pairs={{0,0},{1,1},{2,64},{3,65},{4,128},{5,129},{6,192},{7,193},{8,256},... | collective-permute-start | bytes 196616 | tf_op jit(solution)/shard_map/ppermute | solution.py:102
  111.4 3.1 %collective-permute-start.1 = (bf16[64,512]{1,0:T(8,128)(2,1)S(1)}, bf16[64,512]{1,0:T(8,128)(2,1)S(1)}, u32[]{:S(2)}, u32[]{:S(2)}) collective-permute-start(bf16[64,512]{1,0:T(8,128)(2,1)S(1)} %get-tuple-element.17), channel_id=1, source_target_pairs={{0,1},{1,0},{2,65},{3,64},{4,129},{5,128},{6,193},{7,192},{8,257},... | collective-permute-start | bytes 196616 | tf_op jit(solution)/shard_map/ppermute | solution.py:103
  114.5 0.0 copy-done.2
  114.5 0.6 dynamic_slice.3
  115.1 0.7 maximum_reduce_fusion
  115.8 0.0 collective-permute-done
  115.8 4.1 %collective-permute-done.1 = bf16[64,512]{1,0:T(8,128)(2,1)S(1)} collective-permute-done((bf16[64,512]{1,0:T(8,128)(2,1)S(1)}, bf16[64,512]{1,0:T(8,128)(2,1)S(1)}, u32[]{:S(2)}, u32[]{:S(2)}) %collective-permute-start.1) | collective-permute-done | bytes 65568 | tf_op jit(solution)/shard_map/ppermute | solution.py:103
  119.9 1.9 collective-permute-start.2
  121.9 0.7 pad_add_fusion.meta_ref
  124.6 15.8 %collective-permute-done.2 = bf16[16,512]{1,0:T(8,128)(2,1)S(1)} collective-permute-done((bf16[16,512]{1,0:T(8,128)(2,1)S(1)}, bf16[16,512]{1,0:T(8,128)(2,1)S(1)}, u32[]{:S(2)}, u32[]{:S(2)}) %collective-permute-start.2) | collective-permute-done | bytes 16416 | tf_op jit(solution)/shard_map/ppermute | solution.py:105
  140.4 0.0 all-to-all-done.1.parts_ref
  140.5 0.0 copy-done.1
  140.5 2.8 %chain.1 = (bf16[128,512]{1,0:T(8,128)(2,1)}, f32[1,512]{1,0:T(1,128)S(1)}) custom-call(s32[2]{0:T(128)S(1)} %pad_add_fusion.meta_ref, f32[1]{0:T(128)} %bitcast.6.scale_ref, bf16[8,144,512]{2,1,0:T(8,128)(2,1)} %all-to-all-done.1.parts_ref, bf16[144,512]{1,0:T(8,128)(2,1)S(1)} %pad_maximum_fusion.high_ref, f32[1,512]{1,0:T(1,128)S(1)} %bitcast.34), custom_call_target="tpu_custom_call" | custom-call | flops 4423680 | bytes 1179648 | tf_op jit(solution)/shard_map/chain/pallas_call | solution.py:68
  143.3 0.0 all-gather.8.cloned.1.call-update
  143.3 80.6 %psum.7 = f32[512]{0:T(512)} all-reduce(f32[512]{0:T(512)S(1)} %bitcast.35), channel_id=1, replica_groups=mesh['tp'=8,'dp'=4,'draft'=16] {'tp','dp'}, use_global_device_ids=true, to_apply=%region_3.4 | all-reduce | flops 512 | bytes 4096 | tf_op jit(solution)/shard_map/psum | solution.py:143
  223.9 0.0 all-gather.6.cloned.1.call-done
  223.9 11.3 %copy.8 = bf16[3,4,1024,256]{2,1,3,0:T(4,128)(2,1)} copy(bf16[3,4,1024,256]{3,2,0,1:T(8,128)(2,1)} %bitcast.36) | data formatting | bytes 12582912 | tf_op jit(solution)/shard_map/transpose | solution.py:129
  235.2 11.1 %reshape.17 = bf16[3,4096,256]{1,2,0:T(8,128)(2,1)} reshape(bf16[3,4,1024,256]{2,1,3,0:T(4,128)(2,1)} %copy.8) | data formatting | bytes 12582912 | tf_op jit(solution)/shard_map/reshape | solution.py:129
  246.2 3.3 %all-gather.8.cloned.1.call-done = bf16[4096,512]{1,0:T(8,128)(2,1)} async-done(((bf16[128,512]{1,0:T(8,128)(2,1)}), bf16[4096,512]{1,0:T(8,128)(2,1)}) %all-gather.8.cloned.1.call-update) | async-done | bytes 4194320 | tf_op jit(solution)/shard_map/all_gather | solution.py:142
  249.5 8.3 %fusion.11 = bf16[256,3,512]{2,0,1:T(8,128)(2,1)} fusion(bf16[3,4096,256]{1,2,0:T(8,128)(2,1)} %reshape.17, bf16[4096,512]{1,0:T(8,128)(2,1)} %all-gather.8.cloned.1.call-done), kind=kOutput, calls=%fused_computation.10 | convolution fusion | flops 3221618688 | bytes 11272192 | tf_op jit(solution)/shard_map/ltk,tn->lkn/dot_general | solution.py:144
  (6 shorter events, 0.1 us)
Async XLA Ops:
  7.2 85.7 %copy-start = (bf16[1024,3,512]{2,0,1:T(8,128)(2,1)S(1)}, bf16[1024,3,512]{2,0,1:T(8,128)(2,1)}, u32[]{:S(2)}) copy-start(bf16[1024,3,512]{2,0,1:T(8,128)(2,1)} %param.5) | copy-start | bytes 9437188
  7.2 85.7 %all-gather.4.cloned.1.call-start = ((), (), s32[]{:S(2)}) async-start(), calls=%async_computation.2 | async-start | bytes 6684672 | tf_op jit(solution)/shard_map/all_gather | solution.py:121
  7.9 216.0 %all-gather.6.cloned.1.call-start = ((), (), s32[]{:S(2)}) async-start(), calls=%async_computation.3 | async-start | bytes 6684672 | tf_op jit(solution)/shard_map/all_gather | solution.py:128
  99.1 15.4 %copy-start.2 = (s32[4]{0:T(128)S(1)}, s32[4]{0:T(128)}, u32[]{:S(2)}) copy-start(s32[4]{0:T(128)} %param.7) | copy-start | bytes 52
  100.3 40.1 %copy-start.1 = (f32[512]{0:T(512)S(1)}, f32[512]{0:T(512)}, u32[]{:S(2)}) copy-start(f32[512]{0:T(512)} %param.6) | copy-start | bytes 6148
  100.3 40.1 %all-to-all-start.1 = ((bf16[8,144,512]{2,1,0:T(8,128)(2,1)}), bf16[8,144,512]{2,1,0:T(8,128)(2,1)}, u32[]{:S(2)}, u32[]{:S(2)}) async-start(bf16[8,144,512]{2,1,0:T(8,128)(2,1)} %fusion.14), calls=%async_computation.1 | async-start | bytes 2359296 | tf_op jit(solution)/shard_map/all_to_all | solution.py:137
  105.9 143.6 %all-gather.8.cloned.1.call-start = ((), (), s32[]{:S(2)}) async-start(), calls=%async_computation.4 | async-start | bytes 4325376 | tf_op jit(solution)/shard_map/all_gather | solution.py:142
  106.9 9.0 %collective-permute-start = (bf16[64,512]{1,0:T(8,128)(2,1)S(1)}, bf16[64,512]{1,0:T(8,128)(2,1)S(1)}, u32[]{:S(2)}, u32[]{:S(2)}) collective-permute-start(bf16[64,512]{1,0:T(8,128)(2,1)S(1)} %get-tuple-element.18), channel_id=1, source_target_pairs={{0,0},{1,1},{2,64},{3,65},{4,128},{5,129},{6,192},{7,193},{8,256},... | collective-permute-start | bytes 196616 | tf_op jit(solution)/shard_map/ppermute | solution.py:102
  111.4 8.5 %collective-permute-start.1 = (bf16[64,512]{1,0:T(8,128)(2,1)S(1)}, bf16[64,512]{1,0:T(8,128)(2,1)S(1)}, u32[]{:S(2)}, u32[]{:S(2)}) collective-permute-start(bf16[64,512]{1,0:T(8,128)(2,1)S(1)} %get-tuple-element.17), channel_id=1, source_target_pairs={{0,1},{1,0},{2,65},{3,64},{4,129},{5,128},{6,193},{7,192},{8,257},... | collective-permute-start | bytes 196616 | tf_op jit(solution)/shard_map/ppermute | solution.py:103
  119.9 20.5 %collective-permute-start.2 = (bf16[16,512]{1,0:T(8,128)(2,1)S(1)}, bf16[16,512]{1,0:T(8,128)(2,1)S(1)}, u32[]{:S(2)}, u32[]{:S(2)}) collective-permute-start(bf16[16,512]{1,0:T(8,128)(2,1)S(1)} %slice.29), channel_id=1, source_target_pairs={{64,0},{128,64},{192,128},{256,192},{320,256},{384,320},{448,384},... | collective-permute-start | bytes 49160 | tf_op jit(solution)/shard_map/ppermute | solution.py:105
Sparse Core Ops, SparseCore 0:
  11.1 81.7 all-gather.3
  95.9 76.4 all-gather.5
  175.1 74.3 all-gather.7

commit v2 on v1

v2 whole, which is shorter than its diff:
```python
import jax
import jax.numpy as jnp
from jax import lax
from jax.experimental import pallas as pl
from jax.experimental.pallas import tpu as pltpu
from jax.sharding import PartitionSpec as P

LEVELS = 3
UNROLL = 3
LOSS_SCALE = 64.0
HALO = 8
TAIL = 16
X, Y = 4, 4
ZL, CORES, ZH = 4, 2, 4
VMEM = pl.BlockSpec(memory_space=pltpu.VMEM)
SMEM = pl.BlockSpec(memory_space=pltpu.SMEM)
PARAMS = pltpu.CompilerParams(vmem_limit_bytes=48 << 20)


def plane_move(step, first):
    pairs = []
    for t in range(ZL * CORES):
        for x in range(X):
            for y in range(Y):
                along_x = (t % CORES == 0) == first
                source = (x + step) % X * Y + y if along_x else x * Y + (y + step) % Y
                pairs.append((t * X * Y + source, t * X * Y + x * Y + y))
    return lambda block: lax.ppermute(block, ("tp", "draft"), pairs)


def from_other_core(block):
    return lax.ppermute(block, "tp", [(t ^ 1, t) for t in range(ZL * CORES)])


def from_zl(block, step):
    pairs = [((t // CORES + step) % ZL * CORES + t % CORES, t) for t in range(ZL * CORES)]
    return lax.ppermute(block, "tp", pairs)


def from_zh(block, step):
    return lax.ppermute(block, "dp", [((s + step) % ZH, s) for s in range(ZH)])


def from_z(block, step):
    pairs = []
    for t in range(ZL * CORES):
        for s in range(ZH):
            z = (s * ZL + t // CORES + step) % (ZL * ZH)
            pairs.append((((z % ZL) * CORES + t % CORES) * ZH + z // ZL, t * ZH + s))
    return lax.ppermute(block, ("tp", "dp"), pairs)


def project_kernel(*refs):
    *block_refs, weight_ref, out_ref, total_ref = refs
    level = pl.program_id(0)
    rows = jnp.concatenate([r[...].reshape(-1, r.shape[-1]) for r in block_refs], axis=0)
    term = jnp.dot(rows, weight_ref[0], preferred_element_type=jnp.float32)

    @pl.when(level == 0)
    def _():
        total_ref[...] = term

    @pl.when(level > 0)
    def _():
        total_ref[...] += term

    @pl.when(level == LEVELS - 1)
    def _():
        out_ref[...] = total_ref[...].astype(jnp.bfloat16).reshape(out_ref.shape)


def project(blocks, weight):
    _, _, rows, depth = blocks[0].shape
    count = sum(b.shape[0] for b in blocks)
    width = weight.shape[2]
    return pl.pallas_call(
        project_kernel,
        grid=(LEVELS,),
        out_shape=jax.ShapeDtypeStruct((count, rows, width), jnp.bfloat16),
        in_specs=[
            pl.BlockSpec((b.shape[0], 1, rows, depth), lambda l: (0, l, 0, 0)) for b in blocks
        ]
        + [pl.BlockSpec((1, depth, width), lambda l: (l, 0, 0))],
        out_specs=pl.BlockSpec((count, rows, width), lambda l: (0, 0, 0)),
        scratch_shapes=[pltpu.VMEM((count * rows, width), jnp.float32)],
        compiler_params=PARAMS,
        cost_estimate=pl.CostEstimate(
            flops=2 * count * rows * LEVELS * depth * width,
            bytes_accessed=2 * (weight.size + count * rows * LEVELS * depth),
            transcendentals=0,
        ),
        name="project",
    )(*blocks, weight)


def place_kernel(meta_ref, *refs):
    *group_refs, keep_ref, send_ref, token_ref = refs
    core, x, y = meta_ref[0], meta_ref[1], meta_ref[2]
    rows = group_refs[0].shape[1]
    total = rows * X * Y
    edge = jnp.zeros((HALO, token_ref.shape[1]), jnp.float32)
    token_ref[pl.ds(0, HALO), :] = edge
    token_ref[pl.ds(HALO + total, HALO), :] = edge
    for second, group_ref in zip((0, 1, 2, 3), group_refs):
        for first in range(4):
            dx = jnp.where(core == 0, first, second)
            dy = jnp.where(core == 0, second, first)
            e = lax.rem(x + dx, X) * Y + lax.rem(y + dy, Y)
            at = pl.multiple_of(e * rows + HALO, 8)
            token_ref[pl.ds(at, rows), :] = group_ref[first].astype(jnp.float32)
    piece = total // (ZL * CORES)
    for zl in range(ZL):
        for out_ref, whose in ((keep_ref, core), (send_ref, 1 - core)):
            at = pl.multiple_of((zl * CORES + whose) * piece, 8)
            out_ref[zl] = token_ref[pl.ds(at, piece + 2 * HALO), :].astype(jnp.bfloat16)


def place(groups, core, x, y):
    _, rows, width = groups[0].shape
    total = rows * X * Y
    pieces = jax.ShapeDtypeStruct((ZL, total // (ZL * CORES) + 2 * HALO, width), jnp.bfloat16)
    return pl.pallas_call(
        place_kernel,
        out_shape=(pieces, pieces),
        in_specs=[SMEM] + [VMEM] * 4,
        out_specs=(VMEM, VMEM),
        scratch_shapes=[pltpu.VMEM((total + 2 * HALO, width), jnp.float32)],
        compiler_params=PARAMS,
        cost_estimate=pl.CostEstimate(
            flops=total * width, bytes_accessed=4 * total * width, transcendentals=0
        ),
        name="place",
    )(jnp.stack([core, x, y]), *groups)


def join_kernel(meta_ref, keep_ref, got_ref, own_ref, *away_refs):
    zl = meta_ref[0]

    def piece(index):
        return keep_ref[index].astype(jnp.float32) + got_ref[index].astype(jnp.float32)

    own_ref[...] = piece(zl).astype(jnp.bfloat16)
    for step, away_ref in zip((1, 2, 3), away_refs):
        away_ref[...] = piece(lax.rem(zl + ZL - step, ZL)).astype(jnp.bfloat16)


def join(keep, got, zl):
    piece = jax.ShapeDtypeStruct(keep.shape[1:], jnp.bfloat16)
    return pl.pallas_call(
        join_kernel,
        out_shape=(piece,) * ZL,
        in_specs=[SMEM, VMEM, VMEM],
        out_specs=(VMEM,) * ZL,
        compiler_params=PARAMS,
        cost_estimate=pl.CostEstimate(
            flops=keep.size, bytes_accessed=6 * keep.size, transcendentals=0
        ),
        name="join",
    )(zl.reshape(1), keep, got)


def sigmoid(v):
    return 1.0 / (1.0 + jnp.exp(-v))


def chain_kernel(meta_ref, scale_ref, *refs):
    *part_refs, high_ref, gain_ref, grad_ref = refs
    rows, width = part_refs[0].shape
    own = rows - 2 * HALO
    joined = part_refs[0][...].astype(jnp.float32)
    for part_ref in part_refs[1:]:
        joined = joined + part_ref[...].astype(jnp.float32)
    high = high_ref[...].astype(jnp.float32)
    gain = gain_ref[...]
    scale = scale_ref[0]
    start, length = meta_ref[0], meta_ref[1]
    position = start - HALO + lax.broadcasted_iota(jnp.int32, (rows, width), 0)

    def down(values):
        return jnp.concatenate([jnp.zeros((1, width), jnp.float32), values[:-1]], axis=0)

    def up(values):
        return jnp.concatenate([values[1:], jnp.zeros((1, width), jnp.float32)], axis=0)

    def target(step):
        lead = jnp.zeros((HALO - step, width), jnp.float32)
        return jnp.concatenate([lead, high[: rows - HALO + step]], axis=0)

    def state_and_slope(v):
        gate = sigmoid(v)
        return v * gate, gate * (1.0 + v * (1.0 - gate))

    def residual(state, step):
        return jnp.where(position + step < length, scale * (state - target(step)), 0.0)

    state_1, slope_1 = state_and_slope(joined)
    before_1 = down(state_1)
    state_2, slope_2 = state_and_slope(joined + gain * before_1)
    before_2 = down(state_2)
    state_3, slope_3 = state_and_slope(joined + gain * before_2)
    delta_3 = residual(state_3, 3) * slope_3
    delta_2 = (residual(state_2, 2) + up(gain * delta_3)) * slope_2
    delta_1 = (residual(state_1, 1) + up(gain * delta_2)) * slope_1
    total = delta_1 + delta_2 + delta_3
    mix = (delta_2 * before_1 + delta_3 * before_2)[HALO : HALO + own]
    rest = jnp.sum(mix, axis=0, keepdims=True)
    tail = []
    for _ in range(3):
        term = rest.astype(jnp.bfloat16).astype(jnp.float32)
        tail.append(term)
        rest = rest - term
    tail.append(jnp.zeros((TAIL - 3, width), jnp.float32))
    grad_ref[pl.ds(0, own), :] = total[HALO : HALO + own].astype(jnp.bfloat16)
    grad_ref[pl.ds(own, TAIL), :] = jnp.concatenate(tail, axis=0).astype(jnp.bfloat16)


def chain(parts, high, gain, start, length, scale):
    rows, width = parts[0].shape
    own = rows - 2 * HALO
    return pl.pallas_call(
        chain_kernel,
        out_shape=jax.ShapeDtypeStruct((own + TAIL, width), jnp.bfloat16),
        in_specs=[SMEM, SMEM] + [VMEM] * (len(parts) + 2),
        out_specs=VMEM,
        compiler_params=PARAMS,
        cost_estimate=pl.CostEstimate(
            flops=60 * rows * width, bytes_accessed=10 * rows * width, transcendentals=3 * rows * width
        ),
        name="chain",
    )(jnp.stack([start, length]), scale.reshape(1), *parts, high, gain.reshape(1, width))


def pieces_of(zl, zh, core):
    found = []

    def chip(step):
        z = lax.rem(zh * ZL + zl + step + ZL * ZH, ZL * ZH)
        return lax.rem(z, ZL), z // ZL

    layout = [(0, 0, 0, (0, 1, 2, 3)), (1, 0, 1, (0, 1, 2, 3))]
    layout += [(2, 1, 0, (0, 1, 2, 3)), (3, -1, 0, (0, 1, 2, 3))]
    layout += [(4, 1, 1, (0, 1, 2, 3)), (5, -1, 1, (0, 1, 2, 3))]
    layout += [(6, 2, 0, (2, 3)), (7, -2, 0, (1, 2)), (8, 2, 1, (2, 3)), (9, -2, 1, (1, 2))]
    for group, step, other, rows in layout:
        there_zl, there_zh = chip(step)
        member = there_zl * CORES + (1 - core if other else core)
        for at, row in enumerate(rows):
            found.append((group, at, member, lax.rem(there_zh + row, ZH)))
    return found


def weight_grad_kernel(meta_ref, features_ref, *refs):
    *group_refs, out_ref, mix_ref, grads_ref = refs
    zl, zh, core = meta_ref[0], meta_ref[1], meta_ref[2]
    half = grads_ref.shape[1] // ZH
    width = grads_ref.shape[2]

    @pl.when(pl.program_id(0) == 0)
    def _():
        mix = jnp.zeros((TAIL, width), jnp.float32)
        for group, at, member, sequence in pieces_of(zl, zh, core):
            rank = lax.rem(sequence - zh + ZH, ZH)
            slot = pl.ds(pl.multiple_of(rank * half, 16), half)
            for part in range(2):
                rows = group_refs[group][at, pl.ds(part * half, half), :]
                grads_ref[member * 2 + part, slot, :] = rows
            mix = mix + group_refs[group][at, pl.ds(2 * half, TAIL), :].astype(jnp.float32)
        mix_ref[...] = jnp.sum(mix, axis=0, keepdims=True)

    blocks = features_ref.shape[0]
    left = jnp.concatenate([features_ref[e, 0] for e in range(blocks)], axis=1)
    right = grads_ref[...].reshape(-1, width)
    out_ref[0] = jnp.dot(left, right, preferred_element_type=jnp.float32).astype(jnp.bfloat16)


def weight_grad(features, groups, zl, zh, core):
    draft, _, columns, tokens = features.shape
    width = groups[0].shape[2]
    whole = [pl.BlockSpec(g.shape, lambda l: (0, 0, 0)) for g in groups]
    return pl.pallas_call(
        weight_grad_kernel,
        grid=(LEVELS,),
        out_shape=(
            jax.ShapeDtypeStruct((LEVELS, columns, width), jnp.bfloat16),
            jax.ShapeDtypeStruct((1, width), jnp.float32),
        ),
        in_specs=[SMEM, pl.BlockSpec((draft, 1, columns, tokens), lambda l: (0, l, 0, 0))] + whole,
        out_specs=(
            pl.BlockSpec((1, columns, width), lambda l: (l, 0, 0)),
            pl.BlockSpec((1, width), lambda l: (0, 0)),
        ),
        scratch_shapes=[pltpu.VMEM((draft, tokens, width), jnp.bfloat16)],
        compiler_params=PARAMS,
        cost_estimate=pl.CostEstimate(
            flops=2 * draft * LEVELS * columns * tokens * width,
            bytes_accessed=2 * features.size + 2 * draft * tokens * width,
            transcendentals=0,
        ),
        name="weight_grad",
    )(jnp.stack([zl, zh, core]), features, *groups)


def valid_total(lengths):
    running = jnp.zeros((), jnp.float32)
    for unroll in range(1, UNROLL + 1):
        running = running + jnp.sum(jnp.maximum(lengths - unroll, 0)).astype(jnp.float32)
    return running


def high_halves(top, draft_index):
    members, draft_count = ZL * CORES, X * Y
    width = top.shape[1] // 2
    even = draft_index % 2 == 0
    left, right = top[:, :width], top[:, width:]
    first, second = [], []
    for t in range(members):
        for e in range(draft_count):
            target = e // 2 * draft_count + 2 * t
            first.append((t * draft_count + e, target + e % 2))
            second.append((t * draft_count + e, target + 1 - e % 2))
    axes = ("tp", "draft")
    one = lax.ppermute(jnp.where(even, left, right), axes, first)
    two = lax.ppermute(jnp.where(even, right, left), axes, second)
    return one, two


def high_rows(one, two, draft_index):
    even = draft_index % 2 == 0
    return jnp.concatenate([jnp.where(even, one, two), jnp.where(even, two, one)], axis=0)


def high_after(rows):
    return lax.ppermute(rows[:TAIL], "tp", [(j, j - 1) for j in range(1, ZL * CORES)])


def trade_columns(own, zh):
    part = own.shape[2] // ZH

    def quarter(index):
        return lax.dynamic_slice_in_dim(own, index * part, part, 2)

    blocks = [quarter(zh)]
    for step in (1, 2, 3):
        blocks.append(from_zh(quarter((zh + ZH - step) % ZH), step))
    return [b.transpose(0, 2, 1) for b in blocks]


def gather_grads(grad):
    stack = jnp.stack([grad] + [from_zh(grad, step) for step in (1, 2, 3)])
    above, below = from_z(stack, 1), from_z(stack, -1)
    other = from_other_core(stack)
    far_above, far_below = from_z(above[2:4], 1), from_z(below[1:3], -1)
    other_above, other_below = from_other_core(above), from_other_core(below)
    far = from_other_core(jnp.concatenate([far_above, far_below]))
    return [stack, other, above, below, other_above, other_below, far_above, far_below, far[:2], far[2:]]


def local(features, fc_weight, mix_gain, lengths):
    tp_index, zh = lax.axis_index("tp"), lax.axis_index("dp")
    draft_index = lax.axis_index("draft")
    zl, core = tp_index // CORES, tp_index % CORES
    x, y = draft_index // Y, draft_index % Y
    own_rows = features.shape[0]
    piece = own_rows * X * Y // (ZL * CORES)
    own = features.transpose(1, 0, 2)
    weight = fc_weight.transpose(1, 0, 2)

    along = jnp.stack([own] + [plane_move(step, True)(own) for step in (1, 2, 3)])
    along, later = lax.optimization_barrier((along, own))
    up, down = plane_move(1, False)(along), plane_move(-1, False)(along)
    traded = trade_columns(later, zh)
    halves = high_halves(later[LEVELS - 1], draft_index)
    zero = project([along], weight)
    up, down, traded, halves, zero = lax.optimization_barrier((up, down, traded, halves, zero))
    opposite = [plane_move(1, False)(up[:2]), plane_move(-1, False)(down[2:])]
    high = high_rows(*halves, draft_index)
    after = high_after(high)
    one, three = project([up], weight), project([down], weight)
    traded = jnp.concatenate(traded, axis=2)
    opposite, after, one, three, traded = lax.optimization_barrier((opposite, after, one, three, traded))
    every = lax.all_gather(traded, "draft", axis=0, tiled=False)
    groups = [zero, one, project(opposite, weight), three]
    high = jnp.concatenate([high, after], axis=0)

    keep, send = place(groups, core, x, y)
    mine, *away = join(keep, from_other_core(send), zl)
    parts = [mine] + [from_zl(block, step) for step, block in zip((1, 2, 3), away)]
    scale = LOSS_SCALE / valid_total(lengths)
    grad = chain(parts, high, mix_gain, tp_index * piece, lengths[zh], scale)
    fc_grad, mix_total = weight_grad(every, gather_grads(grad), zl, zh, core)
    return (fc_grad.transpose(1, 0, 2), mix_total[0])


def solution(mesh):
    placed = (P(("dp", "draft"), None, "tp"), P("tp", None, "draft"), P("draft"), P())
    return jax.shard_map(
        local,
        mesh=mesh,
        in_specs=placed,
        out_specs=(P(("tp", "dp"), None, "draft"), P("draft")),
        check_vma=False,
    )
```

time: 269 us -> 238 us (0.88)
  blocking collectives: 114 us -> 0 us
  starting transfers between devices: 15.3 us -> 109 us
  Pallas kernels: 2.81 us -> 20.1 us
  matrix products: 14.5 us -> 0 us
  local copies, waits for them, and re-layouts: 25.4 us -> 15.1 us
  waiting for transfers between devices: 74.1 us -> 68.5 us
  other arithmetic: 2.68 us -> 5.72 us
    ppermute x3 -> x28, starting transfers between devices: 9.57 us -> 109 us  [the longest x6 33.7 us: from_zh(): return lax.ppermute(block, 'dp', [((s + step) % ZH, s) for s in range(ZH)])]
    psum x1 -> x0, blocking collectives: 80.6 us -> none  [local(): mix_total = lax.psum(mix[0], ('tp', 'dp'))]
    all_gather x3 -> x1, waiting for transfers between devices: 53.4 us -> 0.01 us  [local(): every = lax.all_gather(traded, 'draft', axis=0, tiled=False)]
    ppermute x3 -> x28, waiting for transfers between devices: 19.9 us -> 68.5 us  [the longest x6 31 us: from_zh(): return lax.ppermute(block, 'dp', [((s + step) % ZH, s) for s in range(ZH)])]
    all_to_all x1 -> x0, blocking collectives: 33.2 us -> none  [local(): lax.all_to_all(own.reshape(LEVELS, own_rows, dp_count, part), 'dp', split...]
    pallas_call x1 -> x8, Pallas kernels: 2.81 us -> 20.1 us  [the longest x4 10.9 us: project(): pl.pallas_call(project_kernel, grid=(LEVELS,), out_shape=jax.ShapeDtypeSt...]
    dot_general x2 -> x0, matrix products: 14.5 us -> none  [the longest x1 8.29 us: local(): jnp.einsum('ltk,tn->lkn', every, grads, preferred_element_type=jnp.float32)]
    transpose x1 -> x0, local copies, waits for them, and re-layouts: 11.3 us -> none  [local(): every = every.transpose(1, 0, 2, 3).reshape(LEVELS, dp_count * rows, part)]
  transfers between devices with their start and end apart: 7 -> 29, of which waited for: 4 -> 12; matrix products, arithmetic and copies ran while one was open for 13% -> 2% of each run, Pallas kernels for 1% -> 6%
where the time goes in v2:
time: 238 us; the launch traced here: 235 us
  starting transfers between devices  109 us (46%)
  waiting for transfers between devices  68.5 us (29%)
  Pallas kernels  20.1 us (8%)
  between operations  16.6 us (7%)
  local copies, waits for them, and re-layouts  15.1 us (6%)
  other arithmetic  5.72 us (2%)
    ppermute x6, starting transfers between devices, from_zh(): return lax.ppermute(block, 'dp', [((s + step) % ZH, s) for s in range(ZH)])  33.7 us
    ppermute x6, waiting for transfers between devices, from_zh(): return lax.ppermute(block, 'dp', [((s + step) % ZH, s) for s in range(ZH)])  31 us
    ppermute x7, starting transfers between devices, plane_move(): return lambda block: lax.ppermute(block, ('tp', 'draft'), pairs)  26.3 us
    ppermute x4, waiting for transfers between devices, from_z(): return lax.ppermute(block, ('tp', 'dp'), pairs)  15.7 us
    ppermute x4, starting transfers between devices, from_z(): return lax.ppermute(block, ('tp', 'dp'), pairs)  13 us
    ppermute x5, starting transfers between devices, from_other_core(): return lax.ppermute(block, 'tp', [(t ^ 1, t) for t in range(ZL * CORES)])  12.6 us
    pallas_call x4, Pallas kernels, project(): pl.pallas_call(project_kernel, grid=(LEVELS,), out_shape=jax.ShapeDtypeSt...  10.9 us
    ppermute x1, starting transfers between devices, high_halves(): two = lax.ppermute(jnp.where(even, right, left), axes, second)  9.24 us
  transfers between devices with their start and end apart: 29, of which 12 were waited for; matrix products, arithmetic and copies ran while one was open for 2% of the time, Pallas kernels for 6%

profile of v2, /device:TPU:1, one launch (start us, length us, event | category | flops | bytes accessed | tf_op | source)
XLA Modules:
  0.0 235.3 jit_solution(11481692092380789098)
XLA Ops:
  7.2 4.0 %collective-permute-start.2 = (bf16[3,64,1024]{2,1,0:T(8,128)(2,1)}, bf16[3,64,1024]{2,1,0:T(8,128)(2,1)S(1)}, u32[]{:S(2)}, u32[]{:S(2)}) collective-permute-start(bf16[3,64,1024]{2,1,0:T(8,128)(2,1)} %bitcast.35), channel_id=1, source_target_pairs={{12,0},{13,1},{14,2},{15,3},{0,4},{1,5},{2,6},{3,7},{4,8},{5,9},{6... | collective-permute-start | bytes 1179656 | tf_op jit(solution)/shard_map/ppermute | solution.py:28
  11.3 4.5 %collective-permute-start.1 = (bf16[3,64,1024]{2,1,0:T(8,128)(2,1)}, bf16[3,64,1024]{2,1,0:T(8,128)(2,1)S(1)}, u32[]{:S(2)}, u32[]{:S(2)}) collective-permute-start(bf16[3,64,1024]{2,1,0:T(8,128)(2,1)} %bitcast.36), channel_id=1, source_target_pairs={{8,0},{9,1},{10,2},{11,3},{12,4},{13,5},{14,6},{15,7},{0,8},{1,9},... | collective-permute-start | bytes 1179656 | tf_op jit(solution)/shard_map/ppermute | solution.py:28
  15.8 3.0 %collective-permute-start = (bf16[3,64,1024]{2,1,0:T(8,128)(2,1)}, bf16[3,64,1024]{2,1,0:T(8,128)(2,1)S(1)}, u32[]{:S(2)}, u32[]{:S(2)}) collective-permute-start(bf16[3,64,1024]{2,1,0:T(8,128)(2,1)} %bitcast.37), channel_id=1, source_target_pairs={{4,0},{5,1},{6,2},{7,3},{8,4},{9,5},{10,6},{11,7},{12,8},{13,9},{1... | collective-permute-start | bytes 1179656 | tf_op jit(solution)/shard_map/ppermute | solution.py:28
  18.8 4.9 %collective-permute-done.1 = bf16[3,64,1024]{2,1,0:T(8,128)(2,1)S(1)} collective-permute-done((bf16[3,64,1024]{2,1,0:T(8,128)(2,1)}, bf16[3,64,1024]{2,1,0:T(8,128)(2,1)S(1)}, u32[]{:S(2)}, u32[]{:S(2)}) %collective-permute-start.1) | collective-permute-done | bytes 393248 | tf_op jit(solution)/shard_map/ppermute | solution.py:28
  23.7 1.3 collective-permute-done
  25.1 2.5 %pad_maximum_fusion.refs_0_ = bf16[4,3,64,1024]{3,2,1,0:T(8,128)(2,1)} fusion(bf16[1,3,64,1024]{3,2,1,0:T(8,128)(2,1)S(1)} %bitcast.41, bf16[1,3,64,1024]{3,2,1,0:T(8,128)(2,1)S(1)} %bitcast.42, bf16[1,3,64,1024]{3,2,1,0:T(8,128)(2,1)S(1)} %bitcast.43, bf16[1,3,64,1024]{3,2,1,0:T(8,128)(2,1)} %bitcast.38), kind=kLoop, calls=%fused_computation | loop fusion | flops 2359296 | bytes 3145728 | tf_op jit(solution)/shard_map/stack | solution.py:368
  27.6 3.1 %collective-permute-start.4 = (bf16[4,3,64,1024]{3,2,1,0:T(8,128)(2,1)}, bf16[4,3,64,1024]{3,2,1,0:T(8,128)(2,1)}, u32[]{:S(2)}, u32[]{:S(2)}) collective-permute-start(bf16[4,3,64,1024]{3,2,1,0:T(8,128)(2,1)} %pad_maximum_fusion.refs_0_), channel_id=1, source_target_pairs={{3,0},{0,1},{1,2},{2,3},{7,4},{4,5},{5,6},{6,7},{11,8},{8,9},{9,10... | collective-permute-start | bytes 4718600 | tf_op jit(solution)/shard_map/ppermute | solution.py:28
  30.7 3.4 %collective-permute-start.3 = (bf16[4,3,64,1024]{3,2,1,0:T(8,128)(2,1)}, bf16[4,3,64,1024]{3,2,1,0:T(8,128)(2,1)}, u32[]{:S(2)}, u32[]{:S(2)}) collective-permute-start(bf16[4,3,64,1024]{3,2,1,0:T(8,128)(2,1)} %pad_maximum_fusion.refs_0_), channel_id=1, source_target_pairs={{1,0},{2,1},{3,2},{0,3},{5,4},{6,5},{7,6},{4,7},{9,8},{10,9},{11,1... | collective-permute-start | bytes 4718600 | tf_op jit(solution)/shard_map/ppermute | solution.py:28
  34.1 0.9 slice_bitcast_fusion
  35.1 9.2 %collective-permute-start.9 = (bf16[64,512]{1,0:T(8,128)(2,1)S(1)}, bf16[64,512]{1,0:T(8,128)(2,1)S(1)}, u32[]{:S(2)}, u32[]{:S(2)}) collective-permute-start(bf16[64,512]{1,0:T(8,128)(2,1)S(1)} %get-tuple-element.63), channel_id=1, source_target_pairs={{0,1},{1,0},{2,65},{3,64},{4,129},{5,128},{6,193},{7,192},{8,257},... | collective-permute-start | bytes 196616 | tf_op jit(solution)/shard_map/ppermute | solution.py:323
  44.3 1.9 collective-permute-start.8
  46.3 5.8 %collective-permute-start.7 = (bf16[3,64,256]{2,1,0:T(8,128)(2,1)S(1)}, bf16[3,64,256]{2,1,0:T(8,128)(2,1)S(1)}, u32[]{:S(2)}, u32[]{:S(2)}) collective-permute-start(bf16[3,64,256]{2,1,0:T(8,128)(2,1)S(1)} %get-tuple-element.57), channel_id=1, source_target_pairs={{48,0},{0,16},{16,32},{32,48},{49,1},{1,17},{17,33},{33,49},{50,2}... | collective-permute-start | bytes 294920 | tf_op jit(solution)/shard_map/ppermute | solution.py:41
  52.1 7.0 %collective-permute-done.9 = bf16[64,512]{1,0:T(8,128)(2,1)S(1)} collective-permute-done((bf16[64,512]{1,0:T(8,128)(2,1)S(1)}, bf16[64,512]{1,0:T(8,128)(2,1)S(1)}, u32[]{:S(2)}, u32[]{:S(2)}) %collective-permute-start.9) | collective-permute-done | bytes 65568 | tf_op jit(solution)/shard_map/ppermute | solution.py:323
  59.2 9.3 %collective-permute-start.6 = (bf16[3,64,256]{2,1,0:T(8,128)(2,1)S(1)}, bf16[3,64,256]{2,1,0:T(8,128)(2,1)S(1)}, u32[]{:S(2)}, u32[]{:S(2)}) collective-permute-start(bf16[3,64,256]{2,1,0:T(8,128)(2,1)S(1)} %get-tuple-element.58), channel_id=1, source_target_pairs={{32,0},{48,16},{0,32},{16,48},{33,1},{49,17},{1,33},{17,49},{34,2}... | collective-permute-start | bytes 294920 | tf_op jit(solution)/shard_map/ppermute | solution.py:41
  68.5 1.9 collective-permute-start.5
  70.4 3.1 %project.4.refs_0_ = bf16[4,64,512]{2,1,0:T(8,128)(2,1)S(1)} custom-call(bf16[4,3,64,1024]{3,2,1,0:T(8,128)(2,1)} %pad_maximum_fusion.refs_0_, bf16[3,1024,512]{2,1,0:T(8,128)(2,1)S(1)} %bitcast.29), custom_call_target="tpu_custom_call" | custom-call | flops 805306368 | bytes 4718592 | tf_op jit(solution)/shard_map/project/pallas_call | solution.py:76
  73.6 6.9 %collective-permute-done.6 = bf16[3,64,256]{2,1,0:T(8,128)(2,1)S(1)} collective-permute-done((bf16[3,64,256]{2,1,0:T(8,128)(2,1)S(1)}, bf16[3,64,256]{2,1,0:T(8,128)(2,1)S(1)}, u32[]{:S(2)}, u32[]{:S(2)}) %collective-permute-start.6) | collective-permute-done | bytes 98336 | tf_op jit(solution)/shard_map/ppermute | solution.py:41
  80.5 1.3 collective-permute-done.5
  81.8 1.2 slice.33
  83.0 1.2 slice.34
  84.2 6.4 %collective-permute-start.11 = (bf16[2,3,64,1024]{3,2,1,0:T(8,128)(2,1)S(1)}, bf16[2,3,64,1024]{3,2,1,0:T(8,128)(2,1)S(1)}, u32[]{:S(2)}, u32[]{:S(2)}) collective-permute-start(bf16[2,3,64,1024]{3,2,1,0:T(8,128)(2,1)S(1)} %slice.34), channel_id=1, source_target_pairs={{3,0},{0,1},{1,2},{2,3},{7,4},{4,5},{5,6},{6,7},{11,8},{8,9},{9,10... | collective-permute-start | bytes 2359304 | tf_op jit(solution)/shard_map/ppermute | solution.py:28
  90.6 1.9 collective-permute-start.10
  92.6 4.3 %collective-permute-start.12 = (bf16[16,512]{1,0:T(8,128)(2,1)S(1)}, bf16[16,512]{1,0:T(8,128)(2,1)S(1)}, u32[]{:S(2)}, u32[]{:S(2)}) collective-permute-start(bf16[16,512]{1,0:T(8,128)(2,1)S(1)} %slice.42), channel_id=1, source_target_pairs={{64,0},{128,64},{192,128},{256,192},{320,256},{384,320},{448,384},... | collective-permute-start | bytes 49160 | tf_op jit(solution)/shard_map/ppermute | solution.py:333
  96.9 3.1 %project.5.refs_1_ = bf16[4,64,512]{2,1,0:T(8,128)(2,1)S(1)} custom-call(bf16[4,3,64,1024]{3,2,1,0:T(8,128)(2,1)} %collective-permute-done.3.refs_0_, bf16[3,1024,512]{2,1,0:T(8,128)(2,1)S(1)} %bitcast.30), custom_call_target="tpu_custom_call" | custom-call | flops 805306368 | bytes 4718592 | tf_op jit(solution)/shard_map/project/pallas_call | solution.py:76
  100.0 0.9 pad_maximum_fusion.3
  100.8 3.1 %project.6.refs_3_ = bf16[4,64,512]{2,1,0:T(8,128)(2,1)S(1)} custom-call(bf16[4,3,64,1024]{3,2,1,0:T(8,128)(2,1)} %collective-permute-done.4.refs_0_, bf16[3,1024,512]{2,1,0:T(8,128)(2,1)S(1)} %bitcast.31), custom_call_target="tpu_custom_call" | custom-call | flops 805306368 | bytes 4718592 | tf_op jit(solution)/shard_map/project/pallas_call | solution.py:76
  104.0 0.7 copy-done.3
  104.7 0.9 copy-done.5
  105.6 0.9 copy-done.7
  106.4 1.9 copy.7
  108.5 1.1 copy-done.6
  109.6 1.1 copy-done.8
  110.8 1.6 project.7.refs_2_
  112.4 0.8 place.1
  113.3 1.9 collective-permute-start.13
  115.2 1.2 dynamic_slice.19
  116.4 1.4 maximum_reduce_fusion
  118.0 3.3 %collective-permute-start.14 = (bf16[144,512]{1,0:T(8,128)(2,1)S(1)}, bf16[144,512]{1,0:T(8,128)(2,1)S(1)}, u32[]{:S(2)}, u32[]{:S(2)}) collective-permute-start(bf16[144,512]{1,0:T(8,128)(2,1)S(1)} %get-tuple-element.46), channel_id=1, source_target_pairs={{128,0},{192,64},{256,128},{320,192},{384,256},{448,320},{0,384},{... | collective-permute-start | bytes 442376 | tf_op jit(solution)/shard_map/ppermute | solution.py:37
  121.3 1.9 collective-permute-start.15
  123.2 2.8 %collective-permute-start.16 = (bf16[144,512]{1,0:T(8,128)(2,1)S(1)}, bf16[144,512]{1,0:T(8,128)(2,1)S(1)}, u32[]{:S(2)}, u32[]{:S(2)}) collective-permute-start(bf16[144,512]{1,0:T(8,128)(2,1)S(1)} %get-tuple-element.48), channel_id=1, source_target_pairs={{384,0},{448,64},{0,128},{64,192},{128,256},{192,320},{256,384},{3... | collective-permute-start | bytes 442376 | tf_op jit(solution)/shard_map/ppermute | solution.py:37
  128.6 7.5 %collective-permute-done.15.refs_2_ = bf16[144,512]{1,0:T(8,128)(2,1)S(1)} collective-permute-done((bf16[144,512]{1,0:T(8,128)(2,1)S(1)}, bf16[144,512]{1,0:T(8,128)(2,1)S(1)}, u32[]{:S(2)}, u32[]{:S(2)}) %collective-permute-start.15) | collective-permute-done | bytes 147488 | tf_op jit(solution)/shard_map/ppermute | solution.py:37
  136.1 1.4 chain.1
  137.5 6.8 %collective-permute-start.19 = (bf16[144,512]{1,0:T(8,128)(2,1)S(1)}, bf16[144,512]{1,0:T(8,128)(2,1)S(1)}, u32[]{:S(2)}, u32[]{:S(2)}) collective-permute-start(bf16[144,512]{1,0:T(8,128)(2,1)S(1)} %chain.1), channel_id=1, source_target_pairs={{48,0},{0,16},{16,32},{32,48},{49,1},{1,17},{17,33},{33,49},{50,2}... | collective-permute-start | bytes 442376 | tf_op jit(solution)/shard_map/ppermute | solution.py:41
  144.2 5.3 %collective-permute-start.18 = (bf16[144,512]{1,0:T(8,128)(2,1)S(1)}, bf16[144,512]{1,0:T(8,128)(2,1)S(1)}, u32[]{:S(2)}, u32[]{:S(2)}) collective-permute-start(bf16[144,512]{1,0:T(8,128)(2,1)S(1)} %chain.1), channel_id=1, source_target_pairs={{32,0},{48,16},{0,32},{16,48},{33,1},{49,17},{1,33},{17,49},{34,2}... | collective-permute-start | bytes 442376 | tf_op jit(solution)/shard_map/ppermute | solution.py:41
  149.5 4.7 %collective-permute-start.17 = (bf16[144,512]{1,0:T(8,128)(2,1)S(1)}, bf16[144,512]{1,0:T(8,128)(2,1)S(1)}, u32[]{:S(2)}, u32[]{:S(2)}) collective-permute-start(bf16[144,512]{1,0:T(8,128)(2,1)S(1)} %chain.1), channel_id=1, source_target_pairs={{16,0},{32,16},{48,32},{0,48},{17,1},{33,17},{49,33},{1,49},{18,2}... | collective-permute-start | bytes 442376 | tf_op jit(solution)/shard_map/ppermute | solution.py:41
  154.2 9.2 %collective-permute-done.18 = bf16[144,512]{1,0:T(8,128)(2,1)S(1)} collective-permute-done((bf16[144,512]{1,0:T(8,128)(2,1)S(1)}, bf16[144,512]{1,0:T(8,128)(2,1)S(1)}, u32[]{:S(2)}, u32[]{:S(2)}) %collective-permute-start.18) | collective-permute-done | bytes 147488 | tf_op jit(solution)/shard_map/ppermute | solution.py:41
  163.4 13.6 %collective-permute-done.17 = bf16[144,512]{1,0:T(8,128)(2,1)S(1)} collective-permute-done((bf16[144,512]{1,0:T(8,128)(2,1)S(1)}, bf16[144,512]{1,0:T(8,128)(2,1)S(1)}, u32[]{:S(2)}, u32[]{:S(2)}) %collective-permute-start.17) | collective-permute-done | bytes 147488 | tf_op jit(solution)/shard_map/ppermute | solution.py:41
  177.1 1.9 collective-permute-start.22
  179.0 4.6 %collective-permute-start.21 = (bf16[4,144,512]{2,1,0:T(8,128)(2,1)S(1)}, bf16[4,144,512]{2,1,0:T(8,128)(2,1)S(1)}, u32[]{:S(2)}, u32[]{:S(2)}) collective-permute-start(bf16[4,144,512]{2,1,0:T(8,128)(2,1)S(1)} %pad_maximum_fusion.1.refs_0_), channel_id=1, source_target_pairs={{128,0},{144,16},{160,32},{176,48},{192,64},{208,80},{224,96},{240... | collective-permute-start | bytes 1769480 | tf_op jit(solution)/shard_map/ppermute | solution.py:50
  183.6 11.0 %collective-permute-done.22.refs_3_ = bf16[4,144,512]{2,1,0:T(8,128)(2,1)S(1)} collective-permute-done((bf16[4,144,512]{2,1,0:T(8,128)(2,1)S(1)}, bf16[4,144,512]{2,1,0:T(8,128)(2,1)S(1)}, u32[]{:S(2)}, u32[]{:S(2)}) %collective-permute-start.22) | collective-permute-done | bytes 589856 | tf_op jit(solution)/shard_map/ppermute | solution.py:50
  194.6 1.9 collective-permute-start.26
  196.6 4.6 %collective-permute-start.25 = (bf16[2,144,512]{2,1,0:T(8,128)(2,1)S(1)}, bf16[2,144,512]{2,1,0:T(8,128)(2,1)S(1)}, u32[]{:S(2)}, u32[]{:S(2)}) collective-permute-start(bf16[2,144,512]{2,1,0:T(8,128)(2,1)S(1)} %slice.43), channel_id=1, source_target_pairs={{128,0},{144,16},{160,32},{176,48},{192,64},{208,80},{224,96},{240... | collective-permute-start | bytes 884744 | tf_op jit(solution)/shard_map/ppermute | solution.py:50
  201.2 3.7 %collective-permute-done.26.refs_7_ = bf16[2,144,512]{2,1,0:T(8,128)(2,1)S(1)} collective-permute-done((bf16[2,144,512]{2,1,0:T(8,128)(2,1)S(1)}, bf16[2,144,512]{2,1,0:T(8,128)(2,1)S(1)}, u32[]{:S(2)}, u32[]{:S(2)}) %collective-permute-start.26) | collective-permute-done | bytes 294944 | tf_op jit(solution)/shard_map/ppermute | solution.py:50
  204.9 0.9 collective-permute-done.25.refs_6_
  205.9 4.4 %collective-permute-start.27 = (bf16[4,144,512]{2,1,0:T(8,128)(2,1)S(1)}, bf16[4,144,512]{2,1,0:T(8,128)(2,1)S(1)}, u32[]{:S(2)}, u32[]{:S(2)}) collective-permute-start(bf16[4,144,512]{2,1,0:T(8,128)(2,1)S(1)} %pad_maximum_fusion.2), channel_id=1, source_target_pairs={{64,0},{0,64},{192,128},{128,192},{320,256},{256,320},{448,384},{3... | collective-permute-start | bytes 1769480 | tf_op jit(solution)/shard_map/ppermute | solution.py:32
  210.3 1.9 collective-permute-start.20
  212.3 2.4 %collective-permute-start.24 = (bf16[4,144,512]{2,1,0:T(8,128)(2,1)S(1)}, bf16[4,144,512]{2,1,0:T(8,128)(2,1)S(1)}, u32[]{:S(2)}, u32[]{:S(2)}) collective-permute-start(bf16[4,144,512]{2,1,0:T(8,128)(2,1)S(1)} %collective-permute-done.22.refs_3_), channel_id=1, source_target_pairs={{64,0},{0,64},{192,128},{128,192},{320,256},{256,320},{448,384},{3... | collective-permute-start | bytes 1769480 | tf_op jit(solution)/shard_map/ppermute | solution.py:32
  214.7 1.9 collective-permute-start.23
  216.8 0.8 copy-done.10
  217.5 1.0 collective-permute-done.23.refs_4_
  218.6 0.8 copy-done.12
  219.4 1.1 copy-done.11
  220.5 1.1 copy-done.13
  221.5 6.9 %weight_grad.1 = (bf16[3,256,512]{2,1,0:T(8,128)(2,1)}, f32[1,512]{1,0:T(1,128)}) custom-call(s32[3]{0:T(128)S(1)} %pad_add_fusion.meta_ref, bf16[16,3,256,256]{3,2,1,0:T(8,128)(2,1)} %bitcast.50, bf16[4,144,512]{2,1,0:T(8,128)(2,1)S(1)} %pad_maximum_fusion.1.refs_0_, bf16[4,144,512]{2,1,0:T(8,128)(2,1)S(1)} %collective-permute-done.20.refs_1_, ...), custom_call_target="tpu_custom_call" | custom-call | flops 3221225472 | bytes 10485760 | tf_op jit(solution)/shard_map/weight_grad/pallas_call | solution.py:280
  (54 shorter events, 1.4 us)
Async XLA Ops:
  7.2 212.2 %all-gather.3.cloned.1.call-start = ((), (), s32[]{:S(2)}) async-start(), calls=%async_computation | async-start | bytes 6684672 | tf_op jit(solution)/shard_map/all_gather | solution.py:381
  7.2 11.6 %collective-permute-start.2 = (bf16[3,64,1024]{2,1,0:T(8,128)(2,1)}, bf16[3,64,1024]{2,1,0:T(8,128)(2,1)S(1)}, u32[]{:S(2)}, u32[]{:S(2)}) collective-permute-start(bf16[3,64,1024]{2,1,0:T(8,128)(2,1)} %bitcast.35), channel_id=1, source_target_pairs={{12,0},{13,1},{14,2},{15,3},{0,4},{1,5},{2,6},{3,7},{4,8},{5,9},{6... | collective-permute-start | bytes 1179656 | tf_op jit(solution)/shard_map/ppermute | solution.py:28
  11.3 12.5 %collective-permute-start.1 = (bf16[3,64,1024]{2,1,0:T(8,128)(2,1)}, bf16[3,64,1024]{2,1,0:T(8,128)(2,1)S(1)}, u32[]{:S(2)}, u32[]{:S(2)}) collective-permute-start(bf16[3,64,1024]{2,1,0:T(8,128)(2,1)} %bitcast.36), channel_id=1, source_target_pairs={{8,0},{9,1},{10,2},{11,3},{12,4},{13,5},{14,6},{15,7},{0,8},{1,9},... | collective-permute-start | bytes 1179656 | tf_op jit(solution)/shard_map/ppermute | solution.py:28
  15.8 9.3 %collective-permute-start = (bf16[3,64,1024]{2,1,0:T(8,128)(2,1)}, bf16[3,64,1024]{2,1,0:T(8,128)(2,1)S(1)}, u32[]{:S(2)}, u32[]{:S(2)}) collective-permute-start(bf16[3,64,1024]{2,1,0:T(8,128)(2,1)} %bitcast.37), channel_id=1, source_target_pairs={{4,0},{5,1},{6,2},{7,3},{8,4},{9,5},{10,6},{11,7},{12,8},{13,9},{1... | collective-permute-start | bytes 1179656 | tf_op jit(solution)/shard_map/ppermute | solution.py:28
  25.1 21.2 %copy-start.14 = (bf16[64,3,1024]{2,0,1:T(8,128)(2,1)S(1)}, bf16[64,3,1024]{2,0,1:T(8,128)(2,1)}, u32[]{:S(2)}) copy-start(bf16[64,3,1024]{2,0,1:T(8,128)(2,1)} %param.4) | copy-start | bytes 1179652
  25.1 45.4 %copy-start = (bf16[1024,3,512]{2,0,1:T(8,128)(2,1)S(1)}, bf16[1024,3,512]{2,0,1:T(8,128)(2,1)}, u32[]{:S(2)}) copy-start(bf16[1024,3,512]{2,0,1:T(8,128)(2,1)} %param.5) | copy-start | bytes 9437188
  27.6 54.2 %collective-permute-start.4 = (bf16[4,3,64,1024]{3,2,1,0:T(8,128)(2,1)}, bf16[4,3,64,1024]{3,2,1,0:T(8,128)(2,1)}, u32[]{:S(2)}, u32[]{:S(2)}) collective-permute-start(bf16[4,3,64,1024]{3,2,1,0:T(8,128)(2,1)} %pad_maximum_fusion.refs_0_), channel_id=1, source_target_pairs={{3,0},{0,1},{1,2},{2,3},{7,4},{4,5},{5,6},{6,7},{11,8},{8,9},{9,10... | collective-permute-start | bytes 4718600 | tf_op jit(solution)/shard_map/ppermute | solution.py:28
  30.7 51.1 %collective-permute-start.3 = (bf16[4,3,64,1024]{3,2,1,0:T(8,128)(2,1)}, bf16[4,3,64,1024]{3,2,1,0:T(8,128)(2,1)}, u32[]{:S(2)}, u32[]{:S(2)}) collective-permute-start(bf16[4,3,64,1024]{3,2,1,0:T(8,128)(2,1)} %pad_maximum_fusion.refs_0_), channel_id=1, source_target_pairs={{1,0},{2,1},{3,2},{0,3},{5,4},{6,5},{7,6},{4,7},{9,8},{10,9},{11,1... | collective-permute-start | bytes 4718600 | tf_op jit(solution)/shard_map/ppermute | solution.py:28
  35.1 24.1 %collective-permute-start.9 = (bf16[64,512]{1,0:T(8,128)(2,1)S(1)}, bf16[64,512]{1,0:T(8,128)(2,1)S(1)}, u32[]{:S(2)}, u32[]{:S(2)}) collective-permute-start(bf16[64,512]{1,0:T(8,128)(2,1)S(1)} %get-tuple-element.63), channel_id=1, source_target_pairs={{0,1},{1,0},{2,65},{3,64},{4,129},{5,128},{6,193},{7,192},{8,257},... | collective-permute-start | bytes 196616 | tf_op jit(solution)/shard_map/ppermute | solution.py:323
  44.3 24.2 %collective-permute-start.8 = (bf16[64,512]{1,0:T(8,128)(2,1)S(1)}, bf16[64,512]{1,0:T(8,128)(2,1)S(1)}, u32[]{:S(2)}, u32[]{:S(2)}) collective-permute-start(bf16[64,512]{1,0:T(8,128)(2,1)S(1)} %get-tuple-element.64), channel_id=1, source_target_pairs={{0,0},{1,1},{2,64},{3,65},{4,128},{5,129},{6,192},{7,193},{8,256},... | collective-permute-start | bytes 196616 | tf_op jit(solution)/shard_map/ppermute | solution.py:322
  46.3 27.2 %collective-permute-start.7 = (bf16[3,64,256]{2,1,0:T(8,128)(2,1)S(1)}, bf16[3,64,256]{2,1,0:T(8,128)(2,1)S(1)}, u32[]{:S(2)}, u32[]{:S(2)}) collective-permute-start(bf16[3,64,256]{2,1,0:T(8,128)(2,1)S(1)} %get-tuple-element.57), channel_id=1, source_target_pairs={{48,0},{0,16},{16,32},{32,48},{49,1},{1,17},{17,33},{33,49},{50,2}... | collective-permute-start | bytes 294920 | tf_op jit(solution)/shard_map/ppermute | solution.py:41
  59.2 21.3 %collective-permute-start.6 = (bf16[3,64,256]{2,1,0:T(8,128)(2,1)S(1)}, bf16[3,64,256]{2,1,0:T(8,128)(2,1)S(1)}, u32[]{:S(2)}, u32[]{:S(2)}) collective-permute-start(bf16[3,64,256]{2,1,0:T(8,128)(2,1)S(1)} %get-tuple-element.58), channel_id=1, source_target_pairs={{32,0},{48,16},{0,32},{16,48},{33,1},{49,17},{1,33},{17,49},{34,2}... | collective-permute-start | bytes 294920 | tf_op jit(solution)/shard_map/ppermute | solution.py:41
  68.5 13.3 %collective-permute-start.5 = (bf16[3,64,256]{2,1,0:T(8,128)(2,1)S(1)}, bf16[3,64,256]{2,1,0:T(8,128)(2,1)S(1)}, u32[]{:S(2)}, u32[]{:S(2)}) collective-permute-start(bf16[3,64,256]{2,1,0:T(8,128)(2,1)S(1)} %get-tuple-element.59), channel_id=1, source_target_pairs={{16,0},{32,16},{48,32},{0,48},{17,1},{33,17},{49,33},{1,49},{18,2}... | collective-permute-start | bytes 294920 | tf_op jit(solution)/shard_map/ppermute | solution.py:41
  84.2 20.5 %collective-permute-start.11 = (bf16[2,3,64,1024]{3,2,1,0:T(8,128)(2,1)S(1)}, bf16[2,3,64,1024]{3,2,1,0:T(8,128)(2,1)S(1)}, u32[]{:S(2)}, u32[]{:S(2)}) collective-permute-start(bf16[2,3,64,1024]{3,2,1,0:T(8,128)(2,1)S(1)} %slice.34), channel_id=1, source_target_pairs={{3,0},{0,1},{1,2},{2,3},{7,4},{4,5},{5,6},{6,7},{11,8},{8,9},{9,10... | collective-permute-start | bytes 2359304 | tf_op jit(solution)/shard_map/ppermute | solution.py:28
  90.6 15.0 %collective-permute-start.10 = (bf16[2,3,64,1024]{3,2,1,0:T(8,128)(2,1)S(1)}, bf16[2,3,64,1024]{3,2,1,0:T(8,128)(2,1)S(1)}, u32[]{:S(2)}, u32[]{:S(2)}) collective-permute-start(bf16[2,3,64,1024]{3,2,1,0:T(8,128)(2,1)S(1)} %slice.33), channel_id=1, source_target_pairs={{1,0},{2,1},{3,2},{0,3},{5,4},{6,5},{7,6},{4,7},{9,8},{10,9},{11,1... | collective-permute-start | bytes 2359304 | tf_op jit(solution)/shard_map/ppermute | solution.py:28
  92.6 12.1 %collective-permute-start.12 = (bf16[16,512]{1,0:T(8,128)(2,1)S(1)}, bf16[16,512]{1,0:T(8,128)(2,1)S(1)}, u32[]{:S(2)}, u32[]{:S(2)}) collective-permute-start(bf16[16,512]{1,0:T(8,128)(2,1)S(1)} %slice.42), channel_id=1, source_target_pairs={{64,0},{128,64},{192,128},{256,192},{320,256},{384,320},{448,384},... | collective-permute-start | bytes 49160 | tf_op jit(solution)/shard_map/ppermute | solution.py:333
  100.0 4.0 %copy-start.1 = (bf16[4,64,512]{2,1,0:T(8,128)(2,1)}, bf16[4,64,512]{2,1,0:T(8,128)(2,1)S(1)}, u32[]{:S(2)}) copy-start(bf16[4,64,512]{2,1,0:T(8,128)(2,1)S(1)} %project.5.refs_1_) | copy-start | bytes 786436
  103.9 0.7 copy-start.3
  104.7 0.9 copy-start.5
  105.6 0.9 copy-start.7
  108.5 1.1 copy-start.6
  109.6 1.1 copy-start.8
  110.8 1.6 copy-start.2
  110.8 1.6 copy-start.4
  112.4 23.7 %copy-start.9 = (f32[512]{0:T(512)S(1)}, f32[512]{0:T(512)}, u32[]{:S(2)}) copy-start(f32[512]{0:T(512)} %param.6) | copy-start | bytes 6148
  113.3 4.6 %collective-permute-start.13 = (bf16[4,144,512]{2,1,0:T(8,128)(2,1)S(1)}, bf16[4,144,512]{2,1,0:T(8,128)(2,1)S(1)}, u32[]{:S(2)}, u32[]{:S(2)}) collective-permute-start(bf16[4,144,512]{2,1,0:T(8,128)(2,1)S(1)} %get-tuple-element.44), channel_id=1, source_target_pairs={{64,0},{0,64},{192,128},{128,192},{320,256},{256,320},{448,384},{3... | collective-permute-start | bytes 1769480 | tf_op jit(solution)/shard_map/ppermute | solution.py:32
  118.0 10.6 %collective-permute-start.14 = (bf16[144,512]{1,0:T(8,128)(2,1)S(1)}, bf16[144,512]{1,0:T(8,128)(2,1)S(1)}, u32[]{:S(2)}, u32[]{:S(2)}) collective-permute-start(bf16[144,512]{1,0:T(8,128)(2,1)S(1)} %get-tuple-element.46), channel_id=1, source_target_pairs={{128,0},{192,64},{256,128},{320,192},{384,256},{448,320},{0,384},{... | collective-permute-start | bytes 442376 | tf_op jit(solution)/shard_map/ppermute | solution.py:37
  121.3 14.8 %collective-permute-start.15 = (bf16[144,512]{1,0:T(8,128)(2,1)S(1)}, bf16[144,512]{1,0:T(8,128)(2,1)S(1)}, u32[]{:S(2)}, u32[]{:S(2)}) collective-permute-start(bf16[144,512]{1,0:T(8,128)(2,1)S(1)} %get-tuple-element.47), channel_id=1, source_target_pairs={{256,0},{320,64},{384,128},{448,192},{0,256},{64,320},{128,384},{1... | collective-permute-start | bytes 442376 | tf_op jit(solution)/shard_map/ppermute | solution.py:37
  123.2 12.9 %collective-permute-start.16 = (bf16[144,512]{1,0:T(8,128)(2,1)S(1)}, bf16[144,512]{1,0:T(8,128)(2,1)S(1)}, u32[]{:S(2)}, u32[]{:S(2)}) collective-permute-start(bf16[144,512]{1,0:T(8,128)(2,1)S(1)} %get-tuple-element.48), channel_id=1, source_target_pairs={{384,0},{448,64},{0,128},{64,192},{128,256},{192,320},{256,384},{3... | collective-permute-start | bytes 442376 | tf_op jit(solution)/shard_map/ppermute | solution.py:37
  137.5 16.7 %collective-permute-start.19 = (bf16[144,512]{1,0:T(8,128)(2,1)S(1)}, bf16[144,512]{1,0:T(8,128)(2,1)S(1)}, u32[]{:S(2)}, u32[]{:S(2)}) collective-permute-start(bf16[144,512]{1,0:T(8,128)(2,1)S(1)} %chain.1), channel_id=1, source_target_pairs={{48,0},{0,16},{16,32},{32,48},{49,1},{1,17},{17,33},{33,49},{50,2}... | collective-permute-start | bytes 442376 | tf_op jit(solution)/shard_map/ppermute | solution.py:41
  144.2 19.2 %collective-permute-start.18 = (bf16[144,512]{1,0:T(8,128)(2,1)S(1)}, bf16[144,512]{1,0:T(8,128)(2,1)S(1)}, u32[]{:S(2)}, u32[]{:S(2)}) collective-permute-start(bf16[144,512]{1,0:T(8,128)(2,1)S(1)} %chain.1), channel_id=1, source_target_pairs={{32,0},{48,16},{0,32},{16,48},{33,1},{49,17},{1,33},{17,49},{34,2}... | collective-permute-start | bytes 442376 | tf_op jit(solution)/shard_map/ppermute | solution.py:41
  149.5 27.5 %collective-permute-start.17 = (bf16[144,512]{1,0:T(8,128)(2,1)S(1)}, bf16[144,512]{1,0:T(8,128)(2,1)S(1)}, u32[]{:S(2)}, u32[]{:S(2)}) collective-permute-start(bf16[144,512]{1,0:T(8,128)(2,1)S(1)} %chain.1), channel_id=1, source_target_pairs={{16,0},{32,16},{48,32},{0,48},{17,1},{33,17},{49,33},{1,49},{18,2}... | collective-permute-start | bytes 442376 | tf_op jit(solution)/shard_map/ppermute | solution.py:41
  177.1 17.5 %collective-permute-start.22 = (bf16[4,144,512]{2,1,0:T(8,128)(2,1)S(1)}, bf16[4,144,512]{2,1,0:T(8,128)(2,1)S(1)}, u32[]{:S(2)}, u32[]{:S(2)}) collective-permute-start(bf16[4,144,512]{2,1,0:T(8,128)(2,1)S(1)} %pad_maximum_fusion.1.refs_0_), channel_id=1, source_target_pairs={{432,0},{384,16},{400,32},{416,48},{496,64},{448,80},{464,96},{480... | collective-permute-start | bytes 1769480 | tf_op jit(solution)/shard_map/ppermute | solution.py:50
  179.0 17.5 %collective-permute-start.21 = (bf16[4,144,512]{2,1,0:T(8,128)(2,1)S(1)}, bf16[4,144,512]{2,1,0:T(8,128)(2,1)S(1)}, u32[]{:S(2)}, u32[]{:S(2)}) collective-permute-start(bf16[4,144,512]{2,1,0:T(8,128)(2,1)S(1)} %pad_maximum_fusion.1.refs_0_), channel_id=1, source_target_pairs={{128,0},{144,16},{160,32},{176,48},{192,64},{208,80},{224,96},{240... | collective-permute-start | bytes 1769480 | tf_op jit(solution)/shard_map/ppermute | solution.py:50
  194.6 10.3 %collective-permute-start.26 = (bf16[2,144,512]{2,1,0:T(8,128)(2,1)S(1)}, bf16[2,144,512]{2,1,0:T(8,128)(2,1)S(1)}, u32[]{:S(2)}, u32[]{:S(2)}) collective-permute-start(bf16[2,144,512]{2,1,0:T(8,128)(2,1)S(1)} %slice.44), channel_id=1, source_target_pairs={{432,0},{384,16},{400,32},{416,48},{496,64},{448,80},{464,96},{480... | collective-permute-start | bytes 884744 | tf_op jit(solution)/shard_map/ppermute | solution.py:50
  196.6 9.2 %collective-permute-start.25 = (bf16[2,144,512]{2,1,0:T(8,128)(2,1)S(1)}, bf16[2,144,512]{2,1,0:T(8,128)(2,1)S(1)}, u32[]{:S(2)}, u32[]{:S(2)}) collective-permute-start(bf16[2,144,512]{2,1,0:T(8,128)(2,1)S(1)} %slice.43), channel_id=1, source_target_pairs={{128,0},{144,16},{160,32},{176,48},{192,64},{208,80},{224,96},{240... | collective-permute-start | bytes 884744 | tf_op jit(solution)/shard_map/ppermute | solution.py:50
  205.9 10.8 %collective-permute-start.27 = (bf16[4,144,512]{2,1,0:T(8,128)(2,1)S(1)}, bf16[4,144,512]{2,1,0:T(8,128)(2,1)S(1)}, u32[]{:S(2)}, u32[]{:S(2)}) collective-permute-start(bf16[4,144,512]{2,1,0:T(8,128)(2,1)S(1)} %pad_maximum_fusion.2), channel_id=1, source_target_pairs={{64,0},{0,64},{192,128},{128,192},{320,256},{256,320},{448,384},{3... | collective-permute-start | bytes 1769480 | tf_op jit(solution)/shard_map/ppermute | solution.py:32
  210.3 6.4 %collective-permute-start.20 = (bf16[4,144,512]{2,1,0:T(8,128)(2,1)S(1)}, bf16[4,144,512]{2,1,0:T(8,128)(2,1)S(1)}, u32[]{:S(2)}, u32[]{:S(2)}) collective-permute-start(bf16[4,144,512]{2,1,0:T(8,128)(2,1)S(1)} %pad_maximum_fusion.1.refs_0_), channel_id=1, source_target_pairs={{64,0},{0,64},{192,128},{128,192},{320,256},{256,320},{448,384},{3... | collective-permute-start | bytes 1769480 | tf_op jit(solution)/shard_map/ppermute | solution.py:32
  212.3 4.5 %collective-permute-start.24 = (bf16[4,144,512]{2,1,0:T(8,128)(2,1)S(1)}, bf16[4,144,512]{2,1,0:T(8,128)(2,1)S(1)}, u32[]{:S(2)}, u32[]{:S(2)}) collective-permute-start(bf16[4,144,512]{2,1,0:T(8,128)(2,1)S(1)} %collective-permute-done.22.refs_3_), channel_id=1, source_target_pairs={{64,0},{0,64},{192,128},{128,192},{320,256},{256,320},{448,384},{3... | collective-permute-start | bytes 1769480 | tf_op jit(solution)/shard_map/ppermute | solution.py:32
  214.7 3.9 %collective-permute-start.23 = (bf16[4,144,512]{2,1,0:T(8,128)(2,1)S(1)}, bf16[4,144,512]{2,1,0:T(8,128)(2,1)S(1)}, u32[]{:S(2)}, u32[]{:S(2)}) collective-permute-start(bf16[4,144,512]{2,1,0:T(8,128)(2,1)S(1)} %collective-permute-done.21.refs_2_), channel_id=1, source_target_pairs={{64,0},{0,64},{192,128},{128,192},{320,256},{256,320},{448,384},{3... | collective-permute-start | bytes 1769480 | tf_op jit(solution)/shard_map/ppermute | solution.py:32
  216.7 0.8 copy-start.10
  218.6 0.8 copy-start.12
  219.4 1.1 copy-start.11
  220.5 1.1 copy-start.13
Sparse Core Ops, SparseCore 0:
  108.5 72.6 all-gather.2

commit v3 on v2

--- a/solution.py
+++ b/solution.py
@@ -230,22 +230,10 @@
     )(jnp.stack([start, length]), scale.reshape(1), *parts, high, gain.reshape(1, width))
 
 
-def pieces_of(zl, zh, core):
+def pieces_of(zl, core):
     found = []
-
-    def chip(step):
-        z = lax.rem(zh * ZL + zl + step + ZL * ZH, ZL * ZH)
-        return lax.rem(z, ZL), z // ZL
-
-    layout = [(0, 0, 0, (0, 1, 2, 3)), (1, 0, 1, (0, 1, 2, 3))]
-    layout += [(2, 1, 0, (0, 1, 2, 3)), (3, -1, 0, (0, 1, 2, 3))]
-    layout += [(4, 1, 1, (0, 1, 2, 3)), (5, -1, 1, (0, 1, 2, 3))]
-    layout += [(6, 2, 0, (2, 3)), (7, -2, 0, (1, 2)), (8, 2, 1, (2, 3)), (9, -2, 1, (1, 2))]
-    for group, step, other, rows in layout:
-        there_zl, there_zh = chip(step)
-        member = there_zl * CORES + (1 - core if other else core)
-        for at, row in enumerate(rows):
-            found.append((group, at, member, lax.rem(there_zh + row, ZH)))
+    for step, other in ((0, 0), (0, 1), (1, 0), (-1, 0), (1, 1), (-1, 1), (2, 0), (2, 1)):
+        found.append(lax.rem(zl + step + ZL, ZL) * CORES + (1 - core if other else core))
     return found
 
 
@@ -258,13 +246,13 @@
     @pl.when(pl.program_id(0) == 0)
     def _():
         mix = jnp.zeros((TAIL, width), jnp.float32)
-        for group, at, member, sequence in pieces_of(zl, zh, core):
-            rank = lax.rem(sequence - zh + ZH, ZH)
-            slot = pl.ds(pl.multiple_of(rank * half, 16), half)
-            for part in range(2):
-                rows = group_refs[group][at, pl.ds(part * half, half), :]
-                grads_ref[member * 2 + part, slot, :] = rows
-            mix = mix + group_refs[group][at, pl.ds(2 * half, TAIL), :].astype(jnp.float32)
+        for group_ref, member in zip(group_refs, pieces_of(zl, core)):
+            for sequence in range(ZH):
+                slot = pl.ds(pl.multiple_of(lax.rem(sequence - zh + ZH, ZH) * half, 16), half)
+                for part in range(2):
+                    rows = group_ref[sequence, pl.ds(part * half, half), :]
+                    grads_ref[member * 2 + part, slot, :] = rows
+                mix = mix + group_ref[sequence, pl.ds(2 * half, TAIL), :].astype(jnp.float32)
         mix_ref[...] = jnp.sum(mix, axis=0, keepdims=True)
 
     blocks = features_ref.shape[0]
@@ -333,26 +321,22 @@
     return lax.ppermute(rows[:TAIL], "tp", [(j, j - 1) for j in range(1, ZL * CORES)])
 
 
-def trade_columns(own, zh):
+def trade_quarter(own, zh, step):
     part = own.shape[2] // ZH
-
-    def quarter(index):
-        return lax.dynamic_slice_in_dim(own, index * part, part, 2)
-
-    blocks = [quarter(zh)]
-    for step in (1, 2, 3):
-        blocks.append(from_zh(quarter((zh + ZH - step) % ZH), step))
-    return [b.transpose(0, 2, 1) for b in blocks]
+    quarter = lax.dynamic_slice_in_dim(own, (zh + ZH - step) % ZH * part, part, 2)
+    return from_zh(quarter, step) if step else quarter
 
 
 def gather_grads(grad):
-    stack = jnp.stack([grad] + [from_zh(grad, step) for step in (1, 2, 3)])
-    above, below = from_z(stack, 1), from_z(stack, -1)
-    other = from_other_core(stack)
-    far_above, far_below = from_z(above[2:4], 1), from_z(below[1:3], -1)
+    stack = lax.all_gather(grad, "dp", axis=0, tiled=False)
+    above, below, other = from_z(stack, 1), from_z(stack, -1), from_other_core(stack)
+    above, below, other = lax.optimization_barrier((above, below, other))
+    far_above, far_below = from_z(above[:2], 1), from_z(below[2:], -1)
     other_above, other_below = from_other_core(above), from_other_core(below)
-    far = from_other_core(jnp.concatenate([far_above, far_below]))
-    return [stack, other, above, below, other_above, other_below, far_above, far_below, far[:2], far[2:]]
+    far, other_above, other_below = lax.optimization_barrier(
+        (jnp.concatenate([far_above, far_below]), other_above, other_below)
+    )
+    return [stack, other, above, below, other_above, other_below, far, from_other_core(far)]
 
 
 def local(features, fc_weight, mix_gain, lengths):
@@ -365,28 +349,35 @@
     own = features.transpose(1, 0, 2)
     weight = fc_weight.transpose(1, 0, 2)
 
-    along = jnp.stack([own] + [plane_move(step, True)(own) for step in (1, 2, 3)])
-    along, later = lax.optimization_barrier((along, own))
-    up, down = plane_move(1, False)(along), plane_move(-1, False)(along)
-    traded = trade_columns(later, zh)
+    next_, last, across = (plane_move(step, True)(own) for step in (1, 3, 2))
+    trades = [trade_quarter(own, zh, 0), trade_quarter(own, zh, 1)]
+    next_, last, across, trades, later = lax.optimization_barrier((next_, last, across, trades, own))
+    low, high = jnp.stack([own, next_]), jnp.stack([across, last])
+    up_low, down_high = plane_move(1, False)(low), plane_move(-1, False)(high)
+    up_high, down_low = plane_move(1, False)(high), plane_move(-1, False)(low)
+    trades += [trade_quarter(later, zh, 2), trade_quarter(later, zh, 3)]
+    zero = project([low, high], weight)
+    up_low, down_high, trades, zero, later = lax.optimization_barrier(
+        (up_low, down_high, trades, zero, later)
+    )
+    far_low, far_high = plane_move(1, False)(up_low), plane_move(-1, False)(down_high)
     halves = high_halves(later[LEVELS - 1], draft_index)
-    zero = project([along], weight)
-    up, down, traded, halves, zero = lax.optimization_barrier((up, down, traded, halves, zero))
-    opposite = [plane_move(1, False)(up[:2]), plane_move(-1, False)(down[2:])]
-    high = high_rows(*halves, draft_index)
-    after = high_after(high)
-    one, three = project([up], weight), project([down], weight)
-    traded = jnp.concatenate(traded, axis=2)
-    opposite, after, one, three, traded = lax.optimization_barrier((opposite, after, one, three, traded))
+    traded = jnp.concatenate([t.transpose(0, 2, 1) for t in trades], axis=2)
+    one, three = project([up_low, up_high], weight), project([down_low, down_high], weight)
+    far_low, far_high, traded, one, three, halves = lax.optimization_barrier(
+        (far_low, far_high, traded, one, three, halves)
+    )
     every = lax.all_gather(traded, "draft", axis=0, tiled=False)
-    groups = [zero, one, project(opposite, weight), three]
-    high = jnp.concatenate([high, after], axis=0)
+    groups = [zero, one, project([far_low, far_high], weight), three]
+    target = high_rows(*halves, draft_index)
 
     keep, send = place(groups, core, x, y)
-    mine, *away = join(keep, from_other_core(send), zl)
+    got, after = lax.optimization_barrier((from_other_core(send), high_after(target)))
+    mine, *away = join(keep, got, zl)
     parts = [mine] + [from_zl(block, step) for step, block in zip((1, 2, 3), away)]
     scale = LOSS_SCALE / valid_total(lengths)
-    grad = chain(parts, high, mix_gain, tp_index * piece, lengths[zh], scale)
+    target = jnp.concatenate([target, after], axis=0)
+    grad = chain(parts, target, mix_gain, tp_index * piece, lengths[zh], scale)
     fc_grad, mix_total = weight_grad(every, gather_grads(grad), zl, zh, core)
     return (fc_grad.transpose(1, 0, 2), mix_total[0])
 

time: 238 us -> 242 us (1.017)
  the two profiles are of different devices: /device:TPU:1 before, /device:TPU:9 now
where the time goes in v3:
time: 242 us; the launch traced here: 241 us
  starting transfers between devices  111 us (46%)
  waiting for transfers between devices  35.3 us (15%)
  blocking collectives  33.5 us (14%)
  Pallas kernels  21.5 us (9%)
  between operations  16.4 us (7%)
  local copies, waits for them, and re-layouts  14.4 us (6%)
  other arithmetic  8.44 us (3%)
    ppermute x9, starting transfers between devices, plane_move(): return lambda block: lax.ppermute(block, ('tp', 'draft'), pairs)  33.6 us
    all_gather x1, blocking collectives, gather_grads(): stack = lax.all_gather(grad, 'dp', axis=0, tiled=False)  33.5 us
    ppermute x3, starting transfers between devices, from_zh(): return lax.ppermute(block, 'dp', [((s + step) % ZH, s) for s in range(ZH)])  27.6 us
    ppermute x4, waiting for transfers between devices, from_z(): return lax.ppermute(block, ('tp', 'dp'), pairs)  19.3 us
    ppermute x5, starting transfers between devices, from_other_core(): return lax.ppermute(block, 'tp', [(t ^ 1, t) for t in range(ZL * CORES)])  15 us
    ppermute x4, starting transfers between devices, from_z(): return lax.ppermute(block, ('tp', 'dp'), pairs)  13.3 us
    pallas_call x4, Pallas kernels, project(): pl.pallas_call(project_kernel, grid=(LEVELS,), out_shape=jax.ShapeDtypeSt...  12.3 us
    ppermute x3, starting transfers between devices, from_zl(): return lax.ppermute(block, 'tp', pairs)  11.2 us
  transfers between devices with their start and end apart: 28, of which 9 were waited for; matrix products, arithmetic and copies ran while one was open for 4% of the time, Pallas kernels for 6%

profile of v3, /device:TPU:9, one launch (start us, length us, event | category | flops | bytes accessed | tf_op | source)
XLA Modules:
  0.0 240.7 jit_solution(5454703926394496025)
XLA Ops:
  7.2 4.2 %collective-permute-start.2 = (bf16[3,64,1024]{2,1,0:T(8,128)(2,1)}, bf16[3,64,1024]{2,1,0:T(8,128)(2,1)}, u32[]{:S(2)}, u32[]{:S(2)}) collective-permute-start(bf16[3,64,1024]{2,1,0:T(8,128)(2,1)} %bitcast.38), channel_id=1, source_target_pairs={{8,0},{9,1},{10,2},{11,3},{12,4},{13,5},{14,6},{15,7},{0,8},{1,9},... | collective-permute-start | bytes 1179656 | tf_op jit(solution)/shard_map/ppermute | solution.py:28
  11.4 1.9 collective-permute-start.1
  13.3 3.4 %collective-permute-start = (bf16[3,64,1024]{2,1,0:T(8,128)(2,1)}, bf16[3,64,1024]{2,1,0:T(8,128)(2,1)}, u32[]{:S(2)}, u32[]{:S(2)}) collective-permute-start(bf16[3,64,1024]{2,1,0:T(8,128)(2,1)} %bitcast.40), channel_id=1, source_target_pairs={{4,0},{5,1},{6,2},{7,3},{8,4},{9,5},{10,6},{11,7},{12,8},{13,9},{1... | collective-permute-start | bytes 1179656 | tf_op jit(solution)/shard_map/ppermute | solution.py:28
  16.8 1.0 dynamic-slice_bitcast_fusion
  17.7 12.5 %collective-permute-start.3 = (bf16[3,64,256]{2,1,0:T(8,128)(2,1)S(1)}, bf16[3,64,256]{2,1,0:T(8,128)(2,1)S(1)}, u32[]{:S(2)}, u32[]{:S(2)}) collective-permute-start(bf16[3,64,256]{2,1,0:T(8,128)(2,1)S(1)} %get-tuple-element.81), channel_id=1, source_target_pairs={{16,0},{32,16},{48,32},{0,48},{17,1},{33,17},{49,33},{1,49},{18,2}... | collective-permute-start | bytes 294920 | tf_op jit(solution)/shard_map/ppermute | solution.py:41
  30.2 3.1 %collective-permute-done.3 = bf16[3,64,256]{2,1,0:T(8,128)(2,1)S(1)} collective-permute-done((bf16[3,64,256]{2,1,0:T(8,128)(2,1)S(1)}, bf16[3,64,256]{2,1,0:T(8,128)(2,1)S(1)}, u32[]{:S(2)}, u32[]{:S(2)}) %collective-permute-start.3) | collective-permute-done | bytes 98336 | tf_op jit(solution)/shard_map/ppermute | solution.py:41
  33.3 2.1 pad_maximum_fusion.refs_0_
  35.4 9.5 %collective-permute-start.4 = (bf16[2,3,64,1024]{3,2,1,0:T(8,128)(2,1)}, bf16[2,3,64,1024]{3,2,1,0:T(8,128)(2,1)}, u32[]{:S(2)}, u32[]{:S(2)}) collective-permute-start(bf16[2,3,64,1024]{3,2,1,0:T(8,128)(2,1)} %pad_maximum_fusion.refs_0_), channel_id=1, source_target_pairs={{1,0},{2,1},{3,2},{0,3},{5,4},{6,5},{7,6},{4,7},{9,8},{10,9},{11,1... | collective-permute-start | bytes 2359304 | tf_op jit(solution)/shard_map/ppermute | solution.py:28
  44.9 2.1 pad_maximum_fusion.1.refs_1_
  47.0 1.9 collective-permute-start.5
  48.9 2.1 collective-permute-start.11
  51.0 1.0 constant_dynamic-slice_fusion
  52.0 6.4 %collective-permute-start.7 = (bf16[3,64,256]{2,1,0:T(8,128)(2,1)S(1)}, bf16[3,64,256]{2,1,0:T(8,128)(2,1)}, u32[]{:S(2)}, u32[]{:S(2)}) collective-permute-start(bf16[3,64,256]{2,1,0:T(8,128)(2,1)S(1)} %get-tuple-element.79), channel_id=1, source_target_pairs={{48,0},{0,16},{16,32},{32,48},{49,1},{1,17},{17,33},{33,49},{50,2}... | collective-permute-start | bytes 294920 | tf_op jit(solution)/shard_map/ppermute | solution.py:41
  58.3 8.8 %collective-permute-start.6 = (bf16[3,64,256]{2,1,0:T(8,128)(2,1)S(1)}, bf16[3,64,256]{2,1,0:T(8,128)(2,1)}, u32[]{:S(2)}, u32[]{:S(2)}) collective-permute-start(bf16[3,64,256]{2,1,0:T(8,128)(2,1)S(1)} %get-tuple-element.80), channel_id=1, source_target_pairs={{32,0},{48,16},{0,32},{16,48},{33,1},{49,17},{1,33},{17,49},{34,2}... | collective-permute-start | bytes 294920 | tf_op jit(solution)/shard_map/ppermute | solution.py:41
  67.2 4.4 %collective-permute-start.10 = (bf16[2,3,64,1024]{3,2,1,0:T(8,128)(2,1)}, bf16[2,3,64,1024]{3,2,1,0:T(8,128)(2,1)}, u32[]{:S(2)}, u32[]{:S(2)}) collective-permute-start(bf16[2,3,64,1024]{3,2,1,0:T(8,128)(2,1)} %pad_maximum_fusion.1.refs_1_), channel_id=1, source_target_pairs={{1,0},{2,1},{3,2},{0,3},{5,4},{6,5},{7,6},{4,7},{9,8},{10,9},{11,1... | collective-permute-start | bytes 2359304 | tf_op jit(solution)/shard_map/ppermute | solution.py:28
  71.6 1.9 copy-done
  73.5 3.1 %project.4.refs_0_ = bf16[4,64,512]{2,1,0:T(8,128)(2,1)S(1)} custom-call(bf16[2,3,64,1024]{3,2,1,0:T(8,128)(2,1)} %pad_maximum_fusion.refs_0_, bf16[2,3,64,1024]{3,2,1,0:T(8,128)(2,1)} %pad_maximum_fusion.1.refs_1_, bf16[3,1024,512]{2,1,0:T(8,128)(2,1)S(1)} %bitcast.29), custom_call_target="tpu_custom_call" | custom-call | flops 805306368 | bytes 4718592 | tf_op jit(solution)/shard_map/project/pallas_call | solution.py:76
  76.5 5.4 %collective-permute-done.6 = bf16[3,64,256]{2,1,0:T(8,128)(2,1)} collective-permute-done((bf16[3,64,256]{2,1,0:T(8,128)(2,1)S(1)}, bf16[3,64,256]{2,1,0:T(8,128)(2,1)}, u32[]{:S(2)}, u32[]{:S(2)}) %collective-permute-start.6) | collective-permute-done | bytes 98336 | tf_op jit(solution)/shard_map/ppermute | solution.py:41
  82.0 4.3 %collective-permute-start.8 = (bf16[2,3,64,1024]{3,2,1,0:T(8,128)(2,1)}, bf16[2,3,64,1024]{3,2,1,0:T(8,128)(2,1)}, u32[]{:S(2)}, u32[]{:S(2)}) collective-permute-start(bf16[2,3,64,1024]{3,2,1,0:T(8,128)(2,1)} %collective-permute-done.4.refs_0_), channel_id=1, source_target_pairs={{1,0},{2,1},{3,2},{0,3},{5,4},{6,5},{7,6},{4,7},{9,8},{10,9},{11,1... | collective-permute-start | bytes 2359304 | tf_op jit(solution)/shard_map/ppermute | solution.py:28
  86.3 1.9 collective-permute-start.9
  88.3 0.9 slice_bitcast_fusion
  89.2 2.5 %collective-permute-start.13 = (bf16[64,512]{1,0:T(8,128)(2,1)S(1)}, bf16[64,512]{1,0:T(8,128)(2,1)}, u32[]{:S(2)}, u32[]{:S(2)}) collective-permute-start(bf16[64,512]{1,0:T(8,128)(2,1)S(1)} %get-tuple-element.85), channel_id=1, source_target_pairs={{0,1},{1,0},{2,65},{3,64},{4,129},{5,128},{6,193},{7,192},{8,257},... | collective-permute-start | bytes 196616 | tf_op jit(solution)/shard_map/ppermute | solution.py:311
  91.7 5.5 %collective-permute-start.12 = (bf16[64,512]{1,0:T(8,128)(2,1)S(1)}, bf16[64,512]{1,0:T(8,128)(2,1)}, u32[]{:S(2)}, u32[]{:S(2)}) collective-permute-start(bf16[64,512]{1,0:T(8,128)(2,1)S(1)} %get-tuple-element.86), channel_id=1, source_target_pairs={{0,0},{1,1},{2,64},{3,65},{4,128},{5,129},{6,192},{7,193},{8,256},... | collective-permute-start | bytes 196616 | tf_op jit(solution)/shard_map/ppermute | solution.py:310
  97.2 3.1 %project.6.refs_3_ = bf16[4,64,512]{2,1,0:T(8,128)(2,1)S(1)} custom-call(bf16[2,3,64,1024]{3,2,1,0:T(8,128)(2,1)} %collective-permute-done.11.refs_0_, bf16[2,3,64,1024]{3,2,1,0:T(8,128)(2,1)} %collective-permute-done.5.refs_1_, bf16[3,1024,512]{2,1,0:T(8,128)(2,1)S(1)} %bitcast.30), custom_call_target="tpu_custom_call" | custom-call | flops 805306368 | bytes 4718592 | tf_op jit(solution)/shard_map/project/pallas_call | solution.py:76
  100.3 0.7 copy-done.2
  101.0 1.8 pad_maximum_fusion.3
  102.8 3.1 %project.5.refs_1_ = bf16[4,64,512]{2,1,0:T(8,128)(2,1)S(1)} custom-call(bf16[2,3,64,1024]{3,2,1,0:T(8,128)(2,1)} %collective-permute-done.4.refs_0_, bf16[2,3,64,1024]{3,2,1,0:T(8,128)(2,1)} %collective-permute-done.10.refs_1_, bf16[3,1024,512]{2,1,0:T(8,128)(2,1)S(1)} %bitcast.31), custom_call_target="tpu_custom_call" | custom-call | flops 805306368 | bytes 4718592 | tf_op jit(solution)/shard_map/project/pallas_call | solution.py:76
  105.9 0.7 copy-done.4
  106.6 2.0 copy.7
  108.7 3.1 %project.7.refs_2_ = bf16[4,64,512]{2,1,0:T(8,128)(2,1)S(1)} custom-call(bf16[2,3,64,1024]{3,2,1,0:T(8,128)(2,1)} %collective-permute-done.8.refs_0_, bf16[2,3,64,1024]{3,2,1,0:T(8,128)(2,1)} %collective-permute-done.9.refs_1_, bf16[3,1024,512]{2,1,0:T(8,128)(2,1)S(1)} %bitcast.32), custom_call_target="tpu_custom_call" | custom-call | flops 805306368 | bytes 4718592 | tf_op jit(solution)/shard_map/project/pallas_call | solution.py:76
  111.8 0.9 copy-done.3
  112.7 0.9 copy-done.5
  113.7 0.8 place.1
  114.5 1.9 collective-permute-start.14
  116.4 0.9 broadcast_select_fusion
  117.3 2.4 collective-permute-start.15
  119.8 0.7 maximum_reduce_fusion
  120.4 0.6 dynamic_slice.19
  121.0 1.4 collective-permute-done.15
  122.5 4.3 %collective-permute-start.16 = (bf16[144,512]{1,0:T(8,128)(2,1)S(1)}, bf16[144,512]{1,0:T(8,128)(2,1)S(1)}, u32[]{:S(2)}, u32[]{:S(2)}) collective-permute-start(bf16[144,512]{1,0:T(8,128)(2,1)S(1)} %get-tuple-element.64), channel_id=1, source_target_pairs={{128,0},{192,64},{256,128},{320,192},{384,256},{448,320},{0,384},{... | collective-permute-start | bytes 442376 | tf_op jit(solution)/shard_map/ppermute | solution.py:37
  126.9 3.7 %collective-permute-start.17 = (bf16[144,512]{1,0:T(8,128)(2,1)S(1)}, bf16[144,512]{1,0:T(8,128)(2,1)S(1)}, u32[]{:S(2)}, u32[]{:S(2)}) collective-permute-start(bf16[144,512]{1,0:T(8,128)(2,1)S(1)} %get-tuple-element.65), channel_id=1, source_target_pairs={{256,0},{320,64},{384,128},{448,192},{0,256},{64,320},{128,384},{1... | collective-permute-start | bytes 442376 | tf_op jit(solution)/shard_map/ppermute | solution.py:37
  130.5 3.3 %collective-permute-start.18 = (bf16[144,512]{1,0:T(8,128)(2,1)S(1)}, bf16[144,512]{1,0:T(8,128)(2,1)S(1)}, u32[]{:S(2)}, u32[]{:S(2)}) collective-permute-start(bf16[144,512]{1,0:T(8,128)(2,1)S(1)} %get-tuple-element.66), channel_id=1, source_target_pairs={{384,0},{448,64},{0,128},{64,192},{128,256},{192,320},{256,384},{3... | collective-permute-start | bytes 442376 | tf_op jit(solution)/shard_map/ppermute | solution.py:37
  133.8 0.7 pad_add_fusion.1.meta_ref
  136.3 4.5 %collective-permute-done.17.refs_2_ = bf16[144,512]{1,0:T(8,128)(2,1)S(1)} collective-permute-done((bf16[144,512]{1,0:T(8,128)(2,1)S(1)}, bf16[144,512]{1,0:T(8,128)(2,1)S(1)}, u32[]{:S(2)}, u32[]{:S(2)}) %collective-permute-start.17) | collective-permute-done | bytes 147488 | tf_op jit(solution)/shard_map/ppermute | solution.py:37
  140.8 1.4 chain.1
  142.2 33.5 %all-gather.1 = bf16[576,512]{1,0:T(8,128)(2,1)S(1)} all-gather(bf16[144,512]{1,0:T(8,128)(2,1)S(1)} %chain.1), channel_id=3, replica_groups=mesh['tp'=8,'dp'=4,'draft'=16] {'dp'}, dimensions={0}, use_global_device_ids=true | all-gather | bytes 737280 | tf_op jit(solution)/shard_map/all_gather | solution.py:331
  175.7 4.9 %collective-permute-start.21 = (bf16[4,144,512]{2,1,0:T(8,128)(2,1)S(1)}, bf16[4,144,512]{2,1,0:T(8,128)(2,1)S(1)}, u32[]{:S(2)}, u32[]{:S(2)}) collective-permute-start(bf16[4,144,512]{2,1,0:T(8,128)(2,1)S(1)} %bitcast.33), channel_id=1, source_target_pairs={{64,0},{0,64},{192,128},{128,192},{320,256},{256,320},{448,384},{3... | collective-permute-start | bytes 1769480 | tf_op jit(solution)/shard_map/ppermute | solution.py:32
  180.6 1.9 collective-permute-start.20
  182.5 4.6 %collective-permute-start.19 = (bf16[4,144,512]{2,1,0:T(8,128)(2,1)S(1)}, bf16[4,144,512]{2,1,0:T(8,128)(2,1)S(1)}, u32[]{:S(2)}, u32[]{:S(2)}) collective-permute-start(bf16[4,144,512]{2,1,0:T(8,128)(2,1)S(1)} %bitcast.35), channel_id=1, source_target_pairs={{128,0},{144,16},{160,32},{176,48},{192,64},{208,80},{224,96},{240... | collective-permute-start | bytes 1769480 | tf_op jit(solution)/shard_map/ppermute | solution.py:50
  187.1 11.5 %collective-permute-done.20.refs_3_ = bf16[4,144,512]{2,1,0:T(8,128)(2,1)S(1)} collective-permute-done((bf16[4,144,512]{2,1,0:T(8,128)(2,1)S(1)}, bf16[4,144,512]{2,1,0:T(8,128)(2,1)S(1)}, u32[]{:S(2)}, u32[]{:S(2)}) %collective-permute-start.20) | collective-permute-done | bytes 589856 | tf_op jit(solution)/shard_map/ppermute | solution.py:50
  198.6 1.6 collective-permute-done.19.refs_2_
  200.2 2.7 %collective-permute-start.24 = (bf16[4,144,512]{2,1,0:T(8,128)(2,1)S(1)}, bf16[4,144,512]{2,1,0:T(8,128)(2,1)S(1)}, u32[]{:S(2)}, u32[]{:S(2)}) collective-permute-start(bf16[4,144,512]{2,1,0:T(8,128)(2,1)S(1)} %collective-permute-done.19.refs_2_), channel_id=1, source_target_pairs={{64,0},{0,64},{192,128},{128,192},{320,256},{256,320},{448,384},{3... | collective-permute-start | bytes 1769480 | tf_op jit(solution)/shard_map/ppermute | solution.py:32
  202.9 1.9 collective-permute-start.25
  204.9 3.4 %collective-permute-start.23 = (bf16[2,144,512]{2,1,0:T(8,128)(2,1)S(1)}, bf16[2,144,512]{2,1,0:T(8,128)(2,1)S(1)}, u32[]{:S(2)}, u32[]{:S(2)}) collective-permute-start(bf16[2,144,512]{2,1,0:T(8,128)(2,1)S(1)} %slice.23), channel_id=1, source_target_pairs={{432,0},{384,16},{400,32},{416,48},{496,64},{448,80},{464,96},{480... | collective-permute-start | bytes 884744 | tf_op jit(solution)/shard_map/ppermute | solution.py:50
  208.3 3.4 %collective-permute-start.22 = (bf16[2,144,512]{2,1,0:T(8,128)(2,1)S(1)}, bf16[2,144,512]{2,1,0:T(8,128)(2,1)S(1)}, u32[]{:S(2)}, u32[]{:S(2)}) collective-permute-start(bf16[2,144,512]{2,1,0:T(8,128)(2,1)S(1)} %slice.22), channel_id=1, source_target_pairs={{128,0},{144,16},{160,32},{176,48},{192,64},{208,80},{224,96},{240... | collective-permute-start | bytes 884744 | tf_op jit(solution)/shard_map/ppermute | solution.py:50
  211.8 5.0 %collective-permute-done.23 = bf16[2,144,512]{2,1,0:T(8,128)(2,1)S(1)} collective-permute-done((bf16[2,144,512]{2,1,0:T(8,128)(2,1)S(1)}, bf16[2,144,512]{2,1,0:T(8,128)(2,1)S(1)}, u32[]{:S(2)}, u32[]{:S(2)}) %collective-permute-start.23) | collective-permute-done | bytes 294944 | tf_op jit(solution)/shard_map/ppermute | solution.py:50
  216.8 1.2 collective-permute-done.22
  218.0 0.8 copy-done.7
  218.9 3.6 %collective-permute-start.26 = (bf16[4,144,512]{2,1,0:T(8,128)(2,1)S(1)}, bf16[4,144,512]{2,1,0:T(8,128)(2,1)S(1)}, u32[]{:S(2)}, u32[]{:S(2)}) collective-permute-start(bf16[4,144,512]{2,1,0:T(8,128)(2,1)S(1)} %pad_maximum_fusion.2.refs_6_), channel_id=1, source_target_pairs={{64,0},{0,64},{192,128},{128,192},{320,256},{256,320},{448,384},{3... | collective-permute-start | bytes 1769480 | tf_op jit(solution)/shard_map/ppermute | solution.py:32
  222.5 1.5 collective-permute-done.26.refs_7_
  224.0 0.8 copy-done.9
  224.9 1.1 copy-done.8
  225.9 1.1 copy-done.10
  227.0 6.9 %weight_grad.1 = (bf16[3,256,512]{2,1,0:T(8,128)(2,1)}, f32[1,512]{1,0:T(1,128)}) custom-call(s32[3]{0:T(128)S(1)} %pad_add_fusion.meta_ref, bf16[16,3,256,256]{3,2,1,0:T(8,128)(2,1)} %bitcast.46, bf16[4,144,512]{2,1,0:T(8,128)(2,1)S(1)} %bitcast.36, bf16[4,144,512]{2,1,0:T(8,128)(2,1)S(1)} %collective-permute-done.21.refs_1_, ...), custom_call_target="tpu_custom_call" | custom-call | flops 3221225472 | bytes 10485760 | tf_op jit(solution)/shard_map/weight_grad/pallas_call | solution.py:268
  (47 shorter events, 0.6 us)
Async XLA Ops:
  7.2 90.0 %copy-start.1 = (bf16[1024,3,512]{2,0,1:T(8,128)(2,1)S(1)}, bf16[1024,3,512]{2,0,1:T(8,128)(2,1)}, u32[]{:S(2)}) copy-start(bf16[1024,3,512]{2,0,1:T(8,128)(2,1)} %param.5) | copy-start | bytes 9437188
  7.2 217.7 %all-gather.4.cloned.1.call-start = ((), (), s32[]{:S(2)}) async-start(), calls=%async_computation | async-start | bytes 6684672 | tf_op jit(solution)/shard_map/all_gather | solution.py:370
  7.2 26.0 %collective-permute-start.2 = (bf16[3,64,1024]{2,1,0:T(8,128)(2,1)}, bf16[3,64,1024]{2,1,0:T(8,128)(2,1)}, u32[]{:S(2)}, u32[]{:S(2)}) collective-permute-start(bf16[3,64,1024]{2,1,0:T(8,128)(2,1)} %bitcast.38), channel_id=1, source_target_pairs={{8,0},{9,1},{10,2},{11,3},{12,4},{13,5},{14,6},{15,7},{0,8},{1,9},... | collective-permute-start | bytes 1179656 | tf_op jit(solution)/shard_map/ppermute | solution.py:28
  11.4 21.9 %collective-permute-start.1 = (bf16[3,64,1024]{2,1,0:T(8,128)(2,1)}, bf16[3,64,1024]{2,1,0:T(8,128)(2,1)}, u32[]{:S(2)}, u32[]{:S(2)}) collective-permute-start(bf16[3,64,1024]{2,1,0:T(8,128)(2,1)} %bitcast.39), channel_id=1, source_target_pairs={{12,0},{13,1},{14,2},{15,3},{0,4},{1,5},{2,6},{3,7},{4,8},{5,9},{6... | collective-permute-start | bytes 1179656 | tf_op jit(solution)/shard_map/ppermute | solution.py:28
  13.3 19.9 %collective-permute-start = (bf16[3,64,1024]{2,1,0:T(8,128)(2,1)}, bf16[3,64,1024]{2,1,0:T(8,128)(2,1)}, u32[]{:S(2)}, u32[]{:S(2)}) collective-permute-start(bf16[3,64,1024]{2,1,0:T(8,128)(2,1)} %bitcast.40), channel_id=1, source_target_pairs={{4,0},{5,1},{6,2},{7,3},{8,4},{9,5},{10,6},{11,7},{12,8},{13,9},{1... | collective-permute-start | bytes 1179656 | tf_op jit(solution)/shard_map/ppermute | solution.py:28
  17.7 15.5 %collective-permute-start.3 = (bf16[3,64,256]{2,1,0:T(8,128)(2,1)S(1)}, bf16[3,64,256]{2,1,0:T(8,128)(2,1)S(1)}, u32[]{:S(2)}, u32[]{:S(2)}) collective-permute-start(bf16[3,64,256]{2,1,0:T(8,128)(2,1)S(1)} %get-tuple-element.81), channel_id=1, source_target_pairs={{16,0},{32,16},{48,32},{0,48},{17,1},{33,17},{49,33},{1,49},{18,2}... | collective-permute-start | bytes 294920 | tf_op jit(solution)/shard_map/ppermute | solution.py:41
  33.3 38.3 %copy-start.11 = (bf16[3,64,256]{2,1,0:T(8,128)(2,1)}, bf16[3,64,256]{2,1,0:T(8,128)(2,1)S(1)}, u32[]{:S(2)}) copy-start(bf16[3,64,256]{2,1,0:T(8,128)(2,1)S(1)} %collective-permute-done.3) | copy-start | bytes 294916
  35.4 46.6 %collective-permute-start.4 = (bf16[2,3,64,1024]{3,2,1,0:T(8,128)(2,1)}, bf16[2,3,64,1024]{3,2,1,0:T(8,128)(2,1)}, u32[]{:S(2)}, u32[]{:S(2)}) collective-permute-start(bf16[2,3,64,1024]{3,2,1,0:T(8,128)(2,1)} %pad_maximum_fusion.refs_0_), channel_id=1, source_target_pairs={{1,0},{2,1},{3,2},{0,3},{5,4},{6,5},{7,6},{4,7},{9,8},{10,9},{11,1... | collective-permute-start | bytes 2359304 | tf_op jit(solution)/shard_map/ppermute | solution.py:28
  47.0 35.0 %collective-permute-start.5 = (bf16[2,3,64,1024]{3,2,1,0:T(8,128)(2,1)}, bf16[2,3,64,1024]{3,2,1,0:T(8,128)(2,1)}, u32[]{:S(2)}, u32[]{:S(2)}) collective-permute-start(bf16[2,3,64,1024]{3,2,1,0:T(8,128)(2,1)} %pad_maximum_fusion.1.refs_1_), channel_id=1, source_target_pairs={{3,0},{0,1},{1,2},{2,3},{7,4},{4,5},{5,6},{6,7},{11,8},{8,9},{9,10... | collective-permute-start | bytes 2359304 | tf_op jit(solution)/shard_map/ppermute | solution.py:28
  48.9 42.8 %collective-permute-start.11 = (bf16[2,3,64,1024]{3,2,1,0:T(8,128)(2,1)}, bf16[2,3,64,1024]{3,2,1,0:T(8,128)(2,1)}, u32[]{:S(2)}, u32[]{:S(2)}) collective-permute-start(bf16[2,3,64,1024]{3,2,1,0:T(8,128)(2,1)} %pad_maximum_fusion.refs_0_), channel_id=1, source_target_pairs={{3,0},{0,1},{1,2},{2,3},{7,4},{4,5},{5,6},{6,7},{11,8},{8,9},{9,10... | collective-permute-start | bytes 2359304 | tf_op jit(solution)/shard_map/ppermute | solution.py:28
  52.0 15.2 %collective-permute-start.7 = (bf16[3,64,256]{2,1,0:T(8,128)(2,1)S(1)}, bf16[3,64,256]{2,1,0:T(8,128)(2,1)}, u32[]{:S(2)}, u32[]{:S(2)}) collective-permute-start(bf16[3,64,256]{2,1,0:T(8,128)(2,1)S(1)} %get-tuple-element.79), channel_id=1, source_target_pairs={{48,0},{0,16},{16,32},{32,48},{49,1},{1,17},{17,33},{33,49},{50,2}... | collective-permute-start | bytes 294920 | tf_op jit(solution)/shard_map/ppermute | solution.py:41
  58.3 23.6 %collective-permute-start.6 = (bf16[3,64,256]{2,1,0:T(8,128)(2,1)S(1)}, bf16[3,64,256]{2,1,0:T(8,128)(2,1)}, u32[]{:S(2)}, u32[]{:S(2)}) collective-permute-start(bf16[3,64,256]{2,1,0:T(8,128)(2,1)S(1)} %get-tuple-element.80), channel_id=1, source_target_pairs={{32,0},{48,16},{0,32},{16,48},{33,1},{49,17},{1,33},{17,49},{34,2}... | collective-permute-start | bytes 294920 | tf_op jit(solution)/shard_map/ppermute | solution.py:41
  67.2 35.6 %collective-permute-start.10 = (bf16[2,3,64,1024]{3,2,1,0:T(8,128)(2,1)}, bf16[2,3,64,1024]{3,2,1,0:T(8,128)(2,1)}, u32[]{:S(2)}, u32[]{:S(2)}) collective-permute-start(bf16[2,3,64,1024]{3,2,1,0:T(8,128)(2,1)} %pad_maximum_fusion.1.refs_1_), channel_id=1, source_target_pairs={{1,0},{2,1},{3,2},{0,3},{5,4},{6,5},{7,6},{4,7},{9,8},{10,9},{11,1... | collective-permute-start | bytes 2359304 | tf_op jit(solution)/shard_map/ppermute | solution.py:28
  71.6 1.9 copy-start
  82.0 24.6 %collective-permute-start.8 = (bf16[2,3,64,1024]{3,2,1,0:T(8,128)(2,1)}, bf16[2,3,64,1024]{3,2,1,0:T(8,128)(2,1)}, u32[]{:S(2)}, u32[]{:S(2)}) collective-permute-start(bf16[2,3,64,1024]{3,2,1,0:T(8,128)(2,1)} %collective-permute-done.4.refs_0_), channel_id=1, source_target_pairs={{1,0},{2,1},{3,2},{0,3},{5,4},{6,5},{7,6},{4,7},{9,8},{10,9},{11,1... | collective-permute-start | bytes 2359304 | tf_op jit(solution)/shard_map/ppermute | solution.py:28
  86.3 20.3 %collective-permute-start.9 = (bf16[2,3,64,1024]{3,2,1,0:T(8,128)(2,1)}, bf16[2,3,64,1024]{3,2,1,0:T(8,128)(2,1)}, u32[]{:S(2)}, u32[]{:S(2)}) collective-permute-start(bf16[2,3,64,1024]{3,2,1,0:T(8,128)(2,1)} %collective-permute-done.5.refs_1_), channel_id=1, source_target_pairs={{3,0},{0,1},{1,2},{2,3},{7,4},{4,5},{5,6},{6,7},{11,8},{8,9},{9,10... | collective-permute-start | bytes 2359304 | tf_op jit(solution)/shard_map/ppermute | solution.py:28
  89.2 17.4 %collective-permute-start.13 = (bf16[64,512]{1,0:T(8,128)(2,1)S(1)}, bf16[64,512]{1,0:T(8,128)(2,1)}, u32[]{:S(2)}, u32[]{:S(2)}) collective-permute-start(bf16[64,512]{1,0:T(8,128)(2,1)S(1)} %get-tuple-element.85), channel_id=1, source_target_pairs={{0,1},{1,0},{2,65},{3,64},{4,129},{5,128},{6,193},{7,192},{8,257},... | collective-permute-start | bytes 196616 | tf_op jit(solution)/shard_map/ppermute | solution.py:311
  91.7 14.9 %collective-permute-start.12 = (bf16[64,512]{1,0:T(8,128)(2,1)S(1)}, bf16[64,512]{1,0:T(8,128)(2,1)}, u32[]{:S(2)}, u32[]{:S(2)}) collective-permute-start(bf16[64,512]{1,0:T(8,128)(2,1)S(1)} %get-tuple-element.86), channel_id=1, source_target_pairs={{0,0},{1,1},{2,64},{3,65},{4,128},{5,129},{6,192},{7,193},{8,256},... | collective-permute-start | bytes 196616 | tf_op jit(solution)/shard_map/ppermute | solution.py:310
  100.3 0.7 copy-start.2
  102.8 17.0 %copy-start.12 = (s32[4]{0:T(128)S(1)}, s32[4]{0:T(128)}, u32[]{:S(2)}) copy-start(s32[4]{0:T(128)} %param.7) | copy-start | bytes 52
  102.8 38.1 %copy-start.6 = (f32[512]{0:T(512)S(1)}, f32[512]{0:T(512)}, u32[]{:S(2)}) copy-start(f32[512]{0:T(512)} %param.6) | copy-start | bytes 6148
  105.9 0.7 copy-start.4
  111.8 1.0 copy-start.3
  112.7 0.9 copy-start.5
  114.5 7.9 %collective-permute-start.14 = (bf16[4,144,512]{2,1,0:T(8,128)(2,1)S(1)}, bf16[4,144,512]{2,1,0:T(8,128)(2,1)S(1)}, u32[]{:S(2)}, u32[]{:S(2)}) collective-permute-start(bf16[4,144,512]{2,1,0:T(8,128)(2,1)S(1)} %get-tuple-element.59), channel_id=1, source_target_pairs={{64,0},{0,64},{192,128},{128,192},{320,256},{256,320},{448,384},{3... | collective-permute-start | bytes 1769480 | tf_op jit(solution)/shard_map/ppermute | solution.py:32
  117.3 5.1 %collective-permute-start.15 = (bf16[16,512]{1,0:T(8,128)(2,1)S(1)}, bf16[16,512]{1,0:T(8,128)(2,1)S(1)}, u32[]{:S(2)}, u32[]{:S(2)}) collective-permute-start(bf16[16,512]{1,0:T(8,128)(2,1)S(1)} %slice.26), channel_id=1, source_target_pairs={{64,0},{128,64},{192,128},{256,192},{320,256},{384,320},{448,384},... | collective-permute-start | bytes 49160 | tf_op jit(solution)/shard_map/ppermute | solution.py:321
  122.5 13.8 %collective-permute-start.16 = (bf16[144,512]{1,0:T(8,128)(2,1)S(1)}, bf16[144,512]{1,0:T(8,128)(2,1)S(1)}, u32[]{:S(2)}, u32[]{:S(2)}) collective-permute-start(bf16[144,512]{1,0:T(8,128)(2,1)S(1)} %get-tuple-element.64), channel_id=1, source_target_pairs={{128,0},{192,64},{256,128},{320,192},{384,256},{448,320},{0,384},{... | collective-permute-start | bytes 442376 | tf_op jit(solution)/shard_map/ppermute | solution.py:37
  126.9 14.0 %collective-permute-start.17 = (bf16[144,512]{1,0:T(8,128)(2,1)S(1)}, bf16[144,512]{1,0:T(8,128)(2,1)S(1)}, u32[]{:S(2)}, u32[]{:S(2)}) collective-permute-start(bf16[144,512]{1,0:T(8,128)(2,1)S(1)} %get-tuple-element.65), channel_id=1, source_target_pairs={{256,0},{320,64},{384,128},{448,192},{0,256},{64,320},{128,384},{1... | collective-permute-start | bytes 442376 | tf_op jit(solution)/shard_map/ppermute | solution.py:37
  130.5 10.3 %collective-permute-start.18 = (bf16[144,512]{1,0:T(8,128)(2,1)S(1)}, bf16[144,512]{1,0:T(8,128)(2,1)S(1)}, u32[]{:S(2)}, u32[]{:S(2)}) collective-permute-start(bf16[144,512]{1,0:T(8,128)(2,1)S(1)} %get-tuple-element.66), channel_id=1, source_target_pairs={{384,0},{448,64},{0,128},{64,192},{128,256},{192,320},{256,384},{3... | collective-permute-start | bytes 442376 | tf_op jit(solution)/shard_map/ppermute | solution.py:37
  175.7 11.4 %collective-permute-start.21 = (bf16[4,144,512]{2,1,0:T(8,128)(2,1)S(1)}, bf16[4,144,512]{2,1,0:T(8,128)(2,1)S(1)}, u32[]{:S(2)}, u32[]{:S(2)}) collective-permute-start(bf16[4,144,512]{2,1,0:T(8,128)(2,1)S(1)} %bitcast.33), channel_id=1, source_target_pairs={{64,0},{0,64},{192,128},{128,192},{320,256},{256,320},{448,384},{3... | collective-permute-start | bytes 1769480 | tf_op jit(solution)/shard_map/ppermute | solution.py:32
  180.6 18.1 %collective-permute-start.20 = (bf16[4,144,512]{2,1,0:T(8,128)(2,1)S(1)}, bf16[4,144,512]{2,1,0:T(8,128)(2,1)S(1)}, u32[]{:S(2)}, u32[]{:S(2)}) collective-permute-start(bf16[4,144,512]{2,1,0:T(8,128)(2,1)S(1)} %bitcast.34), channel_id=1, source_target_pairs={{432,0},{384,16},{400,32},{416,48},{496,64},{448,80},{464,96},{480... | collective-permute-start | bytes 1769480 | tf_op jit(solution)/shard_map/ppermute | solution.py:50
  182.5 17.7 %collective-permute-start.19 = (bf16[4,144,512]{2,1,0:T(8,128)(2,1)S(1)}, bf16[4,144,512]{2,1,0:T(8,128)(2,1)S(1)}, u32[]{:S(2)}, u32[]{:S(2)}) collective-permute-start(bf16[4,144,512]{2,1,0:T(8,128)(2,1)S(1)} %bitcast.35), channel_id=1, source_target_pairs={{128,0},{144,16},{160,32},{176,48},{192,64},{208,80},{224,96},{240... | collective-permute-start | bytes 1769480 | tf_op jit(solution)/shard_map/ppermute | solution.py:50
  200.2 17.8 %collective-permute-start.24 = (bf16[4,144,512]{2,1,0:T(8,128)(2,1)S(1)}, bf16[4,144,512]{2,1,0:T(8,128)(2,1)S(1)}, u32[]{:S(2)}, u32[]{:S(2)}) collective-permute-start(bf16[4,144,512]{2,1,0:T(8,128)(2,1)S(1)} %collective-permute-done.19.refs_2_), channel_id=1, source_target_pairs={{64,0},{0,64},{192,128},{128,192},{320,256},{256,320},{448,384},{3... | collective-permute-start | bytes 1769480 | tf_op jit(solution)/shard_map/ppermute | solution.py:32
  202.9 15.1 %collective-permute-start.25 = (bf16[4,144,512]{2,1,0:T(8,128)(2,1)S(1)}, bf16[4,144,512]{2,1,0:T(8,128)(2,1)S(1)}, u32[]{:S(2)}, u32[]{:S(2)}) collective-permute-start(bf16[4,144,512]{2,1,0:T(8,128)(2,1)S(1)} %collective-permute-done.20.refs_3_), channel_id=1, source_target_pairs={{64,0},{0,64},{192,128},{128,192},{320,256},{256,320},{448,384},{3... | collective-permute-start | bytes 1769480 | tf_op jit(solution)/shard_map/ppermute | solution.py:32
  204.9 11.8 %collective-permute-start.23 = (bf16[2,144,512]{2,1,0:T(8,128)(2,1)S(1)}, bf16[2,144,512]{2,1,0:T(8,128)(2,1)S(1)}, u32[]{:S(2)}, u32[]{:S(2)}) collective-permute-start(bf16[2,144,512]{2,1,0:T(8,128)(2,1)S(1)} %slice.23), channel_id=1, source_target_pairs={{432,0},{384,16},{400,32},{416,48},{496,64},{448,80},{464,96},{480... | collective-permute-start | bytes 884744 | tf_op jit(solution)/shard_map/ppermute | solution.py:50
  208.3 9.6 %collective-permute-start.22 = (bf16[2,144,512]{2,1,0:T(8,128)(2,1)S(1)}, bf16[2,144,512]{2,1,0:T(8,128)(2,1)S(1)}, u32[]{:S(2)}, u32[]{:S(2)}) collective-permute-start(bf16[2,144,512]{2,1,0:T(8,128)(2,1)S(1)} %slice.22), channel_id=1, source_target_pairs={{128,0},{144,16},{160,32},{176,48},{192,64},{208,80},{224,96},{240... | collective-permute-start | bytes 884744 | tf_op jit(solution)/shard_map/ppermute | solution.py:50
  218.0 0.8 copy-start.7
  218.9 5.2 %collective-permute-start.26 = (bf16[4,144,512]{2,1,0:T(8,128)(2,1)S(1)}, bf16[4,144,512]{2,1,0:T(8,128)(2,1)S(1)}, u32[]{:S(2)}, u32[]{:S(2)}) collective-permute-start(bf16[4,144,512]{2,1,0:T(8,128)(2,1)S(1)} %pad_maximum_fusion.2.refs_6_), channel_id=1, source_target_pairs={{64,0},{0,64},{192,128},{128,192},{320,256},{256,320},{448,384},{3... | collective-permute-start | bytes 1769480 | tf_op jit(solution)/shard_map/ppermute | solution.py:32
  224.0 0.8 copy-start.9
  224.8 1.1 copy-start.8
  225.9 1.1 copy-start.10
Sparse Core Ops, SparseCore 0:
  108.7 77.0 all-gather.3

commit v4 on v3

--- a/solution.py
+++ b/solution.py
@@ -14,7 +14,10 @@
 ZL, CORES, ZH = 4, 2, 4
 VMEM = pl.BlockSpec(memory_space=pltpu.VMEM)
 SMEM = pl.BlockSpec(memory_space=pltpu.SMEM)
-PARAMS = pltpu.CompilerParams(vmem_limit_bytes=48 << 20)
+
+
+def params(mebibytes):
+    return pltpu.CompilerParams(vmem_limit_bytes=mebibytes << 20)
 
 
 def plane_move(step, first):
@@ -83,7 +86,7 @@
         + [pl.BlockSpec((1, depth, width), lambda l: (l, 0, 0))],
         out_specs=pl.BlockSpec((count, rows, width), lambda l: (0, 0, 0)),
         scratch_shapes=[pltpu.VMEM((count * rows, width), jnp.float32)],
-        compiler_params=PARAMS,
+        compiler_params=params(12),
         cost_estimate=pl.CostEstimate(
             flops=2 * count * rows * LEVELS * depth * width,
             bytes_accessed=2 * (weight.size + count * rows * LEVELS * depth),
@@ -125,7 +128,7 @@
         in_specs=[SMEM] + [VMEM] * 4,
         out_specs=(VMEM, VMEM),
         scratch_shapes=[pltpu.VMEM((total + 2 * HALO, width), jnp.float32)],
-        compiler_params=PARAMS,
+        compiler_params=params(12),
         cost_estimate=pl.CostEstimate(
             flops=total * width, bytes_accessed=4 * total * width, transcendentals=0
         ),
@@ -151,7 +154,7 @@
         out_shape=(piece,) * ZL,
         in_specs=[SMEM, VMEM, VMEM],
         out_specs=(VMEM,) * ZL,
-        compiler_params=PARAMS,
+        compiler_params=params(8),
         cost_estimate=pl.CostEstimate(
             flops=keep.size, bytes_accessed=6 * keep.size, transcendentals=0
         ),
@@ -222,7 +225,7 @@
         out_shape=jax.ShapeDtypeStruct((own + TAIL, width), jnp.bfloat16),
         in_specs=[SMEM, SMEM] + [VMEM] * (len(parts) + 2),
         out_specs=VMEM,
-        compiler_params=PARAMS,
+        compiler_params=params(14),
         cost_estimate=pl.CostEstimate(
             flops=60 * rows * width, bytes_accessed=10 * rows * width, transcendentals=3 * rows * width
         ),
@@ -239,7 +242,7 @@
 
 def weight_grad_kernel(meta_ref, features_ref, *refs):
     *group_refs, out_ref, mix_ref, grads_ref = refs
-    zl, zh, core = meta_ref[0], meta_ref[1], meta_ref[2]
+    zl, core = meta_ref[0], meta_ref[1]
     half = grads_ref.shape[1] // ZH
     width = grads_ref.shape[2]
 
@@ -248,7 +251,7 @@
         mix = jnp.zeros((TAIL, width), jnp.float32)
         for group_ref, member in zip(group_refs, pieces_of(zl, core)):
             for sequence in range(ZH):
-                slot = pl.ds(pl.multiple_of(lax.rem(sequence - zh + ZH, ZH) * half, 16), half)
+                slot = pl.ds(sequence * half, half)
                 for part in range(2):
                     rows = group_ref[sequence, pl.ds(part * half, half), :]
                     grads_ref[member * 2 + part, slot, :] = rows
@@ -261,10 +264,9 @@
     out_ref[0] = jnp.dot(left, right, preferred_element_type=jnp.float32).astype(jnp.bfloat16)
 
 
-def weight_grad(features, groups, zl, zh, core):
+def weight_grad(features, groups, zl, core):
     draft, _, columns, tokens = features.shape
     width = groups[0].shape[2]
-    whole = [pl.BlockSpec(g.shape, lambda l: (0, 0, 0)) for g in groups]
     return pl.pallas_call(
         weight_grad_kernel,
         grid=(LEVELS,),
@@ -272,20 +274,21 @@
             jax.ShapeDtypeStruct((LEVELS, columns, width), jnp.bfloat16),
             jax.ShapeDtypeStruct((1, width), jnp.float32),
         ),
-        in_specs=[SMEM, pl.BlockSpec((draft, 1, columns, tokens), lambda l: (0, l, 0, 0))] + whole,
+        in_specs=[SMEM, pl.BlockSpec((draft, 1, columns, tokens), lambda l: (0, l, 0, 0))]
+        + [VMEM] * len(groups),
         out_specs=(
             pl.BlockSpec((1, columns, width), lambda l: (l, 0, 0)),
             pl.BlockSpec((1, width), lambda l: (0, 0)),
         ),
         scratch_shapes=[pltpu.VMEM((draft, tokens, width), jnp.bfloat16)],
-        compiler_params=PARAMS,
+        compiler_params=params(26),
         cost_estimate=pl.CostEstimate(
             flops=2 * draft * LEVELS * columns * tokens * width,
             bytes_accessed=2 * features.size + 2 * draft * tokens * width,
             transcendentals=0,
         ),
         name="weight_grad",
-    )(jnp.stack([zl, zh, core]), features, *groups)
+    )(jnp.stack([zl, core]), features, *groups)
 
 
 def valid_total(lengths):
@@ -314,28 +317,28 @@
 
 def high_rows(one, two, draft_index):
     even = draft_index % 2 == 0
-    return jnp.concatenate([jnp.where(even, one, two), jnp.where(even, two, one)], axis=0)
-
-
-def high_after(rows):
-    return lax.ppermute(rows[:TAIL], "tp", [(j, j - 1) for j in range(1, ZL * CORES)])
-
-
-def trade_quarter(own, zh, step):
-    part = own.shape[2] // ZH
-    quarter = lax.dynamic_slice_in_dim(own, (zh + ZH - step) % ZH * part, part, 2)
-    return from_zh(quarter, step) if step else quarter
+    first = jnp.where(even, one, two)[:-TAIL]
+    return jnp.concatenate([first, jnp.where(even, two, one)], axis=0)
+
+
+def rows_ahead(top):
+    return lax.ppermute(top[:TAIL], "draft", [(e, e - 1) for e in range(1, X * Y)])
+
+
+def trade_columns(own):
+    levels, rows, depth = own.shape
+    quarters = own.reshape(levels, rows, ZH, depth // ZH).transpose(2, 0, 1, 3)
+    return lax.all_to_all(quarters, "dp", split_axis=0, concat_axis=0, tiled=True)
 
 
 def gather_grads(grad):
     stack = lax.all_gather(grad, "dp", axis=0, tiled=False)
-    above, below, other = from_z(stack, 1), from_z(stack, -1), from_other_core(stack)
+    above, below = from_z(stack, 1), from_z(stack, -1)
+    far = [from_z(stack[:2], 2), from_z(stack[2:], -2)]
+    other = from_other_core(stack)
     above, below, other = lax.optimization_barrier((above, below, other))
-    far_above, far_below = from_z(above[:2], 1), from_z(below[2:], -1)
     other_above, other_below = from_other_core(above), from_other_core(below)
-    far, other_above, other_below = lax.optimization_barrier(
-        (jnp.concatenate([far_above, far_below]), other_above, other_below)
-    )
+    far = jnp.concatenate(far)
     return [stack, other, above, below, other_above, other_below, far, from_other_core(far)]
 
 
@@ -350,35 +353,33 @@
     weight = fc_weight.transpose(1, 0, 2)
 
     next_, last, across = (plane_move(step, True)(own) for step in (1, 3, 2))
-    trades = [trade_quarter(own, zh, 0), trade_quarter(own, zh, 1)]
-    next_, last, across, trades, later = lax.optimization_barrier((next_, last, across, trades, own))
+    traded = trade_columns(own)
+    ahead = rows_ahead(own[LEVELS - 1])
+    next_, last, across, ahead, later = lax.optimization_barrier((next_, last, across, ahead, own))
     low, high = jnp.stack([own, next_]), jnp.stack([across, last])
     up_low, down_high = plane_move(1, False)(low), plane_move(-1, False)(high)
     up_high, down_low = plane_move(1, False)(high), plane_move(-1, False)(low)
-    trades += [trade_quarter(later, zh, 2), trade_quarter(later, zh, 3)]
     zero = project([low, high], weight)
-    up_low, down_high, trades, zero, later = lax.optimization_barrier(
-        (up_low, down_high, trades, zero, later)
+    up_low, down_high, traded, zero, later = lax.optimization_barrier(
+        (up_low, down_high, traded, zero, later)
     )
     far_low, far_high = plane_move(1, False)(up_low), plane_move(-1, False)(down_high)
-    halves = high_halves(later[LEVELS - 1], draft_index)
-    traded = jnp.concatenate([t.transpose(0, 2, 1) for t in trades], axis=2)
+    halves = high_halves(jnp.concatenate([later[LEVELS - 1], ahead], axis=0), draft_index)
+    traded = traded.transpose(1, 3, 0, 2).reshape(LEVELS, traded.shape[3], -1)
     one, three = project([up_low, up_high], weight), project([down_low, down_high], weight)
     far_low, far_high, traded, one, three, halves = lax.optimization_barrier(
         (far_low, far_high, traded, one, three, halves)
     )
     every = lax.all_gather(traded, "draft", axis=0, tiled=False)
     groups = [zero, one, project([far_low, far_high], weight), three]
-    target = high_rows(*halves, draft_index)
 
     keep, send = place(groups, core, x, y)
-    got, after = lax.optimization_barrier((from_other_core(send), high_after(target)))
-    mine, *away = join(keep, got, zl)
+    mine, *away = join(keep, from_other_core(send), zl)
     parts = [mine] + [from_zl(block, step) for step, block in zip((1, 2, 3), away)]
     scale = LOSS_SCALE / valid_total(lengths)
-    target = jnp.concatenate([target, after], axis=0)
+    target = high_rows(*halves, draft_index)
     grad = chain(parts, target, mix_gain, tp_index * piece, lengths[zh], scale)
-    fc_grad, mix_total = weight_grad(every, gather_grads(grad), zl, zh, core)
+    fc_grad, mix_total = weight_grad(every, gather_grads(grad), zl, core)
     return (fc_grad.transpose(1, 0, 2), mix_total[0])
 
 

time: 242 us -> 230 us (0.950)
  the two profiles are of different devices: /device:TPU:9 before, /device:TPU:1 now
where the time goes in v4:
time: 230 us; the launch traced here: 226 us
  starting transfers between devices  94.8 us (41%)
  waiting for transfers between devices  34.8 us (15%)
  blocking collectives  34.3 us (15%)
  Pallas kernels  20.3 us (9%)
  local copies, waits for them, and re-layouts  17.7 us (8%)
  between operations  16.4 us (7%)
  other arithmetic  7.2 us (3%)
    all_gather x1, blocking collectives, gather_grads(): stack = lax.all_gather(grad, 'dp', axis=0, tiled=False)  34.3 us
    ppermute x9, starting transfers between devices, plane_move(): return lambda block: lax.ppermute(block, ('tp', 'draft'), pairs)  30.5 us
    ppermute x4, waiting for transfers between devices, from_z(): return lax.ppermute(block, ('tp', 'dp'), pairs)  18.6 us
    all_to_all x1, starting transfers between devices, trade_columns(): lax.all_to_all(quarters, 'dp', split_axis=0, concat_axis=0, tiled=True)  14.8 us
    ppermute x4, starting transfers between devices, from_z(): return lax.ppermute(block, ('tp', 'dp'), pairs)  12.7 us
    pallas_call x4, Pallas kernels, project(): pl.pallas_call(project_kernel, grid=(LEVELS,), out_shape=jax.ShapeDtypeSt...  12.3 us
    ppermute x3, starting transfers between devices, from_zl(): return lax.ppermute(block, 'tp', pairs)  12.3 us
    ppermute x5, starting transfers between devices, from_other_core(): return lax.ppermute(block, 'tp', [(t ^ 1, t) for t in range(ZL * CORES)])  11.8 us
  transfers between devices with their start and end apart: 26, of which 5 were waited for; matrix products, arithmetic and copies ran while one was open for 6% of the time, Pallas kernels for 6%

profile of v4, /device:TPU:1, one launch (start us, length us, event | category | flops | bytes accessed | tf_op | source)
XLA Modules:
  0.0 225.6 jit_solution(12354027210619217588)
XLA Ops:
  7.2 5.9 %collective-permute-start.2 = (bf16[3,64,1024]{2,1,0:T(8,128)(2,1)}, bf16[3,64,1024]{2,1,0:T(8,128)(2,1)S(1)}, u32[]{:S(2)}, u32[]{:S(2)}) collective-permute-start(bf16[3,64,1024]{2,1,0:T(8,128)(2,1)} %bitcast.44), channel_id=1, source_target_pairs={{8,0},{9,1},{10,2},{11,3},{12,4},{13,5},{14,6},{15,7},{0,8},{1,9},... | collective-permute-start | bytes 1179656 | tf_op jit(solution)/shard_map/ppermute | solution.py:31
  13.1 2.3 %collective-permute-start.1 = (bf16[3,64,1024]{2,1,0:T(8,128)(2,1)}, bf16[3,64,1024]{2,1,0:T(8,128)(2,1)}, u32[]{:S(2)}, u32[]{:S(2)}) collective-permute-start(bf16[3,64,1024]{2,1,0:T(8,128)(2,1)} %bitcast.45), channel_id=1, source_target_pairs={{12,0},{13,1},{14,2},{15,3},{0,4},{1,5},{2,6},{3,7},{4,8},{5,9},{6... | collective-permute-start | bytes 1179656 | tf_op jit(solution)/shard_map/ppermute | solution.py:31
  15.4 4.2 %collective-permute-start = (bf16[3,64,1024]{2,1,0:T(8,128)(2,1)}, bf16[3,64,1024]{2,1,0:T(8,128)(2,1)}, u32[]{:S(2)}, u32[]{:S(2)}) collective-permute-start(bf16[3,64,1024]{2,1,0:T(8,128)(2,1)} %bitcast.46), channel_id=1, source_target_pairs={{4,0},{5,1},{6,2},{7,3},{8,4},{9,5},{10,6},{11,7},{12,8},{13,9},{1... | collective-permute-start | bytes 1179656 | tf_op jit(solution)/shard_map/ppermute | solution.py:31
  19.6 1.8 copy.14
  21.4 14.8 %all-to-all-start = ((bf16[4,3,64,256]{3,2,1,0:T(8,128)(2,1)}), bf16[4,3,64,256]{3,2,1,0:T(8,128)(2,1)}, u32[]{:S(2)}, u32[]{:S(2)}) async-start(bf16[4,3,64,256]{3,2,1,0:T(8,128)(2,1)} %bitcast.33), calls=%async_computation | async-start | bytes 786432 | tf_op jit(solution)/shard_map/all_to_all | solution.py:331
  36.2 0.8 slice_bitcast_fusion.1
  37.0 1.3 collective-permute-start.3
  38.3 3.5 %collective-permute-done.3 = bf16[16,1024]{1,0:T(8,128)(2,1)} collective-permute-done((bf16[16,1024]{1,0:T(8,128)(2,1)S(1)}, bf16[16,1024]{1,0:T(8,128)(2,1)}, u32[]{:S(2)}, u32[]{:S(2)}) %collective-permute-start.3) | collective-permute-done | bytes 32800 | tf_op jit(solution)/shard_map/ppermute | solution.py:325
  41.7 0.0 collective-permute-done.2
  41.7 2.1 pad_maximum_fusion.refs_0_
  43.8 4.4 %collective-permute-start.4 = (bf16[2,3,64,1024]{3,2,1,0:T(8,128)(2,1)}, bf16[2,3,64,1024]{3,2,1,0:T(8,128)(2,1)}, u32[]{:S(2)}, u32[]{:S(2)}) collective-permute-start(bf16[2,3,64,1024]{3,2,1,0:T(8,128)(2,1)} %pad_maximum_fusion.refs_0_), channel_id=1, source_target_pairs={{1,0},{2,1},{3,2},{0,3},{5,4},{6,5},{7,6},{4,7},{9,8},{10,9},{11,1... | collective-permute-start | bytes 2359304 | tf_op jit(solution)/shard_map/ppermute | solution.py:31
  48.2 2.0 pad_maximum_fusion.1.refs_1_
  50.2 1.9 collective-permute-start.5
  52.1 2.7 %collective-permute-start.9 = (bf16[2,3,64,1024]{3,2,1,0:T(8,128)(2,1)}, bf16[2,3,64,1024]{3,2,1,0:T(8,128)(2,1)}, u32[]{:S(2)}, u32[]{:S(2)}) collective-permute-start(bf16[2,3,64,1024]{3,2,1,0:T(8,128)(2,1)} %pad_maximum_fusion.refs_0_), channel_id=1, source_target_pairs={{3,0},{0,1},{1,2},{2,3},{7,4},{4,5},{5,6},{6,7},{11,8},{8,9},{9,10... | collective-permute-start | bytes 2359304 | tf_op jit(solution)/shard_map/ppermute | solution.py:31
  54.8 3.8 %collective-permute-start.8 = (bf16[2,3,64,1024]{3,2,1,0:T(8,128)(2,1)}, bf16[2,3,64,1024]{3,2,1,0:T(8,128)(2,1)}, u32[]{:S(2)}, u32[]{:S(2)}) collective-permute-start(bf16[2,3,64,1024]{3,2,1,0:T(8,128)(2,1)} %pad_maximum_fusion.1.refs_1_), channel_id=1, source_target_pairs={{1,0},{2,1},{3,2},{0,3},{5,4},{6,5},{7,6},{4,7},{9,8},{10,9},{11,1... | collective-permute-start | bytes 2359304 | tf_op jit(solution)/shard_map/ppermute | solution.py:31
  58.6 3.1 %project.4.refs_0_ = bf16[4,64,512]{2,1,0:T(8,128)(2,1)S(1)} custom-call(bf16[2,3,64,1024]{3,2,1,0:T(8,128)(2,1)} %pad_maximum_fusion.refs_0_, bf16[2,3,64,1024]{3,2,1,0:T(8,128)(2,1)} %pad_maximum_fusion.1.refs_1_, bf16[3,1024,512]{2,1,0:T(8,128)(2,1)S(1)} %bitcast.34), custom_call_target="tpu_custom_call" | custom-call | flops 805306368 | bytes 4718592 | tf_op jit(solution)/shard_map/project/pallas_call | solution.py:79
  61.7 3.0 %collective-permute-done.5.refs_1_ = bf16[2,3,64,1024]{3,2,1,0:T(8,128)(2,1)} collective-permute-done((bf16[2,3,64,1024]{3,2,1,0:T(8,128)(2,1)}, bf16[2,3,64,1024]{3,2,1,0:T(8,128)(2,1)}, u32[]{:S(2)}, u32[]{:S(2)}) %collective-permute-start.5) | collective-permute-done | bytes 786464 | tf_op jit(solution)/shard_map/ppermute | solution.py:31
  64.7 1.9 collective-permute-start.6
  66.6 3.4 %collective-permute-start.7 = (bf16[2,3,64,1024]{3,2,1,0:T(8,128)(2,1)}, bf16[2,3,64,1024]{3,2,1,0:T(8,128)(2,1)}, u32[]{:S(2)}, u32[]{:S(2)}) collective-permute-start(bf16[2,3,64,1024]{3,2,1,0:T(8,128)(2,1)} %collective-permute-done.5.refs_1_), channel_id=1, source_target_pairs={{3,0},{0,1},{1,2},{2,3},{7,4},{4,5},{5,6},{6,7},{11,8},{8,9},{9,10... | collective-permute-start | bytes 2359304 | tf_op jit(solution)/shard_map/ppermute | solution.py:31
  70.0 0.9 slice_bitcast_fusion
  70.9 0.8 broadcast_select_fusion.1
  71.8 9.6 %collective-permute-start.11 = (bf16[80,512]{1,0:T(8,128)(2,1)S(1)}, bf16[80,512]{1,0:T(8,128)(2,1)S(1)}, u32[]{:S(2)}, u32[]{:S(2)}) collective-permute-start(bf16[80,512]{1,0:T(8,128)(2,1)S(1)} %get-tuple-element.63), channel_id=1, source_target_pairs={{0,1},{1,0},{2,65},{3,64},{4,129},{5,128},{6,193},{7,192},{8,257},... | collective-permute-start | bytes 245768 | tf_op jit(solution)/shard_map/ppermute | solution.py:314
  81.3 1.9 collective-permute-start.10
  83.3 3.1 %project.6.refs_3_ = bf16[4,64,512]{2,1,0:T(8,128)(2,1)S(1)} custom-call(bf16[2,3,64,1024]{3,2,1,0:T(8,128)(2,1)} %collective-permute-done.9.refs_0_, bf16[2,3,64,1024]{3,2,1,0:T(8,128)(2,1)} %collective-permute-done.5.refs_1_, bf16[3,1024,512]{2,1,0:T(8,128)(2,1)S(1)} %bitcast.35), custom_call_target="tpu_custom_call" | custom-call | flops 805306368 | bytes 4718592 | tf_op jit(solution)/shard_map/project/pallas_call | solution.py:79
  86.4 0.7 copy-done.1
  87.1 1.8 copy.10
  88.9 3.1 %project.5.refs_1_ = bf16[4,64,512]{2,1,0:T(8,128)(2,1)S(1)} custom-call(bf16[2,3,64,1024]{3,2,1,0:T(8,128)(2,1)} %collective-permute-done.4.refs_0_, bf16[2,3,64,1024]{3,2,1,0:T(8,128)(2,1)} %collective-permute-done.8.refs_1_, bf16[3,1024,512]{2,1,0:T(8,128)(2,1)S(1)} %bitcast.36), custom_call_target="tpu_custom_call" | custom-call | flops 805306368 | bytes 4718592 | tf_op jit(solution)/shard_map/project/pallas_call | solution.py:79
  92.0 0.7 copy-done.3
  92.7 2.0 copy.11
  94.7 0.0 all-gather.4.cloned.1.call-update
  94.7 0.1 pad_add_fusion.2.meta_ref
  94.8 3.1 %project.7.refs_2_ = bf16[4,64,512]{2,1,0:T(8,128)(2,1)S(1)} custom-call(bf16[2,3,64,1024]{3,2,1,0:T(8,128)(2,1)} %collective-permute-done.6.refs_0_, bf16[2,3,64,1024]{3,2,1,0:T(8,128)(2,1)} %collective-permute-done.7.refs_1_, bf16[3,1024,512]{2,1,0:T(8,128)(2,1)S(1)} %bitcast.37), custom_call_target="tpu_custom_call" | custom-call | flops 805306368 | bytes 4718592 | tf_op jit(solution)/shard_map/project/pallas_call | solution.py:79
  97.9 0.9 copy-done.2
  98.8 0.9 copy-done.4
  99.8 0.8 place.1
  100.6 1.9 collective-permute-start.12
  102.6 0.6 dynamic_slice.3
  103.1 0.7 maximum_reduce_fusion
  105.7 0.6 pad_add_fusion.1.meta_ref
  106.3 0.1 join.1
  106.5 8.1 %collective-permute-start.13 = (bf16[144,512]{1,0:T(8,128)(2,1)S(1)}, bf16[144,512]{1,0:T(8,128)(2,1)S(1)}, u32[]{:S(2)}, u32[]{:S(2)}) collective-permute-start(bf16[144,512]{1,0:T(8,128)(2,1)S(1)} %get-tuple-element.48), channel_id=1, source_target_pairs={{128,0},{192,64},{256,128},{320,192},{384,256},{448,320},{0,384},{... | collective-permute-start | bytes 442376 | tf_op jit(solution)/shard_map/ppermute | solution.py:40
  114.6 1.9 collective-permute-start.14
  116.5 2.3 %collective-permute-start.15 = (bf16[144,512]{1,0:T(8,128)(2,1)S(1)}, bf16[144,512]{1,0:T(8,128)(2,1)S(1)}, u32[]{:S(2)}, u32[]{:S(2)}) collective-permute-start(bf16[144,512]{1,0:T(8,128)(2,1)S(1)} %get-tuple-element.50), channel_id=1, source_target_pairs={{384,0},{448,64},{0,128},{64,192},{128,256},{192,320},{256,384},{3... | collective-permute-start | bytes 442376 | tf_op jit(solution)/shard_map/ppermute | solution.py:40
  118.8 0.9 slice_select_fusion
  119.7 8.9 %collective-permute-done.14.refs_2_ = bf16[144,512]{1,0:T(8,128)(2,1)S(1)} collective-permute-done((bf16[144,512]{1,0:T(8,128)(2,1)S(1)}, bf16[144,512]{1,0:T(8,128)(2,1)S(1)}, u32[]{:S(2)}, u32[]{:S(2)}) %collective-permute-start.14) | collective-permute-done | bytes 147488 | tf_op jit(solution)/shard_map/ppermute | solution.py:40
  128.6 1.4 chain.1
  130.0 34.3 %all-gather.1 = bf16[576,512]{1,0:T(8,128)(2,1)S(1)} all-gather(bf16[144,512]{1,0:T(8,128)(2,1)S(1)} %chain.1), channel_id=3, replica_groups=mesh['tp'=8,'dp'=4,'draft'=16] {'dp'}, dimensions={0}, use_global_device_ids=true | all-gather | bytes 737280 | tf_op jit(solution)/shard_map/all_gather | solution.py:335
  164.3 2.4 %collective-permute-start.18 = (bf16[4,144,512]{2,1,0:T(8,128)(2,1)S(1)}, bf16[4,144,512]{2,1,0:T(8,128)(2,1)S(1)}, u32[]{:S(2)}, u32[]{:S(2)}) collective-permute-start(bf16[4,144,512]{2,1,0:T(8,128)(2,1)S(1)} %bitcast.38), channel_id=1, source_target_pairs={{64,0},{0,64},{192,128},{128,192},{320,256},{256,320},{448,384},{3... | collective-permute-start | bytes 1769480 | tf_op jit(solution)/shard_map/ppermute | solution.py:35
  166.6 1.9 collective-permute-start.17
  168.6 4.6 %collective-permute-start.16 = (bf16[4,144,512]{2,1,0:T(8,128)(2,1)S(1)}, bf16[4,144,512]{2,1,0:T(8,128)(2,1)S(1)}, u32[]{:S(2)}, u32[]{:S(2)}) collective-permute-start(bf16[4,144,512]{2,1,0:T(8,128)(2,1)S(1)} %bitcast.40), channel_id=1, source_target_pairs={{128,0},{144,16},{160,32},{176,48},{192,64},{208,80},{224,96},{240... | collective-permute-start | bytes 1769480 | tf_op jit(solution)/shard_map/ppermute | solution.py:53
  173.2 1.9 collective-permute-start.21
  175.1 4.3 %collective-permute-start.22 = (bf16[2,144,512]{2,1,0:T(8,128)(2,1)S(1)}, bf16[2,144,512]{2,1,0:T(8,128)(2,1)S(1)}, u32[]{:S(2)}, u32[]{:S(2)}) collective-permute-start(bf16[2,144,512]{2,1,0:T(8,128)(2,1)S(1)} %bitcast.53), channel_id=1, source_target_pairs={{304,0},{256,16},{272,32},{288,48},{368,64},{320,80},{336,96},{352... | collective-permute-start | bytes 884744 | tf_op jit(solution)/shard_map/ppermute | solution.py:53
  179.4 18.6 %collective-permute-done.21 = bf16[2,144,512]{2,1,0:T(8,128)(2,1)S(1)} collective-permute-done((bf16[2,144,512]{2,1,0:T(8,128)(2,1)S(1)}, bf16[2,144,512]{2,1,0:T(8,128)(2,1)S(1)}, u32[]{:S(2)}, u32[]{:S(2)}) %collective-permute-start.21) | collective-permute-done | bytes 294944 | tf_op jit(solution)/shard_map/ppermute | solution.py:53
  198.1 3.2 %collective-permute-start.23 = (bf16[4,144,512]{2,1,0:T(8,128)(2,1)S(1)}, bf16[4,144,512]{2,1,0:T(8,128)(2,1)S(1)}, u32[]{:S(2)}, u32[]{:S(2)}) collective-permute-start(bf16[4,144,512]{2,1,0:T(8,128)(2,1)S(1)} %constant_dynamic-update-slice_fusion.refs_6_), channel_id=1, source_target_pairs={{64,0},{0,64},{192,128},{128,192},{320,256},{256,320},{448,384},{3... | collective-permute-start | bytes 1769480 | tf_op jit(solution)/shard_map/ppermute | solution.py:35
  201.3 1.9 collective-permute-start.19
  203.3 2.4 %collective-permute-start.20 = (bf16[4,144,512]{2,1,0:T(8,128)(2,1)S(1)}, bf16[4,144,512]{2,1,0:T(8,128)(2,1)S(1)}, u32[]{:S(2)}, u32[]{:S(2)}) collective-permute-start(bf16[4,144,512]{2,1,0:T(8,128)(2,1)S(1)} %collective-permute-done.17.refs_3_), channel_id=1, source_target_pairs={{64,0},{0,64},{192,128},{128,192},{320,256},{256,320},{448,384},{3... | collective-permute-start | bytes 1769480 | tf_op jit(solution)/shard_map/ppermute | solution.py:35
  205.7 0.1 pad_add_fusion.meta_ref
  205.8 0.8 copy-done.7
  206.6 0.7 collective-permute-done.20.refs_5_
  207.3 0.8 copy-done.9
  208.1 2.8 %copy-done.6 = bf16[48,256,256]{2,1,0:T(8,128)(2,1)S(1)} copy-done((bf16[48,256,256]{2,1,0:T(8,128)(2,1)S(1)}, bf16[48,256,256]{2,1,0:T(8,128)(2,1)}, u32[]{:S(2)}) %copy-start.6) | copy-done | bytes 6291480
  210.9 1.1 copy-done.8
  212.0 1.1 copy-done.10
  213.0 5.7 %weight_grad.1 = (bf16[3,256,512]{2,1,0:T(8,128)(2,1)}, f32[1,512]{1,0:T(1,128)}) custom-call(s32[2]{0:T(128)S(1)} %pad_add_fusion.meta_ref, bf16[16,3,256,256]{3,2,1,0:T(8,128)(2,1)S(1)} %bitcast.43, bf16[4,144,512]{2,1,0:T(8,128)(2,1)S(1)} %bitcast.41, bf16[4,144,512]{2,1,0:T(8,128)(2,1)S(1)} %collective-permute-done.18.refs_1_, ...), custom_call_target="tpu_custom_call" | custom-call | flops 3221225472 | bytes 10485760 | tf_op jit(solution)/shard_map/weight_grad/pallas_call | solution.py:270
  (41 shorter events, 0.2 us)
Async XLA Ops:
  7.2 51.4 %copy-start = (bf16[1024,3,512]{2,0,1:T(8,128)(2,1)S(1)}, bf16[1024,3,512]{2,0,1:T(8,128)(2,1)}, u32[]{:S(2)}) copy-start(bf16[1024,3,512]{2,0,1:T(8,128)(2,1)} %param.5) | copy-start | bytes 9437188
  7.2 34.6 %collective-permute-start.2 = (bf16[3,64,1024]{2,1,0:T(8,128)(2,1)}, bf16[3,64,1024]{2,1,0:T(8,128)(2,1)S(1)}, u32[]{:S(2)}, u32[]{:S(2)}) collective-permute-start(bf16[3,64,1024]{2,1,0:T(8,128)(2,1)} %bitcast.44), channel_id=1, source_target_pairs={{8,0},{9,1},{10,2},{11,3},{12,4},{13,5},{14,6},{15,7},{0,8},{1,9},... | collective-permute-start | bytes 1179656 | tf_op jit(solution)/shard_map/ppermute | solution.py:31
  13.1 28.6 %collective-permute-start.1 = (bf16[3,64,1024]{2,1,0:T(8,128)(2,1)}, bf16[3,64,1024]{2,1,0:T(8,128)(2,1)}, u32[]{:S(2)}, u32[]{:S(2)}) collective-permute-start(bf16[3,64,1024]{2,1,0:T(8,128)(2,1)} %bitcast.45), channel_id=1, source_target_pairs={{12,0},{13,1},{14,2},{15,3},{0,4},{1,5},{2,6},{3,7},{4,8},{5,9},{6... | collective-permute-start | bytes 1179656 | tf_op jit(solution)/shard_map/ppermute | solution.py:31
  15.4 26.3 %collective-permute-start = (bf16[3,64,1024]{2,1,0:T(8,128)(2,1)}, bf16[3,64,1024]{2,1,0:T(8,128)(2,1)}, u32[]{:S(2)}, u32[]{:S(2)}) collective-permute-start(bf16[3,64,1024]{2,1,0:T(8,128)(2,1)} %bitcast.46), channel_id=1, source_target_pairs={{4,0},{5,1},{6,2},{7,3},{8,4},{9,5},{10,6},{11,7},{12,8},{13,9},{1... | collective-permute-start | bytes 1179656 | tf_op jit(solution)/shard_map/ppermute | solution.py:31
  21.4 40.3 %all-to-all-start = ((bf16[4,3,64,256]{3,2,1,0:T(8,128)(2,1)}), bf16[4,3,64,256]{3,2,1,0:T(8,128)(2,1)}, u32[]{:S(2)}, u32[]{:S(2)}) async-start(bf16[4,3,64,256]{3,2,1,0:T(8,128)(2,1)} %bitcast.33), calls=%async_computation | async-start | bytes 786432 | tf_op jit(solution)/shard_map/all_to_all | solution.py:331
  36.2 171.9 %all-gather.4.cloned.1.call-start = ((), (), s32[]{:S(2)}) async-start(), calls=%async_computation.1 | async-start | bytes 6684672 | tf_op jit(solution)/shard_map/all_gather | solution.py:373
  37.0 4.8 %collective-permute-start.3 = (bf16[16,1024]{1,0:T(8,128)(2,1)S(1)}, bf16[16,1024]{1,0:T(8,128)(2,1)}, u32[]{:S(2)}, u32[]{:S(2)}) collective-permute-start(bf16[16,1024]{1,0:T(8,128)(2,1)S(1)} %slice_bitcast_fusion.1), channel_id=1, source_target_pairs={{1,0},{2,1},{3,2},{4,3},{5,4},{6,5},{7,6},{8,7},{9,8},{10,9},{11,1... | collective-permute-start | bytes 98312 | tf_op jit(solution)/shard_map/ppermute | solution.py:325
  43.8 17.9 %collective-permute-start.4 = (bf16[2,3,64,1024]{3,2,1,0:T(8,128)(2,1)}, bf16[2,3,64,1024]{3,2,1,0:T(8,128)(2,1)}, u32[]{:S(2)}, u32[]{:S(2)}) collective-permute-start(bf16[2,3,64,1024]{3,2,1,0:T(8,128)(2,1)} %pad_maximum_fusion.refs_0_), channel_id=1, source_target_pairs={{1,0},{2,1},{3,2},{0,3},{5,4},{6,5},{7,6},{4,7},{9,8},{10,9},{11,1... | collective-permute-start | bytes 2359304 | tf_op jit(solution)/shard_map/ppermute | solution.py:31
  50.2 14.5 %collective-permute-start.5 = (bf16[2,3,64,1024]{3,2,1,0:T(8,128)(2,1)}, bf16[2,3,64,1024]{3,2,1,0:T(8,128)(2,1)}, u32[]{:S(2)}, u32[]{:S(2)}) collective-permute-start(bf16[2,3,64,1024]{3,2,1,0:T(8,128)(2,1)} %pad_maximum_fusion.1.refs_1_), channel_id=1, source_target_pairs={{3,0},{0,1},{1,2},{2,3},{7,4},{4,5},{5,6},{6,7},{11,8},{8,9},{9,10... | collective-permute-start | bytes 2359304 | tf_op jit(solution)/shard_map/ppermute | solution.py:31
  52.1 29.3 %collective-permute-start.9 = (bf16[2,3,64,1024]{3,2,1,0:T(8,128)(2,1)}, bf16[2,3,64,1024]{3,2,1,0:T(8,128)(2,1)}, u32[]{:S(2)}, u32[]{:S(2)}) collective-permute-start(bf16[2,3,64,1024]{3,2,1,0:T(8,128)(2,1)} %pad_maximum_fusion.refs_0_), channel_id=1, source_target_pairs={{3,0},{0,1},{1,2},{2,3},{7,4},{4,5},{5,6},{6,7},{11,8},{8,9},{9,10... | collective-permute-start | bytes 2359304 | tf_op jit(solution)/shard_map/ppermute | solution.py:31
  54.8 34.1 %collective-permute-start.8 = (bf16[2,3,64,1024]{3,2,1,0:T(8,128)(2,1)}, bf16[2,3,64,1024]{3,2,1,0:T(8,128)(2,1)}, u32[]{:S(2)}, u32[]{:S(2)}) collective-permute-start(bf16[2,3,64,1024]{3,2,1,0:T(8,128)(2,1)} %pad_maximum_fusion.1.refs_1_), channel_id=1, source_target_pairs={{1,0},{2,1},{3,2},{0,3},{5,4},{6,5},{7,6},{4,7},{9,8},{10,9},{11,1... | collective-permute-start | bytes 2359304 | tf_op jit(solution)/shard_map/ppermute | solution.py:31
  64.7 28.0 %collective-permute-start.6 = (bf16[2,3,64,1024]{3,2,1,0:T(8,128)(2,1)}, bf16[2,3,64,1024]{3,2,1,0:T(8,128)(2,1)}, u32[]{:S(2)}, u32[]{:S(2)}) collective-permute-start(bf16[2,3,64,1024]{3,2,1,0:T(8,128)(2,1)} %collective-permute-done.4.refs_0_), channel_id=1, source_target_pairs={{1,0},{2,1},{3,2},{0,3},{5,4},{6,5},{7,6},{4,7},{9,8},{10,9},{11,1... | collective-permute-start | bytes 2359304 | tf_op jit(solution)/shard_map/ppermute | solution.py:31
  66.6 26.1 %collective-permute-start.7 = (bf16[2,3,64,1024]{3,2,1,0:T(8,128)(2,1)}, bf16[2,3,64,1024]{3,2,1,0:T(8,128)(2,1)}, u32[]{:S(2)}, u32[]{:S(2)}) collective-permute-start(bf16[2,3,64,1024]{3,2,1,0:T(8,128)(2,1)} %collective-permute-done.5.refs_1_), channel_id=1, source_target_pairs={{3,0},{0,1},{1,2},{2,3},{7,4},{4,5},{5,6},{6,7},{11,8},{8,9},{9,10... | collective-permute-start | bytes 2359304 | tf_op jit(solution)/shard_map/ppermute | solution.py:31
  71.8 20.9 %collective-permute-start.11 = (bf16[80,512]{1,0:T(8,128)(2,1)S(1)}, bf16[80,512]{1,0:T(8,128)(2,1)S(1)}, u32[]{:S(2)}, u32[]{:S(2)}) collective-permute-start(bf16[80,512]{1,0:T(8,128)(2,1)S(1)} %get-tuple-element.63), channel_id=1, source_target_pairs={{0,1},{1,0},{2,65},{3,64},{4,129},{5,128},{6,193},{7,192},{8,257},... | collective-permute-start | bytes 245768 | tf_op jit(solution)/shard_map/ppermute | solution.py:314
  81.3 11.4 %collective-permute-start.10 = (bf16[80,512]{1,0:T(8,128)(2,1)S(1)}, bf16[80,512]{1,0:T(8,128)(2,1)}, u32[]{:S(2)}, u32[]{:S(2)}) collective-permute-start(bf16[80,512]{1,0:T(8,128)(2,1)S(1)} %get-tuple-element.64), channel_id=1, source_target_pairs={{0,0},{1,1},{2,64},{3,65},{4,128},{5,129},{6,192},{7,193},{8,256},... | collective-permute-start | bytes 245768 | tf_op jit(solution)/shard_map/ppermute | solution.py:313
  86.4 0.7 copy-start.1
  88.8 13.7 %copy-start.11 = (s32[4]{0:T(128)S(1)}, s32[4]{0:T(128)}, u32[]{:S(2)}) copy-start(s32[4]{0:T(128)} %param.7) | copy-start | bytes 52
  88.8 39.8 %copy-start.5 = (f32[512]{0:T(512)S(1)}, f32[512]{0:T(512)}, u32[]{:S(2)}) copy-start(f32[512]{0:T(512)} %param.6) | copy-start | bytes 6148
  91.9 0.7 copy-start.3
  97.9 1.0 copy-start.2
  98.8 0.9 copy-start.4
  100.6 5.7 %collective-permute-start.12 = (bf16[4,144,512]{2,1,0:T(8,128)(2,1)S(1)}, bf16[4,144,512]{2,1,0:T(8,128)(2,1)S(1)}, u32[]{:S(2)}, u32[]{:S(2)}) collective-permute-start(bf16[4,144,512]{2,1,0:T(8,128)(2,1)S(1)} %get-tuple-element.46), channel_id=1, source_target_pairs={{64,0},{0,64},{192,128},{128,192},{320,256},{256,320},{448,384},{3... | collective-permute-start | bytes 1769480 | tf_op jit(solution)/shard_map/ppermute | solution.py:35
  106.5 13.2 %collective-permute-start.13 = (bf16[144,512]{1,0:T(8,128)(2,1)S(1)}, bf16[144,512]{1,0:T(8,128)(2,1)S(1)}, u32[]{:S(2)}, u32[]{:S(2)}) collective-permute-start(bf16[144,512]{1,0:T(8,128)(2,1)S(1)} %get-tuple-element.48), channel_id=1, source_target_pairs={{128,0},{192,64},{256,128},{320,192},{384,256},{448,320},{0,384},{... | collective-permute-start | bytes 442376 | tf_op jit(solution)/shard_map/ppermute | solution.py:40
  114.6 14.0 %collective-permute-start.14 = (bf16[144,512]{1,0:T(8,128)(2,1)S(1)}, bf16[144,512]{1,0:T(8,128)(2,1)S(1)}, u32[]{:S(2)}, u32[]{:S(2)}) collective-permute-start(bf16[144,512]{1,0:T(8,128)(2,1)S(1)} %get-tuple-element.49), channel_id=1, source_target_pairs={{256,0},{320,64},{384,128},{448,192},{0,256},{64,320},{128,384},{1... | collective-permute-start | bytes 442376 | tf_op jit(solution)/shard_map/ppermute | solution.py:40
  116.5 12.1 %collective-permute-start.15 = (bf16[144,512]{1,0:T(8,128)(2,1)S(1)}, bf16[144,512]{1,0:T(8,128)(2,1)S(1)}, u32[]{:S(2)}, u32[]{:S(2)}) collective-permute-start(bf16[144,512]{1,0:T(8,128)(2,1)S(1)} %get-tuple-element.50), channel_id=1, source_target_pairs={{384,0},{448,64},{0,128},{64,192},{128,256},{192,320},{256,384},{3... | collective-permute-start | bytes 442376 | tf_op jit(solution)/shard_map/ppermute | solution.py:40
  164.3 37.0 %collective-permute-start.18 = (bf16[4,144,512]{2,1,0:T(8,128)(2,1)S(1)}, bf16[4,144,512]{2,1,0:T(8,128)(2,1)S(1)}, u32[]{:S(2)}, u32[]{:S(2)}) collective-permute-start(bf16[4,144,512]{2,1,0:T(8,128)(2,1)S(1)} %bitcast.38), channel_id=1, source_target_pairs={{64,0},{0,64},{192,128},{128,192},{320,256},{256,320},{448,384},{3... | collective-permute-start | bytes 1769480 | tf_op jit(solution)/shard_map/ppermute | solution.py:35
  166.6 34.7 %collective-permute-start.17 = (bf16[4,144,512]{2,1,0:T(8,128)(2,1)S(1)}, bf16[4,144,512]{2,1,0:T(8,128)(2,1)S(1)}, u32[]{:S(2)}, u32[]{:S(2)}) collective-permute-start(bf16[4,144,512]{2,1,0:T(8,128)(2,1)S(1)} %bitcast.39), channel_id=1, source_target_pairs={{432,0},{384,16},{400,32},{416,48},{496,64},{448,80},{464,96},{480... | collective-permute-start | bytes 1769480 | tf_op jit(solution)/shard_map/ppermute | solution.py:53
  168.6 32.7 %collective-permute-start.16 = (bf16[4,144,512]{2,1,0:T(8,128)(2,1)S(1)}, bf16[4,144,512]{2,1,0:T(8,128)(2,1)S(1)}, u32[]{:S(2)}, u32[]{:S(2)}) collective-permute-start(bf16[4,144,512]{2,1,0:T(8,128)(2,1)S(1)} %bitcast.40), channel_id=1, source_target_pairs={{128,0},{144,16},{160,32},{176,48},{192,64},{208,80},{224,96},{240... | collective-permute-start | bytes 1769480 | tf_op jit(solution)/shard_map/ppermute | solution.py:53
  173.2 24.8 %collective-permute-start.21 = (bf16[2,144,512]{2,1,0:T(8,128)(2,1)S(1)}, bf16[2,144,512]{2,1,0:T(8,128)(2,1)S(1)}, u32[]{:S(2)}, u32[]{:S(2)}) collective-permute-start(bf16[2,144,512]{2,1,0:T(8,128)(2,1)S(1)} %bitcast.54), channel_id=1, source_target_pairs={{256,0},{272,16},{288,32},{304,48},{320,64},{336,80},{352,96},{368... | collective-permute-start | bytes 884744 | tf_op jit(solution)/shard_map/ppermute | solution.py:53
  175.1 22.9 %collective-permute-start.22 = (bf16[2,144,512]{2,1,0:T(8,128)(2,1)S(1)}, bf16[2,144,512]{2,1,0:T(8,128)(2,1)S(1)}, u32[]{:S(2)}, u32[]{:S(2)}) collective-permute-start(bf16[2,144,512]{2,1,0:T(8,128)(2,1)S(1)} %bitcast.53), channel_id=1, source_target_pairs={{304,0},{256,16},{272,32},{288,48},{368,64},{320,80},{336,96},{352... | collective-permute-start | bytes 884744 | tf_op jit(solution)/shard_map/ppermute | solution.py:53
  198.1 7.7 %collective-permute-start.23 = (bf16[4,144,512]{2,1,0:T(8,128)(2,1)S(1)}, bf16[4,144,512]{2,1,0:T(8,128)(2,1)S(1)}, u32[]{:S(2)}, u32[]{:S(2)}) collective-permute-start(bf16[4,144,512]{2,1,0:T(8,128)(2,1)S(1)} %constant_dynamic-update-slice_fusion.refs_6_), channel_id=1, source_target_pairs={{64,0},{0,64},{192,128},{128,192},{320,256},{256,320},{448,384},{3... | collective-permute-start | bytes 1769480 | tf_op jit(solution)/shard_map/ppermute | solution.py:35
  201.3 4.4 %collective-permute-start.19 = (bf16[4,144,512]{2,1,0:T(8,128)(2,1)S(1)}, bf16[4,144,512]{2,1,0:T(8,128)(2,1)S(1)}, u32[]{:S(2)}, u32[]{:S(2)}) collective-permute-start(bf16[4,144,512]{2,1,0:T(8,128)(2,1)S(1)} %collective-permute-done.16.refs_2_), channel_id=1, source_target_pairs={{64,0},{0,64},{192,128},{128,192},{320,256},{256,320},{448,384},{3... | collective-permute-start | bytes 1769480 | tf_op jit(solution)/shard_map/ppermute | solution.py:35
  203.3 4.0 %collective-permute-start.20 = (bf16[4,144,512]{2,1,0:T(8,128)(2,1)S(1)}, bf16[4,144,512]{2,1,0:T(8,128)(2,1)S(1)}, u32[]{:S(2)}, u32[]{:S(2)}) collective-permute-start(bf16[4,144,512]{2,1,0:T(8,128)(2,1)S(1)} %collective-permute-done.17.refs_3_), channel_id=1, source_target_pairs={{64,0},{0,64},{192,128},{128,192},{320,256},{256,320},{448,384},{3... | collective-permute-start | bytes 1769480 | tf_op jit(solution)/shard_map/ppermute | solution.py:35
  205.8 0.8 copy-start.7
  207.3 0.8 copy-start.9
  208.1 2.8 %copy-start.6 = (bf16[48,256,256]{2,1,0:T(8,128)(2,1)S(1)}, bf16[48,256,256]{2,1,0:T(8,128)(2,1)}, u32[]{:S(2)}) copy-start(bf16[48,256,256]{2,1,0:T(8,128)(2,1)} %all-gather.4.cloned.1.call-done) | copy-start | bytes 18874372
  210.9 1.1 copy-start.8
  211.9 1.1 copy-start.10
Sparse Core Ops, SparseCore 0:
  94.8 78.8 all-gather.3

commit v5 on v4

--- a/solution.py
+++ b/solution.py
@@ -53,11 +53,34 @@
     return lax.ppermute(block, ("tp", "dp"), pairs)
 
 
-def project_kernel(*refs):
-    *block_refs, weight_ref, out_ref, total_ref = refs
+def pair_kernel(first_ref, second_ref, out_ref, sem):
+    first = pltpu.make_async_copy(first_ref, out_ref.at[0], sem.at[0])
+    second = pltpu.make_async_copy(second_ref, out_ref.at[1], sem.at[1])
+    first.start()
+    second.start()
+    first.wait()
+    second.wait()
+
+
+def pair(first, second):
+    anywhere = pl.BlockSpec(memory_space=pl.ANY)
+    return pl.pallas_call(
+        pair_kernel,
+        out_shape=jax.ShapeDtypeStruct((2,) + first.shape, first.dtype),
+        in_specs=[anywhere] * 2,
+        out_specs=anywhere,
+        scratch_shapes=[pltpu.SemaphoreType.DMA((2,))],
+        cost_estimate=pl.CostEstimate(flops=0, bytes_accessed=8 * first.size, transcendentals=0),
+        name="pair",
+    )(first, second)
+
+
+def rows_of(block_refs):
+    return jnp.concatenate([r[...].reshape(-1, r.shape[-1]) for r in block_refs], axis=0)
+
+
+def accumulate(total_ref, term):
     level = pl.program_id(0)
-    rows = jnp.concatenate([r[...].reshape(-1, r.shape[-1]) for r in block_refs], axis=0)
-    term = jnp.dot(rows, weight_ref[0], preferred_element_type=jnp.float32)
 
     @pl.when(level == 0)
     def _():
@@ -67,73 +90,104 @@
     def _():
         total_ref[...] += term
 
-    @pl.when(level == LEVELS - 1)
+
+def project_kernel(*refs):
+    *block_refs, weight_ref, out_ref, total_ref = refs
+    accumulate(
+        total_ref, jnp.dot(rows_of(block_refs), weight_ref[0], preferred_element_type=jnp.float32)
+    )
+
+    @pl.when(pl.program_id(0) == LEVELS - 1)
     def _():
         out_ref[...] = total_ref[...].astype(jnp.bfloat16).reshape(out_ref.shape)
 
 
+def product_specs(blocks, weight):
+    _, _, rows, depth = blocks[0].shape
+    specs = [pl.BlockSpec((b.shape[0], 1, rows, depth), lambda l, *_: (0, l, 0, 0)) for b in blocks]
+    return specs + [pl.BlockSpec((1, depth, weight.shape[2]), lambda l, *_: (l, 0, 0))]
+
+
+def product_cost(blocks, weight):
+    size = sum(b.size for b in blocks)
+    return pl.CostEstimate(
+        flops=2 * size * weight.shape[2], bytes_accessed=2 * (weight.size + size), transcendentals=0
+    )
+
+
 def project(blocks, weight):
-    _, _, rows, depth = blocks[0].shape
+    rows, width = blocks[0].shape[2], weight.shape[2]
     count = sum(b.shape[0] for b in blocks)
-    width = weight.shape[2]
     return pl.pallas_call(
         project_kernel,
         grid=(LEVELS,),
         out_shape=jax.ShapeDtypeStruct((count, rows, width), jnp.bfloat16),
-        in_specs=[
-            pl.BlockSpec((b.shape[0], 1, rows, depth), lambda l: (0, l, 0, 0)) for b in blocks
-        ]
-        + [pl.BlockSpec((1, depth, width), lambda l: (l, 0, 0))],
+        in_specs=product_specs(blocks, weight),
         out_specs=pl.BlockSpec((count, rows, width), lambda l: (0, 0, 0)),
         scratch_shapes=[pltpu.VMEM((count * rows, width), jnp.float32)],
-        compiler_params=params(12),
-        cost_estimate=pl.CostEstimate(
-            flops=2 * count * rows * LEVELS * depth * width,
-            bytes_accessed=2 * (weight.size + count * rows * LEVELS * depth),
-            transcendentals=0,
-        ),
+        compiler_params=params(14),
+        cost_estimate=product_cost(blocks, weight),
         name="project",
     )(*blocks, weight)
 
 
-def place_kernel(meta_ref, *refs):
-    *group_refs, keep_ref, send_ref, token_ref = refs
-    core, x, y = meta_ref[0], meta_ref[1], meta_ref[2]
-    rows = group_refs[0].shape[1]
+def project_place_kernel(meta_ref, *refs):
+    *block_refs, weight_ref, zero_ref, sides_ref, keep_ref, send_ref, total_ref, token_ref = refs
+    accumulate(
+        total_ref, jnp.dot(rows_of(block_refs), weight_ref[0], preferred_element_type=jnp.float32)
+    )
+
+    @pl.when(pl.program_id(0) == LEVELS - 1)
+    def _():
+        core, x, y = meta_ref[0], meta_ref[1], meta_ref[2]
+        rows = zero_ref.shape[1]
+        total = rows * X * Y
+        edge = jnp.zeros((HALO, token_ref.shape[1]), jnp.float32)
+        token_ref[pl.ds(0, HALO), :] = edge
+        token_ref[pl.ds(HALO + total, HALO), :] = edge
+        for second in range(4):
+            for first in range(4):
+                dx = jnp.where(core == 0, first, second)
+                dy = jnp.where(core == 0, second, first)
+                e = lax.rem(x + dx, X) * Y + lax.rem(y + dy, Y)
+                at = pl.multiple_of(e * rows + HALO, 8)
+                if second == 0:
+                    block = zero_ref[first].astype(jnp.float32)
+                elif second == 2:
+                    block = total_ref[pl.ds(first * rows, rows), :]
+                else:
+                    block = sides_ref[second // 2 * 4 + first].astype(jnp.float32)
+                token_ref[pl.ds(at, rows), :] = block
+        piece = total // (ZL * CORES)
+        for zl in range(ZL):
+            for out_ref, whose in ((keep_ref, core), (send_ref, 1 - core)):
+                at = pl.multiple_of((zl * CORES + whose) * piece, 8)
+                out_ref[zl] = token_ref[pl.ds(at, piece + 2 * HALO), :].astype(jnp.bfloat16)
+
+
+def project_place(blocks, weight, zero, sides, core, x, y):
+    _, rows, width = zero.shape
+    count = sum(b.shape[0] for b in blocks)
     total = rows * X * Y
-    edge = jnp.zeros((HALO, token_ref.shape[1]), jnp.float32)
-    token_ref[pl.ds(0, HALO), :] = edge
-    token_ref[pl.ds(HALO + total, HALO), :] = edge
-    for second, group_ref in zip((0, 1, 2, 3), group_refs):
-        for first in range(4):
-            dx = jnp.where(core == 0, first, second)
-            dy = jnp.where(core == 0, second, first)
-            e = lax.rem(x + dx, X) * Y + lax.rem(y + dy, Y)
-            at = pl.multiple_of(e * rows + HALO, 8)
-            token_ref[pl.ds(at, rows), :] = group_ref[first].astype(jnp.float32)
-    piece = total // (ZL * CORES)
-    for zl in range(ZL):
-        for out_ref, whose in ((keep_ref, core), (send_ref, 1 - core)):
-            at = pl.multiple_of((zl * CORES + whose) * piece, 8)
-            out_ref[zl] = token_ref[pl.ds(at, piece + 2 * HALO), :].astype(jnp.bfloat16)
-
-
-def place(groups, core, x, y):
-    _, rows, width = groups[0].shape
-    total = rows * X * Y
-    pieces = jax.ShapeDtypeStruct((ZL, total // (ZL * CORES) + 2 * HALO, width), jnp.bfloat16)
-    return pl.pallas_call(
-        place_kernel,
-        out_shape=(pieces, pieces),
-        in_specs=[SMEM] + [VMEM] * 4,
-        out_specs=(VMEM, VMEM),
-        scratch_shapes=[pltpu.VMEM((total + 2 * HALO, width), jnp.float32)],
-        compiler_params=params(12),
-        cost_estimate=pl.CostEstimate(
-            flops=total * width, bytes_accessed=4 * total * width, transcendentals=0
-        ),
-        name="place",
-    )(jnp.stack([core, x, y]), *groups)
+    pieces = (ZL, total // (ZL * CORES) + 2 * HALO, width)
+    whole = lambda shape: pl.BlockSpec(shape, lambda l, *_: (0, 0, 0))
+    return pl.pallas_call(
+        project_place_kernel,
+        out_shape=(jax.ShapeDtypeStruct(pieces, jnp.bfloat16),) * 2,
+        grid_spec=pltpu.PrefetchScalarGridSpec(
+            num_scalar_prefetch=1,
+            grid=(LEVELS,),
+            in_specs=product_specs(blocks, weight) + [whole(zero.shape), whole(sides.shape)],
+            out_specs=(whole(pieces),) * 2,
+            scratch_shapes=[
+                pltpu.VMEM((count * rows, width), jnp.float32),
+                pltpu.VMEM((total + 2 * HALO, width), jnp.float32),
+            ],
+        ),
+        compiler_params=params(18),
+        cost_estimate=product_cost(blocks, weight),
+        name="project_place",
+    )(jnp.stack([core, x, y]), *blocks, weight, zero, sides)
 
 
 def join_kernel(meta_ref, keep_ref, got_ref, own_ref, *away_refs):
@@ -241,25 +295,42 @@
 
 
 def weight_grad_kernel(meta_ref, features_ref, *refs):
-    *group_refs, out_ref, mix_ref, grads_ref = refs
+    *group_refs, out_ref, mix_ref, grads_ref, tail_ref, held_ref, sem, held_sem = refs
+    level = pl.program_id(0)
     zl, core = meta_ref[0], meta_ref[1]
     half = grads_ref.shape[1] // ZH
     width = grads_ref.shape[2]
 
-    @pl.when(pl.program_id(0) == 0)
+    def held(at):
+        return pltpu.make_async_copy(features_ref.at[:, at], held_ref.at[at], held_sem.at[at])
+
+    @pl.when(level == 0)
     def _():
-        mix = jnp.zeros((TAIL, width), jnp.float32)
-        for group_ref, member in zip(group_refs, pieces_of(zl, core)):
+        copies = []
+        for group, (group_ref, member) in enumerate(zip(group_refs, pieces_of(zl, core))):
             for sequence in range(ZH):
-                slot = pl.ds(sequence * half, half)
                 for part in range(2):
-                    rows = group_ref[sequence, pl.ds(part * half, half), :]
-                    grads_ref[member * 2 + part, slot, :] = rows
-                mix = mix + group_ref[sequence, pl.ds(2 * half, TAIL), :].astype(jnp.float32)
+                    rows = group_ref.at[sequence, pl.ds(part * half, half), :]
+                    slot = grads_ref.at[member * 2 + part, pl.ds(sequence * half, half), :]
+                    copies.append((rows, slot))
+            rows = group_ref.at[:, pl.ds(2 * half, TAIL), :]
+            copies.append((rows, tail_ref.at[pl.ds(group * ZH, ZH)]))
+        copies = [
+            pltpu.make_async_copy(source, target, sem.at[at])
+            for at, (source, target) in enumerate(copies)
+        ]
+        for copy in copies:
+            copy.start()
+        for at in range(LEVELS):
+            held(at).start()
+        for copy in copies:
+            copy.wait()
+        mix = jnp.sum(tail_ref[...].astype(jnp.float32), axis=0)
         mix_ref[...] = jnp.sum(mix, axis=0, keepdims=True)
 
+    held(level).wait()
     blocks = features_ref.shape[0]
-    left = jnp.concatenate([features_ref[e, 0] for e in range(blocks)], axis=1)
+    left = jnp.concatenate([held_ref[level, e] for e in range(blocks)], axis=1)
     right = grads_ref[...].reshape(-1, width)
     out_ref[0] = jnp.dot(left, right, preferred_element_type=jnp.float32).astype(jnp.bfloat16)
 
@@ -267,6 +338,7 @@
 def weight_grad(features, groups, zl, core):
     draft, _, columns, tokens = features.shape
     width = groups[0].shape[2]
+    count = len(groups)
     return pl.pallas_call(
         weight_grad_kernel,
         grid=(LEVELS,),
@@ -274,14 +346,19 @@
             jax.ShapeDtypeStruct((LEVELS, columns, width), jnp.bfloat16),
             jax.ShapeDtypeStruct((1, width), jnp.float32),
         ),
-        in_specs=[SMEM, pl.BlockSpec((draft, 1, columns, tokens), lambda l: (0, l, 0, 0))]
-        + [VMEM] * len(groups),
+        in_specs=[SMEM] + [pl.BlockSpec(memory_space=pltpu.HBM)] * (count + 1),
         out_specs=(
             pl.BlockSpec((1, columns, width), lambda l: (l, 0, 0)),
             pl.BlockSpec((1, width), lambda l: (0, 0)),
         ),
-        scratch_shapes=[pltpu.VMEM((draft, tokens, width), jnp.bfloat16)],
-        compiler_params=params(26),
+        scratch_shapes=[
+            pltpu.VMEM((draft, tokens, width), jnp.bfloat16),
+            pltpu.VMEM((count * ZH, TAIL, width), jnp.bfloat16),
+            pltpu.VMEM((LEVELS, draft, columns, tokens), jnp.bfloat16),
+            pltpu.SemaphoreType.DMA((count * (2 * ZH + 1),)),
+            pltpu.SemaphoreType.DMA((LEVELS,)),
+        ],
+        compiler_params=params(58),
         cost_estimate=pl.CostEstimate(
             flops=2 * draft * LEVELS * columns * tokens * width,
             bytes_accessed=2 * features.size + 2 * draft * tokens * width,
@@ -289,6 +366,25 @@
         ),
         name="weight_grad",
     )(jnp.stack([zl, core]), features, *groups)
+
+
+def turn_kernel(traded_ref, out_ref):
+    rows = traded_ref[:, 0].reshape(-1, traded_ref.shape[3])
+    out_ref[0] = rows.astype(jnp.float32).T.astype(jnp.bfloat16)
+
+
+def turn(traded):
+    sequences, levels, rows, columns = traded.shape
+    return pl.pallas_call(
+        turn_kernel,
+        grid=(levels,),
+        out_shape=jax.ShapeDtypeStruct((levels, columns, sequences * rows), jnp.bfloat16),
+        in_specs=[pl.BlockSpec((sequences, 1, rows, columns), lambda l: (0, l, 0, 0))],
+        out_specs=pl.BlockSpec((1, columns, sequences * rows), lambda l: (l, 0, 0)),
+        compiler_params=params(8),
+        cost_estimate=pl.CostEstimate(flops=0, bytes_accessed=4 * traded.size, transcendentals=0),
+        name="turn",
+    )(traded)
 
 
 def valid_total(lengths):
@@ -352,28 +448,24 @@
     own = features.transpose(1, 0, 2)
     weight = fc_weight.transpose(1, 0, 2)
 
+    traded = trade_columns(own)
     next_, last, across = (plane_move(step, True)(own) for step in (1, 3, 2))
-    traded = trade_columns(own)
-    ahead = rows_ahead(own[LEVELS - 1])
-    next_, last, across, ahead, later = lax.optimization_barrier((next_, last, across, ahead, own))
-    low, high = jnp.stack([own, next_]), jnp.stack([across, last])
+    low, high = pair(own, next_), pair(across, last)
     up_low, down_high = plane_move(1, False)(low), plane_move(-1, False)(high)
     up_high, down_low = plane_move(1, False)(high), plane_move(-1, False)(low)
     zero = project([low, high], weight)
-    up_low, down_high, traded, zero, later = lax.optimization_barrier(
-        (up_low, down_high, traded, zero, later)
+    ahead = rows_ahead(own[LEVELS - 1])
+    up_low, down_high, zero, ahead, traded, later = lax.optimization_barrier(
+        (up_low, down_high, zero, ahead, traded, own)
     )
     far_low, far_high = plane_move(1, False)(up_low), plane_move(-1, False)(down_high)
     halves = high_halves(jnp.concatenate([later[LEVELS - 1], ahead], axis=0), draft_index)
-    traded = traded.transpose(1, 3, 0, 2).reshape(LEVELS, traded.shape[3], -1)
-    one, three = project([up_low, up_high], weight), project([down_low, down_high], weight)
-    far_low, far_high, traded, one, three, halves = lax.optimization_barrier(
-        (far_low, far_high, traded, one, three, halves)
-    )
-    every = lax.all_gather(traded, "draft", axis=0, tiled=False)
-    groups = [zero, one, project([far_low, far_high], weight), three]
-
-    keep, send = place(groups, core, x, y)
+    sides = project([up_low, up_high, down_low, down_high], weight)
+    far_low, far_high, halves, sides, turned = lax.optimization_barrier(
+        (far_low, far_high, halves, sides, turn(traded))
+    )
+    every = lax.all_gather(turned, "draft", axis=0, tiled=False)
+    keep, send = project_place([far_low, far_high], weight, zero, sides, core, x, y)
     mine, *away = join(keep, from_other_core(send), zl)
     parts = [mine] + [from_zl(block, step) for step, block in zip((1, 2, 3), away)]
     scale = LOSS_SCALE / valid_total(lengths)

time: 230 us -> 268 us (1.17)
  Pallas kernels: 20.3 us -> 72.8 us
  waiting for transfers between devices: 34.8 us -> 27.7 us
  local copies, waits for them, and re-layouts: 17.7 us -> 11.7 us
  starting transfers between devices: 94.8 us -> 98.1 us
    pallas_call x1 -> x4, Pallas kernels: 0.81 us -> 56.1 us  [the longest x2 49.9 us: pair(): pl.pallas_call(pair_kernel, out_shape=jax.ShapeDtypeStruct((2,) + first.s...]
    pallas_call x4 -> x2, Pallas kernels: 12.3 us -> 5.67 us  [project(): pl.pallas_call(project_kernel, grid=(LEVELS,), out_shape=jax.ShapeDtypeSt...]
    another operation x3 -> x1, other arithmetic: 4.1 us -> 0.08 us  [project_place(): jnp.stack([core, x, y])]
    pallas_call x1, Pallas kernels: 5.7 us -> 9.55 us  [weight_grad(): pl.pallas_call(weight_grad_kernel, grid=(LEVELS,), out_shape=(jax.ShapeDt...]
    optimization_barrier x2 -> x0, local copies, waits for them, and re-layouts: 3.73 us -> none  [the longest x1 1.97 us: local(): lax.optimization_barrier((far_low, far_high, traded, one, three, halves))]
    ppermute x1, waiting for transfers between devices: 3.47 us -> 0.01 us  [rows_ahead(): lax.ppermute(top[:TAIL], 'draft', [(e, e - 1) for e in range(1, X * Y)])]
    ppermute x9, waiting for transfers between devices: 3.02 us -> 0.02 us  [plane_move(): return lambda block: lax.ppermute(block, ('tp', 'draft'), pairs)]
    unnamed x25 -> x37, local copies, waits for them, and re-layouts: 9.91 us -> 7.61 us
  transfers between devices with their start and end apart: 26 -> 26, of which waited for: 5 -> 3; matrix products, arithmetic and copies ran while one was open for 6% -> 4% of each run, Pallas kernels for 6% -> 24%
where the time goes in v5:
time: 268 us; the launch traced here: 266 us
  starting transfers between devices  98.1 us (37%)
  Pallas kernels  72.8 us (27%)
  blocking collectives  33.9 us (13%)
  waiting for transfers between devices  27.7 us (10%)
  between operations  16.5 us (6%)
  local copies, waits for them, and re-layouts  11.7 us (4%)
  other arithmetic  5.36 us (2%)
    pallas_call x2, Pallas kernels, pair(): pl.pallas_call(pair_kernel, out_shape=jax.ShapeDtypeStruct((2,) + first.s...  49.9 us
    all_gather x1, blocking collectives, gather_grads(): stack = lax.all_gather(grad, 'dp', axis=0, tiled=False)  33.9 us
    ppermute x9, starting transfers between devices, plane_move(): return lambda block: lax.ppermute(block, ('tp', 'draft'), pairs)  33 us
    ppermute x4, waiting for transfers between devices, from_z(): return lax.ppermute(block, ('tp', 'dp'), pairs)  18.6 us
    all_to_all x1, starting transfers between devices, trade_columns(): lax.all_to_all(quarters, 'dp', split_axis=0, concat_axis=0, tiled=True)  14.8 us
    ppermute x3, starting transfers between devices, from_zl(): return lax.ppermute(block, 'tp', pairs)  13.4 us
    ppermute x4, starting transfers between devices, from_z(): return lax.ppermute(block, ('tp', 'dp'), pairs)  12.7 us
    ppermute x5, starting transfers between devices, from_other_core(): return lax.ppermute(block, 'tp', [(t ^ 1, t) for t in range(ZL * CORES)])  11.8 us
  transfers between devices with their start and end apart: 26, of which 3 were waited for; matrix products, arithmetic and copies ran while one was open for 4% of the time, Pallas kernels for 24%

profile of v5, /device:TPU:1, one launch (start us, length us, event | category | flops | bytes accessed | tf_op | source)
XLA Modules:
  0.0 266.1 jit_solution(15661309358442487772)
XLA Ops:
  7.2 4.3 %collective-permute-start.3 = (bf16[3,64,1024]{2,1,0:T(8,128)(2,1)}, bf16[3,64,1024]{2,1,0:T(8,128)(2,1)}, u32[]{:S(2)}, u32[]{:S(2)}) collective-permute-start(bf16[3,64,1024]{2,1,0:T(8,128)(2,1)} %bitcast.34), channel_id=1, source_target_pairs={{12,0},{13,1},{14,2},{15,3},{0,4},{1,5},{2,6},{3,7},{4,8},{5,9},{6... | collective-permute-start | bytes 1179656 | tf_op jit(solution)/shard_map/ppermute | solution.py:31
  11.5 4.5 %collective-permute-start.2 = (bf16[3,64,1024]{2,1,0:T(8,128)(2,1)}, bf16[3,64,1024]{2,1,0:T(8,128)(2,1)}, u32[]{:S(2)}, u32[]{:S(2)}) collective-permute-start(bf16[3,64,1024]{2,1,0:T(8,128)(2,1)} %bitcast.35), channel_id=1, source_target_pairs={{8,0},{9,1},{10,2},{11,3},{12,4},{13,5},{14,6},{15,7},{0,8},{1,9},... | collective-permute-start | bytes 1179656 | tf_op jit(solution)/shard_map/ppermute | solution.py:31
  16.0 3.0 %collective-permute-start = (bf16[3,64,1024]{2,1,0:T(8,128)(2,1)}, bf16[3,64,1024]{2,1,0:T(8,128)(2,1)}, u32[]{:S(2)}, u32[]{:S(2)}) collective-permute-start(bf16[3,64,1024]{2,1,0:T(8,128)(2,1)} %bitcast.36), channel_id=1, source_target_pairs={{4,0},{5,1},{6,2},{7,3},{8,4},{9,5},{10,6},{11,7},{12,8},{13,9},{1... | collective-permute-start | bytes 1179656 | tf_op jit(solution)/shard_map/ppermute | solution.py:31
  19.0 1.8 copy.10
  20.8 14.8 %all-to-all-start = ((bf16[4,3,64,256]{3,2,1,0:T(8,128)(2,1)}), bf16[4,3,64,256]{3,2,1,0:T(8,128)(2,1)S(1)}, u32[]{:S(2)}, u32[]{:S(2)}) async-start(bf16[4,3,64,256]{3,2,1,0:T(8,128)(2,1)} %bitcast.41), calls=%async_computation | async-start | bytes 786432 | tf_op jit(solution)/shard_map/all_to_all | solution.py:427
  35.6 0.0 collective-permute-done.second_ref
  35.6 24.9 %pair.2.refs_0_ = bf16[2,3,64,1024]{3,2,1,0:T(8,128)(2,1)} custom-call(bf16[3,64,1024]{2,1,0:T(8,128)(2,1)} %bitcast.38, bf16[3,64,1024]{2,1,0:T(8,128)(2,1)} %collective-permute-done.second_ref), custom_call_target="tpu_custom_call" | custom-call | bytes 1572864 | tf_op jit(solution)/shard_map/pair/pallas_call | solution.py:67
  60.6 4.4 %collective-permute-start.1 = (bf16[2,3,64,1024]{3,2,1,0:T(8,128)(2,1)}, bf16[2,3,64,1024]{3,2,1,0:T(8,128)(2,1)}, u32[]{:S(2)}, u32[]{:S(2)}) collective-permute-start(bf16[2,3,64,1024]{3,2,1,0:T(8,128)(2,1)} %pair.2.refs_0_), channel_id=1, source_target_pairs={{1,0},{2,1},{3,2},{0,3},{5,4},{6,5},{7,6},{4,7},{9,8},{10,9},{11,1... | collective-permute-start | bytes 2359304 | tf_op jit(solution)/shard_map/ppermute | solution.py:31
  65.0 0.0 collective-permute-done.2.first_ref
  65.0 24.9 %pair.3.refs_1_ = bf16[2,3,64,1024]{3,2,1,0:T(8,128)(2,1)} custom-call(bf16[3,64,1024]{2,1,0:T(8,128)(2,1)} %collective-permute-done.2.first_ref, bf16[3,64,1024]{2,1,0:T(8,128)(2,1)} %collective-permute-done.3.second_ref), custom_call_target="tpu_custom_call" | custom-call | bytes 1572864 | tf_op jit(solution)/shard_map/pair/pallas_call | solution.py:67
  89.9 1.9 collective-permute-start.4
  91.9 2.1 collective-permute-start.11
  94.0 4.4 %collective-permute-start.10 = (bf16[2,3,64,1024]{3,2,1,0:T(8,128)(2,1)}, bf16[2,3,64,1024]{3,2,1,0:T(8,128)(2,1)}, u32[]{:S(2)}, u32[]{:S(2)}) collective-permute-start(bf16[2,3,64,1024]{3,2,1,0:T(8,128)(2,1)} %pair.3.refs_1_), channel_id=1, source_target_pairs={{1,0},{2,1},{3,2},{0,3},{5,4},{6,5},{7,6},{4,7},{9,8},{10,9},{11,1... | collective-permute-start | bytes 2359304 | tf_op jit(solution)/shard_map/ppermute | solution.py:31
  98.4 0.8 slice_bitcast_fusion.1
  99.1 1.3 collective-permute-start.5
  100.4 0.0 copy-start.1
  100.5 1.1 copy-done.1
  101.6 1.1 copy-done.2
  102.7 1.6 project.2.refs_3_
  104.4 0.7 copy-done.5
  105.1 0.0 all-to-all-done.traded_ref
  105.1 0.0 collective-permute-done.1.refs_0_
  105.1 6.5 %collective-permute-start.6 = (bf16[2,3,64,1024]{3,2,1,0:T(8,128)(2,1)}, bf16[2,3,64,1024]{3,2,1,0:T(8,128)(2,1)}, u32[]{:S(2)}, u32[]{:S(2)}) collective-permute-start(bf16[2,3,64,1024]{3,2,1,0:T(8,128)(2,1)} %collective-permute-done.1.refs_0_), channel_id=1, source_target_pairs={{1,0},{2,1},{3,2},{0,3},{5,4},{6,5},{7,6},{4,7},{9,8},{10,9},{11,1... | collective-permute-start | bytes 2359304 | tf_op jit(solution)/shard_map/ppermute | solution.py:31
  111.6 1.9 collective-permute-start.7
  113.5 0.9 slice_bitcast_fusion
  114.5 1.5 broadcast_select_fusion.1
  116.0 8.2 %collective-permute-start.9 = (bf16[80,512]{1,0:T(8,128)(2,1)}, bf16[80,512]{1,0:T(8,128)(2,1)}, u32[]{:S(2)}, u32[]{:S(2)}) collective-permute-start(bf16[80,512]{1,0:T(8,128)(2,1)} %get-tuple-element.53), channel_id=1, source_target_pairs={{0,1},{1,0},{2,65},{3,64},{4,129},{5,128},{6,193},{7,192},{8,257},... | collective-permute-start | bytes 245768 | tf_op jit(solution)/shard_map/ppermute | solution.py:410
  124.2 1.6 turn.1
  125.8 2.9 %collective-permute-start.8 = (bf16[80,512]{1,0:T(8,128)(2,1)}, bf16[80,512]{1,0:T(8,128)(2,1)S(1)}, u32[]{:S(2)}, u32[]{:S(2)}) collective-permute-start(bf16[80,512]{1,0:T(8,128)(2,1)} %get-tuple-element.54), channel_id=1, source_target_pairs={{0,0},{1,1},{2,64},{3,65},{4,128},{5,129},{6,192},{7,193},{8,256},... | collective-permute-start | bytes 245768 | tf_op jit(solution)/shard_map/ppermute | solution.py:409
  128.6 4.0 %project.3.refs_4_ = bf16[8,64,512]{2,1,0:T(8,128)(2,1)S(1)} custom-call(bf16[2,3,64,1024]{3,2,1,0:T(8,128)(2,1)} %collective-permute-done.1.refs_0_, bf16[2,3,64,1024]{3,2,1,0:T(8,128)(2,1)} %collective-permute-done.10.refs_1_, bf16[2,3,64,1024]{3,2,1,0:T(8,128)(2,1)} %collective-permute-done.11.refs_2_, ...), custom_call_target="tpu_custom_call" | custom-call | flops 1610612736 | bytes 6291456 | tf_op jit(solution)/shard_map/project/pallas_call | solution.py:121
  132.7 0.0 copy-start.3
  132.7 0.8 copy-done.3
  133.5 0.0 all-gather.4.cloned.1.call-update
  133.6 0.1 pad_add_fusion.2.meta_ref
  133.7 1.0 copy-done.4
  134.7 4.7 %project_place.1 = (bf16[4,144,512]{2,1,0:T(8,128)(2,1)S(1)}, bf16[4,144,512]{2,1,0:T(8,128)(2,1)}) custom-call(s32[3]{0:T(128)S(1)} %pad_add_fusion.2.meta_ref, bf16[2,3,64,1024]{3,2,1,0:T(8,128)(2,1)} %collective-permute-done.6.refs_0_, bf16[2,3,64,1024]{3,2,1,0:T(8,128)(2,1)} %collective-permute-done.7.refs_1_, bf16[3,1024,512]{2,1,0:T(8,128)(2,1)S(1)} %bitcast.28, ...), custom_call_target="tpu_custom_call" | custom-call | flops 805306368 | bytes 4718592 | tf_op jit(solution)/shard_map/project_place/pallas_call | solution.py:174
  139.4 0.8 copy-done.7
  140.2 1.9 collective-permute-start.12
  142.1 0.6 dynamic_slice.3
  142.7 0.7 maximum_reduce_fusion
  145.3 0.7 pad_add_fusion.1.meta_ref
  146.0 0.9 broadcast_select_fusion
  147.0 1.1 copy-done.8
  148.0 0.1 join.1
  148.2 9.3 %collective-permute-start.13 = (bf16[144,512]{1,0:T(8,128)(2,1)S(1)}, bf16[144,512]{1,0:T(8,128)(2,1)S(1)}, u32[]{:S(2)}, u32[]{:S(2)}) collective-permute-start(bf16[144,512]{1,0:T(8,128)(2,1)S(1)} %get-tuple-element.38), channel_id=1, source_target_pairs={{128,0},{192,64},{256,128},{320,192},{384,256},{448,320},{0,384},{... | collective-permute-start | bytes 442376 | tf_op jit(solution)/shard_map/ppermute | solution.py:40
  157.5 1.9 collective-permute-start.14
  159.4 2.2 collective-permute-start.15
  161.6 0.9 slice_select_fusion
  162.5 8.8 %collective-permute-done.14.refs_2_ = bf16[144,512]{1,0:T(8,128)(2,1)S(1)} collective-permute-done((bf16[144,512]{1,0:T(8,128)(2,1)S(1)}, bf16[144,512]{1,0:T(8,128)(2,1)S(1)}, u32[]{:S(2)}, u32[]{:S(2)}) %collective-permute-start.14) | collective-permute-done | bytes 147488 | tf_op jit(solution)/shard_map/ppermute | solution.py:40
  171.2 1.4 chain.1
  172.6 33.9 %all-gather.1 = bf16[576,512]{1,0:T(8,128)(2,1)S(1)} all-gather(bf16[144,512]{1,0:T(8,128)(2,1)S(1)} %chain.1), channel_id=3, replica_groups=mesh['tp'=8,'dp'=4,'draft'=16] {'dp'}, dimensions={0}, use_global_device_ids=true | all-gather | bytes 737280 | tf_op jit(solution)/shard_map/all_gather | solution.py:431
  206.5 2.4 collective-permute-start.18
  208.9 1.9 collective-permute-start.17
  210.8 4.6 %collective-permute-start.16 = (bf16[4,144,512]{2,1,0:T(8,128)(2,1)S(1)}, bf16[4,144,512]{2,1,0:T(8,128)(2,1)S(1)}, u32[]{:S(2)}, u32[]{:S(2)}) collective-permute-start(bf16[4,144,512]{2,1,0:T(8,128)(2,1)S(1)} %bitcast.32), channel_id=1, source_target_pairs={{128,0},{144,16},{160,32},{176,48},{192,64},{208,80},{224,96},{240... | collective-permute-start | bytes 1769480 | tf_op jit(solution)/shard_map/ppermute | solution.py:53
  215.5 1.9 collective-permute-start.21
  217.4 4.3 %collective-permute-start.22 = (bf16[2,144,512]{2,1,0:T(8,128)(2,1)S(1)}, bf16[2,144,512]{2,1,0:T(8,128)(2,1)S(1)}, u32[]{:S(2)}, u32[]{:S(2)}) collective-permute-start(bf16[2,144,512]{2,1,0:T(8,128)(2,1)S(1)} %bitcast.42), channel_id=1, source_target_pairs={{304,0},{256,16},{272,32},{288,48},{368,64},{320,80},{336,96},{352... | collective-permute-start | bytes 884744 | tf_op jit(solution)/shard_map/ppermute | solution.py:53
  221.6 18.6 %collective-permute-done.21 = bf16[2,144,512]{2,1,0:T(8,128)(2,1)S(1)} collective-permute-done((bf16[2,144,512]{2,1,0:T(8,128)(2,1)S(1)}, bf16[2,144,512]{2,1,0:T(8,128)(2,1)S(1)}, u32[]{:S(2)}, u32[]{:S(2)}) %collective-permute-start.21) | collective-permute-done | bytes 294944 | tf_op jit(solution)/shard_map/ppermute | solution.py:53
  240.3 3.2 %collective-permute-start.23 = (bf16[4,144,512]{2,1,0:T(8,128)(2,1)S(1)}, bf16[4,144,512]{2,1,0:T(8,128)(2,1)S(1)}, u32[]{:S(2)}, u32[]{:S(2)}) collective-permute-start(bf16[4,144,512]{2,1,0:T(8,128)(2,1)S(1)} %constant_dynamic-update-slice_fusion.refs_6_), channel_id=1, source_target_pairs={{64,0},{0,64},{192,128},{128,192},{320,256},{256,320},{448,384},{3... | collective-permute-start | bytes 1769480 | tf_op jit(solution)/shard_map/ppermute | solution.py:35
  243.6 1.9 collective-permute-start.19
  245.5 2.4 collective-permute-start.20
  248.0 0.6 pad_add_fusion.meta_ref
  248.6 0.9 copy-done.17
  249.5 0.2 collective-permute-done.20.refs_5_
  249.7 9.6 %weight_grad.1 = (bf16[3,256,512]{2,1,0:T(8,128)(2,1)}, f32[1,512]{1,0:T(1,128)}) custom-call(s32[2]{0:T(128)} %pad_add_fusion.meta_ref, bf16[16,3,256,256]{3,2,1,0:T(8,128)(2,1)} %bitcast.44, bf16[4,144,512]{2,1,0:T(8,128)(2,1)} %bitcast.33, bf16[4,144,512]{2,1,0:T(8,128)(2,1)} %copy-done.13, bf16[4,144,512]{2,1,0:T(8,128)(2,1)} %copy-done.15, ...), custom_call_target="tpu_custom_call" | custom-call | flops 3221225472 | bytes 10485760 | tf_op jit(solution)/shard_map/weight_grad/pallas_call | solution.py:342
  (50 shorter events, 0.2 us)
Async XLA Ops:
  7.2 93.3 %copy-start = (bf16[1024,3,512]{2,0,1:T(8,128)(2,1)S(1)}, bf16[1024,3,512]{2,0,1:T(8,128)(2,1)}, u32[]{:S(2)}) copy-start(bf16[1024,3,512]{2,0,1:T(8,128)(2,1)} %param.5) | copy-start | bytes 9437188
  7.2 57.8 %collective-permute-start.3 = (bf16[3,64,1024]{2,1,0:T(8,128)(2,1)}, bf16[3,64,1024]{2,1,0:T(8,128)(2,1)}, u32[]{:S(2)}, u32[]{:S(2)}) collective-permute-start(bf16[3,64,1024]{2,1,0:T(8,128)(2,1)} %bitcast.34), channel_id=1, source_target_pairs={{12,0},{13,1},{14,2},{15,3},{0,4},{1,5},{2,6},{3,7},{4,8},{5,9},{6... | collective-permute-start | bytes 1179656 | tf_op jit(solution)/shard_map/ppermute | solution.py:31
  11.5 53.5 %collective-permute-start.2 = (bf16[3,64,1024]{2,1,0:T(8,128)(2,1)}, bf16[3,64,1024]{2,1,0:T(8,128)(2,1)}, u32[]{:S(2)}, u32[]{:S(2)}) collective-permute-start(bf16[3,64,1024]{2,1,0:T(8,128)(2,1)} %bitcast.35), channel_id=1, source_target_pairs={{8,0},{9,1},{10,2},{11,3},{12,4},{13,5},{14,6},{15,7},{0,8},{1,9},... | collective-permute-start | bytes 1179656 | tf_op jit(solution)/shard_map/ppermute | solution.py:31
  16.0 19.6 %collective-permute-start = (bf16[3,64,1024]{2,1,0:T(8,128)(2,1)}, bf16[3,64,1024]{2,1,0:T(8,128)(2,1)}, u32[]{:S(2)}, u32[]{:S(2)}) collective-permute-start(bf16[3,64,1024]{2,1,0:T(8,128)(2,1)} %bitcast.36), channel_id=1, source_target_pairs={{4,0},{5,1},{6,2},{7,3},{8,4},{9,5},{10,6},{11,7},{12,8},{13,9},{1... | collective-permute-start | bytes 1179656 | tf_op jit(solution)/shard_map/ppermute | solution.py:31
  20.8 84.3 %all-to-all-start = ((bf16[4,3,64,256]{3,2,1,0:T(8,128)(2,1)}), bf16[4,3,64,256]{3,2,1,0:T(8,128)(2,1)S(1)}, u32[]{:S(2)}, u32[]{:S(2)}) async-start(bf16[4,3,64,256]{3,2,1,0:T(8,128)(2,1)} %bitcast.41), calls=%async_computation | async-start | bytes 786432 | tf_op jit(solution)/shard_map/all_to_all | solution.py:427
  35.6 214.1 %all-gather.4.cloned.1.call-start = ((), (), s32[]{:S(2)}) async-start(), calls=%async_computation.1 | async-start | bytes 6684672 | tf_op jit(solution)/shard_map/all_gather | solution.py:467
  60.6 44.5 %collective-permute-start.1 = (bf16[2,3,64,1024]{3,2,1,0:T(8,128)(2,1)}, bf16[2,3,64,1024]{3,2,1,0:T(8,128)(2,1)}, u32[]{:S(2)}, u32[]{:S(2)}) collective-permute-start(bf16[2,3,64,1024]{3,2,1,0:T(8,128)(2,1)} %pair.2.refs_0_), channel_id=1, source_target_pairs={{1,0},{2,1},{3,2},{0,3},{5,4},{6,5},{7,6},{4,7},{9,8},{10,9},{11,1... | collective-permute-start | bytes 2359304 | tf_op jit(solution)/shard_map/ppermute | solution.py:31
  89.9 15.2 %collective-permute-start.4 = (bf16[2,3,64,1024]{3,2,1,0:T(8,128)(2,1)}, bf16[2,3,64,1024]{3,2,1,0:T(8,128)(2,1)}, u32[]{:S(2)}, u32[]{:S(2)}) collective-permute-start(bf16[2,3,64,1024]{3,2,1,0:T(8,128)(2,1)} %pair.3.refs_1_), channel_id=1, source_target_pairs={{3,0},{0,1},{1,2},{2,3},{7,4},{4,5},{5,6},{6,7},{11,8},{8,9},{9,10... | collective-permute-start | bytes 2359304 | tf_op jit(solution)/shard_map/ppermute | solution.py:31
  91.9 33.9 %collective-permute-start.11 = (bf16[2,3,64,1024]{3,2,1,0:T(8,128)(2,1)}, bf16[2,3,64,1024]{3,2,1,0:T(8,128)(2,1)}, u32[]{:S(2)}, u32[]{:S(2)}) collective-permute-start(bf16[2,3,64,1024]{3,2,1,0:T(8,128)(2,1)} %pair.2.refs_0_), channel_id=1, source_target_pairs={{3,0},{0,1},{1,2},{2,3},{7,4},{4,5},{5,6},{6,7},{11,8},{8,9},{9,10... | collective-permute-start | bytes 2359304 | tf_op jit(solution)/shard_map/ppermute | solution.py:31
  94.0 34.7 %collective-permute-start.10 = (bf16[2,3,64,1024]{3,2,1,0:T(8,128)(2,1)}, bf16[2,3,64,1024]{3,2,1,0:T(8,128)(2,1)}, u32[]{:S(2)}, u32[]{:S(2)}) collective-permute-start(bf16[2,3,64,1024]{3,2,1,0:T(8,128)(2,1)} %pair.3.refs_1_), channel_id=1, source_target_pairs={{1,0},{2,1},{3,2},{0,3},{5,4},{6,5},{7,6},{4,7},{9,8},{10,9},{11,1... | collective-permute-start | bytes 2359304 | tf_op jit(solution)/shard_map/ppermute | solution.py:31
  99.1 5.9 %collective-permute-start.5 = (bf16[16,1024]{1,0:T(8,128)(2,1)S(1)}, bf16[16,1024]{1,0:T(8,128)(2,1)}, u32[]{:S(2)}, u32[]{:S(2)}) collective-permute-start(bf16[16,1024]{1,0:T(8,128)(2,1)S(1)} %slice_bitcast_fusion.1), channel_id=1, source_target_pairs={{1,0},{2,1},{3,2},{4,3},{5,4},{6,5},{7,6},{8,7},{9,8},{10,9},{11,1... | collective-permute-start | bytes 98312 | tf_op jit(solution)/shard_map/ppermute | solution.py:421
  100.4 1.1 copy-start.1
  101.6 1.1 copy-start.2
  104.3 0.7 copy-start.5
  105.1 28.4 %collective-permute-start.6 = (bf16[2,3,64,1024]{3,2,1,0:T(8,128)(2,1)}, bf16[2,3,64,1024]{3,2,1,0:T(8,128)(2,1)}, u32[]{:S(2)}, u32[]{:S(2)}) collective-permute-start(bf16[2,3,64,1024]{3,2,1,0:T(8,128)(2,1)} %collective-permute-done.1.refs_0_), channel_id=1, source_target_pairs={{1,0},{2,1},{3,2},{0,3},{5,4},{6,5},{7,6},{4,7},{9,8},{10,9},{11,1... | collective-permute-start | bytes 2359304 | tf_op jit(solution)/shard_map/ppermute | solution.py:31
  111.6 21.9 %collective-permute-start.7 = (bf16[2,3,64,1024]{3,2,1,0:T(8,128)(2,1)}, bf16[2,3,64,1024]{3,2,1,0:T(8,128)(2,1)}, u32[]{:S(2)}, u32[]{:S(2)}) collective-permute-start(bf16[2,3,64,1024]{3,2,1,0:T(8,128)(2,1)} %collective-permute-done.4.refs_3_), channel_id=1, source_target_pairs={{3,0},{0,1},{1,2},{2,3},{7,4},{4,5},{5,6},{6,7},{11,8},{8,9},{9,10... | collective-permute-start | bytes 2359304 | tf_op jit(solution)/shard_map/ppermute | solution.py:31
  116.0 17.5 %collective-permute-start.9 = (bf16[80,512]{1,0:T(8,128)(2,1)}, bf16[80,512]{1,0:T(8,128)(2,1)}, u32[]{:S(2)}, u32[]{:S(2)}) collective-permute-start(bf16[80,512]{1,0:T(8,128)(2,1)} %get-tuple-element.53), channel_id=1, source_target_pairs={{0,1},{1,0},{2,65},{3,64},{4,129},{5,128},{6,193},{7,192},{8,257},... | collective-permute-start | bytes 245768 | tf_op jit(solution)/shard_map/ppermute | solution.py:410
  125.7 7.9 %copy-start.6 = (bf16[4,64,512]{2,1,0:T(8,128)(2,1)S(1)}, bf16[4,64,512]{2,1,0:T(8,128)(2,1)}, u32[]{:S(2)}) copy-start(bf16[4,64,512]{2,1,0:T(8,128)(2,1)} %copy-done.5) | copy-start | bytes 786436
  125.7 16.4 %copy-start.12 = (s32[4]{0:T(128)S(1)}, s32[4]{0:T(128)}, u32[]{:S(2)}) copy-start(s32[4]{0:T(128)} %param.7) | copy-start | bytes 52
  125.8 45.5 %copy-start.9 = (f32[512]{0:T(512)S(1)}, f32[512]{0:T(512)}, u32[]{:S(2)}) copy-start(f32[512]{0:T(512)} %param.6) | copy-start | bytes 6148
  125.8 7.7 %collective-permute-start.8 = (bf16[80,512]{1,0:T(8,128)(2,1)}, bf16[80,512]{1,0:T(8,128)(2,1)S(1)}, u32[]{:S(2)}, u32[]{:S(2)}) collective-permute-start(bf16[80,512]{1,0:T(8,128)(2,1)} %get-tuple-element.54), channel_id=1, source_target_pairs={{0,0},{1,1},{2,64},{3,65},{4,128},{5,129},{6,192},{7,193},{8,256},... | collective-permute-start | bytes 245768 | tf_op jit(solution)/shard_map/ppermute | solution.py:409
  132.7 0.8 copy-start.3
  133.7 1.0 copy-start.4
  139.4 0.8 copy-start.7
  140.2 6.8 %collective-permute-start.12 = (bf16[4,144,512]{2,1,0:T(8,128)(2,1)}, bf16[4,144,512]{2,1,0:T(8,128)(2,1)S(1)}, u32[]{:S(2)}, u32[]{:S(2)}) collective-permute-start(bf16[4,144,512]{2,1,0:T(8,128)(2,1)} %get-tuple-element.36), channel_id=1, source_target_pairs={{64,0},{0,64},{192,128},{128,192},{320,256},{256,320},{448,384},{3... | collective-permute-start | bytes 1769480 | tf_op jit(solution)/shard_map/ppermute | solution.py:35
  146.9 1.1 copy-start.8
  148.2 14.3 %collective-permute-start.13 = (bf16[144,512]{1,0:T(8,128)(2,1)S(1)}, bf16[144,512]{1,0:T(8,128)(2,1)S(1)}, u32[]{:S(2)}, u32[]{:S(2)}) collective-permute-start(bf16[144,512]{1,0:T(8,128)(2,1)S(1)} %get-tuple-element.38), channel_id=1, source_target_pairs={{128,0},{192,64},{256,128},{320,192},{384,256},{448,320},{0,384},{... | collective-permute-start | bytes 442376 | tf_op jit(solution)/shard_map/ppermute | solution.py:40
  157.5 13.8 %collective-permute-start.14 = (bf16[144,512]{1,0:T(8,128)(2,1)S(1)}, bf16[144,512]{1,0:T(8,128)(2,1)S(1)}, u32[]{:S(2)}, u32[]{:S(2)}) collective-permute-start(bf16[144,512]{1,0:T(8,128)(2,1)S(1)} %get-tuple-element.39), channel_id=1, source_target_pairs={{256,0},{320,64},{384,128},{448,192},{0,256},{64,320},{128,384},{1... | collective-permute-start | bytes 442376 | tf_op jit(solution)/shard_map/ppermute | solution.py:40
  159.4 11.8 %collective-permute-start.15 = (bf16[144,512]{1,0:T(8,128)(2,1)S(1)}, bf16[144,512]{1,0:T(8,128)(2,1)S(1)}, u32[]{:S(2)}, u32[]{:S(2)}) collective-permute-start(bf16[144,512]{1,0:T(8,128)(2,1)S(1)} %get-tuple-element.40), channel_id=1, source_target_pairs={{384,0},{448,64},{0,128},{64,192},{128,256},{192,320},{256,384},{3... | collective-permute-start | bytes 442376 | tf_op jit(solution)/shard_map/ppermute | solution.py:40
  206.5 43.2 %copy-start.10 = (bf16[576,512]{1,0:T(8,128)(2,1)}, bf16[576,512]{1,0:T(8,128)(2,1)S(1)}, u32[]{:S(2)}) copy-start(bf16[576,512]{1,0:T(8,128)(2,1)S(1)} %all-gather.1) | copy-start | bytes 1769476
  206.5 37.0 %collective-permute-start.18 = (bf16[4,144,512]{2,1,0:T(8,128)(2,1)S(1)}, bf16[4,144,512]{2,1,0:T(8,128)(2,1)S(1)}, u32[]{:S(2)}, u32[]{:S(2)}) collective-permute-start(bf16[4,144,512]{2,1,0:T(8,128)(2,1)S(1)} %bitcast.30), channel_id=1, source_target_pairs={{64,0},{0,64},{192,128},{128,192},{320,256},{256,320},{448,384},{3... | collective-permute-start | bytes 1769480 | tf_op jit(solution)/shard_map/ppermute | solution.py:35
  208.9 34.7 %collective-permute-start.17 = (bf16[4,144,512]{2,1,0:T(8,128)(2,1)S(1)}, bf16[4,144,512]{2,1,0:T(8,128)(2,1)S(1)}, u32[]{:S(2)}, u32[]{:S(2)}) collective-permute-start(bf16[4,144,512]{2,1,0:T(8,128)(2,1)S(1)} %bitcast.31), channel_id=1, source_target_pairs={{432,0},{384,16},{400,32},{416,48},{496,64},{448,80},{464,96},{480... | collective-permute-start | bytes 1769480 | tf_op jit(solution)/shard_map/ppermute | solution.py:53
  210.8 32.8 %collective-permute-start.16 = (bf16[4,144,512]{2,1,0:T(8,128)(2,1)S(1)}, bf16[4,144,512]{2,1,0:T(8,128)(2,1)S(1)}, u32[]{:S(2)}, u32[]{:S(2)}) collective-permute-start(bf16[4,144,512]{2,1,0:T(8,128)(2,1)S(1)} %bitcast.32), channel_id=1, source_target_pairs={{128,0},{144,16},{160,32},{176,48},{192,64},{208,80},{224,96},{240... | collective-permute-start | bytes 1769480 | tf_op jit(solution)/shard_map/ppermute | solution.py:53
  215.5 24.8 %collective-permute-start.21 = (bf16[2,144,512]{2,1,0:T(8,128)(2,1)S(1)}, bf16[2,144,512]{2,1,0:T(8,128)(2,1)S(1)}, u32[]{:S(2)}, u32[]{:S(2)}) collective-permute-start(bf16[2,144,512]{2,1,0:T(8,128)(2,1)S(1)} %bitcast.43), channel_id=1, source_target_pairs={{256,0},{272,16},{288,32},{304,48},{320,64},{336,80},{352,96},{368... | collective-permute-start | bytes 884744 | tf_op jit(solution)/shard_map/ppermute | solution.py:53
  217.4 22.9 %collective-permute-start.22 = (bf16[2,144,512]{2,1,0:T(8,128)(2,1)S(1)}, bf16[2,144,512]{2,1,0:T(8,128)(2,1)S(1)}, u32[]{:S(2)}, u32[]{:S(2)}) collective-permute-start(bf16[2,144,512]{2,1,0:T(8,128)(2,1)S(1)} %bitcast.42), channel_id=1, source_target_pairs={{304,0},{256,16},{272,32},{288,48},{368,64},{320,80},{336,96},{352... | collective-permute-start | bytes 884744 | tf_op jit(solution)/shard_map/ppermute | solution.py:53
  240.3 9.4 %copy-start.11 = (bf16[4,144,512]{2,1,0:T(8,128)(2,1)}, bf16[4,144,512]{2,1,0:T(8,128)(2,1)S(1)}, u32[]{:S(2)}) copy-start(bf16[4,144,512]{2,1,0:T(8,128)(2,1)S(1)} %constant_dynamic-update-slice_fusion.refs_6_) | copy-start | bytes 1769476
  240.3 8.2 %collective-permute-start.23 = (bf16[4,144,512]{2,1,0:T(8,128)(2,1)S(1)}, bf16[4,144,512]{2,1,0:T(8,128)(2,1)S(1)}, u32[]{:S(2)}, u32[]{:S(2)}) collective-permute-start(bf16[4,144,512]{2,1,0:T(8,128)(2,1)S(1)} %constant_dynamic-update-slice_fusion.refs_6_), channel_id=1, source_target_pairs={{64,0},{0,64},{192,128},{128,192},{320,256},{256,320},{448,384},{3... | collective-permute-start | bytes 1769480 | tf_op jit(solution)/shard_map/ppermute | solution.py:35
  243.6 6.1 %copy-start.13 = (bf16[4,144,512]{2,1,0:T(8,128)(2,1)}, bf16[4,144,512]{2,1,0:T(8,128)(2,1)S(1)}, u32[]{:S(2)}) copy-start(bf16[4,144,512]{2,1,0:T(8,128)(2,1)S(1)} %collective-permute-done.18.refs_1_) | copy-start | bytes 1769476
  243.6 5.0 %copy-start.14 = (bf16[4,144,512]{2,1,0:T(8,128)(2,1)}, bf16[4,144,512]{2,1,0:T(8,128)(2,1)S(1)}, u32[]{:S(2)}) copy-start(bf16[4,144,512]{2,1,0:T(8,128)(2,1)S(1)} %collective-permute-done.17.refs_3_) | copy-start | bytes 1769476
  243.6 5.0 %copy-start.15 = (bf16[4,144,512]{2,1,0:T(8,128)(2,1)}, bf16[4,144,512]{2,1,0:T(8,128)(2,1)S(1)}, u32[]{:S(2)}) copy-start(bf16[4,144,512]{2,1,0:T(8,128)(2,1)S(1)} %collective-permute-done.16.refs_2_) | copy-start | bytes 1769476
  243.6 5.0 %collective-permute-start.19 = (bf16[4,144,512]{2,1,0:T(8,128)(2,1)S(1)}, bf16[4,144,512]{2,1,0:T(8,128)(2,1)S(1)}, u32[]{:S(2)}, u32[]{:S(2)}) collective-permute-start(bf16[4,144,512]{2,1,0:T(8,128)(2,1)S(1)} %collective-permute-done.16.refs_2_), channel_id=1, source_target_pairs={{64,0},{0,64},{192,128},{128,192},{320,256},{256,320},{448,384},{3... | collective-permute-start | bytes 1769480 | tf_op jit(solution)/shard_map/ppermute | solution.py:35
  245.5 4.2 %collective-permute-start.20 = (bf16[4,144,512]{2,1,0:T(8,128)(2,1)S(1)}, bf16[4,144,512]{2,1,0:T(8,128)(2,1)}, u32[]{:S(2)}, u32[]{:S(2)}) collective-permute-start(bf16[4,144,512]{2,1,0:T(8,128)(2,1)S(1)} %collective-permute-done.17.refs_3_), channel_id=1, source_target_pairs={{64,0},{0,64},{192,128},{128,192},{320,256},{256,320},{448,384},{3... | collective-permute-start | bytes 1769480 | tf_op jit(solution)/shard_map/ppermute | solution.py:35
  248.6 1.1 copy-start.16
  248.6 0.9 copy-start.17
Sparse Core Ops, SparseCore 0:
  133.7 80.7 all-gather.3

commit v6 on v5

--- a/solution.py
+++ b/solution.py
@@ -53,23 +53,21 @@
     return lax.ppermute(block, ("tp", "dp"), pairs)
 
 
-def pair_kernel(first_ref, second_ref, out_ref, sem):
-    first = pltpu.make_async_copy(first_ref, out_ref.at[0], sem.at[0])
-    second = pltpu.make_async_copy(second_ref, out_ref.at[1], sem.at[1])
-    first.start()
-    second.start()
-    first.wait()
-    second.wait()
+def pair_kernel(first_ref, second_ref, out_ref):
+    out_ref[0] = first_ref[...]
+    out_ref[1] = second_ref[...]
 
 
 def pair(first, second):
-    anywhere = pl.BlockSpec(memory_space=pl.ANY)
+    levels, rows, depth = first.shape
+    spec = pl.BlockSpec((1, rows, depth), lambda l: (l, 0, 0))
     return pl.pallas_call(
         pair_kernel,
+        grid=(levels,),
         out_shape=jax.ShapeDtypeStruct((2,) + first.shape, first.dtype),
-        in_specs=[anywhere] * 2,
-        out_specs=anywhere,
-        scratch_shapes=[pltpu.SemaphoreType.DMA((2,))],
+        in_specs=[spec] * 2,
+        out_specs=pl.BlockSpec((2, 1, rows, depth), lambda l: (0, l, 0, 0)),
+        compiler_params=params(8),
         cost_estimate=pl.CostEstimate(flops=0, bytes_accessed=8 * first.size, transcendentals=0),
         name="pair",
     )(first, second)
@@ -184,7 +182,7 @@
                 pltpu.VMEM((total + 2 * HALO, width), jnp.float32),
             ],
         ),
-        compiler_params=params(18),
+        compiler_params=params(58),
         cost_estimate=product_cost(blocks, weight),
         name="project_place",
     )(jnp.stack([core, x, y]), *blocks, weight, zero, sides)
@@ -202,13 +200,16 @@
 
 
 def join(keep, got, zl):
-    piece = jax.ShapeDtypeStruct(keep.shape[1:], jnp.bfloat16)
+    count, rows, width = keep.shape
+    whole = pl.BlockSpec(keep.shape, lambda i, m: (0, 0, 0))
+    piece = pl.BlockSpec((rows, width), lambda i, m: (0, 0))
     return pl.pallas_call(
         join_kernel,
-        out_shape=(piece,) * ZL,
-        in_specs=[SMEM, VMEM, VMEM],
-        out_specs=(VMEM,) * ZL,
-        compiler_params=params(8),
+        out_shape=(jax.ShapeDtypeStruct((rows, width), jnp.bfloat16),) * count,
+        grid_spec=pltpu.PrefetchScalarGridSpec(
+            num_scalar_prefetch=1, grid=(1,), in_specs=[whole] * 2, out_specs=(piece,) * count
+        ),
+        compiler_params=params(58),
         cost_estimate=pl.CostEstimate(
             flops=keep.size, bytes_accessed=6 * keep.size, transcendentals=0
         ),
@@ -287,85 +288,105 @@
     )(jnp.stack([start, length]), scale.reshape(1), *parts, high, gain.reshape(1, width))
 
 
-def pieces_of(zl, core):
-    found = []
-    for step, other in ((0, 0), (0, 1), (1, 0), (-1, 0), (1, 1), (-1, 1), (2, 0), (2, 1)):
-        found.append(lax.rem(zl + step + ZL, ZL) * CORES + (1 - core if other else core))
-    return found
-
-
-def weight_grad_kernel(meta_ref, features_ref, *refs):
-    *group_refs, out_ref, mix_ref, grads_ref, tail_ref, held_ref, sem, held_sem = refs
-    level = pl.program_id(0)
-    zl, core = meta_ref[0], meta_ref[1]
+def take_pieces(groups, members, features_ref, grads_ref, tails_ref, held_ref, sem):
     half = grads_ref.shape[1] // ZH
-    width = grads_ref.shape[2]
-
-    def held(at):
-        return pltpu.make_async_copy(features_ref.at[:, at], held_ref.at[at], held_sem.at[at])
-
-    @pl.when(level == 0)
-    def _():
-        copies = []
-        for group, (group_ref, member) in enumerate(zip(group_refs, pieces_of(zl, core))):
+    copies, held = [], [[] for _ in range(LEVELS)]
+    at = 0
+
+    def start(source, target, into):
+        nonlocal at
+        copy = pltpu.make_async_copy(source, target, sem.at[at])
+        copy.start()
+        into.append(copy)
+        at += 1
+
+    for group, (group_ref, member) in enumerate(zip(groups, members)):
+        for part in range(2):
             for sequence in range(ZH):
-                for part in range(2):
-                    rows = group_ref.at[sequence, pl.ds(part * half, half), :]
-                    slot = grads_ref.at[member * 2 + part, pl.ds(sequence * half, half), :]
-                    copies.append((rows, slot))
-            rows = group_ref.at[:, pl.ds(2 * half, TAIL), :]
-            copies.append((rows, tail_ref.at[pl.ds(group * ZH, ZH)]))
-        copies = [
-            pltpu.make_async_copy(source, target, sem.at[at])
-            for at, (source, target) in enumerate(copies)
-        ]
-        for copy in copies:
-            copy.start()
-        for at in range(LEVELS):
-            held(at).start()
-        for copy in copies:
+                source = group_ref.at[sequence, pl.ds(part * half, half), :]
+                target = grads_ref.at[2 * group + part, pl.ds(sequence * half, half), :]
+                start(source, target, copies)
+        source = group_ref.at[:, pl.ds(2 * half, TAIL), :]
+        start(source, tails_ref.at[pl.ds(group * ZH, ZH)], copies)
+    for level in range(LEVELS):
+        for group, member in enumerate(members):
+            source = features_ref.at[pl.ds(member * 2, 2), level]
+            start(source, held_ref.at[level, pl.ds(group * 2, 2)], held[level])
+    return copies, held
+
+
+def copy_count(groups):
+    return groups * (2 * ZH + 1 + LEVELS)
+
+
+def products(held_ref, grads_ref, held):
+    right = grads_ref[...].reshape(-1, grads_ref.shape[2])
+    for level in range(LEVELS):
+        for copy in held[level]:
             copy.wait()
-        mix = jnp.sum(tail_ref[...].astype(jnp.float32), axis=0)
-        mix_ref[...] = jnp.sum(mix, axis=0, keepdims=True)
-
-    held(level).wait()
-    blocks = features_ref.shape[0]
-    left = jnp.concatenate([held_ref[level, e] for e in range(blocks)], axis=1)
-    right = grads_ref[...].reshape(-1, width)
-    out_ref[0] = jnp.dot(left, right, preferred_element_type=jnp.float32).astype(jnp.bfloat16)
-
-
-def weight_grad(features, groups, zl, core):
-    draft, _, columns, tokens = features.shape
+        left = jnp.concatenate([held_ref[level, e] for e in range(held_ref.shape[1])], axis=1)
+        yield level, jnp.dot(left, right, preferred_element_type=jnp.float32)
+
+
+def mix_of(tails_ref):
+    return jnp.sum(jnp.sum(tails_ref[...].astype(jnp.float32), axis=0), axis=0, keepdims=True)
+
+
+def near_kernel(meta_ref, features_ref, *refs):
+    *group_refs, out_ref, mix_ref, grads_ref, tails_ref, held_ref, sem = refs
+    members = [meta_ref[at] for at in range(len(group_refs))]
+    copies, held = take_pieces(group_refs, members, features_ref, grads_ref, tails_ref, held_ref, sem)
+    for copy in copies:
+        copy.wait()
+    mix_ref[...] = mix_of(tails_ref)
+    for level, term in products(held_ref, grads_ref, held):
+        out_ref[level] = term
+
+
+def far_kernel(meta_ref, features_ref, near_ref, near_mix_ref, *refs):
+    *group_refs, out_ref, mix_ref, grads_ref, tails_ref, held_ref, sem = refs
+    members = [meta_ref[at] for at in range(len(group_refs))]
+    copies, held = take_pieces(group_refs, members, features_ref, grads_ref, tails_ref, held_ref, sem)
+    for copy in copies:
+        copy.wait()
+    mix_ref[...] = near_mix_ref[...] + mix_of(tails_ref)
+    for level, term in products(held_ref, grads_ref, held):
+        out_ref[level] = (near_ref[level] + term).astype(jnp.bfloat16)
+
+
+def weight_grad(kernel, name, features, groups, members, before, held_as):
+    _, _, columns, tokens = features.shape
     width = groups[0].shape[2]
     count = len(groups)
-    return pl.pallas_call(
-        weight_grad_kernel,
-        grid=(LEVELS,),
+    hbm = pl.BlockSpec(memory_space=pltpu.HBM)
+    whole = pl.BlockSpec((LEVELS, columns, width), lambda i, m: (0, 0, 0))
+    line = pl.BlockSpec((1, width), lambda i, m: (0, 0))
+    return pl.pallas_call(
+        kernel,
         out_shape=(
-            jax.ShapeDtypeStruct((LEVELS, columns, width), jnp.bfloat16),
+            jax.ShapeDtypeStruct((LEVELS, columns, width), held_as),
             jax.ShapeDtypeStruct((1, width), jnp.float32),
         ),
-        in_specs=[SMEM] + [pl.BlockSpec(memory_space=pltpu.HBM)] * (count + 1),
-        out_specs=(
-            pl.BlockSpec((1, columns, width), lambda l: (l, 0, 0)),
-            pl.BlockSpec((1, width), lambda l: (0, 0)),
-        ),
-        scratch_shapes=[
-            pltpu.VMEM((draft, tokens, width), jnp.bfloat16),
-            pltpu.VMEM((count * ZH, TAIL, width), jnp.bfloat16),
-            pltpu.VMEM((LEVELS, draft, columns, tokens), jnp.bfloat16),
-            pltpu.SemaphoreType.DMA((count * (2 * ZH + 1),)),
-            pltpu.SemaphoreType.DMA((LEVELS,)),
-        ],
+        grid_spec=pltpu.PrefetchScalarGridSpec(
+            num_scalar_prefetch=1,
+            grid=(1,),
+            in_specs=[hbm] + [whole, line][: len(before)] + [hbm] * count,
+            out_specs=(whole, line),
+            scratch_shapes=[
+                pltpu.VMEM((2 * count, tokens, width), jnp.bfloat16),
+                pltpu.VMEM((count * ZH, TAIL, width), jnp.bfloat16),
+                pltpu.VMEM((LEVELS, 2 * count, columns, tokens), jnp.bfloat16),
+                pltpu.SemaphoreType.DMA((copy_count(count),)),
+            ],
+        ),
         compiler_params=params(58),
         cost_estimate=pl.CostEstimate(
-            flops=2 * draft * LEVELS * columns * tokens * width,
-            bytes_accessed=2 * features.size + 2 * draft * tokens * width,
+            flops=4 * count * LEVELS * columns * tokens * width,
+            bytes_accessed=4 * count * tokens * (LEVELS * columns + width),
             transcendentals=0,
         ),
-        name="weight_grad",
-    )(jnp.stack([zl, core]), features, *groups)
+        name=name,
+    )(jnp.stack(members), features, *before, *groups)
 
 
 def turn_kernel(traded_ref, out_ref):
@@ -427,15 +448,22 @@
     return lax.all_to_all(quarters, "dp", split_axis=0, concat_axis=0, tiled=True)
 
 
-def gather_grads(grad):
+def gather_grads(grad, features, zl, core):
     stack = lax.all_gather(grad, "dp", axis=0, tiled=False)
     above, below = from_z(stack, 1), from_z(stack, -1)
-    far = [from_z(stack[:2], 2), from_z(stack[2:], -2)]
+    far = jnp.concatenate([from_z(stack[:2], 2), from_z(stack[2:], -2)])
     other = from_other_core(stack)
-    above, below, other = lax.optimization_barrier((above, below, other))
-    other_above, other_below = from_other_core(above), from_other_core(below)
-    far = jnp.concatenate(far)
-    return [stack, other, above, below, other_above, other_below, far, from_other_core(far)]
+    above, below, other, far = lax.optimization_barrier((above, below, other, far))
+    swapped = [from_other_core(block) for block in (above, below, far)]
+
+    def member(step, of_core):
+        return (zl + step) % ZL * CORES + of_core
+
+    near = [stack, other, above, below, far]
+    owners = [member(0, core), member(0, 1 - core)] + [member(step, core) for step in (1, 3, 2)]
+    before = weight_grad(near_kernel, "near", features, near, owners, (), jnp.float32)
+    owners = [member(step, 1 - core) for step in (1, 3, 2)]
+    return weight_grad(far_kernel, "far", features, swapped, owners, tuple(before), jnp.bfloat16)
 
 
 def local(features, fc_weight, mix_gain, lengths):
@@ -471,7 +499,7 @@
     scale = LOSS_SCALE / valid_total(lengths)
     target = high_rows(*halves, draft_index)
     grad = chain(parts, target, mix_gain, tp_index * piece, lengths[zh], scale)
-    fc_grad, mix_total = weight_grad(every, gather_grads(grad), zl, core)
+    fc_grad, mix_total = gather_grads(grad, every, zl, core)
     return (fc_grad.transpose(1, 0, 2), mix_total[0])
 
 

time: 268 us -> 232 us (0.87)
  Pallas kernels: 72.8 us -> 37.8 us
    pallas_call x4 -> x5, Pallas kernels: 59.6 us -> 21.7 us  [the longest x2 13.9 us: weight_grad(): pl.pallas_call(kernel, out_shape=(jax.ShapeDtypeStruct((LEVELS, columns,...]
    unnamed x37 -> x28, local copies, waits for them, and re-layouts: 7.61 us -> 5.05 us
  transfers between devices with their start and end apart: 26 -> 26, of which waited for: 3 -> 4; matrix products, arithmetic and copies ran while one was open for 4% -> 5% of each run, Pallas kernels for 24% -> 14%
where the time goes in v6:
time: 232 us; the launch traced here: 230 us
  starting transfers between devices  99.5 us (43%)
  Pallas kernels  37.8 us (16%)
  blocking collectives  33.6 us (14%)
  waiting for transfers between devices  27 us (12%)
  between operations  16.5 us (7%)
  local copies, waits for them, and re-layouts  9.7 us (4%)
  other arithmetic  5.81 us (3%)
    all_gather x1, blocking collectives, gather_grads(): stack = lax.all_gather(grad, 'dp', axis=0, tiled=False)  33.6 us
    ppermute x9, starting transfers between devices, plane_move(): return lambda block: lax.ppermute(block, ('tp', 'draft'), pairs)  33.5 us
    ppermute x4, waiting for transfers between devices, from_z(): return lax.ppermute(block, ('tp', 'dp'), pairs)  17.6 us
    all_to_all x1, starting transfers between devices, trade_columns(): lax.all_to_all(quarters, 'dp', split_axis=0, concat_axis=0, tiled=True)  14.8 us
    pallas_call x2, Pallas kernels, weight_grad(): pl.pallas_call(kernel, out_shape=(jax.ShapeDtypeStruct((LEVELS, columns,...  13.9 us
    ppermute x4, starting transfers between devices, from_z(): return lax.ppermute(block, ('tp', 'dp'), pairs)  13.9 us
    ppermute x3, starting transfers between devices, from_zl(): return lax.ppermute(block, 'tp', pairs)  13.3 us
    ppermute x5, starting transfers between devices, from_other_core(): return lax.ppermute(block, 'tp', [(t ^ 1, t) for t in range(ZL * CORES)])  11.8 us
  transfers between devices with their start and end apart: 26, of which 4 were waited for; matrix products, arithmetic and copies ran while one was open for 5% of the time, Pallas kernels for 14%

profile of v6, /device:TPU:1, one launch (start us, length us, event | category | flops | bytes accessed | tf_op | source)
XLA Modules:
  0.0 230.0 jit_solution(16901005687716373776)
XLA Ops:
  7.2 0.0 copy-start
  7.2 4.3 %collective-permute-start.3 = (bf16[3,64,1024]{2,1,0:T(8,128)(2,1)}, bf16[3,64,1024]{2,1,0:T(8,128)(2,1)}, u32[]{:S(2)}, u32[]{:S(2)}) collective-permute-start(bf16[3,64,1024]{2,1,0:T(8,128)(2,1)} %bitcast.37), channel_id=1, source_target_pairs={{12,0},{13,1},{14,2},{15,3},{0,4},{1,5},{2,6},{3,7},{4,8},{5,9},{6... | collective-permute-start | bytes 1179656 | tf_op jit(solution)/shard_map/ppermute | solution.py:31
  11.5 4.5 %collective-permute-start.2 = (bf16[3,64,1024]{2,1,0:T(8,128)(2,1)}, bf16[3,64,1024]{2,1,0:T(8,128)(2,1)}, u32[]{:S(2)}, u32[]{:S(2)}) collective-permute-start(bf16[3,64,1024]{2,1,0:T(8,128)(2,1)} %bitcast.38), channel_id=1, source_target_pairs={{8,0},{9,1},{10,2},{11,3},{12,4},{13,5},{14,6},{15,7},{0,8},{1,9},... | collective-permute-start | bytes 1179656 | tf_op jit(solution)/shard_map/ppermute | solution.py:31
  16.0 3.0 %collective-permute-start = (bf16[3,64,1024]{2,1,0:T(8,128)(2,1)}, bf16[3,64,1024]{2,1,0:T(8,128)(2,1)}, u32[]{:S(2)}, u32[]{:S(2)}) collective-permute-start(bf16[3,64,1024]{2,1,0:T(8,128)(2,1)} %bitcast.39), channel_id=1, source_target_pairs={{4,0},{5,1},{6,2},{7,3},{8,4},{9,5},{10,6},{11,7},{12,8},{13,9},{1... | collective-permute-start | bytes 1179656 | tf_op jit(solution)/shard_map/ppermute | solution.py:31
  19.0 1.8 copy.10
  20.8 14.8 %all-to-all-start = ((bf16[4,3,64,256]{3,2,1,0:T(8,128)(2,1)}), bf16[4,3,64,256]{3,2,1,0:T(8,128)(2,1)S(1)}, u32[]{:S(2)}, u32[]{:S(2)}) async-start(bf16[4,3,64,256]{3,2,1,0:T(8,128)(2,1)} %bitcast.51), calls=%async_computation | async-start | bytes 786432 | tf_op jit(solution)/shard_map/all_to_all | solution.py:448
  35.6 0.0 copy-start.1
  35.6 1.0 copy-done.1
  36.6 2.7 %pair.2.refs_0_ = bf16[2,3,64,1024]{3,2,1,0:T(8,128)(2,1)} custom-call(bf16[3,64,1024]{2,1,0:T(8,128)(2,1)S(1)} %bitcast.43, bf16[3,64,1024]{2,1,0:T(8,128)(2,1)} %collective-permute-done.second_ref), custom_call_target="tpu_custom_call" | custom-call | bytes 1572864 | tf_op jit(solution)/shard_map/pair/pallas_call | solution.py:64
  39.3 4.4 %collective-permute-start.1 = (bf16[2,3,64,1024]{3,2,1,0:T(8,128)(2,1)}, bf16[2,3,64,1024]{3,2,1,0:T(8,128)(2,1)}, u32[]{:S(2)}, u32[]{:S(2)}) collective-permute-start(bf16[2,3,64,1024]{3,2,1,0:T(8,128)(2,1)} %pair.2.refs_0_), channel_id=1, source_target_pairs={{1,0},{2,1},{3,2},{0,3},{5,4},{6,5},{7,6},{4,7},{9,8},{10,9},{11,1... | collective-permute-start | bytes 2359304 | tf_op jit(solution)/shard_map/ppermute | solution.py:31
  43.7 0.0 collective-permute-done.3.second_ref
  43.7 0.0 collective-permute-done.2.first_ref
  43.7 2.9 %pair.3.refs_1_ = bf16[2,3,64,1024]{3,2,1,0:T(8,128)(2,1)} custom-call(bf16[3,64,1024]{2,1,0:T(8,128)(2,1)} %collective-permute-done.2.first_ref, bf16[3,64,1024]{2,1,0:T(8,128)(2,1)} %collective-permute-done.3.second_ref), custom_call_target="tpu_custom_call" | custom-call | bytes 1572864 | tf_op jit(solution)/shard_map/pair/pallas_call | solution.py:64
  46.6 1.9 collective-permute-start.4
  48.6 2.1 collective-permute-start.11
  50.7 4.4 %collective-permute-start.10 = (bf16[2,3,64,1024]{3,2,1,0:T(8,128)(2,1)}, bf16[2,3,64,1024]{3,2,1,0:T(8,128)(2,1)}, u32[]{:S(2)}, u32[]{:S(2)}) collective-permute-start(bf16[2,3,64,1024]{3,2,1,0:T(8,128)(2,1)} %pair.3.refs_1_), channel_id=1, source_target_pairs={{1,0},{2,1},{3,2},{0,3},{5,4},{6,5},{7,6},{4,7},{9,8},{10,9},{11,1... | collective-permute-start | bytes 2359304 | tf_op jit(solution)/shard_map/ppermute | solution.py:31
  55.1 0.8 slice_bitcast_fusion.1
  55.8 1.3 collective-permute-start.5
  57.1 3.1 %project.2.refs_3_ = bf16[4,64,512]{2,1,0:T(8,128)(2,1)S(1)} custom-call(bf16[2,3,64,1024]{3,2,1,0:T(8,128)(2,1)} %pair.2.refs_0_, bf16[2,3,64,1024]{3,2,1,0:T(8,128)(2,1)} %pair.3.refs_1_, bf16[3,1024,512]{2,1,0:T(8,128)(2,1)S(1)} %bitcast.35), custom_call_target="tpu_custom_call" | custom-call | flops 805306368 | bytes 4718592 | tf_op jit(solution)/shard_map/project/pallas_call | solution.py:119
  60.2 0.7 copy-done.3
  60.9 0.4 collective-permute-done.5
  61.3 7.0 %collective-permute-start.6 = (bf16[2,3,64,1024]{3,2,1,0:T(8,128)(2,1)}, bf16[2,3,64,1024]{3,2,1,0:T(8,128)(2,1)}, u32[]{:S(2)}, u32[]{:S(2)}) collective-permute-start(bf16[2,3,64,1024]{3,2,1,0:T(8,128)(2,1)} %collective-permute-done.1.refs_0_), channel_id=1, source_target_pairs={{1,0},{2,1},{3,2},{0,3},{5,4},{6,5},{7,6},{4,7},{9,8},{10,9},{11,1... | collective-permute-start | bytes 2359304 | tf_op jit(solution)/shard_map/ppermute | solution.py:31
  68.3 1.9 collective-permute-start.7
  70.2 0.9 slice_bitcast_fusion
  71.1 1.5 broadcast_select_fusion.1
  72.7 8.2 %collective-permute-start.9 = (bf16[80,512]{1,0:T(8,128)(2,1)}, bf16[80,512]{1,0:T(8,128)(2,1)}, u32[]{:S(2)}, u32[]{:S(2)}) collective-permute-start(bf16[80,512]{1,0:T(8,128)(2,1)} %get-tuple-element.59), channel_id=1, source_target_pairs={{0,1},{1,0},{2,65},{3,64},{4,129},{5,128},{6,193},{7,192},{8,257},... | collective-permute-start | bytes 245768 | tf_op jit(solution)/shard_map/ppermute | solution.py:431
  80.9 1.5 turn.1
  82.4 2.7 %collective-permute-start.8 = (bf16[80,512]{1,0:T(8,128)(2,1)}, bf16[80,512]{1,0:T(8,128)(2,1)S(1)}, u32[]{:S(2)}, u32[]{:S(2)}) collective-permute-start(bf16[80,512]{1,0:T(8,128)(2,1)} %get-tuple-element.60), channel_id=1, source_target_pairs={{0,0},{1,1},{2,64},{3,65},{4,128},{5,129},{6,192},{7,193},{8,256},... | collective-permute-start | bytes 245768 | tf_op jit(solution)/shard_map/ppermute | solution.py:430
  85.2 4.0 %project.3.refs_4_ = bf16[8,64,512]{2,1,0:T(8,128)(2,1)S(1)} custom-call(bf16[2,3,64,1024]{3,2,1,0:T(8,128)(2,1)} %collective-permute-done.1.refs_0_, bf16[2,3,64,1024]{3,2,1,0:T(8,128)(2,1)} %collective-permute-done.10.refs_1_, bf16[2,3,64,1024]{3,2,1,0:T(8,128)(2,1)} %collective-permute-done.11.refs_2_, ...), custom_call_target="tpu_custom_call" | custom-call | flops 1610612736 | bytes 6291456 | tf_op jit(solution)/shard_map/project/pallas_call | solution.py:119
  89.3 0.8 copy-done.2
  90.1 0.0 all-gather.4.cloned.1.call-update
  90.2 0.6 pad_add_fusion.2.meta_ref
  90.8 6.1 %project_place.1 = (bf16[4,144,512]{2,1,0:T(8,128)(2,1)}, bf16[4,144,512]{2,1,0:T(8,128)(2,1)}) custom-call(s32[3]{0:T(128)} %pad_add_fusion.2.meta_ref, bf16[2,3,64,1024]{3,2,1,0:T(8,128)(2,1)} %collective-permute-done.6.refs_0_, bf16[2,3,64,1024]{3,2,1,0:T(8,128)(2,1)} %collective-permute-done.7.refs_1_, bf16[3,1024,512]{2,1,0:T(8,128)(2,1)} %bitcast.34, ...), custom_call_target="tpu_custom_call" | custom-call | flops 805306368 | bytes 4718592 | tf_op jit(solution)/shard_map/project_place/pallas_call | solution.py:172
  96.9 1.9 collective-permute-start.12
  98.8 0.6 dynamic_slice.3
  99.4 0.7 maximum_reduce_fusion
  101.9 0.6 pad_add_fusion.1.meta_ref
  102.5 0.9 broadcast_select_fusion
  103.4 0.8 copy-done.11
  104.3 2.1 join.1
  106.4 9.2 %collective-permute-start.13 = (bf16[144,512]{1,0:T(8,128)(2,1)}, bf16[144,512]{1,0:T(8,128)(2,1)S(1)}, u32[]{:S(2)}, u32[]{:S(2)}) collective-permute-start(bf16[144,512]{1,0:T(8,128)(2,1)} %get-tuple-element.41), channel_id=1, source_target_pairs={{128,0},{192,64},{256,128},{320,192},{384,256},{448,320},{0,384},{... | collective-permute-start | bytes 442376 | tf_op jit(solution)/shard_map/ppermute | solution.py:40
  115.6 1.9 collective-permute-start.14
  117.5 2.2 collective-permute-start.15
  119.7 0.9 slice_select_fusion
  120.6 9.0 %collective-permute-done.14.refs_2_ = bf16[144,512]{1,0:T(8,128)(2,1)S(1)} collective-permute-done((bf16[144,512]{1,0:T(8,128)(2,1)}, bf16[144,512]{1,0:T(8,128)(2,1)S(1)}, u32[]{:S(2)}, u32[]{:S(2)}) %collective-permute-start.14) | collective-permute-done | bytes 147488 | tf_op jit(solution)/shard_map/ppermute | solution.py:40
  129.6 0.9 copy-done.4
  130.5 1.4 chain.1
  131.9 33.6 %all-gather.1 = bf16[576,512]{1,0:T(8,128)(2,1)S(1)} all-gather(bf16[144,512]{1,0:T(8,128)(2,1)S(1)} %chain.1), channel_id=3, replica_groups=mesh['tp'=8,'dp'=4,'draft'=16] {'dp'}, dimensions={0}, use_global_device_ids=true | all-gather | bytes 737280 | tf_op jit(solution)/shard_map/all_gather | solution.py:452
  165.5 2.5 %collective-permute-start.18 = (bf16[4,144,512]{2,1,0:T(8,128)(2,1)S(1)}, bf16[4,144,512]{2,1,0:T(8,128)(2,1)S(1)}, u32[]{:S(2)}, u32[]{:S(2)}) collective-permute-start(bf16[4,144,512]{2,1,0:T(8,128)(2,1)S(1)} %bitcast.47), channel_id=1, source_target_pairs={{64,0},{0,64},{192,128},{128,192},{320,256},{256,320},{448,384},{3... | collective-permute-start | bytes 1769480 | tf_op jit(solution)/shard_map/ppermute | solution.py:35
  168.0 1.9 collective-permute-start.17
  169.9 4.6 %collective-permute-start.16 = (bf16[4,144,512]{2,1,0:T(8,128)(2,1)S(1)}, bf16[4,144,512]{2,1,0:T(8,128)(2,1)S(1)}, u32[]{:S(2)}, u32[]{:S(2)}) collective-permute-start(bf16[4,144,512]{2,1,0:T(8,128)(2,1)S(1)} %bitcast.49), channel_id=1, source_target_pairs={{128,0},{144,16},{160,32},{176,48},{192,64},{208,80},{224,96},{240... | collective-permute-start | bytes 1769480 | tf_op jit(solution)/shard_map/ppermute | solution.py:53
  174.6 1.9 collective-permute-start.20
  176.5 5.5 %collective-permute-start.19 = (bf16[2,144,512]{2,1,0:T(8,128)(2,1)S(1)}, bf16[2,144,512]{2,1,0:T(8,128)(2,1)S(1)}, u32[]{:S(2)}, u32[]{:S(2)}) collective-permute-start(bf16[2,144,512]{2,1,0:T(8,128)(2,1)S(1)} %bitcast.52), channel_id=1, source_target_pairs={{256,0},{272,16},{288,32},{304,48},{320,64},{336,80},{352,96},{368... | collective-permute-start | bytes 884744 | tf_op jit(solution)/shard_map/ppermute | solution.py:53
  182.0 9.4 %collective-permute-done.20 = bf16[2,144,512]{2,1,0:T(8,128)(2,1)S(1)} collective-permute-done((bf16[2,144,512]{2,1,0:T(8,128)(2,1)S(1)}, bf16[2,144,512]{2,1,0:T(8,128)(2,1)S(1)}, u32[]{:S(2)}, u32[]{:S(2)}) %collective-permute-start.20) | collective-permute-done | bytes 294944 | tf_op jit(solution)/shard_map/ppermute | solution.py:53
  191.4 8.2 %collective-permute-done.19 = bf16[2,144,512]{2,1,0:T(8,128)(2,1)S(1)} collective-permute-done((bf16[2,144,512]{2,1,0:T(8,128)(2,1)S(1)}, bf16[2,144,512]{2,1,0:T(8,128)(2,1)S(1)}, u32[]{:S(2)}, u32[]{:S(2)}) %collective-permute-start.19) | collective-permute-done | bytes 294944 | tf_op jit(solution)/shard_map/ppermute | solution.py:53
  199.6 0.1 pad_maximum_fusion.refs_4_
  199.7 3.0 %collective-permute-start.21 = (bf16[4,144,512]{2,1,0:T(8,128)(2,1)S(1)}, bf16[4,144,512]{2,1,0:T(8,128)(2,1)S(1)}, u32[]{:S(2)}, u32[]{:S(2)}) collective-permute-start(bf16[4,144,512]{2,1,0:T(8,128)(2,1)S(1)} %collective-permute-done.16.refs_2_), channel_id=1, source_target_pairs={{64,0},{0,64},{192,128},{128,192},{320,256},{256,320},{448,384},{3... | collective-permute-start | bytes 1769480 | tf_op jit(solution)/shard_map/ppermute | solution.py:35
  202.7 1.9 collective-permute-start.22
  204.7 2.4 %collective-permute-start.23 = (bf16[4,144,512]{2,1,0:T(8,128)(2,1)S(1)}, bf16[4,144,512]{2,1,0:T(8,128)(2,1)}, u32[]{:S(2)}, u32[]{:S(2)}) collective-permute-start(bf16[4,144,512]{2,1,0:T(8,128)(2,1)S(1)} %pad_maximum_fusion.refs_4_), channel_id=1, source_target_pairs={{64,0},{0,64},{192,128},{128,192},{320,256},{256,320},{448,384},{3... | collective-permute-start | bytes 1769480 | tf_op jit(solution)/shard_map/ppermute | solution.py:35
  207.1 0.6 stack.57.meta_ref
  207.7 0.6 pad_add_fusion.meta_ref
  208.3 7.2 %near.1 = (f32[3,256,512]{2,1,0:T(8,128)}, f32[1,512]{1,0:T(1,128)}) custom-call(s32[5]{0:T(128)} %stack.57.meta_ref, bf16[16,3,256,256]{3,2,1,0:T(8,128)(2,1)} %bitcast.45, bf16[4,144,512]{2,1,0:T(8,128)(2,1)} %bitcast.50, bf16[4,144,512]{2,1,0:T(8,128)(2,1)} %copy-done.9, bf16[4,144,512]{2,1,0:T(8,128)(2,1)} %copy-done.10, bf16[4,144,512]{2,1,0:T(8,128)(2,1)} %copy-done.8, ...), custom_call_target="tpu_custom_call" | custom-call | flops 2013265920 | bytes 6553600 | tf_op jit(solution)/shard_map/near/pallas_call | solution.py:364
  215.6 0.8 copy-done.12
  216.4 6.7 %far.1 = (bf16[3,256,512]{2,1,0:T(8,128)(2,1)}, f32[1,512]{1,0:T(1,128)}) custom-call(s32[3]{0:T(128)} %pad_add_fusion.meta_ref, bf16[16,3,256,256]{3,2,1,0:T(8,128)(2,1)} %bitcast.46, f32[3,256,512]{2,1,0:T(8,128)} %get-tuple-element.50.near_ref, f32[1,512]{1,0:T(1,128)} %get-tuple-element.51.near_mix_ref, bf16[4,144,512]{2,1,0:T(8,128)(2,1)} %copy-done.12, ...), custom_call_target="tpu_custom_call" | custom-call | flops 1207959552 | bytes 3932160 | tf_op jit(solution)/shard_map/far/pallas_call | solution.py:364
  (43 shorter events, 0.1 us)
Async XLA Ops:
  7.2 50.0 %copy-start = (bf16[1024,3,512]{2,0,1:T(8,128)(2,1)S(1)}, bf16[1024,3,512]{2,0,1:T(8,128)(2,1)}, u32[]{:S(2)}) copy-start(bf16[1024,3,512]{2,0,1:T(8,128)(2,1)} %param.5) | copy-start | bytes 9437188
  7.2 36.5 %collective-permute-start.3 = (bf16[3,64,1024]{2,1,0:T(8,128)(2,1)}, bf16[3,64,1024]{2,1,0:T(8,128)(2,1)}, u32[]{:S(2)}, u32[]{:S(2)}) collective-permute-start(bf16[3,64,1024]{2,1,0:T(8,128)(2,1)} %bitcast.37), channel_id=1, source_target_pairs={{12,0},{13,1},{14,2},{15,3},{0,4},{1,5},{2,6},{3,7},{4,8},{5,9},{6... | collective-permute-start | bytes 1179656 | tf_op jit(solution)/shard_map/ppermute | solution.py:31
  11.5 32.2 %collective-permute-start.2 = (bf16[3,64,1024]{2,1,0:T(8,128)(2,1)}, bf16[3,64,1024]{2,1,0:T(8,128)(2,1)}, u32[]{:S(2)}, u32[]{:S(2)}) collective-permute-start(bf16[3,64,1024]{2,1,0:T(8,128)(2,1)} %bitcast.38), channel_id=1, source_target_pairs={{8,0},{9,1},{10,2},{11,3},{12,4},{13,5},{14,6},{15,7},{0,8},{1,9},... | collective-permute-start | bytes 1179656 | tf_op jit(solution)/shard_map/ppermute | solution.py:31
  16.0 19.6 %collective-permute-start = (bf16[3,64,1024]{2,1,0:T(8,128)(2,1)}, bf16[3,64,1024]{2,1,0:T(8,128)(2,1)}, u32[]{:S(2)}, u32[]{:S(2)}) collective-permute-start(bf16[3,64,1024]{2,1,0:T(8,128)(2,1)} %bitcast.39), channel_id=1, source_target_pairs={{4,0},{5,1},{6,2},{7,3},{8,4},{9,5},{10,6},{11,7},{12,8},{13,9},{1... | collective-permute-start | bytes 1179656 | tf_op jit(solution)/shard_map/ppermute | solution.py:31
  20.8 40.5 %all-to-all-start = ((bf16[4,3,64,256]{3,2,1,0:T(8,128)(2,1)}), bf16[4,3,64,256]{3,2,1,0:T(8,128)(2,1)S(1)}, u32[]{:S(2)}, u32[]{:S(2)}) async-start(bf16[4,3,64,256]{3,2,1,0:T(8,128)(2,1)} %bitcast.51), calls=%async_computation | async-start | bytes 786432 | tf_op jit(solution)/shard_map/all_to_all | solution.py:448
  35.6 172.7 %all-gather.4.cloned.1.call-start = ((), (), s32[]{:S(2)}) async-start(), calls=%async_computation.1 | async-start | bytes 6684672 | tf_op jit(solution)/shard_map/all_gather | solution.py:495
  35.6 1.0 copy-start.1
  39.3 22.0 %collective-permute-start.1 = (bf16[2,3,64,1024]{3,2,1,0:T(8,128)(2,1)}, bf16[2,3,64,1024]{3,2,1,0:T(8,128)(2,1)}, u32[]{:S(2)}, u32[]{:S(2)}) collective-permute-start(bf16[2,3,64,1024]{3,2,1,0:T(8,128)(2,1)} %pair.2.refs_0_), channel_id=1, source_target_pairs={{1,0},{2,1},{3,2},{0,3},{5,4},{6,5},{7,6},{4,7},{9,8},{10,9},{11,1... | collective-permute-start | bytes 2359304 | tf_op jit(solution)/shard_map/ppermute | solution.py:31
  46.6 14.7 %collective-permute-start.4 = (bf16[2,3,64,1024]{3,2,1,0:T(8,128)(2,1)}, bf16[2,3,64,1024]{3,2,1,0:T(8,128)(2,1)}, u32[]{:S(2)}, u32[]{:S(2)}) collective-permute-start(bf16[2,3,64,1024]{3,2,1,0:T(8,128)(2,1)} %pair.3.refs_1_), channel_id=1, source_target_pairs={{3,0},{0,1},{1,2},{2,3},{7,4},{4,5},{5,6},{6,7},{11,8},{8,9},{9,10... | collective-permute-start | bytes 2359304 | tf_op jit(solution)/shard_map/ppermute | solution.py:31
  48.6 33.9 %collective-permute-start.11 = (bf16[2,3,64,1024]{3,2,1,0:T(8,128)(2,1)}, bf16[2,3,64,1024]{3,2,1,0:T(8,128)(2,1)}, u32[]{:S(2)}, u32[]{:S(2)}) collective-permute-start(bf16[2,3,64,1024]{3,2,1,0:T(8,128)(2,1)} %pair.2.refs_0_), channel_id=1, source_target_pairs={{3,0},{0,1},{1,2},{2,3},{7,4},{4,5},{5,6},{6,7},{11,8},{8,9},{9,10... | collective-permute-start | bytes 2359304 | tf_op jit(solution)/shard_map/ppermute | solution.py:31
  50.7 34.5 %collective-permute-start.10 = (bf16[2,3,64,1024]{3,2,1,0:T(8,128)(2,1)}, bf16[2,3,64,1024]{3,2,1,0:T(8,128)(2,1)}, u32[]{:S(2)}, u32[]{:S(2)}) collective-permute-start(bf16[2,3,64,1024]{3,2,1,0:T(8,128)(2,1)} %pair.3.refs_1_), channel_id=1, source_target_pairs={{1,0},{2,1},{3,2},{0,3},{5,4},{6,5},{7,6},{4,7},{9,8},{10,9},{11,1... | collective-permute-start | bytes 2359304 | tf_op jit(solution)/shard_map/ppermute | solution.py:31
  55.8 5.5 %collective-permute-start.5 = (bf16[16,1024]{1,0:T(8,128)(2,1)S(1)}, bf16[16,1024]{1,0:T(8,128)(2,1)}, u32[]{:S(2)}, u32[]{:S(2)}) collective-permute-start(bf16[16,1024]{1,0:T(8,128)(2,1)S(1)} %slice_bitcast_fusion.1), channel_id=1, source_target_pairs={{1,0},{2,1},{3,2},{4,3},{5,4},{6,5},{7,6},{8,7},{9,8},{10,9},{11,1... | collective-permute-start | bytes 98312 | tf_op jit(solution)/shard_map/ppermute | solution.py:442
  60.2 0.7 copy-start.3
  61.3 28.8 %collective-permute-start.6 = (bf16[2,3,64,1024]{3,2,1,0:T(8,128)(2,1)}, bf16[2,3,64,1024]{3,2,1,0:T(8,128)(2,1)}, u32[]{:S(2)}, u32[]{:S(2)}) collective-permute-start(bf16[2,3,64,1024]{3,2,1,0:T(8,128)(2,1)} %collective-permute-done.1.refs_0_), channel_id=1, source_target_pairs={{1,0},{2,1},{3,2},{0,3},{5,4},{6,5},{7,6},{4,7},{9,8},{10,9},{11,1... | collective-permute-start | bytes 2359304 | tf_op jit(solution)/shard_map/ppermute | solution.py:31
  68.3 21.8 %collective-permute-start.7 = (bf16[2,3,64,1024]{3,2,1,0:T(8,128)(2,1)}, bf16[2,3,64,1024]{3,2,1,0:T(8,128)(2,1)}, u32[]{:S(2)}, u32[]{:S(2)}) collective-permute-start(bf16[2,3,64,1024]{3,2,1,0:T(8,128)(2,1)} %collective-permute-done.4.refs_3_), channel_id=1, source_target_pairs={{3,0},{0,1},{1,2},{2,3},{7,4},{4,5},{5,6},{6,7},{11,8},{8,9},{9,10... | collective-permute-start | bytes 2359304 | tf_op jit(solution)/shard_map/ppermute | solution.py:31
  72.7 17.4 %collective-permute-start.9 = (bf16[80,512]{1,0:T(8,128)(2,1)}, bf16[80,512]{1,0:T(8,128)(2,1)}, u32[]{:S(2)}, u32[]{:S(2)}) collective-permute-start(bf16[80,512]{1,0:T(8,128)(2,1)} %get-tuple-element.59), channel_id=1, source_target_pairs={{0,1},{1,0},{2,65},{3,64},{4,129},{5,128},{6,193},{7,192},{8,257},... | collective-permute-start | bytes 245768 | tf_op jit(solution)/shard_map/ppermute | solution.py:431
  82.4 7.7 %collective-permute-start.8 = (bf16[80,512]{1,0:T(8,128)(2,1)}, bf16[80,512]{1,0:T(8,128)(2,1)S(1)}, u32[]{:S(2)}, u32[]{:S(2)}) collective-permute-start(bf16[80,512]{1,0:T(8,128)(2,1)} %get-tuple-element.60), channel_id=1, source_target_pairs={{0,0},{1,1},{2,64},{3,65},{4,128},{5,129},{6,192},{7,193},{8,256},... | collective-permute-start | bytes 245768 | tf_op jit(solution)/shard_map/ppermute | solution.py:430
  89.3 0.8 copy-start.2
  90.1 8.7 %copy-start.13 = (s32[4]{0:T(128)S(1)}, s32[4]{0:T(128)}, u32[]{:S(2)}) copy-start(s32[4]{0:T(128)} %param.7) | copy-start | bytes 52
  90.8 38.8 %copy-start.5 = (f32[512]{0:T(512)S(1)}, f32[512]{0:T(512)}, u32[]{:S(2)}) copy-start(f32[512]{0:T(512)} %param.6) | copy-start | bytes 6148
  96.9 6.5 %collective-permute-start.12 = (bf16[4,144,512]{2,1,0:T(8,128)(2,1)}, bf16[4,144,512]{2,1,0:T(8,128)(2,1)S(1)}, u32[]{:S(2)}, u32[]{:S(2)}) collective-permute-start(bf16[4,144,512]{2,1,0:T(8,128)(2,1)} %get-tuple-element.39), channel_id=1, source_target_pairs={{64,0},{0,64},{192,128},{128,192},{320,256},{256,320},{448,384},{3... | collective-permute-start | bytes 1769480 | tf_op jit(solution)/shard_map/ppermute | solution.py:35
  103.4 0.8 copy-start.11
  106.4 14.2 %collective-permute-start.13 = (bf16[144,512]{1,0:T(8,128)(2,1)}, bf16[144,512]{1,0:T(8,128)(2,1)S(1)}, u32[]{:S(2)}, u32[]{:S(2)}) collective-permute-start(bf16[144,512]{1,0:T(8,128)(2,1)} %get-tuple-element.41), channel_id=1, source_target_pairs={{128,0},{192,64},{256,128},{320,192},{384,256},{448,320},{0,384},{... | collective-permute-start | bytes 442376 | tf_op jit(solution)/shard_map/ppermute | solution.py:40
  115.6 14.0 %collective-permute-start.14 = (bf16[144,512]{1,0:T(8,128)(2,1)}, bf16[144,512]{1,0:T(8,128)(2,1)S(1)}, u32[]{:S(2)}, u32[]{:S(2)}) collective-permute-start(bf16[144,512]{1,0:T(8,128)(2,1)} %get-tuple-element.42), channel_id=1, source_target_pairs={{256,0},{320,64},{384,128},{448,192},{0,256},{64,320},{128,384},{1... | collective-permute-start | bytes 442376 | tf_op jit(solution)/shard_map/ppermute | solution.py:40
  117.5 12.1 %collective-permute-start.15 = (bf16[144,512]{1,0:T(8,128)(2,1)}, bf16[144,512]{1,0:T(8,128)(2,1)S(1)}, u32[]{:S(2)}, u32[]{:S(2)}) collective-permute-start(bf16[144,512]{1,0:T(8,128)(2,1)} %get-tuple-element.43), channel_id=1, source_target_pairs={{384,0},{448,64},{0,128},{64,192},{128,256},{192,320},{256,384},{3... | collective-permute-start | bytes 442376 | tf_op jit(solution)/shard_map/ppermute | solution.py:40
  129.6 0.9 copy-start.4
  165.5 42.8 %copy-start.6 = (bf16[576,512]{1,0:T(8,128)(2,1)}, bf16[576,512]{1,0:T(8,128)(2,1)S(1)}, u32[]{:S(2)}) copy-start(bf16[576,512]{1,0:T(8,128)(2,1)S(1)} %all-gather.1) | copy-start | bytes 1769476
  165.5 34.2 %collective-permute-start.18 = (bf16[4,144,512]{2,1,0:T(8,128)(2,1)S(1)}, bf16[4,144,512]{2,1,0:T(8,128)(2,1)S(1)}, u32[]{:S(2)}, u32[]{:S(2)}) collective-permute-start(bf16[4,144,512]{2,1,0:T(8,128)(2,1)S(1)} %bitcast.47), channel_id=1, source_target_pairs={{64,0},{0,64},{192,128},{128,192},{320,256},{256,320},{448,384},{3... | collective-permute-start | bytes 1769480 | tf_op jit(solution)/shard_map/ppermute | solution.py:35
  168.0 31.6 %collective-permute-start.17 = (bf16[4,144,512]{2,1,0:T(8,128)(2,1)S(1)}, bf16[4,144,512]{2,1,0:T(8,128)(2,1)S(1)}, u32[]{:S(2)}, u32[]{:S(2)}) collective-permute-start(bf16[4,144,512]{2,1,0:T(8,128)(2,1)S(1)} %bitcast.48), channel_id=1, source_target_pairs={{432,0},{384,16},{400,32},{416,48},{496,64},{448,80},{464,96},{480... | collective-permute-start | bytes 1769480 | tf_op jit(solution)/shard_map/ppermute | solution.py:53
  169.9 29.7 %collective-permute-start.16 = (bf16[4,144,512]{2,1,0:T(8,128)(2,1)S(1)}, bf16[4,144,512]{2,1,0:T(8,128)(2,1)S(1)}, u32[]{:S(2)}, u32[]{:S(2)}) collective-permute-start(bf16[4,144,512]{2,1,0:T(8,128)(2,1)S(1)} %bitcast.49), channel_id=1, source_target_pairs={{128,0},{144,16},{160,32},{176,48},{192,64},{208,80},{224,96},{240... | collective-permute-start | bytes 1769480 | tf_op jit(solution)/shard_map/ppermute | solution.py:53
  174.6 16.8 %collective-permute-start.20 = (bf16[2,144,512]{2,1,0:T(8,128)(2,1)S(1)}, bf16[2,144,512]{2,1,0:T(8,128)(2,1)S(1)}, u32[]{:S(2)}, u32[]{:S(2)}) collective-permute-start(bf16[2,144,512]{2,1,0:T(8,128)(2,1)S(1)} %bitcast.53), channel_id=1, source_target_pairs={{304,0},{256,16},{272,32},{288,48},{368,64},{320,80},{336,96},{352... | collective-permute-start | bytes 884744 | tf_op jit(solution)/shard_map/ppermute | solution.py:53
  176.5 23.1 %collective-permute-start.19 = (bf16[2,144,512]{2,1,0:T(8,128)(2,1)S(1)}, bf16[2,144,512]{2,1,0:T(8,128)(2,1)S(1)}, u32[]{:S(2)}, u32[]{:S(2)}) collective-permute-start(bf16[2,144,512]{2,1,0:T(8,128)(2,1)S(1)} %bitcast.52), channel_id=1, source_target_pairs={{256,0},{272,16},{288,32},{304,48},{320,64},{336,80},{352,96},{368... | collective-permute-start | bytes 884744 | tf_op jit(solution)/shard_map/ppermute | solution.py:53
  199.6 8.7 %copy-start.7 = (bf16[4,144,512]{2,1,0:T(8,128)(2,1)}, bf16[4,144,512]{2,1,0:T(8,128)(2,1)S(1)}, u32[]{:S(2)}) copy-start(bf16[4,144,512]{2,1,0:T(8,128)(2,1)S(1)} %pad_maximum_fusion.refs_4_) | copy-start | bytes 1769476
  199.6 8.7 %copy-start.9 = (bf16[4,144,512]{2,1,0:T(8,128)(2,1)}, bf16[4,144,512]{2,1,0:T(8,128)(2,1)S(1)}, u32[]{:S(2)}) copy-start(bf16[4,144,512]{2,1,0:T(8,128)(2,1)S(1)} %collective-permute-done.18.refs_1_) | copy-start | bytes 1769476
  199.7 8.7 %copy-start.8 = (bf16[4,144,512]{2,1,0:T(8,128)(2,1)}, bf16[4,144,512]{2,1,0:T(8,128)(2,1)S(1)}, u32[]{:S(2)}) copy-start(bf16[4,144,512]{2,1,0:T(8,128)(2,1)S(1)} %collective-permute-done.17.refs_3_) | copy-start | bytes 1769476
  199.7 8.7 %copy-start.10 = (bf16[4,144,512]{2,1,0:T(8,128)(2,1)}, bf16[4,144,512]{2,1,0:T(8,128)(2,1)S(1)}, u32[]{:S(2)}) copy-start(bf16[4,144,512]{2,1,0:T(8,128)(2,1)S(1)} %collective-permute-done.16.refs_2_) | copy-start | bytes 1769476
  199.7 15.8 %collective-permute-start.21 = (bf16[4,144,512]{2,1,0:T(8,128)(2,1)S(1)}, bf16[4,144,512]{2,1,0:T(8,128)(2,1)S(1)}, u32[]{:S(2)}, u32[]{:S(2)}) collective-permute-start(bf16[4,144,512]{2,1,0:T(8,128)(2,1)S(1)} %collective-permute-done.16.refs_2_), channel_id=1, source_target_pairs={{64,0},{0,64},{192,128},{128,192},{320,256},{256,320},{448,384},{3... | collective-permute-start | bytes 1769480 | tf_op jit(solution)/shard_map/ppermute | solution.py:35
  202.7 12.8 %collective-permute-start.22 = (bf16[4,144,512]{2,1,0:T(8,128)(2,1)S(1)}, bf16[4,144,512]{2,1,0:T(8,128)(2,1)}, u32[]{:S(2)}, u32[]{:S(2)}) collective-permute-start(bf16[4,144,512]{2,1,0:T(8,128)(2,1)S(1)} %collective-permute-done.17.refs_3_), channel_id=1, source_target_pairs={{64,0},{0,64},{192,128},{128,192},{320,256},{256,320},{448,384},{3... | collective-permute-start | bytes 1769480 | tf_op jit(solution)/shard_map/ppermute | solution.py:35
  204.7 10.9 %collective-permute-start.23 = (bf16[4,144,512]{2,1,0:T(8,128)(2,1)S(1)}, bf16[4,144,512]{2,1,0:T(8,128)(2,1)}, u32[]{:S(2)}, u32[]{:S(2)}) collective-permute-start(bf16[4,144,512]{2,1,0:T(8,128)(2,1)S(1)} %pad_maximum_fusion.refs_4_), channel_id=1, source_target_pairs={{64,0},{0,64},{192,128},{128,192},{320,256},{256,320},{448,384},{3... | collective-permute-start | bytes 1769480 | tf_op jit(solution)/shard_map/ppermute | solution.py:35
  215.5 0.8 copy-start.12
Sparse Core Ops, SparseCore 0:
  90.3 80.7 all-gather.3

commit v7 on v5

--- a/solution.py
+++ b/solution.py
@@ -53,23 +53,18 @@
     return lax.ppermute(block, ("tp", "dp"), pairs)
 
 
-def pair_kernel(first_ref, second_ref, out_ref, sem):
-    first = pltpu.make_async_copy(first_ref, out_ref.at[0], sem.at[0])
-    second = pltpu.make_async_copy(second_ref, out_ref.at[1], sem.at[1])
-    first.start()
-    second.start()
-    first.wait()
-    second.wait()
+def pair_kernel(first_ref, second_ref, out_ref):
+    out_ref[0] = first_ref[...]
+    out_ref[1] = second_ref[...]
 
 
 def pair(first, second):
-    anywhere = pl.BlockSpec(memory_space=pl.ANY)
     return pl.pallas_call(
         pair_kernel,
         out_shape=jax.ShapeDtypeStruct((2,) + first.shape, first.dtype),
-        in_specs=[anywhere] * 2,
-        out_specs=anywhere,
-        scratch_shapes=[pltpu.SemaphoreType.DMA((2,))],
+        in_specs=[VMEM] * 2,
+        out_specs=VMEM,
+        compiler_params=params(4),
         cost_estimate=pl.CostEstimate(flops=0, bytes_accessed=8 * first.size, transcendentals=0),
         name="pair",
     )(first, second)
@@ -202,12 +197,15 @@
 
 
 def join(keep, got, zl):
-    piece = jax.ShapeDtypeStruct(keep.shape[1:], jnp.bfloat16)
+    count, rows, width = keep.shape
+    whole = pl.BlockSpec(keep.shape, lambda i, m: (0, 0, 0))
+    piece = pl.BlockSpec((rows, width), lambda i, m: (0, 0))
     return pl.pallas_call(
         join_kernel,
-        out_shape=(piece,) * ZL,
-        in_specs=[SMEM, VMEM, VMEM],
-        out_specs=(VMEM,) * ZL,
+        out_shape=(jax.ShapeDtypeStruct((rows, width), jnp.bfloat16),) * count,
+        grid_spec=pltpu.PrefetchScalarGridSpec(
+            num_scalar_prefetch=1, grid=(1,), in_specs=[whole] * 2, out_specs=(piece,) * count
+        ),
         compiler_params=params(8),
         cost_estimate=pl.CostEstimate(
             flops=keep.size, bytes_accessed=6 * keep.size, transcendentals=0
@@ -287,75 +285,57 @@
     )(jnp.stack([start, length]), scale.reshape(1), *parts, high, gain.reshape(1, width))
 
 
-def pieces_of(zl, core):
-    found = []
-    for step, other in ((0, 0), (0, 1), (1, 0), (-1, 0), (1, 1), (-1, 1), (2, 0), (2, 1)):
-        found.append(lax.rem(zl + step + ZL, ZL) * CORES + (1 - core if other else core))
-    return found
-
-
 def weight_grad_kernel(meta_ref, features_ref, *refs):
-    *group_refs, out_ref, mix_ref, grads_ref, tail_ref, held_ref, sem, held_sem = refs
-    level = pl.program_id(0)
-    zl, core = meta_ref[0], meta_ref[1]
+    *group_refs, out_ref, mix_ref, got_ref, grads_ref, held_ref, got_sem, held_sem = refs
     half = grads_ref.shape[1] // ZH
     width = grads_ref.shape[2]
-
-    def held(at):
-        return pltpu.make_async_copy(features_ref.at[:, at], held_ref.at[at], held_sem.at[at])
-
-    @pl.when(level == 0)
-    def _():
-        copies = []
-        for group, (group_ref, member) in enumerate(zip(group_refs, pieces_of(zl, core))):
+    got = [
+        pltpu.make_async_copy(group_ref, got_ref.at[at], got_sem.at[at])
+        for at, group_ref in enumerate(group_refs)
+    ]
+    held = [
+        pltpu.make_async_copy(features_ref.at[:, at], held_ref.at[at], held_sem.at[at])
+        for at in range(LEVELS)
+    ]
+    for copy in got + held:
+        copy.start()
+    mix = jnp.zeros((TAIL, width), jnp.float32)
+    for at, copy in enumerate(got):
+        copy.wait()
+        for part in range(2):
+            slab = grads_ref.at[meta_ref[at] * 2 + part]
             for sequence in range(ZH):
-                for part in range(2):
-                    rows = group_ref.at[sequence, pl.ds(part * half, half), :]
-                    slot = grads_ref.at[member * 2 + part, pl.ds(sequence * half, half), :]
-                    copies.append((rows, slot))
-            rows = group_ref.at[:, pl.ds(2 * half, TAIL), :]
-            copies.append((rows, tail_ref.at[pl.ds(group * ZH, ZH)]))
-        copies = [
-            pltpu.make_async_copy(source, target, sem.at[at])
-            for at, (source, target) in enumerate(copies)
-        ]
-        for copy in copies:
-            copy.start()
-        for at in range(LEVELS):
-            held(at).start()
-        for copy in copies:
-            copy.wait()
-        mix = jnp.sum(tail_ref[...].astype(jnp.float32), axis=0)
-        mix_ref[...] = jnp.sum(mix, axis=0, keepdims=True)
-
-    held(level).wait()
-    blocks = features_ref.shape[0]
-    left = jnp.concatenate([held_ref[level, e] for e in range(blocks)], axis=1)
-    right = grads_ref[...].reshape(-1, width)
-    out_ref[0] = jnp.dot(left, right, preferred_element_type=jnp.float32).astype(jnp.bfloat16)
-
-
-def weight_grad(features, groups, zl, core):
+                rows = got_ref[at, sequence, pl.ds(part * half, half), :]
+                slab[pl.ds(sequence * half, half), :] = rows
+        for sequence in range(ZH):
+            mix = mix + got_ref[at, sequence, pl.ds(2 * half, TAIL), :].astype(jnp.float32)
+    mix_ref[...] = jnp.sum(mix, axis=0, keepdims=True)
+    blocks = held_ref.shape[1]
+    for at, copy in enumerate(held):
+        copy.wait()
+        left = jnp.concatenate([held_ref[at, e] for e in range(blocks)], axis=1)
+        right = grads_ref[...].reshape(-1, width)
+        term = jnp.dot(left, right, preferred_element_type=jnp.float32)
+        out_ref[at] = term.astype(jnp.bfloat16)
+
+
+def weight_grad(features, groups, members):
     draft, _, columns, tokens = features.shape
-    width = groups[0].shape[2]
-    count = len(groups)
+    count, width = len(groups), groups[0].shape[2]
+    hbm = pl.BlockSpec(memory_space=pltpu.HBM)
     return pl.pallas_call(
         weight_grad_kernel,
-        grid=(LEVELS,),
         out_shape=(
             jax.ShapeDtypeStruct((LEVELS, columns, width), jnp.bfloat16),
             jax.ShapeDtypeStruct((1, width), jnp.float32),
         ),
-        in_specs=[SMEM] + [pl.BlockSpec(memory_space=pltpu.HBM)] * (count + 1),
-        out_specs=(
-            pl.BlockSpec((1, columns, width), lambda l: (l, 0, 0)),
-            pl.BlockSpec((1, width), lambda l: (0, 0)),
-        ),
+        in_specs=[SMEM] + [hbm] * (count + 1),
+        out_specs=(VMEM, VMEM),
         scratch_shapes=[
+            pltpu.VMEM((count,) + groups[0].shape, jnp.bfloat16),
             pltpu.VMEM((draft, tokens, width), jnp.bfloat16),
-            pltpu.VMEM((count * ZH, TAIL, width), jnp.bfloat16),
             pltpu.VMEM((LEVELS, draft, columns, tokens), jnp.bfloat16),
-            pltpu.SemaphoreType.DMA((count * (2 * ZH + 1),)),
+            pltpu.SemaphoreType.DMA((count,)),
             pltpu.SemaphoreType.DMA((LEVELS,)),
         ],
         compiler_params=params(58),
@@ -365,7 +345,7 @@
             transcendentals=0,
         ),
         name="weight_grad",
-    )(jnp.stack([zl, core]), features, *groups)
+    )(jnp.stack(members), features, *groups)
 
 
 def turn_kernel(traded_ref, out_ref):
@@ -394,31 +374,34 @@
     return running
 
 
-def high_halves(top, draft_index):
+def send_high(top, draft_index):
     members, draft_count = ZL * CORES, X * Y
     width = top.shape[1] // 2
     even = draft_index % 2 == 0
     left, right = top[:, :width], top[:, width:]
-    first, second = [], []
+    straight, crossed, after_left, after_right = [], [], [], []
     for t in range(members):
         for e in range(draft_count):
+            source = t * draft_count + e
             target = e // 2 * draft_count + 2 * t
-            first.append((t * draft_count + e, target + e % 2))
-            second.append((t * draft_count + e, target + 1 - e % 2))
+            straight.append((source, target + e % 2))
+            crossed.append((source, target + 1 - e % 2))
+            if e % 2 == 0 and e > 0:
+                after_left.append((source, target - draft_count))
+                after_right.append((source, target - draft_count + 1))
     axes = ("tp", "draft")
-    one = lax.ppermute(jnp.where(even, left, right), axes, first)
-    two = lax.ppermute(jnp.where(even, right, left), axes, second)
-    return one, two
-
-
-def high_rows(one, two, draft_index):
+    return (
+        lax.ppermute(jnp.where(even, left, right), axes, straight),
+        lax.ppermute(jnp.where(even, right, left), axes, crossed),
+        lax.ppermute(left[:TAIL], axes, after_left),
+        lax.ppermute(right[:TAIL], axes, after_right),
+    )
+
+
+def high_rows(one, two, after_left, after_right, draft_index):
     even = draft_index % 2 == 0
-    first = jnp.where(even, one, two)[:-TAIL]
-    return jnp.concatenate([first, jnp.where(even, two, one)], axis=0)
-
-
-def rows_ahead(top):
-    return lax.ppermute(top[:TAIL], "draft", [(e, e - 1) for e in range(1, X * Y)])
+    after = jnp.where(even, after_left, after_right)
+    return jnp.concatenate([jnp.where(even, one, two), jnp.where(even, two, one), after], axis=0)
 
 
 def trade_columns(own):
@@ -427,15 +410,22 @@
     return lax.all_to_all(quarters, "dp", split_axis=0, concat_axis=0, tiled=True)
 
 
-def gather_grads(grad):
+def gather_grads(grad, features, zl, core):
     stack = lax.all_gather(grad, "dp", axis=0, tiled=False)
     above, below = from_z(stack, 1), from_z(stack, -1)
-    far = [from_z(stack[:2], 2), from_z(stack[2:], -2)]
+    far = jnp.concatenate([from_z(stack[:2], 2), from_z(stack[2:], -2)])
     other = from_other_core(stack)
-    above, below, other = lax.optimization_barrier((above, below, other))
-    other_above, other_below = from_other_core(above), from_other_core(below)
-    far = jnp.concatenate(far)
-    return [stack, other, above, below, other_above, other_below, far, from_other_core(far)]
+    above, below, other, far = lax.optimization_barrier((above, below, other, far))
+    swapped = [from_other_core(block) for block in (above, below, far)]
+
+    def member(step, of_core):
+        return (zl + step) % ZL * CORES + of_core
+
+    groups = [stack, other, above, below, far] + swapped
+    members = [member(0, core), member(0, 1 - core)]
+    members += [member(step, core) for step in (1, 3, 2)]
+    members += [member(step, 1 - core) for step in (1, 3, 2)]
+    return weight_grad(features, groups, members)
 
 
 def local(features, fc_weight, mix_gain, lengths):
@@ -454,24 +444,24 @@
     up_low, down_high = plane_move(1, False)(low), plane_move(-1, False)(high)
     up_high, down_low = plane_move(1, False)(high), plane_move(-1, False)(low)
     zero = project([low, high], weight)
-    ahead = rows_ahead(own[LEVELS - 1])
-    up_low, down_high, zero, ahead, traded, later = lax.optimization_barrier(
-        (up_low, down_high, zero, ahead, traded, own)
+    up_low, down_high, zero, traded, later = lax.optimization_barrier(
+        (up_low, down_high, zero, traded, own)
     )
     far_low, far_high = plane_move(1, False)(up_low), plane_move(-1, False)(down_high)
-    halves = high_halves(jnp.concatenate([later[LEVELS - 1], ahead], axis=0), draft_index)
+    halves = send_high(later[LEVELS - 1], draft_index)
     sides = project([up_low, up_high, down_low, down_high], weight)
     far_low, far_high, halves, sides, turned = lax.optimization_barrier(
         (far_low, far_high, halves, sides, turn(traded))
     )
+    keep, send = project_place([far_low, far_high], weight, zero, sides, core, x, y)
+    keep, send, turned = lax.optimization_barrier((keep, send, turned))
     every = lax.all_gather(turned, "draft", axis=0, tiled=False)
-    keep, send = project_place([far_low, far_high], weight, zero, sides, core, x, y)
     mine, *away = join(keep, from_other_core(send), zl)
     parts = [mine] + [from_zl(block, step) for step, block in zip((1, 2, 3), away)]
     scale = LOSS_SCALE / valid_total(lengths)
     target = high_rows(*halves, draft_index)
     grad = chain(parts, target, mix_gain, tp_index * piece, lengths[zh], scale)
-    fc_grad, mix_total = weight_grad(every, gather_grads(grad), zl, core)
+    fc_grad, mix_total = gather_grads(grad, every, zl, core)
     return (fc_grad.transpose(1, 0, 2), mix_total[0])
 
 

time: 268 us -> 227 us (0.85)
  the two profiles are of different devices: /device:TPU:1 before, /device:TPU:75 now
where the time goes in v7:
time: 227 us; the launch traced here: 226 us
  starting transfers between devices  97.1 us (43%)
  waiting for transfers between devices  38.5 us (17%)
  blocking collectives  31 us (14%)
  Pallas kernels  27 us (12%)
  between operations  16.6 us (7%)
  local copies, waits for them, and re-layouts  12.4 us (5%)
  other arithmetic  3.19 us (1%)
    all_gather x1, blocking collectives, gather_grads(): stack = lax.all_gather(grad, 'dp', axis=0, tiled=False)  31 us
    ppermute x9, starting transfers between devices, plane_move(): return lambda block: lax.ppermute(block, ('tp', 'draft'), pairs)  25.9 us
    ppermute x4, waiting for transfers between devices, from_z(): return lax.ppermute(block, ('tp', 'dp'), pairs)  21.9 us
    ppermute x4, starting transfers between devices, from_z(): return lax.ppermute(block, ('tp', 'dp'), pairs)  13.4 us
    all_to_all x1, starting transfers between devices, trade_columns(): lax.all_to_all(quarters, 'dp', split_axis=0, concat_axis=0, tiled=True)  13 us
    ppermute x3, starting transfers between devices, from_zl(): return lax.ppermute(block, 'tp', pairs)  12.4 us
    ppermute x5, starting transfers between devices, from_other_core(): return lax.ppermute(block, 'tp', [(t ^ 1, t) for t in range(ZL * CORES)])  11.9 us
    ppermute x3, waiting for transfers between devices, from_zl(): return lax.ppermute(block, 'tp', pairs)  10 us
  transfers between devices with their start and end apart: 27, of which 6 were waited for; matrix products, arithmetic and copies ran while one was open for 3% of the time, Pallas kernels for 6%

profile of v7, /device:TPU:75, one launch (start us, length us, event | category | flops | bytes accessed | tf_op | source)
XLA Modules:
  0.0 225.8 jit_solution(17746640715761079658)
XLA Ops:
  7.2 3.5 %collective-permute-start.3 = (bf16[3,64,1024]{2,1,0:T(8,128)(2,1)}, bf16[3,64,1024]{2,1,0:T(8,128)(2,1)}, u32[]{:S(2)}, u32[]{:S(2)}) collective-permute-start(bf16[3,64,1024]{2,1,0:T(8,128)(2,1)} %bitcast.35), channel_id=1, source_target_pairs={{12,0},{13,1},{14,2},{15,3},{0,4},{1,5},{2,6},{3,7},{4,8},{5,9},{6... | collective-permute-start | bytes 1179656 | tf_op jit(solution)/shard_map/ppermute | solution.py:31
  10.7 2.6 %collective-permute-start.2 = (bf16[3,64,1024]{2,1,0:T(8,128)(2,1)}, bf16[3,64,1024]{2,1,0:T(8,128)(2,1)}, u32[]{:S(2)}, u32[]{:S(2)}) collective-permute-start(bf16[3,64,1024]{2,1,0:T(8,128)(2,1)} %bitcast.36), channel_id=1, source_target_pairs={{8,0},{9,1},{10,2},{11,3},{12,4},{13,5},{14,6},{15,7},{0,8},{1,9},... | collective-permute-start | bytes 1179656 | tf_op jit(solution)/shard_map/ppermute | solution.py:31
  13.3 4.0 %collective-permute-start = (bf16[3,64,1024]{2,1,0:T(8,128)(2,1)}, bf16[3,64,1024]{2,1,0:T(8,128)(2,1)}, u32[]{:S(2)}, u32[]{:S(2)}) collective-permute-start(bf16[3,64,1024]{2,1,0:T(8,128)(2,1)} %bitcast.37), channel_id=1, source_target_pairs={{4,0},{5,1},{6,2},{7,3},{8,4},{9,5},{10,6},{11,7},{12,8},{13,9},{1... | collective-permute-start | bytes 1179656 | tf_op jit(solution)/shard_map/ppermute | solution.py:31
  17.3 1.8 copy.10
  19.1 13.0 %all-to-all-start = ((bf16[4,3,64,256]{3,2,1,0:T(8,128)(2,1)}), bf16[4,3,64,256]{3,2,1,0:T(8,128)(2,1)S(1)}, u32[]{:S(2)}, u32[]{:S(2)}) async-start(bf16[4,3,64,256]{3,2,1,0:T(8,128)(2,1)} %bitcast.46), calls=%async_computation | async-start | bytes 786432 | tf_op jit(solution)/shard_map/all_to_all | solution.py:410
  32.1 1.0 copy-done.1
  33.1 1.9 pair.2.refs_0_
  35.0 2.2 collective-permute-start.1
  37.2 2.0 pair.3.refs_1_
  39.2 3.1 %collective-permute-start.4 = (bf16[2,3,64,1024]{3,2,1,0:T(8,128)(2,1)}, bf16[2,3,64,1024]{3,2,1,0:T(8,128)(2,1)}, u32[]{:S(2)}, u32[]{:S(2)}) collective-permute-start(bf16[2,3,64,1024]{3,2,1,0:T(8,128)(2,1)} %pair.3.refs_1_), channel_id=1, source_target_pairs={{3,0},{0,1},{1,2},{2,3},{7,4},{4,5},{5,6},{6,7},{11,8},{8,9},{9,10... | collective-permute-start | bytes 2359304 | tf_op jit(solution)/shard_map/ppermute | solution.py:31
  42.4 3.1 %collective-permute-start.12 = (bf16[2,3,64,1024]{3,2,1,0:T(8,128)(2,1)}, bf16[2,3,64,1024]{3,2,1,0:T(8,128)(2,1)}, u32[]{:S(2)}, u32[]{:S(2)}) collective-permute-start(bf16[2,3,64,1024]{3,2,1,0:T(8,128)(2,1)} %pair.2.refs_0_), channel_id=1, source_target_pairs={{3,0},{0,1},{1,2},{2,3},{7,4},{4,5},{5,6},{6,7},{11,8},{8,9},{9,10... | collective-permute-start | bytes 2359304 | tf_op jit(solution)/shard_map/ppermute | solution.py:31
  45.5 2.2 collective-permute-start.11
  47.7 0.1 pad_add_fusion.meta_ref
  47.8 3.1 %project.2.refs_3_ = bf16[4,64,512]{2,1,0:T(8,128)(2,1)S(1)} custom-call(bf16[2,3,64,1024]{3,2,1,0:T(8,128)(2,1)} %pair.2.refs_0_, bf16[2,3,64,1024]{3,2,1,0:T(8,128)(2,1)} %pair.3.refs_1_, bf16[3,1024,512]{2,1,0:T(8,128)(2,1)S(1)} %bitcast.32), custom_call_target="tpu_custom_call" | custom-call | flops 805306368 | bytes 4718592 | tf_op jit(solution)/shard_map/project/pallas_call | solution.py:116
  50.9 0.7 copy-done.4
  51.6 5.4 %all-to-all-done.traded_ref = bf16[4,3,64,256]{3,2,1,0:T(8,128)(2,1)S(1)} async-done(((bf16[4,3,64,256]{3,2,1,0:T(8,128)(2,1)}), bf16[4,3,64,256]{3,2,1,0:T(8,128)(2,1)S(1)}, u32[]{:S(2)}, u32[]{:S(2)}) %all-to-all-start) | async-done | bytes 393248 | tf_op jit(solution)/shard_map/all_to_all | solution.py:410
  57.0 1.9 collective-permute-start.5
  58.9 3.4 %collective-permute-start.6 = (bf16[2,3,64,1024]{3,2,1,0:T(8,128)(2,1)}, bf16[2,3,64,1024]{3,2,1,0:T(8,128)(2,1)}, u32[]{:S(2)}, u32[]{:S(2)}) collective-permute-start(bf16[2,3,64,1024]{3,2,1,0:T(8,128)(2,1)} %collective-permute-done.4.refs_3_), channel_id=1, source_target_pairs={{3,0},{0,1},{1,2},{2,3},{7,4},{4,5},{5,6},{6,7},{11,8},{8,9},{9,10... | collective-permute-start | bytes 2359304 | tf_op jit(solution)/shard_map/ppermute | solution.py:31
  62.3 0.9 slice_bitcast_fusion
  63.2 0.6 fusion.1
  63.8 1.3 collective-permute-start.10
  65.1 0.7 broadcast_select_fusion.2
  65.8 1.2 collective-permute-start.9
  67.0 9.3 %collective-permute-start.8 = (bf16[64,512]{1,0:T(8,128)(2,1)}, bf16[64,512]{1,0:T(8,128)(2,1)}, u32[]{:S(2)}, u32[]{:S(2)}) collective-permute-start(bf16[64,512]{1,0:T(8,128)(2,1)} %get-tuple-element.67), channel_id=1, source_target_pairs={{0,1},{1,0},{2,65},{3,64},{4,129},{5,128},{6,193},{7,192},{8,257},... | collective-permute-start | bytes 196616 | tf_op jit(solution)/shard_map/ppermute | solution.py:395
  76.3 0.6 copy-done.12
  76.9 8.8 %collective-permute-start.7 = (bf16[64,512]{1,0:T(8,128)(2,1)}, bf16[64,512]{1,0:T(8,128)(2,1)}, u32[]{:S(2)}, u32[]{:S(2)}) collective-permute-start(bf16[64,512]{1,0:T(8,128)(2,1)} %get-tuple-element.68), channel_id=1, source_target_pairs={{0,0},{1,1},{2,64},{3,65},{4,128},{5,129},{6,192},{7,193},{8,256},... | collective-permute-start | bytes 196616 | tf_op jit(solution)/shard_map/ppermute | solution.py:394
  85.7 4.0 %project.3.refs_4_ = bf16[8,64,512]{2,1,0:T(8,128)(2,1)S(1)} custom-call(bf16[2,3,64,1024]{3,2,1,0:T(8,128)(2,1)} %collective-permute-done.1.refs_0_, bf16[2,3,64,1024]{3,2,1,0:T(8,128)(2,1)} %collective-permute-done.11.refs_1_, bf16[2,3,64,1024]{3,2,1,0:T(8,128)(2,1)} %collective-permute-done.12.refs_2_, ...), custom_call_target="tpu_custom_call" | custom-call | flops 1610612736 | bytes 6291456 | tf_op jit(solution)/shard_map/project/pallas_call | solution.py:116
  89.8 0.8 copy-done.2
  90.6 1.5 turn.1
  92.2 0.0 copy-start.3
  92.2 1.0 copy-done.3
  93.2 0.9 copy-done.5
  94.2 3.9 %project_place.1 = (bf16[4,144,512]{2,1,0:T(8,128)(2,1)S(1)}, bf16[4,144,512]{2,1,0:T(8,128)(2,1)S(1)}) custom-call(s32[3]{0:T(128)S(1)} %pad_add_fusion.meta_ref, bf16[2,3,64,1024]{3,2,1,0:T(8,128)(2,1)} %collective-permute-done.5.refs_0_, bf16[2,3,64,1024]{3,2,1,0:T(8,128)(2,1)} %collective-permute-done.6.refs_1_, bf16[3,1024,512]{2,1,0:T(8,128)(2,1)S(1)} %bitcast.34, ...), custom_call_target="tpu_custom_call" | custom-call | flops 805306368 | bytes 4718592 | tf_op jit(solution)/shard_map/project_place/pallas_call | solution.py:169
  98.1 0.8 copy-done.6
  98.9 0.8 copy-done.9
  99.7 0.0 all-gather.4.cloned.1.call-update
  99.7 1.9 collective-permute-start.13
  101.7 0.7 dynamic_slice.3
  102.3 0.7 maximum_reduce_fusion
  105.0 0.8 pad_add_fusion.1.meta_ref
  105.8 0.9 broadcast_select_fusion.1
  106.7 1.1 copy-done.7
  107.8 0.1 join.1
  107.9 1.9 collective-permute-start.14
  109.8 8.5 %collective-permute-start.15 = (bf16[144,512]{1,0:T(8,128)(2,1)S(1)}, bf16[144,512]{1,0:T(8,128)(2,1)S(1)}, u32[]{:S(2)}, u32[]{:S(2)}) collective-permute-start(bf16[144,512]{1,0:T(8,128)(2,1)S(1)} %get-tuple-element.46), channel_id=1, source_target_pairs={{256,0},{320,64},{384,128},{448,192},{0,256},{64,320},{128,384},{1... | collective-permute-start | bytes 442376 | tf_op jit(solution)/shard_map/ppermute | solution.py:40
  118.4 1.9 collective-permute-start.16
  120.3 6.8 %collective-permute-done.15.refs_2_ = bf16[144,512]{1,0:T(8,128)(2,1)S(1)} collective-permute-done((bf16[144,512]{1,0:T(8,128)(2,1)S(1)}, bf16[144,512]{1,0:T(8,128)(2,1)S(1)}, u32[]{:S(2)}, u32[]{:S(2)}) %collective-permute-start.15) | collective-permute-done | bytes 147488 | tf_op jit(solution)/shard_map/ppermute | solution.py:40
  127.1 3.2 %collective-permute-done.16.refs_3_ = bf16[144,512]{1,0:T(8,128)(2,1)S(1)} collective-permute-done((bf16[144,512]{1,0:T(8,128)(2,1)S(1)}, bf16[144,512]{1,0:T(8,128)(2,1)S(1)}, u32[]{:S(2)}, u32[]{:S(2)}) %collective-permute-start.16) | collective-permute-done | bytes 147488 | tf_op jit(solution)/shard_map/ppermute | solution.py:40
  130.4 1.4 chain.1
  131.7 31.0 %all-gather.1 = bf16[576,512]{1,0:T(8,128)(2,1)S(1)} all-gather(bf16[144,512]{1,0:T(8,128)(2,1)S(1)} %chain.1), channel_id=3, replica_groups=mesh['tp'=8,'dp'=4,'draft'=16] {'dp'}, dimensions={0}, use_global_device_ids=true | all-gather | bytes 737280 | tf_op jit(solution)/shard_map/all_gather | solution.py:414
  162.8 2.6 %collective-permute-start.19 = (bf16[4,144,512]{2,1,0:T(8,128)(2,1)S(1)}, bf16[4,144,512]{2,1,0:T(8,128)(2,1)S(1)}, u32[]{:S(2)}, u32[]{:S(2)}) collective-permute-start(bf16[4,144,512]{2,1,0:T(8,128)(2,1)S(1)} %bitcast.42), channel_id=1, source_target_pairs={{64,0},{0,64},{192,128},{128,192},{320,256},{256,320},{448,384},{3... | collective-permute-start | bytes 1769480 | tf_op jit(solution)/shard_map/ppermute | solution.py:35
  165.4 1.9 collective-permute-start.18
  167.3 3.4 %collective-permute-start.17 = (bf16[4,144,512]{2,1,0:T(8,128)(2,1)S(1)}, bf16[4,144,512]{2,1,0:T(8,128)(2,1)S(1)}, u32[]{:S(2)}, u32[]{:S(2)}) collective-permute-start(bf16[4,144,512]{2,1,0:T(8,128)(2,1)S(1)} %bitcast.44), channel_id=1, source_target_pairs={{128,0},{144,16},{160,32},{176,48},{192,64},{208,80},{224,96},{240... | collective-permute-start | bytes 1769480 | tf_op jit(solution)/shard_map/ppermute | solution.py:53
  170.8 6.2 %collective-permute-start.21 = (bf16[2,144,512]{2,1,0:T(8,128)(2,1)S(1)}, bf16[2,144,512]{2,1,0:T(8,128)(2,1)S(1)}, u32[]{:S(2)}, u32[]{:S(2)}) collective-permute-start(bf16[2,144,512]{2,1,0:T(8,128)(2,1)S(1)} %bitcast.48), channel_id=1, source_target_pairs={{304,0},{256,16},{272,32},{288,48},{368,64},{320,80},{336,96},{352... | collective-permute-start | bytes 884744 | tf_op jit(solution)/shard_map/ppermute | solution.py:53
  176.9 1.9 collective-permute-start.20
  178.9 10.4 %collective-permute-done.21 = bf16[2,144,512]{2,1,0:T(8,128)(2,1)S(1)} collective-permute-done((bf16[2,144,512]{2,1,0:T(8,128)(2,1)S(1)}, bf16[2,144,512]{2,1,0:T(8,128)(2,1)S(1)}, u32[]{:S(2)}, u32[]{:S(2)}) %collective-permute-start.21) | collective-permute-done | bytes 294944 | tf_op jit(solution)/shard_map/ppermute | solution.py:53
  189.2 11.5 %collective-permute-done.20 = bf16[2,144,512]{2,1,0:T(8,128)(2,1)S(1)} collective-permute-done((bf16[2,144,512]{2,1,0:T(8,128)(2,1)S(1)}, bf16[2,144,512]{2,1,0:T(8,128)(2,1)S(1)}, u32[]{:S(2)}, u32[]{:S(2)}) %collective-permute-start.20) | collective-permute-done | bytes 294944 | tf_op jit(solution)/shard_map/ppermute | solution.py:53
  200.7 0.1 pad_maximum_fusion.refs_4_
  200.9 3.0 %collective-permute-start.22 = (bf16[4,144,512]{2,1,0:T(8,128)(2,1)S(1)}, bf16[4,144,512]{2,1,0:T(8,128)(2,1)S(1)}, u32[]{:S(2)}, u32[]{:S(2)}) collective-permute-start(bf16[4,144,512]{2,1,0:T(8,128)(2,1)S(1)} %collective-permute-done.17.refs_2_), channel_id=1, source_target_pairs={{64,0},{0,64},{192,128},{128,192},{320,256},{256,320},{448,384},{3... | collective-permute-start | bytes 1769480 | tf_op jit(solution)/shard_map/ppermute | solution.py:35
  203.9 1.9 collective-permute-start.23
  205.8 2.4 %collective-permute-start.24 = (bf16[4,144,512]{2,1,0:T(8,128)(2,1)S(1)}, bf16[4,144,512]{2,1,0:T(8,128)(2,1)}, u32[]{:S(2)}, u32[]{:S(2)}) collective-permute-start(bf16[4,144,512]{2,1,0:T(8,128)(2,1)S(1)} %pad_maximum_fusion.refs_4_), channel_id=1, source_target_pairs={{64,0},{0,64},{192,128},{128,192},{320,256},{256,320},{448,384},{3... | collective-permute-start | bytes 1769480 | tf_op jit(solution)/shard_map/ppermute | solution.py:35
  208.3 0.6 stack.53.meta_ref
  208.9 1.1 collective-permute-done.24.refs_7_
  210.0 9.0 %weight_grad.1 = (bf16[3,256,512]{2,1,0:T(8,128)(2,1)}, f32[1,512]{1,0:T(1,128)}) custom-call(s32[8]{0:T(128)} %stack.53.meta_ref, bf16[16,3,256,256]{3,2,1,0:T(8,128)(2,1)} %bitcast.49, bf16[4,144,512]{2,1,0:T(8,128)(2,1)} %bitcast.45, bf16[4,144,512]{2,1,0:T(8,128)(2,1)} %copy-done.15, bf16[4,144,512]{2,1,0:T(8,128)(2,1)} %copy-done.17, ...), custom_call_target="tpu_custom_call" | custom-call | flops 3221225472 | bytes 10485760 | tf_op jit(solution)/shard_map/weight_grad/pallas_call | solution.py:326
  (53 shorter events, 0.2 us)
Async XLA Ops:
  7.2 40.6 %copy-start = (bf16[1024,3,512]{2,0,1:T(8,128)(2,1)S(1)}, bf16[1024,3,512]{2,0,1:T(8,128)(2,1)}, u32[]{:S(2)}) copy-start(bf16[1024,3,512]{2,0,1:T(8,128)(2,1)} %param.5) | copy-start | bytes 9437188
  7.2 30.0 %collective-permute-start.3 = (bf16[3,64,1024]{2,1,0:T(8,128)(2,1)}, bf16[3,64,1024]{2,1,0:T(8,128)(2,1)}, u32[]{:S(2)}, u32[]{:S(2)}) collective-permute-start(bf16[3,64,1024]{2,1,0:T(8,128)(2,1)} %bitcast.35), channel_id=1, source_target_pairs={{12,0},{13,1},{14,2},{15,3},{0,4},{1,5},{2,6},{3,7},{4,8},{5,9},{6... | collective-permute-start | bytes 1179656 | tf_op jit(solution)/shard_map/ppermute | solution.py:31
  10.7 26.5 %collective-permute-start.2 = (bf16[3,64,1024]{2,1,0:T(8,128)(2,1)}, bf16[3,64,1024]{2,1,0:T(8,128)(2,1)}, u32[]{:S(2)}, u32[]{:S(2)}) collective-permute-start(bf16[3,64,1024]{2,1,0:T(8,128)(2,1)} %bitcast.36), channel_id=1, source_target_pairs={{8,0},{9,1},{10,2},{11,3},{12,4},{13,5},{14,6},{15,7},{0,8},{1,9},... | collective-permute-start | bytes 1179656 | tf_op jit(solution)/shard_map/ppermute | solution.py:31
  13.3 18.8 %collective-permute-start = (bf16[3,64,1024]{2,1,0:T(8,128)(2,1)}, bf16[3,64,1024]{2,1,0:T(8,128)(2,1)}, u32[]{:S(2)}, u32[]{:S(2)}) collective-permute-start(bf16[3,64,1024]{2,1,0:T(8,128)(2,1)} %bitcast.37), channel_id=1, source_target_pairs={{4,0},{5,1},{6,2},{7,3},{8,4},{9,5},{10,6},{11,7},{12,8},{13,9},{1... | collective-permute-start | bytes 1179656 | tf_op jit(solution)/shard_map/ppermute | solution.py:31
  19.1 37.9 %all-to-all-start = ((bf16[4,3,64,256]{3,2,1,0:T(8,128)(2,1)}), bf16[4,3,64,256]{3,2,1,0:T(8,128)(2,1)S(1)}, u32[]{:S(2)}, u32[]{:S(2)}) async-start(bf16[4,3,64,256]{3,2,1,0:T(8,128)(2,1)} %bitcast.46), calls=%async_computation | async-start | bytes 786432 | tf_op jit(solution)/shard_map/all_to_all | solution.py:410
  32.1 177.9 %all-gather.4.cloned.1.call-start = ((), (), s32[]{:S(2)}) async-start(), calls=%async_computation.1 | async-start | bytes 6684672 | tf_op jit(solution)/shard_map/all_gather | solution.py:458
  32.1 1.0 copy-start.1
  35.0 22.0 %collective-permute-start.1 = (bf16[2,3,64,1024]{3,2,1,0:T(8,128)(2,1)}, bf16[2,3,64,1024]{3,2,1,0:T(8,128)(2,1)}, u32[]{:S(2)}, u32[]{:S(2)}) collective-permute-start(bf16[2,3,64,1024]{3,2,1,0:T(8,128)(2,1)} %pair.2.refs_0_), channel_id=1, source_target_pairs={{1,0},{2,1},{3,2},{0,3},{5,4},{6,5},{7,6},{4,7},{9,8},{10,9},{11,1... | collective-permute-start | bytes 2359304 | tf_op jit(solution)/shard_map/ppermute | solution.py:31
  39.2 17.8 %collective-permute-start.4 = (bf16[2,3,64,1024]{3,2,1,0:T(8,128)(2,1)}, bf16[2,3,64,1024]{3,2,1,0:T(8,128)(2,1)}, u32[]{:S(2)}, u32[]{:S(2)}) collective-permute-start(bf16[2,3,64,1024]{3,2,1,0:T(8,128)(2,1)} %pair.3.refs_1_), channel_id=1, source_target_pairs={{3,0},{0,1},{1,2},{2,3},{7,4},{4,5},{5,6},{6,7},{11,8},{8,9},{9,10... | collective-permute-start | bytes 2359304 | tf_op jit(solution)/shard_map/ppermute | solution.py:31
  42.4 23.4 %collective-permute-start.12 = (bf16[2,3,64,1024]{3,2,1,0:T(8,128)(2,1)}, bf16[2,3,64,1024]{3,2,1,0:T(8,128)(2,1)}, u32[]{:S(2)}, u32[]{:S(2)}) collective-permute-start(bf16[2,3,64,1024]{3,2,1,0:T(8,128)(2,1)} %pair.2.refs_0_), channel_id=1, source_target_pairs={{3,0},{0,1},{1,2},{2,3},{7,4},{4,5},{5,6},{6,7},{11,8},{8,9},{9,10... | collective-permute-start | bytes 2359304 | tf_op jit(solution)/shard_map/ppermute | solution.py:31
  45.5 21.5 %collective-permute-start.11 = (bf16[2,3,64,1024]{3,2,1,0:T(8,128)(2,1)}, bf16[2,3,64,1024]{3,2,1,0:T(8,128)(2,1)}, u32[]{:S(2)}, u32[]{:S(2)}) collective-permute-start(bf16[2,3,64,1024]{3,2,1,0:T(8,128)(2,1)} %pair.3.refs_1_), channel_id=1, source_target_pairs={{1,0},{2,1},{3,2},{0,3},{5,4},{6,5},{7,6},{4,7},{9,8},{10,9},{11,1... | collective-permute-start | bytes 2359304 | tf_op jit(solution)/shard_map/ppermute | solution.py:31
  50.8 0.7 copy-start.4
  57.0 35.1 %collective-permute-start.5 = (bf16[2,3,64,1024]{3,2,1,0:T(8,128)(2,1)}, bf16[2,3,64,1024]{3,2,1,0:T(8,128)(2,1)}, u32[]{:S(2)}, u32[]{:S(2)}) collective-permute-start(bf16[2,3,64,1024]{3,2,1,0:T(8,128)(2,1)} %collective-permute-done.1.refs_0_), channel_id=1, source_target_pairs={{1,0},{2,1},{3,2},{0,3},{5,4},{6,5},{7,6},{4,7},{9,8},{10,9},{11,1... | collective-permute-start | bytes 2359304 | tf_op jit(solution)/shard_map/ppermute | solution.py:31
  58.9 33.2 %collective-permute-start.6 = (bf16[2,3,64,1024]{3,2,1,0:T(8,128)(2,1)}, bf16[2,3,64,1024]{3,2,1,0:T(8,128)(2,1)}, u32[]{:S(2)}, u32[]{:S(2)}) collective-permute-start(bf16[2,3,64,1024]{3,2,1,0:T(8,128)(2,1)} %collective-permute-done.4.refs_3_), channel_id=1, source_target_pairs={{3,0},{0,1},{1,2},{2,3},{7,4},{4,5},{5,6},{6,7},{11,8},{8,9},{9,10... | collective-permute-start | bytes 2359304 | tf_op jit(solution)/shard_map/ppermute | solution.py:31
  63.8 12.5 %collective-permute-start.10 = (bf16[16,512]{1,0:T(8,128)(2,1)S(1)}, bf16[16,512]{1,0:T(8,128)(2,1)S(1)}, u32[]{:S(2)}, u32[]{:S(2)}) collective-permute-start(bf16[16,512]{1,0:T(8,128)(2,1)S(1)} %get-tuple-element.65), channel_id=1, source_target_pairs={{2,1},{4,65},{6,129},{8,193},{10,257},{12,321},{14,385},{66,3},{68... | collective-permute-start | bytes 49160 | tf_op jit(solution)/shard_map/ppermute | solution.py:397
  65.8 26.3 %collective-permute-start.9 = (bf16[16,512]{1,0:T(8,128)(2,1)}, bf16[16,512]{1,0:T(8,128)(2,1)}, u32[]{:S(2)}, u32[]{:S(2)}) collective-permute-start(bf16[16,512]{1,0:T(8,128)(2,1)} %get-tuple-element.66), channel_id=1, source_target_pairs={{2,0},{4,64},{6,128},{8,192},{10,256},{12,320},{14,384},{66,2},{68... | collective-permute-start | bytes 49160 | tf_op jit(solution)/shard_map/ppermute | solution.py:396
  67.0 25.1 %collective-permute-start.8 = (bf16[64,512]{1,0:T(8,128)(2,1)}, bf16[64,512]{1,0:T(8,128)(2,1)}, u32[]{:S(2)}, u32[]{:S(2)}) collective-permute-start(bf16[64,512]{1,0:T(8,128)(2,1)} %get-tuple-element.67), channel_id=1, source_target_pairs={{0,1},{1,0},{2,65},{3,64},{4,129},{5,128},{6,193},{7,192},{8,257},... | collective-permute-start | bytes 196616 | tf_op jit(solution)/shard_map/ppermute | solution.py:395
  76.3 0.6 copy-start.12
  76.9 24.8 %copy-start.14 = (s32[4]{0:T(128)S(1)}, s32[4]{0:T(128)}, u32[]{:S(2)}) copy-start(s32[4]{0:T(128)} %param.7) | copy-start | bytes 52
  76.9 53.4 %copy-start.8 = (f32[512]{0:T(512)S(1)}, f32[512]{0:T(512)}, u32[]{:S(2)}) copy-start(f32[512]{0:T(512)} %param.6) | copy-start | bytes 6148
  76.9 15.2 %collective-permute-start.7 = (bf16[64,512]{1,0:T(8,128)(2,1)}, bf16[64,512]{1,0:T(8,128)(2,1)}, u32[]{:S(2)}, u32[]{:S(2)}) collective-permute-start(bf16[64,512]{1,0:T(8,128)(2,1)} %get-tuple-element.68), channel_id=1, source_target_pairs={{0,0},{1,1},{2,64},{3,65},{4,128},{5,129},{6,192},{7,193},{8,256},... | collective-permute-start | bytes 196616 | tf_op jit(solution)/shard_map/ppermute | solution.py:394
  89.8 0.8 copy-start.2
  92.2 1.0 copy-start.3
  93.2 0.9 copy-start.5
  94.2 26.1 %copy-start.13 = (bf16[16,512]{1,0:T(8,128)(2,1)S(1)}, bf16[16,512]{1,0:T(8,128)(2,1)}, u32[]{:S(2)}) copy-start(bf16[16,512]{1,0:T(8,128)(2,1)} %copy-done.12) | copy-start | bytes 49156
  98.0 0.8 copy-start.6
  98.9 0.8 copy-start.9
  99.7 7.0 %collective-permute-start.13 = (bf16[4,144,512]{2,1,0:T(8,128)(2,1)}, bf16[4,144,512]{2,1,0:T(8,128)(2,1)S(1)}, u32[]{:S(2)}, u32[]{:S(2)}) collective-permute-start(bf16[4,144,512]{2,1,0:T(8,128)(2,1)} %copy-done.9), channel_id=1, source_target_pairs={{64,0},{0,64},{192,128},{128,192},{320,256},{256,320},{448,384},{3... | collective-permute-start | bytes 1769480 | tf_op jit(solution)/shard_map/ppermute | solution.py:35
  106.7 1.1 copy-start.7
  107.9 12.4 %collective-permute-start.14 = (bf16[144,512]{1,0:T(8,128)(2,1)S(1)}, bf16[144,512]{1,0:T(8,128)(2,1)S(1)}, u32[]{:S(2)}, u32[]{:S(2)}) collective-permute-start(bf16[144,512]{1,0:T(8,128)(2,1)S(1)} %get-tuple-element.45), channel_id=1, source_target_pairs={{128,0},{192,64},{256,128},{320,192},{384,256},{448,320},{0,384},{... | collective-permute-start | bytes 442376 | tf_op jit(solution)/shard_map/ppermute | solution.py:40
  109.8 17.3 %collective-permute-start.15 = (bf16[144,512]{1,0:T(8,128)(2,1)S(1)}, bf16[144,512]{1,0:T(8,128)(2,1)S(1)}, u32[]{:S(2)}, u32[]{:S(2)}) collective-permute-start(bf16[144,512]{1,0:T(8,128)(2,1)S(1)} %get-tuple-element.46), channel_id=1, source_target_pairs={{256,0},{320,64},{384,128},{448,192},{0,256},{64,320},{128,384},{1... | collective-permute-start | bytes 442376 | tf_op jit(solution)/shard_map/ppermute | solution.py:40
  118.4 12.0 %collective-permute-start.16 = (bf16[144,512]{1,0:T(8,128)(2,1)S(1)}, bf16[144,512]{1,0:T(8,128)(2,1)S(1)}, u32[]{:S(2)}, u32[]{:S(2)}) collective-permute-start(bf16[144,512]{1,0:T(8,128)(2,1)S(1)} %get-tuple-element.47), channel_id=1, source_target_pairs={{384,0},{448,64},{0,128},{64,192},{128,256},{192,320},{256,384},{3... | collective-permute-start | bytes 442376 | tf_op jit(solution)/shard_map/ppermute | solution.py:40
  162.8 47.2 %copy-start.10 = (bf16[576,512]{1,0:T(8,128)(2,1)}, bf16[576,512]{1,0:T(8,128)(2,1)S(1)}, u32[]{:S(2)}) copy-start(bf16[576,512]{1,0:T(8,128)(2,1)S(1)} %all-gather.1) | copy-start | bytes 1769476
  162.8 38.0 %collective-permute-start.19 = (bf16[4,144,512]{2,1,0:T(8,128)(2,1)S(1)}, bf16[4,144,512]{2,1,0:T(8,128)(2,1)S(1)}, u32[]{:S(2)}, u32[]{:S(2)}) collective-permute-start(bf16[4,144,512]{2,1,0:T(8,128)(2,1)S(1)} %bitcast.42), channel_id=1, source_target_pairs={{64,0},{0,64},{192,128},{128,192},{320,256},{256,320},{448,384},{3... | collective-permute-start | bytes 1769480 | tf_op jit(solution)/shard_map/ppermute | solution.py:35
  165.4 35.4 %collective-permute-start.18 = (bf16[4,144,512]{2,1,0:T(8,128)(2,1)S(1)}, bf16[4,144,512]{2,1,0:T(8,128)(2,1)S(1)}, u32[]{:S(2)}, u32[]{:S(2)}) collective-permute-start(bf16[4,144,512]{2,1,0:T(8,128)(2,1)S(1)} %bitcast.43), channel_id=1, source_target_pairs={{432,0},{384,16},{400,32},{416,48},{496,64},{448,80},{464,96},{480... | collective-permute-start | bytes 1769480 | tf_op jit(solution)/shard_map/ppermute | solution.py:53
  167.3 33.5 %collective-permute-start.17 = (bf16[4,144,512]{2,1,0:T(8,128)(2,1)S(1)}, bf16[4,144,512]{2,1,0:T(8,128)(2,1)S(1)}, u32[]{:S(2)}, u32[]{:S(2)}) collective-permute-start(bf16[4,144,512]{2,1,0:T(8,128)(2,1)S(1)} %bitcast.44), channel_id=1, source_target_pairs={{128,0},{144,16},{160,32},{176,48},{192,64},{208,80},{224,96},{240... | collective-permute-start | bytes 1769480 | tf_op jit(solution)/shard_map/ppermute | solution.py:53
  170.8 18.5 %collective-permute-start.21 = (bf16[2,144,512]{2,1,0:T(8,128)(2,1)S(1)}, bf16[2,144,512]{2,1,0:T(8,128)(2,1)S(1)}, u32[]{:S(2)}, u32[]{:S(2)}) collective-permute-start(bf16[2,144,512]{2,1,0:T(8,128)(2,1)S(1)} %bitcast.48), channel_id=1, source_target_pairs={{304,0},{256,16},{272,32},{288,48},{368,64},{320,80},{336,96},{352... | collective-permute-start | bytes 884744 | tf_op jit(solution)/shard_map/ppermute | solution.py:53
  176.9 23.8 %collective-permute-start.20 = (bf16[2,144,512]{2,1,0:T(8,128)(2,1)S(1)}, bf16[2,144,512]{2,1,0:T(8,128)(2,1)S(1)}, u32[]{:S(2)}, u32[]{:S(2)}) collective-permute-start(bf16[2,144,512]{2,1,0:T(8,128)(2,1)S(1)} %bitcast.47), channel_id=1, source_target_pairs={{256,0},{272,16},{288,32},{304,48},{320,64},{336,80},{352,96},{368... | collective-permute-start | bytes 884744 | tf_op jit(solution)/shard_map/ppermute | solution.py:53
  200.8 9.2 %copy-start.11 = (bf16[4,144,512]{2,1,0:T(8,128)(2,1)}, bf16[4,144,512]{2,1,0:T(8,128)(2,1)S(1)}, u32[]{:S(2)}) copy-start(bf16[4,144,512]{2,1,0:T(8,128)(2,1)S(1)} %pad_maximum_fusion.refs_4_) | copy-start | bytes 1769476
  200.8 9.2 %copy-start.15 = (bf16[4,144,512]{2,1,0:T(8,128)(2,1)}, bf16[4,144,512]{2,1,0:T(8,128)(2,1)S(1)}, u32[]{:S(2)}) copy-start(bf16[4,144,512]{2,1,0:T(8,128)(2,1)S(1)} %collective-permute-done.19.refs_1_) | copy-start | bytes 1769476
  200.8 9.2 %copy-start.16 = (bf16[4,144,512]{2,1,0:T(8,128)(2,1)}, bf16[4,144,512]{2,1,0:T(8,128)(2,1)S(1)}, u32[]{:S(2)}) copy-start(bf16[4,144,512]{2,1,0:T(8,128)(2,1)S(1)} %collective-permute-done.18.refs_3_) | copy-start | bytes 1769476
  200.9 9.2 %copy-start.17 = (bf16[4,144,512]{2,1,0:T(8,128)(2,1)}, bf16[4,144,512]{2,1,0:T(8,128)(2,1)S(1)}, u32[]{:S(2)}) copy-start(bf16[4,144,512]{2,1,0:T(8,128)(2,1)S(1)} %collective-permute-done.17.refs_2_) | copy-start | bytes 1769476
  200.9 8.1 %collective-permute-start.22 = (bf16[4,144,512]{2,1,0:T(8,128)(2,1)S(1)}, bf16[4,144,512]{2,1,0:T(8,128)(2,1)S(1)}, u32[]{:S(2)}, u32[]{:S(2)}) collective-permute-start(bf16[4,144,512]{2,1,0:T(8,128)(2,1)S(1)} %collective-permute-done.17.refs_2_), channel_id=1, source_target_pairs={{64,0},{0,64},{192,128},{128,192},{320,256},{256,320},{448,384},{3... | collective-permute-start | bytes 1769480 | tf_op jit(solution)/shard_map/ppermute | solution.py:35
  203.9 5.0 %collective-permute-start.23 = (bf16[4,144,512]{2,1,0:T(8,128)(2,1)S(1)}, bf16[4,144,512]{2,1,0:T(8,128)(2,1)}, u32[]{:S(2)}, u32[]{:S(2)}) collective-permute-start(bf16[4,144,512]{2,1,0:T(8,128)(2,1)S(1)} %collective-permute-done.18.refs_3_), channel_id=1, source_target_pairs={{64,0},{0,64},{192,128},{128,192},{320,256},{256,320},{448,384},{3... | collective-permute-start | bytes 1769480 | tf_op jit(solution)/shard_map/ppermute | solution.py:35
  205.8 4.2 %collective-permute-start.24 = (bf16[4,144,512]{2,1,0:T(8,128)(2,1)S(1)}, bf16[4,144,512]{2,1,0:T(8,128)(2,1)}, u32[]{:S(2)}, u32[]{:S(2)}) collective-permute-start(bf16[4,144,512]{2,1,0:T(8,128)(2,1)S(1)} %pad_maximum_fusion.refs_4_), channel_id=1, source_target_pairs={{64,0},{0,64},{192,128},{128,192},{320,256},{256,320},{448,384},{3... | collective-permute-start | bytes 1769480 | tf_op jit(solution)/shard_map/ppermute | solution.py:35
  208.9 1.1 copy-start.18
Sparse Core Ops, SparseCore 0:
  99.8 78.9 all-gather.3

commit v8 on v7

--- a/solution.py
+++ b/solution.py
@@ -105,9 +105,7 @@
 
 def product_cost(blocks, weight):
     size = sum(b.size for b in blocks)
-    return pl.CostEstimate(
-        flops=2 * size * weight.shape[2], bytes_accessed=2 * (weight.size + size), transcendentals=0
-    )
+    return pl.CostEstimate(flops=0, bytes_accessed=2 * size, transcendentals=0)
 
 
 def project(blocks, weight):
@@ -297,11 +295,14 @@
         pltpu.make_async_copy(features_ref.at[:, at], held_ref.at[at], held_sem.at[at])
         for at in range(LEVELS)
     ]
-    for copy in got + held:
+    for copy in got:
         copy.start()
     mix = jnp.zeros((TAIL, width), jnp.float32)
     for at, copy in enumerate(got):
         copy.wait()
+        if at == len(got) // 2:
+            for later in held:
+                later.start()
         for part in range(2):
             slab = grads_ref.at[meta_ref[at] * 2 + part]
             for sequence in range(ZH):
@@ -348,23 +349,28 @@
     )(jnp.stack(members), features, *groups)
 
 
-def turn_kernel(traded_ref, out_ref):
-    rows = traded_ref[:, 0].reshape(-1, traded_ref.shape[3])
+def turn_kernel(meta_ref, features_ref, out_ref):
+    del meta_ref
+    rows = features_ref[:, 0].reshape(-1, features_ref.shape[3])
     out_ref[0] = rows.astype(jnp.float32).T.astype(jnp.bfloat16)
 
 
-def turn(traded):
-    sequences, levels, rows, columns = traded.shape
+def turn(sequences, zh):
+    count, levels, rows, depth = sequences.shape
+    part = depth // ZH
     return pl.pallas_call(
         turn_kernel,
-        grid=(levels,),
-        out_shape=jax.ShapeDtypeStruct((levels, columns, sequences * rows), jnp.bfloat16),
-        in_specs=[pl.BlockSpec((sequences, 1, rows, columns), lambda l: (0, l, 0, 0))],
-        out_specs=pl.BlockSpec((1, columns, sequences * rows), lambda l: (l, 0, 0)),
+        out_shape=jax.ShapeDtypeStruct((levels, part, count * rows), jnp.bfloat16),
+        grid_spec=pltpu.PrefetchScalarGridSpec(
+            num_scalar_prefetch=1,
+            grid=(levels,),
+            in_specs=[pl.BlockSpec((count, 1, rows, part), lambda l, m: (0, l, 0, m[0]))],
+            out_specs=pl.BlockSpec((1, part, count * rows), lambda l, m: (l, 0, 0)),
+        ),
         compiler_params=params(8),
-        cost_estimate=pl.CostEstimate(flops=0, bytes_accessed=4 * traded.size, transcendentals=0),
+        cost_estimate=pl.CostEstimate(flops=0, bytes_accessed=sequences.size, transcendentals=0),
         name="turn",
-    )(traded)
+    )(zh.reshape(1), sequences)
 
 
 def valid_total(lengths):
@@ -404,12 +410,6 @@
     return jnp.concatenate([jnp.where(even, one, two), jnp.where(even, two, one), after], axis=0)
 
 
-def trade_columns(own):
-    levels, rows, depth = own.shape
-    quarters = own.reshape(levels, rows, ZH, depth // ZH).transpose(2, 0, 1, 3)
-    return lax.all_to_all(quarters, "dp", split_axis=0, concat_axis=0, tiled=True)
-
-
 def gather_grads(grad, features, zl, core):
     stack = lax.all_gather(grad, "dp", axis=0, tiled=False)
     above, below = from_z(stack, 1), from_z(stack, -1)
@@ -438,26 +438,24 @@
     own = features.transpose(1, 0, 2)
     weight = fc_weight.transpose(1, 0, 2)
 
-    traded = trade_columns(own)
+    sequences = lax.all_gather(own, "dp", axis=0, tiled=False)
     next_, last, across = (plane_move(step, True)(own) for step in (1, 3, 2))
     low, high = pair(own, next_), pair(across, last)
     up_low, down_high = plane_move(1, False)(low), plane_move(-1, False)(high)
     up_high, down_low = plane_move(1, False)(high), plane_move(-1, False)(low)
     zero = project([low, high], weight)
-    up_low, down_high, zero, traded, later = lax.optimization_barrier(
-        (up_low, down_high, zero, traded, own)
+    up_low, down_high, zero, later = lax.optimization_barrier(
+        (up_low, down_high, zero, own)
     )
     far_low, far_high = plane_move(1, False)(up_low), plane_move(-1, False)(down_high)
     halves = send_high(later[LEVELS - 1], draft_index)
     sides = project([up_low, up_high, down_low, down_high], weight)
-    far_low, far_high, halves, sides, turned = lax.optimization_barrier(
-        (far_low, far_high, halves, sides, turn(traded))
-    )
+    far_low, far_high, halves, sides = lax.optimization_barrier((far_low, far_high, halves, sides))
     keep, send = project_place([far_low, far_high], weight, zero, sides, core, x, y)
-    keep, send, turned = lax.optimization_barrier((keep, send, turned))
-    every = lax.all_gather(turned, "draft", axis=0, tiled=False)
     mine, *away = join(keep, from_other_core(send), zl)
     parts = [mine] + [from_zl(block, step) for step, block in zip((1, 2, 3), away)]
+    parts, sequences = lax.optimization_barrier((parts, sequences))
+    every = lax.all_gather(turn(sequences, zh), "draft", axis=0, tiled=False)
     scale = LOSS_SCALE / valid_total(lengths)
     target = high_rows(*halves, draft_index)
     grad = chain(parts, target, mix_gain, tp_index * piece, lengths[zh], scale)

time: 227 us -> 236 us (1.040)
  the two profiles are of different devices: /device:TPU:75 before, /device:TPU:29 now
where the time goes in v8:
time: 236 us; the launch traced here: 235 us
  starting transfers between devices  86.2 us (37%)
  waiting for transfers between devices  61.2 us (26%)
  blocking collectives  36.3 us (15%)
  Pallas kernels  26.2 us (11%)
  between operations  16.6 us (7%)
  local copies, waits for them, and re-layouts  6.6 us (3%)
    all_gather x1, blocking collectives, gather_grads(): stack = lax.all_gather(grad, 'dp', axis=0, tiled=False)  36.3 us
    ppermute x9, starting transfers between devices, plane_move(): return lambda block: lax.ppermute(block, ('tp', 'draft'), pairs)  24.5 us
    ppermute x4, waiting for transfers between devices, from_z(): return lax.ppermute(block, ('tp', 'dp'), pairs)  21.7 us
    ppermute x1, starting transfers between devices, send_high(): lax.ppermute(jnp.where(even, right, left), axes, crossed)  16.1 us
    ppermute x4, starting transfers between devices, from_z(): return lax.ppermute(block, ('tp', 'dp'), pairs)  15.1 us
    ppermute x5, starting transfers between devices, from_other_core(): return lax.ppermute(block, 'tp', [(t ^ 1, t) for t in range(ZL * CORES)])  13 us
    ppermute x1, waiting for transfers between devices, send_high(): lax.ppermute(jnp.where(even, right, left), axes, crossed)  12 us
    ppermute x3, starting transfers between devices, from_zl(): return lax.ppermute(block, 'tp', pairs)  10.1 us
  transfers between devices with their start and end apart: 27, of which 12 were waited for; matrix products, arithmetic and copies ran while one was open for 2% of the time, Pallas kernels for 7%

profile of v8, /device:TPU:29, one launch (start us, length us, event | category | flops | bytes accessed | tf_op | source)
XLA Modules:
  0.0 234.7 jit_solution(7723669534729696434)
XLA Ops:
  7.2 0.0 all-gather.6.cloned.1.call-start
  7.2 2.6 %collective-permute-start = (bf16[3,64,1024]{2,1,0:T(8,128)(2,1)}, bf16[3,64,1024]{2,1,0:T(8,128)(2,1)}, u32[]{:S(2)}, u32[]{:S(2)}) collective-permute-start(bf16[3,64,1024]{2,1,0:T(8,128)(2,1)} %bitcast.30), channel_id=1, source_target_pairs={{4,0},{5,1},{6,2},{7,3},{8,4},{9,5},{10,6},{11,7},{12,8},{13,9},{1... | collective-permute-start | bytes 1179656 | tf_op jit(solution)/shard_map/ppermute | solution.py:31
  9.9 4.1 %collective-permute-start.3 = (bf16[3,64,1024]{2,1,0:T(8,128)(2,1)}, bf16[3,64,1024]{2,1,0:T(8,128)(2,1)S(1)}, u32[]{:S(2)}, u32[]{:S(2)}) collective-permute-start(bf16[3,64,1024]{2,1,0:T(8,128)(2,1)} %bitcast.31), channel_id=1, source_target_pairs={{12,0},{13,1},{14,2},{15,3},{0,4},{1,5},{2,6},{3,7},{4,8},{5,9},{6... | collective-permute-start | bytes 1179656 | tf_op jit(solution)/shard_map/ppermute | solution.py:31
  14.0 1.9 collective-permute-start.2
  15.9 0.0 all-gather.6.cloned.1.call-update
  16.0 0.0 all-gather.8.cloned.1.call-start
  16.0 1.5 collective-permute-done.second_ref
  17.5 1.0 copy-done.1
  18.5 1.9 pair.2.refs_0_
  20.5 2.2 collective-permute-start.1
  22.6 0.6 collective-permute-done.3.second_ref
  23.3 1.1 collective-permute-done.2.first_ref
  24.3 1.9 pair.3.refs_1_
  26.3 3.1 %collective-permute-start.4 = (bf16[2,3,64,1024]{3,2,1,0:T(8,128)(2,1)}, bf16[2,3,64,1024]{3,2,1,0:T(8,128)(2,1)}, u32[]{:S(2)}, u32[]{:S(2)}) collective-permute-start(bf16[2,3,64,1024]{3,2,1,0:T(8,128)(2,1)} %pair.3.refs_1_), channel_id=1, source_target_pairs={{3,0},{0,1},{1,2},{2,3},{7,4},{4,5},{5,6},{6,7},{11,8},{8,9},{9,10... | collective-permute-start | bytes 2359304 | tf_op jit(solution)/shard_map/ppermute | solution.py:31
  29.4 2.6 %collective-permute-start.12 = (bf16[2,3,64,1024]{3,2,1,0:T(8,128)(2,1)}, bf16[2,3,64,1024]{3,2,1,0:T(8,128)(2,1)}, u32[]{:S(2)}, u32[]{:S(2)}) collective-permute-start(bf16[2,3,64,1024]{3,2,1,0:T(8,128)(2,1)} %pair.2.refs_0_), channel_id=1, source_target_pairs={{3,0},{0,1},{1,2},{2,3},{7,4},{4,5},{5,6},{6,7},{11,8},{8,9},{9,10... | collective-permute-start | bytes 2359304 | tf_op jit(solution)/shard_map/ppermute | solution.py:31
  32.0 2.7 %collective-permute-start.11 = (bf16[2,3,64,1024]{3,2,1,0:T(8,128)(2,1)}, bf16[2,3,64,1024]{3,2,1,0:T(8,128)(2,1)}, u32[]{:S(2)}, u32[]{:S(2)}) collective-permute-start(bf16[2,3,64,1024]{3,2,1,0:T(8,128)(2,1)} %pair.3.refs_1_), channel_id=1, source_target_pairs={{1,0},{2,1},{3,2},{0,3},{5,4},{6,5},{7,6},{4,7},{9,8},{10,9},{11,1... | collective-permute-start | bytes 2359304 | tf_op jit(solution)/shard_map/ppermute | solution.py:31
  34.7 3.1 %project.2.refs_3_ = bf16[4,64,512]{2,1,0:T(8,128)(2,1)S(1)} custom-call(bf16[2,3,64,1024]{3,2,1,0:T(8,128)(2,1)} %pair.2.refs_0_, bf16[2,3,64,1024]{3,2,1,0:T(8,128)(2,1)} %pair.3.refs_1_, bf16[3,1024,512]{2,1,0:T(8,128)(2,1)S(1)} %bitcast.27), custom_call_target="tpu_custom_call" | custom-call | bytes 1572864 | tf_op jit(solution)/shard_map/project/pallas_call | solution.py:114
  37.8 0.0 collective-permute-done.1.refs_0_
  37.8 1.8 collective-permute-done.4.refs_3_
  39.6 2.2 collective-permute-start.5
  41.8 3.1 %collective-permute-start.6 = (bf16[2,3,64,1024]{3,2,1,0:T(8,128)(2,1)}, bf16[2,3,64,1024]{3,2,1,0:T(8,128)(2,1)S(1)}, u32[]{:S(2)}, u32[]{:S(2)}) collective-permute-start(bf16[2,3,64,1024]{3,2,1,0:T(8,128)(2,1)} %collective-permute-done.4.refs_3_), channel_id=1, source_target_pairs={{3,0},{0,1},{1,2},{2,3},{7,4},{4,5},{5,6},{6,7},{11,8},{8,9},{9,10... | collective-permute-start | bytes 2359304 | tf_op jit(solution)/shard_map/ppermute | solution.py:31
  44.9 0.9 slice_bitcast_fusion
  45.8 1.3 collective-permute-start.10
  47.1 0.9 collective-permute-done.12.refs_2_
  48.0 0.7 collective-permute-start.9
  48.7 16.1 %collective-permute-start.8 = (bf16[64,512]{1,0:T(8,128)(2,1)S(1)}, bf16[64,512]{1,0:T(8,128)(2,1)S(1)}, u32[]{:S(2)}, u32[]{:S(2)}) collective-permute-start(bf16[64,512]{1,0:T(8,128)(2,1)S(1)} %get-tuple-element.67), channel_id=1, source_target_pairs={{0,1},{1,0},{2,65},{3,64},{4,129},{5,128},{6,193},{7,192},{8,257},... | collective-permute-start | bytes 196616 | tf_op jit(solution)/shard_map/ppermute | solution.py:401
  64.8 5.4 %collective-permute-start.7 = (bf16[64,512]{1,0:T(8,128)(2,1)S(1)}, bf16[64,512]{1,0:T(8,128)(2,1)S(1)}, u32[]{:S(2)}, u32[]{:S(2)}) collective-permute-start(bf16[64,512]{1,0:T(8,128)(2,1)S(1)} %get-tuple-element.68), channel_id=1, source_target_pairs={{0,0},{1,1},{2,64},{3,65},{4,128},{5,129},{6,192},{7,193},{8,256},... | collective-permute-start | bytes 196616 | tf_op jit(solution)/shard_map/ppermute | solution.py:400
  70.2 0.1 pad_add_fusion.meta_ref
  70.3 4.0 %project.3.refs_4_ = bf16[8,64,512]{2,1,0:T(8,128)(2,1)S(1)} custom-call(bf16[2,3,64,1024]{3,2,1,0:T(8,128)(2,1)} %collective-permute-done.1.refs_0_, bf16[2,3,64,1024]{3,2,1,0:T(8,128)(2,1)} %collective-permute-done.11.refs_1_, bf16[2,3,64,1024]{3,2,1,0:T(8,128)(2,1)} %collective-permute-done.12.refs_2_, ...), custom_call_target="tpu_custom_call" | custom-call | bytes 3145728 | tf_op jit(solution)/shard_map/project/pallas_call | solution.py:114
  74.3 12.0 %collective-permute-done.8 = bf16[64,512]{1,0:T(8,128)(2,1)S(1)} collective-permute-done((bf16[64,512]{1,0:T(8,128)(2,1)S(1)}, bf16[64,512]{1,0:T(8,128)(2,1)S(1)}, u32[]{:S(2)}, u32[]{:S(2)}) %collective-permute-start.8) | collective-permute-done | bytes 65568 | tf_op jit(solution)/shard_map/ppermute | solution.py:401
  86.3 9.0 %collective-permute-done.7 = bf16[64,512]{1,0:T(8,128)(2,1)S(1)} collective-permute-done((bf16[64,512]{1,0:T(8,128)(2,1)S(1)}, bf16[64,512]{1,0:T(8,128)(2,1)S(1)}, u32[]{:S(2)}, u32[]{:S(2)}) %collective-permute-start.7) | collective-permute-done | bytes 65568 | tf_op jit(solution)/shard_map/ppermute | solution.py:400
  95.3 3.3 %project_place.1 = (bf16[4,144,512]{2,1,0:T(8,128)(2,1)S(1)}, bf16[4,144,512]{2,1,0:T(8,128)(2,1)}) custom-call(s32[3]{0:T(128)S(1)} %pad_add_fusion.meta_ref, bf16[2,3,64,1024]{3,2,1,0:T(8,128)(2,1)S(1)} %collective-permute-done.5.refs_0_, bf16[2,3,64,1024]{3,2,1,0:T(8,128)(2,1)S(1)} %collective-permute-done.6.refs_1_, bf16[3,1024,512]{2,1,0:T(8,128)(2,1)S(1)} %bitcast.29, ...), custom_call_target="tpu_custom_call" | custom-call | bytes 1572864 | tf_op jit(solution)/shard_map/project_place/pallas_call | solution.py:167
  98.6 0.8 copy-done.3
  99.4 2.3 collective-permute-start.13
  101.7 1.9 collective-permute-done.13.got_ref
  103.6 1.1 copy-done.4
  104.7 0.1 join.1
  104.8 6.0 %collective-permute-start.14 = (bf16[144,512]{1,0:T(8,128)(2,1)S(1)}, bf16[144,512]{1,0:T(8,128)(2,1)S(1)}, u32[]{:S(2)}, u32[]{:S(2)}) collective-permute-start(bf16[144,512]{1,0:T(8,128)(2,1)S(1)} %get-tuple-element.40), channel_id=1, source_target_pairs={{128,0},{192,64},{256,128},{320,192},{384,256},{448,320},{0,384},{... | collective-permute-start | bytes 442376 | tf_op jit(solution)/shard_map/ppermute | solution.py:40
  110.8 1.9 collective-permute-start.15
  112.8 2.2 collective-permute-start.16
  115.0 0.0 all-gather.6.cloned.1.call-done
  115.0 9.6 %collective-permute-done.15.refs_2_ = bf16[144,512]{1,0:T(8,128)(2,1)S(1)} collective-permute-done((bf16[144,512]{1,0:T(8,128)(2,1)S(1)}, bf16[144,512]{1,0:T(8,128)(2,1)S(1)}, u32[]{:S(2)}, u32[]{:S(2)}) %collective-permute-start.15) | collective-permute-done | bytes 147488 | tf_op jit(solution)/shard_map/ppermute | solution.py:40
  124.6 1.4 copy-done.2
  126.0 1.6 turn.1
  127.6 0.0 all-gather.8.cloned.1.call-update
  127.6 0.6 dynamic_slice.3
  128.3 0.7 maximum_reduce_fusion
  131.0 0.7 pad_add_fusion.1.meta_ref
  131.7 1.4 chain.1
  133.1 36.3 %all-gather.2 = bf16[576,512]{1,0:T(8,128)(2,1)S(1)} all-gather(bf16[144,512]{1,0:T(8,128)(2,1)S(1)} %chain.1), channel_id=4, replica_groups=mesh['tp'=8,'dp'=4,'draft'=16] {'dp'}, dimensions={0}, use_global_device_ids=true | all-gather | bytes 737280 | tf_op jit(solution)/shard_map/all_gather | solution.py:414
  169.4 3.2 %collective-permute-start.19 = (bf16[4,144,512]{2,1,0:T(8,128)(2,1)S(1)}, bf16[4,144,512]{2,1,0:T(8,128)(2,1)S(1)}, u32[]{:S(2)}, u32[]{:S(2)}) collective-permute-start(bf16[4,144,512]{2,1,0:T(8,128)(2,1)S(1)} %bitcast.38), channel_id=1, source_target_pairs={{64,0},{0,64},{192,128},{128,192},{320,256},{256,320},{448,384},{3... | collective-permute-start | bytes 1769480 | tf_op jit(solution)/shard_map/ppermute | solution.py:35
  172.6 4.7 %collective-permute-start.18 = (bf16[4,144,512]{2,1,0:T(8,128)(2,1)S(1)}, bf16[4,144,512]{2,1,0:T(8,128)(2,1)S(1)}, u32[]{:S(2)}, u32[]{:S(2)}) collective-permute-start(bf16[4,144,512]{2,1,0:T(8,128)(2,1)S(1)} %bitcast.39), channel_id=1, source_target_pairs={{432,0},{384,16},{400,32},{416,48},{496,64},{448,80},{464,96},{480... | collective-permute-start | bytes 1769480 | tf_op jit(solution)/shard_map/ppermute | solution.py:53
  177.3 1.9 collective-permute-start.17
  179.2 6.6 %collective-permute-start.21 = (bf16[2,144,512]{2,1,0:T(8,128)(2,1)S(1)}, bf16[2,144,512]{2,1,0:T(8,128)(2,1)S(1)}, u32[]{:S(2)}, u32[]{:S(2)}) collective-permute-start(bf16[2,144,512]{2,1,0:T(8,128)(2,1)S(1)} %bitcast.43), channel_id=1, source_target_pairs={{304,0},{256,16},{272,32},{288,48},{368,64},{320,80},{336,96},{352... | collective-permute-start | bytes 884744 | tf_op jit(solution)/shard_map/ppermute | solution.py:53
  185.9 1.9 collective-permute-start.20
  187.8 12.7 %collective-permute-done.21 = bf16[2,144,512]{2,1,0:T(8,128)(2,1)S(1)} collective-permute-done((bf16[2,144,512]{2,1,0:T(8,128)(2,1)S(1)}, bf16[2,144,512]{2,1,0:T(8,128)(2,1)S(1)}, u32[]{:S(2)}, u32[]{:S(2)}) %collective-permute-start.21) | collective-permute-done | bytes 294944 | tf_op jit(solution)/shard_map/ppermute | solution.py:53
  200.5 9.0 %collective-permute-done.20 = bf16[2,144,512]{2,1,0:T(8,128)(2,1)S(1)} collective-permute-done((bf16[2,144,512]{2,1,0:T(8,128)(2,1)S(1)}, bf16[2,144,512]{2,1,0:T(8,128)(2,1)S(1)}, u32[]{:S(2)}, u32[]{:S(2)}) %collective-permute-start.20) | collective-permute-done | bytes 294944 | tf_op jit(solution)/shard_map/ppermute | solution.py:53
  209.5 0.1 pad_maximum_fusion.refs_4_
  209.6 3.2 %collective-permute-start.22 = (bf16[4,144,512]{2,1,0:T(8,128)(2,1)S(1)}, bf16[4,144,512]{2,1,0:T(8,128)(2,1)S(1)}, u32[]{:S(2)}, u32[]{:S(2)}) collective-permute-start(bf16[4,144,512]{2,1,0:T(8,128)(2,1)S(1)} %collective-permute-done.17.refs_2_), channel_id=1, source_target_pairs={{64,0},{0,64},{192,128},{128,192},{320,256},{256,320},{448,384},{3... | collective-permute-start | bytes 1769480 | tf_op jit(solution)/shard_map/ppermute | solution.py:35
  212.8 1.9 collective-permute-start.23
  214.8 2.4 %collective-permute-start.24 = (bf16[4,144,512]{2,1,0:T(8,128)(2,1)S(1)}, bf16[4,144,512]{2,1,0:T(8,128)(2,1)}, u32[]{:S(2)}, u32[]{:S(2)}) collective-permute-start(bf16[4,144,512]{2,1,0:T(8,128)(2,1)S(1)} %pad_maximum_fusion.refs_4_), channel_id=1, source_target_pairs={{64,0},{0,64},{192,128},{128,192},{320,256},{256,320},{448,384},{3... | collective-permute-start | bytes 1769480 | tf_op jit(solution)/shard_map/ppermute | solution.py:35
  217.3 0.7 stack.53.meta_ref
  218.0 1.0 collective-permute-done.24.refs_7_
  219.0 8.9 %weight_grad.1 = (bf16[3,256,512]{2,1,0:T(8,128)(2,1)}, f32[1,512]{1,0:T(1,128)}) custom-call(s32[8]{0:T(128)} %stack.53.meta_ref, bf16[16,3,256,256]{3,2,1,0:T(8,128)(2,1)} %bitcast.44, bf16[4,144,512]{2,1,0:T(8,128)(2,1)} %bitcast.41, bf16[4,144,512]{2,1,0:T(8,128)(2,1)} %copy-done.9, bf16[4,144,512]{2,1,0:T(8,128)(2,1)} %copy-done.11, ...), custom_call_target="tpu_custom_call" | custom-call | flops 3221225472 | bytes 10485760 | tf_op jit(solution)/shard_map/weight_grad/pallas_call | solution.py:327
  (41 shorter events, 0.2 us)
Async XLA Ops:
  7.2 27.6 %copy-start = (bf16[1024,3,512]{2,0,1:T(8,128)(2,1)S(1)}, bf16[1024,3,512]{2,0,1:T(8,128)(2,1)}, u32[]{:S(2)}) copy-start(bf16[1024,3,512]{2,0,1:T(8,128)(2,1)} %param.5) | copy-start | bytes 9437188
  7.2 107.8 %all-gather.6.cloned.1.call-start = ((), (), s32[]{:S(2)}) async-start(), calls=%async_computation | async-start | bytes 1966080 | tf_op jit(solution)/shard_map/all_gather | solution.py:441
  7.2 10.3 %collective-permute-start = (bf16[3,64,1024]{2,1,0:T(8,128)(2,1)}, bf16[3,64,1024]{2,1,0:T(8,128)(2,1)}, u32[]{:S(2)}, u32[]{:S(2)}) collective-permute-start(bf16[3,64,1024]{2,1,0:T(8,128)(2,1)} %bitcast.30), channel_id=1, source_target_pairs={{4,0},{5,1},{6,2},{7,3},{8,4},{9,5},{10,6},{11,7},{12,8},{13,9},{1... | collective-permute-start | bytes 1179656 | tf_op jit(solution)/shard_map/ppermute | solution.py:31
  9.9 13.4 %collective-permute-start.3 = (bf16[3,64,1024]{2,1,0:T(8,128)(2,1)}, bf16[3,64,1024]{2,1,0:T(8,128)(2,1)S(1)}, u32[]{:S(2)}, u32[]{:S(2)}) collective-permute-start(bf16[3,64,1024]{2,1,0:T(8,128)(2,1)} %bitcast.31), channel_id=1, source_target_pairs={{12,0},{13,1},{14,2},{15,3},{0,4},{1,5},{2,6},{3,7},{4,8},{5,9},{6... | collective-permute-start | bytes 1179656 | tf_op jit(solution)/shard_map/ppermute | solution.py:31
  14.0 10.3 %collective-permute-start.2 = (bf16[3,64,1024]{2,1,0:T(8,128)(2,1)}, bf16[3,64,1024]{2,1,0:T(8,128)(2,1)}, u32[]{:S(2)}, u32[]{:S(2)}) collective-permute-start(bf16[3,64,1024]{2,1,0:T(8,128)(2,1)} %bitcast.32), channel_id=1, source_target_pairs={{8,0},{9,1},{10,2},{11,3},{12,4},{13,5},{14,6},{15,7},{0,8},{1,9},... | collective-permute-start | bytes 1179656 | tf_op jit(solution)/shard_map/ppermute | solution.py:31
  16.0 203.0 %all-gather.8.cloned.1.call-start = ((), (), s32[]{:S(2)}) async-start(), calls=%async_computation.1 | async-start | bytes 6684672 | tf_op jit(solution)/shard_map/all_gather | solution.py:458
  17.5 1.0 copy-start.1
  20.5 17.4 %collective-permute-start.1 = (bf16[2,3,64,1024]{3,2,1,0:T(8,128)(2,1)}, bf16[2,3,64,1024]{3,2,1,0:T(8,128)(2,1)}, u32[]{:S(2)}, u32[]{:S(2)}) collective-permute-start(bf16[2,3,64,1024]{3,2,1,0:T(8,128)(2,1)} %pair.2.refs_0_), channel_id=1, source_target_pairs={{1,0},{2,1},{3,2},{0,3},{5,4},{6,5},{7,6},{4,7},{9,8},{10,9},{11,1... | collective-permute-start | bytes 2359304 | tf_op jit(solution)/shard_map/ppermute | solution.py:31
  26.3 13.3 %collective-permute-start.4 = (bf16[2,3,64,1024]{3,2,1,0:T(8,128)(2,1)}, bf16[2,3,64,1024]{3,2,1,0:T(8,128)(2,1)}, u32[]{:S(2)}, u32[]{:S(2)}) collective-permute-start(bf16[2,3,64,1024]{3,2,1,0:T(8,128)(2,1)} %pair.3.refs_1_), channel_id=1, source_target_pairs={{3,0},{0,1},{1,2},{2,3},{7,4},{4,5},{5,6},{6,7},{11,8},{8,9},{9,10... | collective-permute-start | bytes 2359304 | tf_op jit(solution)/shard_map/ppermute | solution.py:31
  29.4 18.6 %collective-permute-start.12 = (bf16[2,3,64,1024]{3,2,1,0:T(8,128)(2,1)}, bf16[2,3,64,1024]{3,2,1,0:T(8,128)(2,1)}, u32[]{:S(2)}, u32[]{:S(2)}) collective-permute-start(bf16[2,3,64,1024]{3,2,1,0:T(8,128)(2,1)} %pair.2.refs_0_), channel_id=1, source_target_pairs={{3,0},{0,1},{1,2},{2,3},{7,4},{4,5},{5,6},{6,7},{11,8},{8,9},{9,10... | collective-permute-start | bytes 2359304 | tf_op jit(solution)/shard_map/ppermute | solution.py:31
  32.0 16.7 %collective-permute-start.11 = (bf16[2,3,64,1024]{3,2,1,0:T(8,128)(2,1)}, bf16[2,3,64,1024]{3,2,1,0:T(8,128)(2,1)}, u32[]{:S(2)}, u32[]{:S(2)}) collective-permute-start(bf16[2,3,64,1024]{3,2,1,0:T(8,128)(2,1)} %pair.3.refs_1_), channel_id=1, source_target_pairs={{1,0},{2,1},{3,2},{0,3},{5,4},{6,5},{7,6},{4,7},{9,8},{10,9},{11,1... | collective-permute-start | bytes 2359304 | tf_op jit(solution)/shard_map/ppermute | solution.py:31
  39.6 55.7 %collective-permute-start.5 = (bf16[2,3,64,1024]{3,2,1,0:T(8,128)(2,1)}, bf16[2,3,64,1024]{3,2,1,0:T(8,128)(2,1)S(1)}, u32[]{:S(2)}, u32[]{:S(2)}) collective-permute-start(bf16[2,3,64,1024]{3,2,1,0:T(8,128)(2,1)} %collective-permute-done.1.refs_0_), channel_id=1, source_target_pairs={{1,0},{2,1},{3,2},{0,3},{5,4},{6,5},{7,6},{4,7},{9,8},{10,9},{11,1... | collective-permute-start | bytes 2359304 | tf_op jit(solution)/shard_map/ppermute | solution.py:31
  41.8 53.5 %collective-permute-start.6 = (bf16[2,3,64,1024]{3,2,1,0:T(8,128)(2,1)}, bf16[2,3,64,1024]{3,2,1,0:T(8,128)(2,1)S(1)}, u32[]{:S(2)}, u32[]{:S(2)}) collective-permute-start(bf16[2,3,64,1024]{3,2,1,0:T(8,128)(2,1)} %collective-permute-done.4.refs_3_), channel_id=1, source_target_pairs={{3,0},{0,1},{1,2},{2,3},{7,4},{4,5},{5,6},{6,7},{11,8},{8,9},{9,10... | collective-permute-start | bytes 2359304 | tf_op jit(solution)/shard_map/ppermute | solution.py:31
  45.8 19.0 %collective-permute-start.10 = (bf16[16,512]{1,0:T(8,128)(2,1)S(1)}, bf16[16,512]{1,0:T(8,128)(2,1)S(1)}, u32[]{:S(2)}, u32[]{:S(2)}) collective-permute-start(bf16[16,512]{1,0:T(8,128)(2,1)S(1)} %get-tuple-element.65), channel_id=1, source_target_pairs={{2,1},{4,65},{6,129},{8,193},{10,257},{12,321},{14,385},{66,3},{68... | collective-permute-start | bytes 49160 | tf_op jit(solution)/shard_map/ppermute | solution.py:403
  48.0 26.3 %collective-permute-start.9 = (bf16[16,512]{1,0:T(8,128)(2,1)S(1)}, bf16[16,512]{1,0:T(8,128)(2,1)S(1)}, u32[]{:S(2)}, u32[]{:S(2)}) collective-permute-start(bf16[16,512]{1,0:T(8,128)(2,1)S(1)} %get-tuple-element.66), channel_id=1, source_target_pairs={{2,0},{4,64},{6,128},{8,192},{10,256},{12,320},{14,384},{66,2},{68... | collective-permute-start | bytes 49160 | tf_op jit(solution)/shard_map/ppermute | solution.py:402
  48.7 37.6 %collective-permute-start.8 = (bf16[64,512]{1,0:T(8,128)(2,1)S(1)}, bf16[64,512]{1,0:T(8,128)(2,1)S(1)}, u32[]{:S(2)}, u32[]{:S(2)}) collective-permute-start(bf16[64,512]{1,0:T(8,128)(2,1)S(1)} %get-tuple-element.67), channel_id=1, source_target_pairs={{0,1},{1,0},{2,65},{3,64},{4,129},{5,128},{6,193},{7,192},{8,257},... | collective-permute-start | bytes 196616 | tf_op jit(solution)/shard_map/ppermute | solution.py:401
  64.8 30.5 %collective-permute-start.7 = (bf16[64,512]{1,0:T(8,128)(2,1)S(1)}, bf16[64,512]{1,0:T(8,128)(2,1)S(1)}, u32[]{:S(2)}, u32[]{:S(2)}) collective-permute-start(bf16[64,512]{1,0:T(8,128)(2,1)S(1)} %get-tuple-element.68), channel_id=1, source_target_pairs={{0,0},{1,1},{2,64},{3,65},{4,128},{5,129},{6,192},{7,193},{8,256},... | collective-permute-start | bytes 196616 | tf_op jit(solution)/shard_map/ppermute | solution.py:400
  98.6 0.8 copy-start.3
  99.4 28.2 %copy-start.8 = (s32[4]{0:T(128)S(1)}, s32[4]{0:T(128)}, u32[]{:S(2)}) copy-start(s32[4]{0:T(128)} %param.7) | copy-start | bytes 52
  99.4 32.3 %copy-start.5 = (f32[512]{0:T(512)S(1)}, f32[512]{0:T(512)}, u32[]{:S(2)}) copy-start(f32[512]{0:T(512)} %param.6) | copy-start | bytes 6148
  99.4 4.2 %collective-permute-start.13 = (bf16[4,144,512]{2,1,0:T(8,128)(2,1)}, bf16[4,144,512]{2,1,0:T(8,128)(2,1)S(1)}, u32[]{:S(2)}, u32[]{:S(2)}) collective-permute-start(bf16[4,144,512]{2,1,0:T(8,128)(2,1)} %get-tuple-element.38), channel_id=1, source_target_pairs={{64,0},{0,64},{192,128},{128,192},{320,256},{256,320},{448,384},{3... | collective-permute-start | bytes 1769480 | tf_op jit(solution)/shard_map/ppermute | solution.py:35
  103.6 1.1 copy-start.4
  104.8 10.2 %collective-permute-start.14 = (bf16[144,512]{1,0:T(8,128)(2,1)S(1)}, bf16[144,512]{1,0:T(8,128)(2,1)S(1)}, u32[]{:S(2)}, u32[]{:S(2)}) collective-permute-start(bf16[144,512]{1,0:T(8,128)(2,1)S(1)} %get-tuple-element.40), channel_id=1, source_target_pairs={{128,0},{192,64},{256,128},{320,192},{384,256},{448,320},{0,384},{... | collective-permute-start | bytes 442376 | tf_op jit(solution)/shard_map/ppermute | solution.py:40
  110.8 13.8 %collective-permute-start.15 = (bf16[144,512]{1,0:T(8,128)(2,1)S(1)}, bf16[144,512]{1,0:T(8,128)(2,1)S(1)}, u32[]{:S(2)}, u32[]{:S(2)}) collective-permute-start(bf16[144,512]{1,0:T(8,128)(2,1)S(1)} %get-tuple-element.41), channel_id=1, source_target_pairs={{256,0},{320,64},{384,128},{448,192},{0,256},{64,320},{128,384},{1... | collective-permute-start | bytes 442376 | tf_op jit(solution)/shard_map/ppermute | solution.py:40
  112.8 11.8 %collective-permute-start.16 = (bf16[144,512]{1,0:T(8,128)(2,1)S(1)}, bf16[144,512]{1,0:T(8,128)(2,1)S(1)}, u32[]{:S(2)}, u32[]{:S(2)}) collective-permute-start(bf16[144,512]{1,0:T(8,128)(2,1)S(1)} %get-tuple-element.42), channel_id=1, source_target_pairs={{384,0},{448,64},{0,128},{64,192},{128,256},{192,320},{256,384},{3... | collective-permute-start | bytes 442376 | tf_op jit(solution)/shard_map/ppermute | solution.py:40
  124.6 1.4 copy-start.2
  169.4 49.5 %copy-start.6 = (bf16[576,512]{1,0:T(8,128)(2,1)}, bf16[576,512]{1,0:T(8,128)(2,1)S(1)}, u32[]{:S(2)}) copy-start(bf16[576,512]{1,0:T(8,128)(2,1)S(1)} %all-gather.2) | copy-start | bytes 1769476
  169.4 40.2 %collective-permute-start.19 = (bf16[4,144,512]{2,1,0:T(8,128)(2,1)S(1)}, bf16[4,144,512]{2,1,0:T(8,128)(2,1)S(1)}, u32[]{:S(2)}, u32[]{:S(2)}) collective-permute-start(bf16[4,144,512]{2,1,0:T(8,128)(2,1)S(1)} %bitcast.38), channel_id=1, source_target_pairs={{64,0},{0,64},{192,128},{128,192},{320,256},{256,320},{448,384},{3... | collective-permute-start | bytes 1769480 | tf_op jit(solution)/shard_map/ppermute | solution.py:35
  172.6 37.0 %collective-permute-start.18 = (bf16[4,144,512]{2,1,0:T(8,128)(2,1)S(1)}, bf16[4,144,512]{2,1,0:T(8,128)(2,1)S(1)}, u32[]{:S(2)}, u32[]{:S(2)}) collective-permute-start(bf16[4,144,512]{2,1,0:T(8,128)(2,1)S(1)} %bitcast.39), channel_id=1, source_target_pairs={{432,0},{384,16},{400,32},{416,48},{496,64},{448,80},{464,96},{480... | collective-permute-start | bytes 1769480 | tf_op jit(solution)/shard_map/ppermute | solution.py:53
  177.3 32.4 %collective-permute-start.17 = (bf16[4,144,512]{2,1,0:T(8,128)(2,1)S(1)}, bf16[4,144,512]{2,1,0:T(8,128)(2,1)S(1)}, u32[]{:S(2)}, u32[]{:S(2)}) collective-permute-start(bf16[4,144,512]{2,1,0:T(8,128)(2,1)S(1)} %bitcast.40), channel_id=1, source_target_pairs={{128,0},{144,16},{160,32},{176,48},{192,64},{208,80},{224,96},{240... | collective-permute-start | bytes 1769480 | tf_op jit(solution)/shard_map/ppermute | solution.py:53
  179.2 21.3 %collective-permute-start.21 = (bf16[2,144,512]{2,1,0:T(8,128)(2,1)S(1)}, bf16[2,144,512]{2,1,0:T(8,128)(2,1)S(1)}, u32[]{:S(2)}, u32[]{:S(2)}) collective-permute-start(bf16[2,144,512]{2,1,0:T(8,128)(2,1)S(1)} %bitcast.43), channel_id=1, source_target_pairs={{304,0},{256,16},{272,32},{288,48},{368,64},{320,80},{336,96},{352... | collective-permute-start | bytes 884744 | tf_op jit(solution)/shard_map/ppermute | solution.py:53
  185.9 23.6 %collective-permute-start.20 = (bf16[2,144,512]{2,1,0:T(8,128)(2,1)S(1)}, bf16[2,144,512]{2,1,0:T(8,128)(2,1)S(1)}, u32[]{:S(2)}, u32[]{:S(2)}) collective-permute-start(bf16[2,144,512]{2,1,0:T(8,128)(2,1)S(1)} %bitcast.42), channel_id=1, source_target_pairs={{256,0},{272,16},{288,32},{304,48},{320,64},{336,80},{352,96},{368... | collective-permute-start | bytes 884744 | tf_op jit(solution)/shard_map/ppermute | solution.py:53
  209.6 9.4 %copy-start.7 = (bf16[4,144,512]{2,1,0:T(8,128)(2,1)}, bf16[4,144,512]{2,1,0:T(8,128)(2,1)S(1)}, u32[]{:S(2)}) copy-start(bf16[4,144,512]{2,1,0:T(8,128)(2,1)S(1)} %pad_maximum_fusion.refs_4_) | copy-start | bytes 1769476
  209.6 9.3 %copy-start.9 = (bf16[4,144,512]{2,1,0:T(8,128)(2,1)}, bf16[4,144,512]{2,1,0:T(8,128)(2,1)S(1)}, u32[]{:S(2)}) copy-start(bf16[4,144,512]{2,1,0:T(8,128)(2,1)S(1)} %collective-permute-done.19.refs_1_) | copy-start | bytes 1769476
  209.6 9.3 %copy-start.10 = (bf16[4,144,512]{2,1,0:T(8,128)(2,1)}, bf16[4,144,512]{2,1,0:T(8,128)(2,1)S(1)}, u32[]{:S(2)}) copy-start(bf16[4,144,512]{2,1,0:T(8,128)(2,1)S(1)} %collective-permute-done.18.refs_3_) | copy-start | bytes 1769476
  209.6 9.3 %copy-start.11 = (bf16[4,144,512]{2,1,0:T(8,128)(2,1)}, bf16[4,144,512]{2,1,0:T(8,128)(2,1)S(1)}, u32[]{:S(2)}) copy-start(bf16[4,144,512]{2,1,0:T(8,128)(2,1)S(1)} %collective-permute-done.17.refs_2_) | copy-start | bytes 1769476
  209.6 8.3 %collective-permute-start.22 = (bf16[4,144,512]{2,1,0:T(8,128)(2,1)S(1)}, bf16[4,144,512]{2,1,0:T(8,128)(2,1)S(1)}, u32[]{:S(2)}, u32[]{:S(2)}) collective-permute-start(bf16[4,144,512]{2,1,0:T(8,128)(2,1)S(1)} %collective-permute-done.17.refs_2_), channel_id=1, source_target_pairs={{64,0},{0,64},{192,128},{128,192},{320,256},{256,320},{448,384},{3... | collective-permute-start | bytes 1769480 | tf_op jit(solution)/shard_map/ppermute | solution.py:35
  212.8 5.1 %collective-permute-start.23 = (bf16[4,144,512]{2,1,0:T(8,128)(2,1)S(1)}, bf16[4,144,512]{2,1,0:T(8,128)(2,1)}, u32[]{:S(2)}, u32[]{:S(2)}) collective-permute-start(bf16[4,144,512]{2,1,0:T(8,128)(2,1)S(1)} %collective-permute-done.18.refs_3_), channel_id=1, source_target_pairs={{64,0},{0,64},{192,128},{128,192},{320,256},{256,320},{448,384},{3... | collective-permute-start | bytes 1769480 | tf_op jit(solution)/shard_map/ppermute | solution.py:35
  214.8 4.2 %collective-permute-start.24 = (bf16[4,144,512]{2,1,0:T(8,128)(2,1)S(1)}, bf16[4,144,512]{2,1,0:T(8,128)(2,1)}, u32[]{:S(2)}, u32[]{:S(2)}) collective-permute-start(bf16[4,144,512]{2,1,0:T(8,128)(2,1)S(1)} %pad_maximum_fusion.refs_4_), channel_id=1, source_target_pairs={{64,0},{0,64},{192,128},{128,192},{320,256},{256,320},{448,384},{3... | collective-permute-start | bytes 1769480 | tf_op jit(solution)/shard_map/ppermute | solution.py:35
  218.0 1.0 copy-start.12
Sparse Core Ops, SparseCore 0:
  16.1 80.6 all-gather.5
  127.8 79.9 all-gather.7

commit v9 on v7

--- a/solution.py
+++ b/solution.py
@@ -105,12 +105,10 @@
 
 def product_cost(blocks, weight):
     size = sum(b.size for b in blocks)
-    return pl.CostEstimate(
-        flops=2 * size * weight.shape[2], bytes_accessed=2 * (weight.size + size), transcendentals=0
-    )
-
-
-def project(blocks, weight):
+    return pl.CostEstimate(flops=0, bytes_accessed=2 * size, transcendentals=0)
+
+
+def project(blocks, weight, mebibytes):
     rows, width = blocks[0].shape[2], weight.shape[2]
     count = sum(b.shape[0] for b in blocks)
     return pl.pallas_call(
@@ -120,7 +118,7 @@
         in_specs=product_specs(blocks, weight),
         out_specs=pl.BlockSpec((count, rows, width), lambda l: (0, 0, 0)),
         scratch_shapes=[pltpu.VMEM((count * rows, width), jnp.float32)],
-        compiler_params=params(14),
+        compiler_params=params(mebibytes),
         cost_estimate=product_cost(blocks, weight),
         name="project",
     )(*blocks, weight)
@@ -219,13 +217,17 @@
 
 
 def chain_kernel(meta_ref, scale_ref, *refs):
-    *part_refs, high_ref, gain_ref, grad_ref = refs
+    *part_refs, one_ref, two_ref, left_ref, right_ref, gain_ref, grad_ref = refs
     rows, width = part_refs[0].shape
     own = rows - 2 * HALO
     joined = part_refs[0][...].astype(jnp.float32)
     for part_ref in part_refs[1:]:
         joined = joined + part_ref[...].astype(jnp.float32)
-    high = high_ref[...].astype(jnp.float32)
+    even = meta_ref[2] == 0
+    pick = lambda a, b: jnp.where(even, a[...].astype(jnp.float32), b[...].astype(jnp.float32))
+    high = jnp.concatenate(
+        [pick(one_ref, two_ref), pick(two_ref, one_ref), pick(left_ref, right_ref)], axis=0
+    )
     gain = gain_ref[...]
     scale = scale_ref[0]
     start, length = meta_ref[0], meta_ref[1]
@@ -269,20 +271,20 @@
     grad_ref[pl.ds(own, TAIL), :] = jnp.concatenate(tail, axis=0).astype(jnp.bfloat16)
 
 
-def chain(parts, high, gain, start, length, scale):
+def chain(parts, halves, gain, start, length, odd, scale):
     rows, width = parts[0].shape
     own = rows - 2 * HALO
     return pl.pallas_call(
         chain_kernel,
         out_shape=jax.ShapeDtypeStruct((own + TAIL, width), jnp.bfloat16),
-        in_specs=[SMEM, SMEM] + [VMEM] * (len(parts) + 2),
+        in_specs=[SMEM, SMEM] + [VMEM] * (len(parts) + len(halves) + 1),
         out_specs=VMEM,
         compiler_params=params(14),
         cost_estimate=pl.CostEstimate(
             flops=60 * rows * width, bytes_accessed=10 * rows * width, transcendentals=3 * rows * width
         ),
         name="chain",
-    )(jnp.stack([start, length]), scale.reshape(1), *parts, high, gain.reshape(1, width))
+    )(jnp.stack([start, length, odd]), scale.reshape(1), *parts, *halves, gain.reshape(1, width))
 
 
 def weight_grad_kernel(meta_ref, features_ref, *refs):
@@ -297,11 +299,14 @@
         pltpu.make_async_copy(features_ref.at[:, at], held_ref.at[at], held_sem.at[at])
         for at in range(LEVELS)
     ]
-    for copy in got + held:
+    for copy in got:
         copy.start()
     mix = jnp.zeros((TAIL, width), jnp.float32)
     for at, copy in enumerate(got):
         copy.wait()
+        if at == len(got) // 2:
+            for later in held:
+                later.start()
         for part in range(2):
             slab = grads_ref.at[meta_ref[at] * 2 + part]
             for sequence in range(ZH):
@@ -398,12 +403,6 @@
     )
 
 
-def high_rows(one, two, after_left, after_right, draft_index):
-    even = draft_index % 2 == 0
-    after = jnp.where(even, after_left, after_right)
-    return jnp.concatenate([jnp.where(even, one, two), jnp.where(even, two, one), after], axis=0)
-
-
 def trade_columns(own):
     levels, rows, depth = own.shape
     quarters = own.reshape(levels, rows, ZH, depth // ZH).transpose(2, 0, 1, 3)
@@ -438,29 +437,27 @@
     own = features.transpose(1, 0, 2)
     weight = fc_weight.transpose(1, 0, 2)
 
-    traded = trade_columns(own)
     next_, last, across = (plane_move(step, True)(own) for step in (1, 3, 2))
     low, high = pair(own, next_), pair(across, last)
     up_low, down_high = plane_move(1, False)(low), plane_move(-1, False)(high)
     up_high, down_low = plane_move(1, False)(high), plane_move(-1, False)(low)
-    zero = project([low, high], weight)
-    up_low, down_high, zero, traded, later = lax.optimization_barrier(
-        (up_low, down_high, zero, traded, own)
-    )
+    zero = project([low, high], weight, 14)
+    up_low, down_high, zero = lax.optimization_barrier((up_low, down_high, zero))
     far_low, far_high = plane_move(1, False)(up_low), plane_move(-1, False)(down_high)
-    halves = send_high(later[LEVELS - 1], draft_index)
-    sides = project([up_low, up_high, down_low, down_high], weight)
-    far_low, far_high, halves, sides, turned = lax.optimization_barrier(
-        (far_low, far_high, halves, sides, turn(traded))
-    )
+    up_high, down_low, later = lax.optimization_barrier((up_high, down_low, own))
+    traded = trade_columns(later)
+    sides = project([up_low, up_high, down_low, down_high], weight, 58)
+    far_low, far_high, sides = lax.optimization_barrier((far_low, far_high, sides))
     keep, send = project_place([far_low, far_high], weight, zero, sides, core, x, y)
-    keep, send, turned = lax.optimization_barrier((keep, send, turned))
-    every = lax.all_gather(turned, "draft", axis=0, tiled=False)
-    mine, *away = join(keep, from_other_core(send), zl)
+    got, traded = lax.optimization_barrier((from_other_core(send), traded))
+    every = lax.all_gather(turn(traded), "draft", axis=0, tiled=False)
+    mine, *away = join(keep, got, zl)
+    top, mine = lax.optimization_barrier((own[LEVELS - 1], mine))
+    halves = send_high(top, draft_index)
     parts = [mine] + [from_zl(block, step) for step, block in zip((1, 2, 3), away)]
     scale = LOSS_SCALE / valid_total(lengths)
-    target = high_rows(*halves, draft_index)
-    grad = chain(parts, target, mix_gain, tp_index * piece, lengths[zh], scale)
+    odd = draft_index % 2
+    grad = chain(parts, halves, mix_gain, tp_index * piece, lengths[zh], odd, scale)
     fc_grad, mix_total = gather_grads(grad, every, zl, core)
     return (fc_grad.transpose(1, 0, 2), mix_total[0])
 

time: 227 us -> 220 us (0.969)
  the two profiles are of different devices: /device:TPU:75 before, /device:TPU:1 now
where the time goes in v9:
time: 220 us; the launch traced here: 217 us
  starting transfers between devices  103 us (47%)
  waiting for transfers between devices  31.7 us (14%)
  blocking collectives  28.5 us (13%)
  Pallas kernels  25.1 us (11%)
  between operations  16.7 us (8%)
  local copies, waits for them, and re-layouts  10.4 us (5%)
    ppermute x9, starting transfers between devices, plane_move(): return lambda block: lax.ppermute(block, ('tp', 'draft'), pairs)  30.2 us
    all_gather x1, blocking collectives, gather_grads(): stack = lax.all_gather(grad, 'dp', axis=0, tiled=False)  28.5 us
    ppermute x4, waiting for transfers between devices, from_z(): return lax.ppermute(block, ('tp', 'dp'), pairs)  19.1 us
    ppermute x4, starting transfers between devices, from_z(): return lax.ppermute(block, ('tp', 'dp'), pairs)  17.6 us
    all_to_all x1, starting transfers between devices, trade_columns(): lax.all_to_all(quarters, 'dp', split_axis=0, concat_axis=0, tiled=True)  14.8 us
    ppermute x3, starting transfers between devices, from_zl(): return lax.ppermute(block, 'tp', pairs)  14 us
    ppermute x5, starting transfers between devices, from_other_core(): return lax.ppermute(block, 'tp', [(t ^ 1, t) for t in range(ZL * CORES)])  13.6 us
    pallas_call x1, Pallas kernels, weight_grad(): pl.pallas_call(weight_grad_kernel, out_shape=(jax.ShapeDtypeStruct((LEVEL...  8.88 us
  transfers between devices with their start and end apart: 27, of which 9 were waited for; matrix products, arithmetic and copies ran while one was open for 2% of the time, Pallas kernels for 6%

profile of v9, /device:TPU:1, one launch (start us, length us, event | category | flops | bytes accessed | tf_op | source)
XLA Modules:
  0.0 216.6 jit_solution(4522531427565416142)
XLA Ops:
  7.2 5.5 %collective-permute-start = (bf16[3,64,1024]{2,1,0:T(8,128)(2,1)}, bf16[3,64,1024]{2,1,0:T(8,128)(2,1)S(1)}, u32[]{:S(2)}, u32[]{:S(2)}) collective-permute-start(bf16[3,64,1024]{2,1,0:T(8,128)(2,1)} %bitcast.36), channel_id=1, source_target_pairs={{4,0},{5,1},{6,2},{7,3},{8,4},{9,5},{10,6},{11,7},{12,8},{13,9},{1... | collective-permute-start | bytes 1179656 | tf_op jit(solution)/shard_map/ppermute | solution.py:31
  12.6 1.9 collective-permute-start.3
  14.6 3.5 %collective-permute-start.2 = (bf16[3,64,1024]{2,1,0:T(8,128)(2,1)}, bf16[3,64,1024]{2,1,0:T(8,128)(2,1)S(1)}, u32[]{:S(2)}, u32[]{:S(2)}) collective-permute-start(bf16[3,64,1024]{2,1,0:T(8,128)(2,1)} %bitcast.38), channel_id=1, source_target_pairs={{8,0},{9,1},{10,2},{11,3},{12,4},{13,5},{14,6},{15,7},{0,8},{1,9},... | collective-permute-start | bytes 1179656 | tf_op jit(solution)/shard_map/ppermute | solution.py:31
  18.1 0.0 collective-permute-done.second_ref
  18.1 1.0 copy-done.2
  19.1 0.1 pair.2.refs_0_
  19.2 4.5 %collective-permute-start.1 = (bf16[2,3,64,1024]{3,2,1,0:T(8,128)(2,1)S(1)}, bf16[2,3,64,1024]{3,2,1,0:T(8,128)(2,1)}, u32[]{:S(2)}, u32[]{:S(2)}) collective-permute-start(bf16[2,3,64,1024]{3,2,1,0:T(8,128)(2,1)S(1)} %pair.2.refs_0_), channel_id=1, source_target_pairs={{1,0},{2,1},{3,2},{0,3},{5,4},{6,5},{7,6},{4,7},{9,8},{10,9},{11,1... | collective-permute-start | bytes 2359304 | tf_op jit(solution)/shard_map/ppermute | solution.py:31
  23.7 3.4 %collective-permute-done.3.second_ref = bf16[3,64,1024]{2,1,0:T(8,128)(2,1)S(1)} collective-permute-done((bf16[3,64,1024]{2,1,0:T(8,128)(2,1)}, bf16[3,64,1024]{2,1,0:T(8,128)(2,1)S(1)}, u32[]{:S(2)}, u32[]{:S(2)}) %collective-permute-start.3) | collective-permute-done | bytes 393248 | tf_op jit(solution)/shard_map/ppermute | solution.py:31
  27.1 0.0 collective-permute-done.2.first_ref
  27.1 0.1 pair.3.refs_1_
  27.2 3.0 %collective-permute-start.4 = (bf16[2,3,64,1024]{3,2,1,0:T(8,128)(2,1)S(1)}, bf16[2,3,64,1024]{3,2,1,0:T(8,128)(2,1)}, u32[]{:S(2)}, u32[]{:S(2)}) collective-permute-start(bf16[2,3,64,1024]{3,2,1,0:T(8,128)(2,1)S(1)} %pair.3.refs_1_), channel_id=1, source_target_pairs={{3,0},{0,1},{1,2},{2,3},{7,4},{4,5},{5,6},{6,7},{11,8},{8,9},{9,10... | collective-permute-start | bytes 2359304 | tf_op jit(solution)/shard_map/ppermute | solution.py:31
  30.1 3.1 %collective-permute-start.8 = (bf16[2,3,64,1024]{3,2,1,0:T(8,128)(2,1)S(1)}, bf16[2,3,64,1024]{3,2,1,0:T(8,128)(2,1)S(1)}, u32[]{:S(2)}, u32[]{:S(2)}) collective-permute-start(bf16[2,3,64,1024]{3,2,1,0:T(8,128)(2,1)S(1)} %pair.2.refs_0_), channel_id=1, source_target_pairs={{3,0},{0,1},{1,2},{2,3},{7,4},{4,5},{5,6},{6,7},{11,8},{8,9},{9,10... | collective-permute-start | bytes 2359304 | tf_op jit(solution)/shard_map/ppermute | solution.py:31
  33.3 3.4 %collective-permute-start.7 = (bf16[2,3,64,1024]{3,2,1,0:T(8,128)(2,1)S(1)}, bf16[2,3,64,1024]{3,2,1,0:T(8,128)(2,1)S(1)}, u32[]{:S(2)}, u32[]{:S(2)}) collective-permute-start(bf16[2,3,64,1024]{3,2,1,0:T(8,128)(2,1)S(1)} %pair.3.refs_1_), channel_id=1, source_target_pairs={{1,0},{2,1},{3,2},{0,3},{5,4},{6,5},{7,6},{4,7},{9,8},{10,9},{11,1... | collective-permute-start | bytes 2359304 | tf_op jit(solution)/shard_map/ppermute | solution.py:31
  36.6 0.0 copy-start
  36.6 1.9 copy-done
  38.5 1.6 project.2.refs_3_
  40.2 0.7 copy-done.5
  40.9 0.6 collective-permute-done.4.refs_3_
  41.5 2.9 %collective-permute-start.5 = (bf16[2,3,64,1024]{3,2,1,0:T(8,128)(2,1)}, bf16[2,3,64,1024]{3,2,1,0:T(8,128)(2,1)}, u32[]{:S(2)}, u32[]{:S(2)}) collective-permute-start(bf16[2,3,64,1024]{3,2,1,0:T(8,128)(2,1)} %collective-permute-done.1.refs_0_), channel_id=1, source_target_pairs={{1,0},{2,1},{3,2},{0,3},{5,4},{6,5},{7,6},{4,7},{9,8},{10,9},{11,1... | collective-permute-start | bytes 2359304 | tf_op jit(solution)/shard_map/ppermute | solution.py:31
  44.4 2.4 %collective-permute-start.6 = (bf16[2,3,64,1024]{3,2,1,0:T(8,128)(2,1)}, bf16[2,3,64,1024]{3,2,1,0:T(8,128)(2,1)}, u32[]{:S(2)}, u32[]{:S(2)}) collective-permute-start(bf16[2,3,64,1024]{3,2,1,0:T(8,128)(2,1)} %collective-permute-done.4.refs_3_), channel_id=1, source_target_pairs={{3,0},{0,1},{1,2},{2,3},{7,4},{4,5},{5,6},{6,7},{11,8},{8,9},{9,10... | collective-permute-start | bytes 2359304 | tf_op jit(solution)/shard_map/ppermute | solution.py:31
  46.8 3.0 %collective-permute-done.8.refs_2_ = bf16[2,3,64,1024]{3,2,1,0:T(8,128)(2,1)S(1)} collective-permute-done((bf16[2,3,64,1024]{3,2,1,0:T(8,128)(2,1)S(1)}, bf16[2,3,64,1024]{3,2,1,0:T(8,128)(2,1)S(1)}, u32[]{:S(2)}, u32[]{:S(2)}) %collective-permute-start.8) | collective-permute-done | bytes 786464 | tf_op jit(solution)/shard_map/ppermute | solution.py:31
  49.8 0.9 copy-done.11
  50.7 0.9 copy-done.12
  51.6 0.8 copy.10
  52.4 14.8 %all-to-all-start = ((bf16[4,3,64,256]{3,2,1,0:T(8,128)(2,1)}), bf16[4,3,64,256]{3,2,1,0:T(8,128)(2,1)}, u32[]{:S(2)}, u32[]{:S(2)}) async-start(bf16[4,3,64,256]{3,2,1,0:T(8,128)(2,1)} %bitcast.47), calls=%async_computation | async-start | bytes 786432 | tf_op jit(solution)/shard_map/all_to_all | solution.py:409
  67.2 0.1 pad_add_fusion.meta_ref
  67.3 5.6 %project.3.refs_4_ = bf16[8,64,512]{2,1,0:T(8,128)(2,1)} custom-call(bf16[2,3,64,1024]{3,2,1,0:T(8,128)(2,1)} %collective-permute-done.1.refs_0_, bf16[2,3,64,1024]{3,2,1,0:T(8,128)(2,1)} %copy-done.12, bf16[2,3,64,1024]{3,2,1,0:T(8,128)(2,1)} %copy-done.11, bf16[2,3,64,1024]{3,2,1,0:T(8,128)(2,1)} %collective-permute-done.4.refs_3_, ...), custom_call_target="tpu_custom_call" | custom-call | bytes 3145728 | tf_op jit(solution)/shard_map/project/pallas_call | solution.py:114
  72.9 1.0 copy-done.4
  73.9 4.7 %project_place.1 = (bf16[4,144,512]{2,1,0:T(8,128)(2,1)S(1)}, bf16[4,144,512]{2,1,0:T(8,128)(2,1)}) custom-call(s32[3]{0:T(128)S(1)} %pad_add_fusion.meta_ref, bf16[2,3,64,1024]{3,2,1,0:T(8,128)(2,1)} %collective-permute-done.5.refs_0_, bf16[2,3,64,1024]{3,2,1,0:T(8,128)(2,1)} %collective-permute-done.6.refs_1_, bf16[3,1024,512]{2,1,0:T(8,128)(2,1)S(1)} %bitcast.35, ...), custom_call_target="tpu_custom_call" | custom-call | bytes 1572864 | tf_op jit(solution)/shard_map/project_place/pallas_call | solution.py:167
  78.6 0.8 copy-done.7
  79.4 4.6 %collective-permute-start.9 = (bf16[4,144,512]{2,1,0:T(8,128)(2,1)}, bf16[4,144,512]{2,1,0:T(8,128)(2,1)S(1)}, u32[]{:S(2)}, u32[]{:S(2)}) collective-permute-start(bf16[4,144,512]{2,1,0:T(8,128)(2,1)} %get-tuple-element.35), channel_id=1, source_target_pairs={{64,0},{0,64},{192,128},{128,192},{320,256},{256,320},{448,384},{3... | collective-permute-start | bytes 1769480 | tf_op jit(solution)/shard_map/ppermute | solution.py:35
  84.0 0.8 all-to-all-done.traded_ref
  84.8 1.0 collective-permute-done.9.got_ref
  85.8 2.7 %turn.1 = bf16[3,256,256]{2,1,0:T(8,128)(2,1)} custom-call(bf16[4,3,64,256]{3,2,1,0:T(8,128)(2,1)} %all-to-all-done.traded_ref), custom_call_target="tpu_custom_call" | custom-call | bytes 786432 | tf_op jit(solution)/shard_map/turn/pallas_call | solution.py:363
  88.6 0.0 all-gather.4.cloned.1.call-update
  88.6 0.6 dynamic_slice.3
  89.2 0.7 maximum_reduce_fusion
  92.1 1.1 copy-done.8
  93.1 0.2 join.1
  93.3 0.7 collective-permute-start.16
  94.0 1.3 collective-permute-start.15
  95.3 5.0 %collective-permute-start.10 = (bf16[144,512]{1,0:T(8,128)(2,1)S(1)}, bf16[144,512]{1,0:T(8,128)(2,1)S(1)}, u32[]{:S(2)}, u32[]{:S(2)}) collective-permute-start(bf16[144,512]{1,0:T(8,128)(2,1)S(1)} %get-tuple-element.42), channel_id=1, source_target_pairs={{128,0},{192,64},{256,128},{320,192},{384,256},{448,320},{0,384},{... | collective-permute-start | bytes 442376 | tf_op jit(solution)/shard_map/ppermute | solution.py:40
  100.2 6.4 %collective-permute-start.11 = (bf16[144,512]{1,0:T(8,128)(2,1)S(1)}, bf16[144,512]{1,0:T(8,128)(2,1)S(1)}, u32[]{:S(2)}, u32[]{:S(2)}) collective-permute-start(bf16[144,512]{1,0:T(8,128)(2,1)S(1)} %get-tuple-element.43), channel_id=1, source_target_pairs={{256,0},{320,64},{384,128},{448,192},{0,256},{64,320},{128,384},{1... | collective-permute-start | bytes 442376 | tf_op jit(solution)/shard_map/ppermute | solution.py:40
  106.6 2.6 %collective-permute-start.12 = (bf16[144,512]{1,0:T(8,128)(2,1)S(1)}, bf16[144,512]{1,0:T(8,128)(2,1)S(1)}, u32[]{:S(2)}, u32[]{:S(2)}) collective-permute-start(bf16[144,512]{1,0:T(8,128)(2,1)S(1)} %get-tuple-element.44), channel_id=1, source_target_pairs={{384,0},{448,64},{0,128},{64,192},{128,256},{192,320},{256,384},{3... | collective-permute-start | bytes 442376 | tf_op jit(solution)/shard_map/ppermute | solution.py:40
  109.3 5.5 %collective-permute-start.14 = (bf16[64,512]{1,0:T(8,128)(2,1)S(1)}, bf16[64,512]{1,0:T(8,128)(2,1)S(1)}, u32[]{:S(2)}, u32[]{:S(2)}) collective-permute-start(bf16[64,512]{1,0:T(8,128)(2,1)S(1)} %get-tuple-element.59), channel_id=1, source_target_pairs={{0,1},{1,0},{2,65},{3,64},{4,129},{5,128},{6,193},{7,192},{8,257},... | collective-permute-start | bytes 196616 | tf_op jit(solution)/shard_map/ppermute | solution.py:400
  114.8 5.0 %collective-permute-start.13 = (bf16[64,512]{1,0:T(8,128)(2,1)S(1)}, bf16[64,512]{1,0:T(8,128)(2,1)S(1)}, u32[]{:S(2)}, u32[]{:S(2)}) collective-permute-start(bf16[64,512]{1,0:T(8,128)(2,1)S(1)} %get-tuple-element.60), channel_id=1, source_target_pairs={{0,0},{1,1},{2,64},{3,65},{4,128},{5,129},{6,192},{7,193},{8,256},... | collective-permute-start | bytes 196616 | tf_op jit(solution)/shard_map/ppermute | solution.py:399
  119.8 0.7 pad_add_fusion.1.meta_ref
  120.5 2.8 %collective-permute-done.13.refs_4_ = bf16[64,512]{1,0:T(8,128)(2,1)S(1)} collective-permute-done((bf16[64,512]{1,0:T(8,128)(2,1)S(1)}, bf16[64,512]{1,0:T(8,128)(2,1)S(1)}, u32[]{:S(2)}, u32[]{:S(2)}) %collective-permute-start.13) | collective-permute-done | bytes 65568 | tf_op jit(solution)/shard_map/ppermute | solution.py:399
  123.3 1.4 chain.1
  124.7 28.5 %all-gather.1 = bf16[576,512]{1,0:T(8,128)(2,1)S(1)} all-gather(bf16[144,512]{1,0:T(8,128)(2,1)S(1)} %chain.1), channel_id=3, replica_groups=mesh['tp'=8,'dp'=4,'draft'=16] {'dp'}, dimensions={0}, use_global_device_ids=true | all-gather | bytes 737280 | tf_op jit(solution)/shard_map/all_gather | solution.py:413
  153.2 1.9 collective-permute-start.19
  155.1 4.3 %collective-permute-start.18 = (bf16[4,144,512]{2,1,0:T(8,128)(2,1)S(1)}, bf16[4,144,512]{2,1,0:T(8,128)(2,1)S(1)}, u32[]{:S(2)}, u32[]{:S(2)}) collective-permute-start(bf16[4,144,512]{2,1,0:T(8,128)(2,1)S(1)} %bitcast.44), channel_id=1, source_target_pairs={{432,0},{384,16},{400,32},{416,48},{496,64},{448,80},{464,96},{480... | collective-permute-start | bytes 1769480 | tf_op jit(solution)/shard_map/ppermute | solution.py:53
  159.4 5.9 %collective-permute-start.17 = (bf16[4,144,512]{2,1,0:T(8,128)(2,1)S(1)}, bf16[4,144,512]{2,1,0:T(8,128)(2,1)S(1)}, u32[]{:S(2)}, u32[]{:S(2)}) collective-permute-start(bf16[4,144,512]{2,1,0:T(8,128)(2,1)S(1)} %bitcast.45), channel_id=1, source_target_pairs={{128,0},{144,16},{160,32},{176,48},{192,64},{208,80},{224,96},{240... | collective-permute-start | bytes 1769480 | tf_op jit(solution)/shard_map/ppermute | solution.py:53
  165.3 2.4 %collective-permute-start.21 = (bf16[2,144,512]{2,1,0:T(8,128)(2,1)S(1)}, bf16[2,144,512]{2,1,0:T(8,128)(2,1)S(1)}, u32[]{:S(2)}, u32[]{:S(2)}) collective-permute-start(bf16[2,144,512]{2,1,0:T(8,128)(2,1)S(1)} %bitcast.49), channel_id=1, source_target_pairs={{304,0},{256,16},{272,32},{288,48},{368,64},{320,80},{336,96},{352... | collective-permute-start | bytes 884744 | tf_op jit(solution)/shard_map/ppermute | solution.py:53
  167.7 5.0 %collective-permute-start.20 = (bf16[2,144,512]{2,1,0:T(8,128)(2,1)S(1)}, bf16[2,144,512]{2,1,0:T(8,128)(2,1)S(1)}, u32[]{:S(2)}, u32[]{:S(2)}) collective-permute-start(bf16[2,144,512]{2,1,0:T(8,128)(2,1)S(1)} %bitcast.48), channel_id=1, source_target_pairs={{256,0},{272,16},{288,32},{304,48},{320,64},{336,80},{352,96},{368... | collective-permute-start | bytes 884744 | tf_op jit(solution)/shard_map/ppermute | solution.py:53
  172.8 17.9 %collective-permute-done.21 = bf16[2,144,512]{2,1,0:T(8,128)(2,1)S(1)} collective-permute-done((bf16[2,144,512]{2,1,0:T(8,128)(2,1)S(1)}, bf16[2,144,512]{2,1,0:T(8,128)(2,1)S(1)}, u32[]{:S(2)}, u32[]{:S(2)}) %collective-permute-start.21) | collective-permute-done | bytes 294944 | tf_op jit(solution)/shard_map/ppermute | solution.py:53
  190.7 1.2 collective-permute-done.20
  191.8 0.1 pad_maximum_fusion.refs_4_
  192.0 2.7 %collective-permute-start.22 = (bf16[4,144,512]{2,1,0:T(8,128)(2,1)S(1)}, bf16[4,144,512]{2,1,0:T(8,128)(2,1)S(1)}, u32[]{:S(2)}, u32[]{:S(2)}) collective-permute-start(bf16[4,144,512]{2,1,0:T(8,128)(2,1)S(1)} %collective-permute-done.17.refs_2_), channel_id=1, source_target_pairs={{64,0},{0,64},{192,128},{128,192},{320,256},{256,320},{448,384},{3... | collective-permute-start | bytes 1769480 | tf_op jit(solution)/shard_map/ppermute | solution.py:35
  194.7 1.9 collective-permute-start.23
  196.7 2.4 %collective-permute-start.24 = (bf16[4,144,512]{2,1,0:T(8,128)(2,1)S(1)}, bf16[4,144,512]{2,1,0:T(8,128)(2,1)}, u32[]{:S(2)}, u32[]{:S(2)}) collective-permute-start(bf16[4,144,512]{2,1,0:T(8,128)(2,1)S(1)} %pad_maximum_fusion.refs_4_), channel_id=1, source_target_pairs={{64,0},{0,64},{192,128},{128,192},{320,256},{256,320},{448,384},{3... | collective-permute-start | bytes 1769480 | tf_op jit(solution)/shard_map/ppermute | solution.py:35
  199.1 0.7 stack.56.meta_ref
  199.8 1.0 collective-permute-done.24.refs_7_
  200.8 8.9 %weight_grad.1 = (bf16[3,256,512]{2,1,0:T(8,128)(2,1)}, f32[1,512]{1,0:T(1,128)}) custom-call(s32[8]{0:T(128)} %stack.56.meta_ref, bf16[16,3,256,256]{3,2,1,0:T(8,128)(2,1)} %bitcast.50, bf16[4,144,512]{2,1,0:T(8,128)(2,1)} %bitcast.46, bf16[4,144,512]{2,1,0:T(8,128)(2,1)} %copy-done.15, bf16[4,144,512]{2,1,0:T(8,128)(2,1)} %copy-done.17, ...), custom_call_target="tpu_custom_call" | custom-call | flops 3221225472 | bytes 10485760 | tf_op jit(solution)/shard_map/weight_grad/pallas_call | solution.py:331
  (50 shorter events, 0.2 us)
Async XLA Ops:
  7.2 11.0 %collective-permute-start = (bf16[3,64,1024]{2,1,0:T(8,128)(2,1)}, bf16[3,64,1024]{2,1,0:T(8,128)(2,1)S(1)}, u32[]{:S(2)}, u32[]{:S(2)}) collective-permute-start(bf16[3,64,1024]{2,1,0:T(8,128)(2,1)} %bitcast.36), channel_id=1, source_target_pairs={{4,0},{5,1},{6,2},{7,3},{8,4},{9,5},{10,6},{11,7},{12,8},{13,9},{1... | collective-permute-start | bytes 1179656 | tf_op jit(solution)/shard_map/ppermute | solution.py:31
  12.6 14.4 %collective-permute-start.3 = (bf16[3,64,1024]{2,1,0:T(8,128)(2,1)}, bf16[3,64,1024]{2,1,0:T(8,128)(2,1)S(1)}, u32[]{:S(2)}, u32[]{:S(2)}) collective-permute-start(bf16[3,64,1024]{2,1,0:T(8,128)(2,1)} %bitcast.37), channel_id=1, source_target_pairs={{12,0},{13,1},{14,2},{15,3},{0,4},{1,5},{2,6},{3,7},{4,8},{5,9},{6... | collective-permute-start | bytes 1179656 | tf_op jit(solution)/shard_map/ppermute | solution.py:31
  14.6 12.5 %collective-permute-start.2 = (bf16[3,64,1024]{2,1,0:T(8,128)(2,1)}, bf16[3,64,1024]{2,1,0:T(8,128)(2,1)S(1)}, u32[]{:S(2)}, u32[]{:S(2)}) collective-permute-start(bf16[3,64,1024]{2,1,0:T(8,128)(2,1)} %bitcast.38), channel_id=1, source_target_pairs={{8,0},{9,1},{10,2},{11,3},{12,4},{13,5},{14,6},{15,7},{0,8},{1,9},... | collective-permute-start | bytes 1179656 | tf_op jit(solution)/shard_map/ppermute | solution.py:31
  18.1 1.0 copy-start.2
  19.1 32.5 %copy-start.3 = (bf16[64,3,1024]{2,0,1:T(8,128)(2,1)S(1)}, bf16[64,3,1024]{2,0,1:T(8,128)(2,1)}, u32[]{:S(2)}) copy-start(bf16[64,3,1024]{2,0,1:T(8,128)(2,1)} %param.4) | copy-start | bytes 1179652
  19.2 21.7 %collective-permute-start.1 = (bf16[2,3,64,1024]{3,2,1,0:T(8,128)(2,1)S(1)}, bf16[2,3,64,1024]{3,2,1,0:T(8,128)(2,1)}, u32[]{:S(2)}, u32[]{:S(2)}) collective-permute-start(bf16[2,3,64,1024]{3,2,1,0:T(8,128)(2,1)S(1)} %pair.2.refs_0_), channel_id=1, source_target_pairs={{1,0},{2,1},{3,2},{0,3},{5,4},{6,5},{7,6},{4,7},{9,8},{10,9},{11,1... | collective-permute-start | bytes 2359304 | tf_op jit(solution)/shard_map/ppermute | solution.py:31
  27.2 14.3 %collective-permute-start.4 = (bf16[2,3,64,1024]{3,2,1,0:T(8,128)(2,1)S(1)}, bf16[2,3,64,1024]{3,2,1,0:T(8,128)(2,1)}, u32[]{:S(2)}, u32[]{:S(2)}) collective-permute-start(bf16[2,3,64,1024]{3,2,1,0:T(8,128)(2,1)S(1)} %pair.3.refs_1_), channel_id=1, source_target_pairs={{3,0},{0,1},{1,2},{2,3},{7,4},{4,5},{5,6},{6,7},{11,8},{8,9},{9,10... | collective-permute-start | bytes 2359304 | tf_op jit(solution)/shard_map/ppermute | solution.py:31
  30.1 19.7 %collective-permute-start.8 = (bf16[2,3,64,1024]{3,2,1,0:T(8,128)(2,1)S(1)}, bf16[2,3,64,1024]{3,2,1,0:T(8,128)(2,1)S(1)}, u32[]{:S(2)}, u32[]{:S(2)}) collective-permute-start(bf16[2,3,64,1024]{3,2,1,0:T(8,128)(2,1)S(1)} %pair.2.refs_0_), channel_id=1, source_target_pairs={{3,0},{0,1},{1,2},{2,3},{7,4},{4,5},{5,6},{6,7},{11,8},{8,9},{9,10... | collective-permute-start | bytes 2359304 | tf_op jit(solution)/shard_map/ppermute | solution.py:31
  33.3 16.6 %collective-permute-start.7 = (bf16[2,3,64,1024]{3,2,1,0:T(8,128)(2,1)S(1)}, bf16[2,3,64,1024]{3,2,1,0:T(8,128)(2,1)S(1)}, u32[]{:S(2)}, u32[]{:S(2)}) collective-permute-start(bf16[2,3,64,1024]{3,2,1,0:T(8,128)(2,1)S(1)} %pair.3.refs_1_), channel_id=1, source_target_pairs={{1,0},{2,1},{3,2},{0,3},{5,4},{6,5},{7,6},{4,7},{9,8},{10,9},{11,1... | collective-permute-start | bytes 2359304 | tf_op jit(solution)/shard_map/ppermute | solution.py:31
  36.6 1.9 copy-start
  38.5 34.3 %copy-start.1 = (bf16[1024,3,512]{2,0,1:T(8,128)(2,1)S(1)}, bf16[1024,3,512]{2,0,1:T(8,128)(2,1)}, u32[]{:S(2)}) copy-start(bf16[1024,3,512]{2,0,1:T(8,128)(2,1)} %param.5) | copy-start | bytes 9437188
  40.2 0.7 copy-start.5
  41.5 31.4 %collective-permute-start.5 = (bf16[2,3,64,1024]{3,2,1,0:T(8,128)(2,1)}, bf16[2,3,64,1024]{3,2,1,0:T(8,128)(2,1)}, u32[]{:S(2)}, u32[]{:S(2)}) collective-permute-start(bf16[2,3,64,1024]{3,2,1,0:T(8,128)(2,1)} %collective-permute-done.1.refs_0_), channel_id=1, source_target_pairs={{1,0},{2,1},{3,2},{0,3},{5,4},{6,5},{7,6},{4,7},{9,8},{10,9},{11,1... | collective-permute-start | bytes 2359304 | tf_op jit(solution)/shard_map/ppermute | solution.py:31
  44.4 28.5 %collective-permute-start.6 = (bf16[2,3,64,1024]{3,2,1,0:T(8,128)(2,1)}, bf16[2,3,64,1024]{3,2,1,0:T(8,128)(2,1)}, u32[]{:S(2)}, u32[]{:S(2)}) collective-permute-start(bf16[2,3,64,1024]{3,2,1,0:T(8,128)(2,1)} %collective-permute-done.4.refs_3_), channel_id=1, source_target_pairs={{3,0},{0,1},{1,2},{2,3},{7,4},{4,5},{5,6},{6,7},{11,8},{8,9},{9,10... | collective-permute-start | bytes 2359304 | tf_op jit(solution)/shard_map/ppermute | solution.py:31
  49.8 0.9 copy-start.11
  50.7 0.9 copy-start.12
  52.4 32.4 %all-to-all-start = ((bf16[4,3,64,256]{3,2,1,0:T(8,128)(2,1)}), bf16[4,3,64,256]{3,2,1,0:T(8,128)(2,1)}, u32[]{:S(2)}, u32[]{:S(2)}) async-start(bf16[4,3,64,256]{3,2,1,0:T(8,128)(2,1)} %bitcast.47), calls=%async_computation | async-start | bytes 786432 | tf_op jit(solution)/shard_map/all_to_all | solution.py:409
  67.2 133.6 %all-gather.4.cloned.1.call-start = ((), (), s32[]{:S(2)}) async-start(), calls=%async_computation.1 | async-start | bytes 6684672 | tf_op jit(solution)/shard_map/all_gather | solution.py:453
  67.2 5.7 %copy-start.6 = (bf16[4,64,512]{2,1,0:T(8,128)(2,1)S(1)}, bf16[4,64,512]{2,1,0:T(8,128)(2,1)}, u32[]{:S(2)}) copy-start(bf16[4,64,512]{2,1,0:T(8,128)(2,1)} %copy-done.5) | copy-start | bytes 786436
  67.3 21.3 %copy-start.14 = (s32[4]{0:T(128)S(1)}, s32[4]{0:T(128)}, u32[]{:S(2)}) copy-start(s32[4]{0:T(128)} %param.7) | copy-start | bytes 52
  67.3 56.0 %copy-start.9 = (f32[512]{0:T(512)S(1)}, f32[512]{0:T(512)}, u32[]{:S(2)}) copy-start(f32[512]{0:T(512)} %param.6) | copy-start | bytes 6148
  72.9 1.0 copy-start.4
  78.6 0.8 copy-start.7
  79.4 6.4 %collective-permute-start.9 = (bf16[4,144,512]{2,1,0:T(8,128)(2,1)}, bf16[4,144,512]{2,1,0:T(8,128)(2,1)S(1)}, u32[]{:S(2)}, u32[]{:S(2)}) collective-permute-start(bf16[4,144,512]{2,1,0:T(8,128)(2,1)} %get-tuple-element.35), channel_id=1, source_target_pairs={{64,0},{0,64},{192,128},{128,192},{320,256},{256,320},{448,384},{3... | collective-permute-start | bytes 1769480 | tf_op jit(solution)/shard_map/ppermute | solution.py:35
  92.1 1.1 copy-start.8
  93.3 16.0 %collective-permute-start.16 = (bf16[16,512]{1,0:T(8,128)(2,1)S(1)}, bf16[16,512]{1,0:T(8,128)(2,1)S(1)}, u32[]{:S(2)}, u32[]{:S(2)}) collective-permute-start(bf16[16,512]{1,0:T(8,128)(2,1)S(1)} %get-tuple-element.57), channel_id=1, source_target_pairs={{2,1},{4,65},{6,129},{8,193},{10,257},{12,321},{14,385},{66,3},{68... | collective-permute-start | bytes 49160 | tf_op jit(solution)/shard_map/ppermute | solution.py:402
  94.0 20.8 %collective-permute-start.15 = (bf16[16,512]{1,0:T(8,128)(2,1)S(1)}, bf16[16,512]{1,0:T(8,128)(2,1)S(1)}, u32[]{:S(2)}, u32[]{:S(2)}) collective-permute-start(bf16[16,512]{1,0:T(8,128)(2,1)S(1)} %get-tuple-element.58), channel_id=1, source_target_pairs={{2,0},{4,64},{6,128},{8,192},{10,256},{12,320},{14,384},{66,2},{68... | collective-permute-start | bytes 49160 | tf_op jit(solution)/shard_map/ppermute | solution.py:401
  95.3 28.0 %collective-permute-start.10 = (bf16[144,512]{1,0:T(8,128)(2,1)S(1)}, bf16[144,512]{1,0:T(8,128)(2,1)S(1)}, u32[]{:S(2)}, u32[]{:S(2)}) collective-permute-start(bf16[144,512]{1,0:T(8,128)(2,1)S(1)} %get-tuple-element.42), channel_id=1, source_target_pairs={{128,0},{192,64},{256,128},{320,192},{384,256},{448,320},{0,384},{... | collective-permute-start | bytes 442376 | tf_op jit(solution)/shard_map/ppermute | solution.py:40
  100.2 23.0 %collective-permute-start.11 = (bf16[144,512]{1,0:T(8,128)(2,1)S(1)}, bf16[144,512]{1,0:T(8,128)(2,1)S(1)}, u32[]{:S(2)}, u32[]{:S(2)}) collective-permute-start(bf16[144,512]{1,0:T(8,128)(2,1)S(1)} %get-tuple-element.43), channel_id=1, source_target_pairs={{256,0},{320,64},{384,128},{448,192},{0,256},{64,320},{128,384},{1... | collective-permute-start | bytes 442376 | tf_op jit(solution)/shard_map/ppermute | solution.py:40
  106.6 16.6 %collective-permute-start.12 = (bf16[144,512]{1,0:T(8,128)(2,1)S(1)}, bf16[144,512]{1,0:T(8,128)(2,1)S(1)}, u32[]{:S(2)}, u32[]{:S(2)}) collective-permute-start(bf16[144,512]{1,0:T(8,128)(2,1)S(1)} %get-tuple-element.44), channel_id=1, source_target_pairs={{384,0},{448,64},{0,128},{64,192},{128,256},{192,320},{256,384},{3... | collective-permute-start | bytes 442376 | tf_op jit(solution)/shard_map/ppermute | solution.py:40
  109.3 11.2 %collective-permute-start.14 = (bf16[64,512]{1,0:T(8,128)(2,1)S(1)}, bf16[64,512]{1,0:T(8,128)(2,1)S(1)}, u32[]{:S(2)}, u32[]{:S(2)}) collective-permute-start(bf16[64,512]{1,0:T(8,128)(2,1)S(1)} %get-tuple-element.59), channel_id=1, source_target_pairs={{0,1},{1,0},{2,65},{3,64},{4,129},{5,128},{6,193},{7,192},{8,257},... | collective-permute-start | bytes 196616 | tf_op jit(solution)/shard_map/ppermute | solution.py:400
  114.8 8.4 %collective-permute-start.13 = (bf16[64,512]{1,0:T(8,128)(2,1)S(1)}, bf16[64,512]{1,0:T(8,128)(2,1)S(1)}, u32[]{:S(2)}, u32[]{:S(2)}) collective-permute-start(bf16[64,512]{1,0:T(8,128)(2,1)S(1)} %get-tuple-element.60), channel_id=1, source_target_pairs={{0,0},{1,1},{2,64},{3,65},{4,128},{5,129},{6,192},{7,193},{8,256},... | collective-permute-start | bytes 196616 | tf_op jit(solution)/shard_map/ppermute | solution.py:399
  153.2 47.6 %copy-start.10 = (bf16[576,512]{1,0:T(8,128)(2,1)}, bf16[576,512]{1,0:T(8,128)(2,1)S(1)}, u32[]{:S(2)}) copy-start(bf16[576,512]{1,0:T(8,128)(2,1)S(1)} %all-gather.1) | copy-start | bytes 1769476
  153.2 38.7 %collective-permute-start.19 = (bf16[4,144,512]{2,1,0:T(8,128)(2,1)S(1)}, bf16[4,144,512]{2,1,0:T(8,128)(2,1)S(1)}, u32[]{:S(2)}, u32[]{:S(2)}) collective-permute-start(bf16[4,144,512]{2,1,0:T(8,128)(2,1)S(1)} %bitcast.43), channel_id=1, source_target_pairs={{64,0},{0,64},{192,128},{128,192},{320,256},{256,320},{448,384},{3... | collective-permute-start | bytes 1769480 | tf_op jit(solution)/shard_map/ppermute | solution.py:35
  155.1 36.8 %collective-permute-start.18 = (bf16[4,144,512]{2,1,0:T(8,128)(2,1)S(1)}, bf16[4,144,512]{2,1,0:T(8,128)(2,1)S(1)}, u32[]{:S(2)}, u32[]{:S(2)}) collective-permute-start(bf16[4,144,512]{2,1,0:T(8,128)(2,1)S(1)} %bitcast.44), channel_id=1, source_target_pairs={{432,0},{384,16},{400,32},{416,48},{496,64},{448,80},{464,96},{480... | collective-permute-start | bytes 1769480 | tf_op jit(solution)/shard_map/ppermute | solution.py:53
  159.4 32.5 %collective-permute-start.17 = (bf16[4,144,512]{2,1,0:T(8,128)(2,1)S(1)}, bf16[4,144,512]{2,1,0:T(8,128)(2,1)S(1)}, u32[]{:S(2)}, u32[]{:S(2)}) collective-permute-start(bf16[4,144,512]{2,1,0:T(8,128)(2,1)S(1)} %bitcast.45), channel_id=1, source_target_pairs={{128,0},{144,16},{160,32},{176,48},{192,64},{208,80},{224,96},{240... | collective-permute-start | bytes 1769480 | tf_op jit(solution)/shard_map/ppermute | solution.py:53
  165.3 25.3 %collective-permute-start.21 = (bf16[2,144,512]{2,1,0:T(8,128)(2,1)S(1)}, bf16[2,144,512]{2,1,0:T(8,128)(2,1)S(1)}, u32[]{:S(2)}, u32[]{:S(2)}) collective-permute-start(bf16[2,144,512]{2,1,0:T(8,128)(2,1)S(1)} %bitcast.49), channel_id=1, source_target_pairs={{304,0},{256,16},{272,32},{288,48},{368,64},{320,80},{336,96},{352... | collective-permute-start | bytes 884744 | tf_op jit(solution)/shard_map/ppermute | solution.py:53
  167.7 24.1 %collective-permute-start.20 = (bf16[2,144,512]{2,1,0:T(8,128)(2,1)S(1)}, bf16[2,144,512]{2,1,0:T(8,128)(2,1)S(1)}, u32[]{:S(2)}, u32[]{:S(2)}) collective-permute-start(bf16[2,144,512]{2,1,0:T(8,128)(2,1)S(1)} %bitcast.48), channel_id=1, source_target_pairs={{256,0},{272,16},{288,32},{304,48},{320,64},{336,80},{352,96},{368... | collective-permute-start | bytes 884744 | tf_op jit(solution)/shard_map/ppermute | solution.py:53
  191.9 8.9 %copy-start.13 = (bf16[4,144,512]{2,1,0:T(8,128)(2,1)}, bf16[4,144,512]{2,1,0:T(8,128)(2,1)S(1)}, u32[]{:S(2)}) copy-start(bf16[4,144,512]{2,1,0:T(8,128)(2,1)S(1)} %pad_maximum_fusion.refs_4_) | copy-start | bytes 1769476
  191.9 8.9 %copy-start.15 = (bf16[4,144,512]{2,1,0:T(8,128)(2,1)}, bf16[4,144,512]{2,1,0:T(8,128)(2,1)S(1)}, u32[]{:S(2)}) copy-start(bf16[4,144,512]{2,1,0:T(8,128)(2,1)S(1)} %collective-permute-done.19.refs_1_) | copy-start | bytes 1769476
  191.9 8.9 %copy-start.16 = (bf16[4,144,512]{2,1,0:T(8,128)(2,1)}, bf16[4,144,512]{2,1,0:T(8,128)(2,1)S(1)}, u32[]{:S(2)}) copy-start(bf16[4,144,512]{2,1,0:T(8,128)(2,1)S(1)} %collective-permute-done.18.refs_3_) | copy-start | bytes 1769476
  192.0 8.9 %copy-start.17 = (bf16[4,144,512]{2,1,0:T(8,128)(2,1)}, bf16[4,144,512]{2,1,0:T(8,128)(2,1)S(1)}, u32[]{:S(2)}) copy-start(bf16[4,144,512]{2,1,0:T(8,128)(2,1)S(1)} %collective-permute-done.17.refs_2_) | copy-start | bytes 1769476
  192.0 7.8 %collective-permute-start.22 = (bf16[4,144,512]{2,1,0:T(8,128)(2,1)S(1)}, bf16[4,144,512]{2,1,0:T(8,128)(2,1)S(1)}, u32[]{:S(2)}, u32[]{:S(2)}) collective-permute-start(bf16[4,144,512]{2,1,0:T(8,128)(2,1)S(1)} %collective-permute-done.17.refs_2_), channel_id=1, source_target_pairs={{64,0},{0,64},{192,128},{128,192},{320,256},{256,320},{448,384},{3... | collective-permute-start | bytes 1769480 | tf_op jit(solution)/shard_map/ppermute | solution.py:35
  194.7 5.1 %collective-permute-start.23 = (bf16[4,144,512]{2,1,0:T(8,128)(2,1)S(1)}, bf16[4,144,512]{2,1,0:T(8,128)(2,1)}, u32[]{:S(2)}, u32[]{:S(2)}) collective-permute-start(bf16[4,144,512]{2,1,0:T(8,128)(2,1)S(1)} %collective-permute-done.18.refs_3_), channel_id=1, source_target_pairs={{64,0},{0,64},{192,128},{128,192},{320,256},{256,320},{448,384},{3... | collective-permute-start | bytes 1769480 | tf_op jit(solution)/shard_map/ppermute | solution.py:35
  196.7 4.2 %collective-permute-start.24 = (bf16[4,144,512]{2,1,0:T(8,128)(2,1)S(1)}, bf16[4,144,512]{2,1,0:T(8,128)(2,1)}, u32[]{:S(2)}, u32[]{:S(2)}) collective-permute-start(bf16[4,144,512]{2,1,0:T(8,128)(2,1)S(1)} %pad_maximum_fusion.refs_4_), channel_id=1, source_target_pairs={{64,0},{0,64},{192,128},{128,192},{320,256},{256,320},{448,384},{3... | collective-permute-start | bytes 1769480 | tf_op jit(solution)/shard_map/ppermute | solution.py:35
  199.8 1.0 copy-start.18
Sparse Core Ops, SparseCore 0:
  88.7 82.3 all-gather.3

commit v10 on v9

--- a/solution.py
+++ b/solution.py
@@ -288,62 +288,40 @@
 
 
 def weight_grad_kernel(meta_ref, features_ref, *refs):
-    *group_refs, out_ref, mix_ref, got_ref, grads_ref, held_ref, got_sem, held_sem = refs
+    *group_refs, out_ref, mix_ref, grads_ref = refs
     half = grads_ref.shape[1] // ZH
     width = grads_ref.shape[2]
-    got = [
-        pltpu.make_async_copy(group_ref, got_ref.at[at], got_sem.at[at])
-        for at, group_ref in enumerate(group_refs)
-    ]
-    held = [
-        pltpu.make_async_copy(features_ref.at[:, at], held_ref.at[at], held_sem.at[at])
-        for at in range(LEVELS)
-    ]
-    for copy in got:
-        copy.start()
     mix = jnp.zeros((TAIL, width), jnp.float32)
-    for at, copy in enumerate(got):
-        copy.wait()
-        if at == len(got) // 2:
-            for later in held:
-                later.start()
+    for at, group_ref in enumerate(group_refs):
         for part in range(2):
             slab = grads_ref.at[meta_ref[at] * 2 + part]
             for sequence in range(ZH):
-                rows = got_ref[at, sequence, pl.ds(part * half, half), :]
+                rows = group_ref[sequence, pl.ds(part * half, half), :]
                 slab[pl.ds(sequence * half, half), :] = rows
         for sequence in range(ZH):
-            mix = mix + got_ref[at, sequence, pl.ds(2 * half, TAIL), :].astype(jnp.float32)
+            mix = mix + group_ref[sequence, pl.ds(2 * half, TAIL), :].astype(jnp.float32)
     mix_ref[...] = jnp.sum(mix, axis=0, keepdims=True)
-    blocks = held_ref.shape[1]
-    for at, copy in enumerate(held):
-        copy.wait()
-        left = jnp.concatenate([held_ref[at, e] for e in range(blocks)], axis=1)
+    blocks = features_ref.shape[0]
+    for level in range(LEVELS):
+        left = jnp.concatenate([features_ref[e, level] for e in range(blocks)], axis=1)
         right = grads_ref[...].reshape(-1, width)
         term = jnp.dot(left, right, preferred_element_type=jnp.float32)
-        out_ref[at] = term.astype(jnp.bfloat16)
+        out_ref[level] = term.astype(jnp.bfloat16)
 
 
 def weight_grad(features, groups, members):
     draft, _, columns, tokens = features.shape
     count, width = len(groups), groups[0].shape[2]
-    hbm = pl.BlockSpec(memory_space=pltpu.HBM)
     return pl.pallas_call(
         weight_grad_kernel,
         out_shape=(
             jax.ShapeDtypeStruct((LEVELS, columns, width), jnp.bfloat16),
             jax.ShapeDtypeStruct((1, width), jnp.float32),
         ),
-        in_specs=[SMEM] + [hbm] * (count + 1),
+        in_specs=[SMEM] + [VMEM] * (count + 1),
         out_specs=(VMEM, VMEM),
-        scratch_shapes=[
-            pltpu.VMEM((count,) + groups[0].shape, jnp.bfloat16),
-            pltpu.VMEM((draft, tokens, width), jnp.bfloat16),
-            pltpu.VMEM((LEVELS, draft, columns, tokens), jnp.bfloat16),
-            pltpu.SemaphoreType.DMA((count,)),
-            pltpu.SemaphoreType.DMA((LEVELS,)),
-        ],
-        compiler_params=params(58),
+        scratch_shapes=[pltpu.VMEM((draft, tokens, width), jnp.bfloat16)],
+        compiler_params=params(28),
         cost_estimate=pl.CostEstimate(
             flops=2 * draft * LEVELS * columns * tokens * width,
             bytes_accessed=2 * features.size + 2 * draft * tokens * width,
@@ -414,7 +392,9 @@
     above, below = from_z(stack, 1), from_z(stack, -1)
     far = jnp.concatenate([from_z(stack[:2], 2), from_z(stack[2:], -2)])
     other = from_other_core(stack)
-    above, below, other, far = lax.optimization_barrier((above, below, other, far))
+    above, below, other, far, features = lax.optimization_barrier(
+        (above, below, other, far, features)
+    )
     swapped = [from_other_core(block) for block in (above, below, far)]
 
     def member(step, of_core):
@@ -442,18 +422,16 @@
     up_low, down_high = plane_move(1, False)(low), plane_move(-1, False)(high)
     up_high, down_low = plane_move(1, False)(high), plane_move(-1, False)(low)
     zero = project([low, high], weight, 14)
-    up_low, down_high, zero = lax.optimization_barrier((up_low, down_high, zero))
+    up_low, down_high, zero, later = lax.optimization_barrier((up_low, down_high, zero, own))
+    traded = trade_columns(later)
     far_low, far_high = plane_move(1, False)(up_low), plane_move(-1, False)(down_high)
-    up_high, down_low, later = lax.optimization_barrier((up_high, down_low, own))
-    traded = trade_columns(later)
+    halves = send_high(later[LEVELS - 1], draft_index)
     sides = project([up_low, up_high, down_low, down_high], weight, 58)
-    far_low, far_high, sides = lax.optimization_barrier((far_low, far_high, sides))
+    far_low, far_high, halves, sides = lax.optimization_barrier((far_low, far_high, halves, sides))
     keep, send = project_place([far_low, far_high], weight, zero, sides, core, x, y)
     got, traded = lax.optimization_barrier((from_other_core(send), traded))
     every = lax.all_gather(turn(traded), "draft", axis=0, tiled=False)
     mine, *away = join(keep, got, zl)
-    top, mine = lax.optimization_barrier((own[LEVELS - 1], mine))
-    halves = send_high(top, draft_index)
     parts = [mine] + [from_zl(block, step) for step, block in zip((1, 2, 3), away)]
     scale = LOSS_SCALE / valid_total(lengths)
     odd = draft_index % 2

time: 220 us -> 220 us (level)
  the two profiles are of different devices: /device:TPU:1 before, /device:TPU:75 now
where the time goes in v10:
time: 220 us; the launch traced here: 219 us
  starting transfers between devices  102 us (46%)
  waiting for transfers between devices  33.1 us (15%)
  blocking collectives  30.8 us (14%)
  Pallas kernels  24 us (11%)
  between operations  16.6 us (8%)
  local copies, waits for them, and re-layouts  10.9 us (5%)
    all_gather x1, blocking collectives, gather_grads(): stack = lax.all_gather(grad, 'dp', axis=0, tiled=False)  30.8 us
    ppermute x9, starting transfers between devices, plane_move(): return lambda block: lax.ppermute(block, ('tp', 'draft'), pairs)  26.4 us
    ppermute x4, waiting for transfers between devices, from_z(): return lax.ppermute(block, ('tp', 'dp'), pairs)  21.9 us
    ppermute x4, starting transfers between devices, from_z(): return lax.ppermute(block, ('tp', 'dp'), pairs)  13.5 us
    ppermute x1, starting transfers between devices, send_high(): lax.ppermute(jnp.where(even, right, left), axes, crossed)  13.3 us
    all_to_all x1, starting transfers between devices, trade_columns(): lax.all_to_all(quarters, 'dp', split_axis=0, concat_axis=0, tiled=True)  13 us
    ppermute x3, starting transfers between devices, from_zl(): return lax.ppermute(block, 'tp', pairs)  12.5 us
    ppermute x5, starting transfers between devices, from_other_core(): return lax.ppermute(block, 'tp', [(t ^ 1, t) for t in range(ZL * CORES)])  12.1 us
  transfers between devices with their start and end apart: 27, of which 7 were waited for; matrix products, arithmetic and copies ran while one was open for 1% of the time, Pallas kernels for 7%

profile of v10, /device:TPU:75, one launch (start us, length us, event | category | flops | bytes accessed | tf_op | source)
XLA Modules:
  0.0 219.0 jit_solution(7014921158342002948)
XLA Ops:
  7.2 2.1 collective-permute-start
  9.2 3.2 %collective-permute-start.3 = (bf16[3,64,1024]{2,1,0:T(8,128)(2,1)}, bf16[3,64,1024]{2,1,0:T(8,128)(2,1)S(1)}, u32[]{:S(2)}, u32[]{:S(2)}) collective-permute-start(bf16[3,64,1024]{2,1,0:T(8,128)(2,1)} %bitcast.41), channel_id=1, source_target_pairs={{12,0},{13,1},{14,2},{15,3},{0,4},{1,5},{2,6},{3,7},{4,8},{5,9},{6... | collective-permute-start | bytes 1179656 | tf_op jit(solution)/shard_map/ppermute | solution.py:31
  12.5 5.1 %collective-permute-start.2 = (bf16[3,64,1024]{2,1,0:T(8,128)(2,1)}, bf16[3,64,1024]{2,1,0:T(8,128)(2,1)S(1)}, u32[]{:S(2)}, u32[]{:S(2)}) collective-permute-start(bf16[3,64,1024]{2,1,0:T(8,128)(2,1)} %bitcast.42), channel_id=1, source_target_pairs={{8,0},{9,1},{10,2},{11,3},{12,4},{13,5},{14,6},{15,7},{0,8},{1,9},... | collective-permute-start | bytes 1179656 | tf_op jit(solution)/shard_map/ppermute | solution.py:31
  17.6 0.0 collective-permute-done.second_ref
  17.6 1.0 copy-done.2
  18.6 0.9 pair.2.refs_0_
  19.5 2.2 collective-permute-start.1
  21.7 1.5 collective-permute-done.2.first_ref
  23.3 0.9 pair.3.refs_1_
  24.2 3.1 %collective-permute-start.4 = (bf16[2,3,64,1024]{3,2,1,0:T(8,128)(2,1)}, bf16[2,3,64,1024]{3,2,1,0:T(8,128)(2,1)}, u32[]{:S(2)}, u32[]{:S(2)}) collective-permute-start(bf16[2,3,64,1024]{3,2,1,0:T(8,128)(2,1)} %pair.3.refs_1_), channel_id=1, source_target_pairs={{3,0},{0,1},{1,2},{2,3},{7,4},{4,5},{5,6},{6,7},{11,8},{8,9},{9,10... | collective-permute-start | bytes 2359304 | tf_op jit(solution)/shard_map/ppermute | solution.py:31
  27.3 2.8 %collective-permute-start.12 = (bf16[2,3,64,1024]{3,2,1,0:T(8,128)(2,1)}, bf16[2,3,64,1024]{3,2,1,0:T(8,128)(2,1)}, u32[]{:S(2)}, u32[]{:S(2)}) collective-permute-start(bf16[2,3,64,1024]{3,2,1,0:T(8,128)(2,1)} %pair.2.refs_0_), channel_id=1, source_target_pairs={{3,0},{0,1},{1,2},{2,3},{7,4},{4,5},{5,6},{6,7},{11,8},{8,9},{9,10... | collective-permute-start | bytes 2359304 | tf_op jit(solution)/shard_map/ppermute | solution.py:31
  30.1 2.5 %collective-permute-start.11 = (bf16[2,3,64,1024]{3,2,1,0:T(8,128)(2,1)}, bf16[2,3,64,1024]{3,2,1,0:T(8,128)(2,1)}, u32[]{:S(2)}, u32[]{:S(2)}) collective-permute-start(bf16[2,3,64,1024]{3,2,1,0:T(8,128)(2,1)} %pair.3.refs_1_), channel_id=1, source_target_pairs={{1,0},{2,1},{3,2},{0,3},{5,4},{6,5},{7,6},{4,7},{9,8},{10,9},{11,1... | collective-permute-start | bytes 2359304 | tf_op jit(solution)/shard_map/ppermute | solution.py:31
  32.6 0.0 copy-start
  32.7 1.9 copy-done
  34.5 3.2 %project.2.refs_3_ = bf16[4,64,512]{2,1,0:T(8,128)(2,1)S(1)} custom-call(bf16[2,3,64,1024]{3,2,1,0:T(8,128)(2,1)} %pair.2.refs_0_, bf16[2,3,64,1024]{3,2,1,0:T(8,128)(2,1)} %pair.3.refs_1_, bf16[3,1024,512]{2,1,0:T(8,128)(2,1)S(1)} %bitcast.34), custom_call_target="tpu_custom_call" | custom-call | bytes 1572864 | tf_op jit(solution)/shard_map/project/pallas_call | solution.py:114
  37.8 0.7 copy-done.5
  38.5 0.0 collective-permute-done.1.refs_0_
  38.5 0.0 collective-permute-done.4.refs_3_
  38.5 0.8 copy.10
  39.3 13.0 %all-to-all-start = ((bf16[4,3,64,256]{3,2,1,0:T(8,128)(2,1)}), bf16[4,3,64,256]{3,2,1,0:T(8,128)(2,1)}, u32[]{:S(2)}, u32[]{:S(2)}) async-start(bf16[4,3,64,256]{3,2,1,0:T(8,128)(2,1)} %bitcast.48), calls=%async_computation | async-start | bytes 786432 | tf_op jit(solution)/shard_map/all_to_all | solution.py:387
  52.3 3.5 %collective-permute-start.5 = (bf16[2,3,64,1024]{3,2,1,0:T(8,128)(2,1)}, bf16[2,3,64,1024]{3,2,1,0:T(8,128)(2,1)S(1)}, u32[]{:S(2)}, u32[]{:S(2)}) collective-permute-start(bf16[2,3,64,1024]{3,2,1,0:T(8,128)(2,1)} %collective-permute-done.1.refs_0_), channel_id=1, source_target_pairs={{1,0},{2,1},{3,2},{0,3},{5,4},{6,5},{7,6},{4,7},{9,8},{10,9},{11,1... | collective-permute-start | bytes 2359304 | tf_op jit(solution)/shard_map/ppermute | solution.py:31
  55.8 1.9 collective-permute-start.6
  57.8 1.3 collective-permute-start.10
  59.1 0.7 collective-permute-start.9
  59.8 13.3 %collective-permute-start.8 = (bf16[64,512]{1,0:T(8,128)(2,1)S(1)}, bf16[64,512]{1,0:T(8,128)(2,1)S(1)}, u32[]{:S(2)}, u32[]{:S(2)}) collective-permute-start(bf16[64,512]{1,0:T(8,128)(2,1)S(1)} %get-tuple-element.61), channel_id=1, source_target_pairs={{0,1},{1,0},{2,65},{3,64},{4,129},{5,128},{6,193},{7,192},{8,257},... | collective-permute-start | bytes 196616 | tf_op jit(solution)/shard_map/ppermute | solution.py:378
  73.1 9.4 %collective-permute-start.7 = (bf16[64,512]{1,0:T(8,128)(2,1)S(1)}, bf16[64,512]{1,0:T(8,128)(2,1)S(1)}, u32[]{:S(2)}, u32[]{:S(2)}) collective-permute-start(bf16[64,512]{1,0:T(8,128)(2,1)S(1)} %get-tuple-element.62), channel_id=1, source_target_pairs={{0,0},{1,1},{2,64},{3,65},{4,128},{5,129},{6,192},{7,193},{8,256},... | collective-permute-start | bytes 196616 | tf_op jit(solution)/shard_map/ppermute | solution.py:377
  82.5 0.1 pad_add_fusion.1.meta_ref
  82.5 5.6 %project.3.refs_4_ = bf16[8,64,512]{2,1,0:T(8,128)(2,1)} custom-call(bf16[2,3,64,1024]{3,2,1,0:T(8,128)(2,1)} %collective-permute-done.1.refs_0_, bf16[2,3,64,1024]{3,2,1,0:T(8,128)(2,1)} %collective-permute-done.11.refs_1_, bf16[2,3,64,1024]{3,2,1,0:T(8,128)(2,1)} %collective-permute-done.12.refs_2_, ...), custom_call_target="tpu_custom_call" | custom-call | bytes 3145728 | tf_op jit(solution)/shard_map/project/pallas_call | solution.py:114
  88.2 0.0 copy-start.4
  88.2 1.0 copy-done.4
  89.2 3.3 %project_place.1 = (bf16[4,144,512]{2,1,0:T(8,128)(2,1)S(1)}, bf16[4,144,512]{2,1,0:T(8,128)(2,1)}) custom-call(s32[3]{0:T(128)S(1)} %pad_add_fusion.1.meta_ref, bf16[2,3,64,1024]{3,2,1,0:T(8,128)(2,1)S(1)} %collective-permute-done.5.refs_0_, bf16[2,3,64,1024]{3,2,1,0:T(8,128)(2,1)S(1)} %collective-permute-done.6.refs_1_, ...), custom_call_target="tpu_custom_call" | custom-call | bytes 1572864 | tf_op jit(solution)/shard_map/project_place/pallas_call | solution.py:167
  92.5 0.8 copy-done.7
  93.3 1.9 collective-permute-start.13
  95.2 2.2 collective-permute-done.13.got_ref
  97.4 2.7 %turn.1 = bf16[3,256,256]{2,1,0:T(8,128)(2,1)} custom-call(bf16[4,3,64,256]{3,2,1,0:T(8,128)(2,1)} %all-to-all-done.traded_ref), custom_call_target="tpu_custom_call" | custom-call | bytes 786432 | tf_op jit(solution)/shard_map/turn/pallas_call | solution.py:341
  100.1 0.0 all-gather.4.cloned.1.call-update
  100.2 1.1 copy-done.8
  101.2 0.2 join.1
  101.4 1.9 collective-permute-start.14
  103.3 8.6 %collective-permute-start.15 = (bf16[144,512]{1,0:T(8,128)(2,1)S(1)}, bf16[144,512]{1,0:T(8,128)(2,1)S(1)}, u32[]{:S(2)}, u32[]{:S(2)}) collective-permute-start(bf16[144,512]{1,0:T(8,128)(2,1)S(1)} %get-tuple-element.40), channel_id=1, source_target_pairs={{256,0},{320,64},{384,128},{448,192},{0,256},{64,320},{128,384},{1... | collective-permute-start | bytes 442376 | tf_op jit(solution)/shard_map/ppermute | solution.py:40
  111.9 1.9 collective-permute-start.16
  113.9 0.7 maximum_reduce_fusion
  114.6 0.7 dynamic_slice.3
  117.2 0.8 pad_add_fusion.meta_ref
  118.0 2.7 %collective-permute-done.15.refs_2_ = bf16[144,512]{1,0:T(8,128)(2,1)S(1)} collective-permute-done((bf16[144,512]{1,0:T(8,128)(2,1)S(1)}, bf16[144,512]{1,0:T(8,128)(2,1)S(1)}, u32[]{:S(2)}, u32[]{:S(2)}) %collective-permute-start.15) | collective-permute-done | bytes 147488 | tf_op jit(solution)/shard_map/ppermute | solution.py:40
  120.7 3.2 %collective-permute-done.16.refs_3_ = bf16[144,512]{1,0:T(8,128)(2,1)S(1)} collective-permute-done((bf16[144,512]{1,0:T(8,128)(2,1)S(1)}, bf16[144,512]{1,0:T(8,128)(2,1)S(1)}, u32[]{:S(2)}, u32[]{:S(2)}) %collective-permute-start.16) | collective-permute-done | bytes 147488 | tf_op jit(solution)/shard_map/ppermute | solution.py:40
  123.9 1.4 chain.1
  125.2 30.8 %all-gather = bf16[576,512]{1,0:T(8,128)(2,1)S(1)} all-gather(bf16[144,512]{1,0:T(8,128)(2,1)S(1)} %chain.1), channel_id=2, replica_groups=mesh['tp'=8,'dp'=4,'draft'=16] {'dp'}, dimensions={0}, use_global_device_ids=true | all-gather | bytes 737280 | tf_op jit(solution)/shard_map/all_gather | solution.py:391
  156.1 2.8 %collective-permute-start.19 = (bf16[4,144,512]{2,1,0:T(8,128)(2,1)S(1)}, bf16[4,144,512]{2,1,0:T(8,128)(2,1)S(1)}, u32[]{:S(2)}, u32[]{:S(2)}) collective-permute-start(bf16[4,144,512]{2,1,0:T(8,128)(2,1)S(1)} %bitcast.36), channel_id=1, source_target_pairs={{64,0},{0,64},{192,128},{128,192},{320,256},{256,320},{448,384},{3... | collective-permute-start | bytes 1769480 | tf_op jit(solution)/shard_map/ppermute | solution.py:35
  158.9 1.9 collective-permute-start.18
  160.8 3.4 %collective-permute-start.17 = (bf16[4,144,512]{2,1,0:T(8,128)(2,1)S(1)}, bf16[4,144,512]{2,1,0:T(8,128)(2,1)S(1)}, u32[]{:S(2)}, u32[]{:S(2)}) collective-permute-start(bf16[4,144,512]{2,1,0:T(8,128)(2,1)S(1)} %bitcast.38), channel_id=1, source_target_pairs={{128,0},{144,16},{160,32},{176,48},{192,64},{208,80},{224,96},{240... | collective-permute-start | bytes 1769480 | tf_op jit(solution)/shard_map/ppermute | solution.py:53
  164.2 6.3 %collective-permute-start.21 = (bf16[2,144,512]{2,1,0:T(8,128)(2,1)S(1)}, bf16[2,144,512]{2,1,0:T(8,128)(2,1)S(1)}, u32[]{:S(2)}, u32[]{:S(2)}) collective-permute-start(bf16[2,144,512]{2,1,0:T(8,128)(2,1)S(1)} %bitcast.50), channel_id=1, source_target_pairs={{304,0},{256,16},{272,32},{288,48},{368,64},{320,80},{336,96},{352... | collective-permute-start | bytes 884744 | tf_op jit(solution)/shard_map/ppermute | solution.py:53
  170.6 1.9 collective-permute-start.20
  172.5 11.1 %collective-permute-done.21 = bf16[2,144,512]{2,1,0:T(8,128)(2,1)S(1)} collective-permute-done((bf16[2,144,512]{2,1,0:T(8,128)(2,1)S(1)}, bf16[2,144,512]{2,1,0:T(8,128)(2,1)S(1)}, u32[]{:S(2)}, u32[]{:S(2)}) %collective-permute-start.21) | collective-permute-done | bytes 294944 | tf_op jit(solution)/shard_map/ppermute | solution.py:53
  183.6 10.8 %collective-permute-done.20 = bf16[2,144,512]{2,1,0:T(8,128)(2,1)S(1)} collective-permute-done((bf16[2,144,512]{2,1,0:T(8,128)(2,1)S(1)}, bf16[2,144,512]{2,1,0:T(8,128)(2,1)S(1)}, u32[]{:S(2)}, u32[]{:S(2)}) %collective-permute-start.20) | collective-permute-done | bytes 294944 | tf_op jit(solution)/shard_map/ppermute | solution.py:53
  194.4 0.1 pad_maximum_fusion.refs_4_
  194.5 0.0 all-gather.4.cloned.1.call-done
  194.5 3.0 %collective-permute-start.22 = (bf16[4,144,512]{2,1,0:T(8,128)(2,1)S(1)}, bf16[4,144,512]{2,1,0:T(8,128)(2,1)S(1)}, u32[]{:S(2)}, u32[]{:S(2)}) collective-permute-start(bf16[4,144,512]{2,1,0:T(8,128)(2,1)S(1)} %collective-permute-done.17.refs_2_), channel_id=1, source_target_pairs={{64,0},{0,64},{192,128},{128,192},{320,256},{256,320},{448,384},{3... | collective-permute-start | bytes 1769480 | tf_op jit(solution)/shard_map/ppermute | solution.py:35
  197.5 1.9 collective-permute-start.23
  199.4 2.4 %collective-permute-start.24 = (bf16[4,144,512]{2,1,0:T(8,128)(2,1)S(1)}, bf16[4,144,512]{2,1,0:T(8,128)(2,1)}, u32[]{:S(2)}, u32[]{:S(2)}) collective-permute-start(bf16[4,144,512]{2,1,0:T(8,128)(2,1)S(1)} %pad_maximum_fusion.refs_4_), channel_id=1, source_target_pairs={{64,0},{0,64},{192,128},{128,192},{320,256},{256,320},{448,384},{3... | collective-permute-start | bytes 1769480 | tf_op jit(solution)/shard_map/ppermute | solution.py:35
  201.9 0.1 stack.56.meta_ref
  202.0 1.6 collective-permute-done.24.refs_7_
  203.6 2.8 %copy-done.10 = bf16[48,256,256]{2,1,0:T(8,128)(2,1)S(1)} copy-done((bf16[48,256,256]{2,1,0:T(8,128)(2,1)S(1)}, bf16[48,256,256]{2,1,0:T(8,128)(2,1)}, u32[]{:S(2)}) %copy-start.10) | copy-done | bytes 6291480
  206.4 5.8 %weight_grad.1 = (bf16[3,256,512]{2,1,0:T(8,128)(2,1)}, f32[1,512]{1,0:T(1,128)}) custom-call(s32[8]{0:T(128)S(1)} %stack.56.meta_ref, bf16[16,3,256,256]{3,2,1,0:T(8,128)(2,1)S(1)} %bitcast.47, bf16[4,144,512]{2,1,0:T(8,128)(2,1)S(1)} %bitcast.39, bf16[4,144,512]{2,1,0:T(8,128)(2,1)S(1)} %collective-permute-done.19.refs_1_, ...), custom_call_target="tpu_custom_call" | custom-call | flops 3221225472 | bytes 10485760 | tf_op jit(solution)/shard_map/weight_grad/pallas_call | solution.py:315
  (36 shorter events, 0.1 us)
Async XLA Ops:
  7.2 10.4 %collective-permute-start = (bf16[3,64,1024]{2,1,0:T(8,128)(2,1)}, bf16[3,64,1024]{2,1,0:T(8,128)(2,1)S(1)}, u32[]{:S(2)}, u32[]{:S(2)}) collective-permute-start(bf16[3,64,1024]{2,1,0:T(8,128)(2,1)} %bitcast.40), channel_id=1, source_target_pairs={{4,0},{5,1},{6,2},{7,3},{8,4},{9,5},{10,6},{11,7},{12,8},{13,9},{1... | collective-permute-start | bytes 1179656 | tf_op jit(solution)/shard_map/ppermute | solution.py:31
  9.2 12.5 %collective-permute-start.3 = (bf16[3,64,1024]{2,1,0:T(8,128)(2,1)}, bf16[3,64,1024]{2,1,0:T(8,128)(2,1)S(1)}, u32[]{:S(2)}, u32[]{:S(2)}) collective-permute-start(bf16[3,64,1024]{2,1,0:T(8,128)(2,1)} %bitcast.41), channel_id=1, source_target_pairs={{12,0},{13,1},{14,2},{15,3},{0,4},{1,5},{2,6},{3,7},{4,8},{5,9},{6... | collective-permute-start | bytes 1179656 | tf_op jit(solution)/shard_map/ppermute | solution.py:31
  12.5 10.8 %collective-permute-start.2 = (bf16[3,64,1024]{2,1,0:T(8,128)(2,1)}, bf16[3,64,1024]{2,1,0:T(8,128)(2,1)S(1)}, u32[]{:S(2)}, u32[]{:S(2)}) collective-permute-start(bf16[3,64,1024]{2,1,0:T(8,128)(2,1)} %bitcast.42), channel_id=1, source_target_pairs={{8,0},{9,1},{10,2},{11,3},{12,4},{13,5},{14,6},{15,7},{0,8},{1,9},... | collective-permute-start | bytes 1179656 | tf_op jit(solution)/shard_map/ppermute | solution.py:31
  17.6 1.0 copy-start.2
  18.6 19.9 %copy-start.3 = (bf16[64,3,1024]{2,0,1:T(8,128)(2,1)S(1)}, bf16[64,3,1024]{2,0,1:T(8,128)(2,1)}, u32[]{:S(2)}) copy-start(bf16[64,3,1024]{2,0,1:T(8,128)(2,1)} %param.4) | copy-start | bytes 1179652
  19.5 19.0 %collective-permute-start.1 = (bf16[2,3,64,1024]{3,2,1,0:T(8,128)(2,1)}, bf16[2,3,64,1024]{3,2,1,0:T(8,128)(2,1)}, u32[]{:S(2)}, u32[]{:S(2)}) collective-permute-start(bf16[2,3,64,1024]{3,2,1,0:T(8,128)(2,1)} %pair.2.refs_0_), channel_id=1, source_target_pairs={{1,0},{2,1},{3,2},{0,3},{5,4},{6,5},{7,6},{4,7},{9,8},{10,9},{11,1... | collective-permute-start | bytes 2359304 | tf_op jit(solution)/shard_map/ppermute | solution.py:31
  24.2 14.3 %collective-permute-start.4 = (bf16[2,3,64,1024]{3,2,1,0:T(8,128)(2,1)}, bf16[2,3,64,1024]{3,2,1,0:T(8,128)(2,1)}, u32[]{:S(2)}, u32[]{:S(2)}) collective-permute-start(bf16[2,3,64,1024]{3,2,1,0:T(8,128)(2,1)} %pair.3.refs_1_), channel_id=1, source_target_pairs={{3,0},{0,1},{1,2},{2,3},{7,4},{4,5},{5,6},{6,7},{11,8},{8,9},{9,10... | collective-permute-start | bytes 2359304 | tf_op jit(solution)/shard_map/ppermute | solution.py:31
  27.3 31.8 %collective-permute-start.12 = (bf16[2,3,64,1024]{3,2,1,0:T(8,128)(2,1)}, bf16[2,3,64,1024]{3,2,1,0:T(8,128)(2,1)}, u32[]{:S(2)}, u32[]{:S(2)}) collective-permute-start(bf16[2,3,64,1024]{3,2,1,0:T(8,128)(2,1)} %pair.2.refs_0_), channel_id=1, source_target_pairs={{3,0},{0,1},{1,2},{2,3},{7,4},{4,5},{5,6},{6,7},{11,8},{8,9},{9,10... | collective-permute-start | bytes 2359304 | tf_op jit(solution)/shard_map/ppermute | solution.py:31
  30.1 29.6 %collective-permute-start.11 = (bf16[2,3,64,1024]{3,2,1,0:T(8,128)(2,1)}, bf16[2,3,64,1024]{3,2,1,0:T(8,128)(2,1)}, u32[]{:S(2)}, u32[]{:S(2)}) collective-permute-start(bf16[2,3,64,1024]{3,2,1,0:T(8,128)(2,1)} %pair.3.refs_1_), channel_id=1, source_target_pairs={{1,0},{2,1},{3,2},{0,3},{5,4},{6,5},{7,6},{4,7},{9,8},{10,9},{11,1... | collective-permute-start | bytes 2359304 | tf_op jit(solution)/shard_map/ppermute | solution.py:31
  32.6 1.9 copy-start
  34.5 53.6 %copy-start.1 = (bf16[1024,3,512]{2,0,1:T(8,128)(2,1)S(1)}, bf16[1024,3,512]{2,0,1:T(8,128)(2,1)}, u32[]{:S(2)}) copy-start(bf16[1024,3,512]{2,0,1:T(8,128)(2,1)} %param.5) | copy-start | bytes 9437188
  37.8 0.7 copy-start.5
  39.3 55.9 %all-to-all-start = ((bf16[4,3,64,256]{3,2,1,0:T(8,128)(2,1)}), bf16[4,3,64,256]{3,2,1,0:T(8,128)(2,1)}, u32[]{:S(2)}, u32[]{:S(2)}) async-start(bf16[4,3,64,256]{3,2,1,0:T(8,128)(2,1)} %bitcast.48), calls=%async_computation | async-start | bytes 786432 | tf_op jit(solution)/shard_map/all_to_all | solution.py:387
  52.3 142.2 %all-gather.4.cloned.1.call-start = ((), (), s32[]{:S(2)}) async-start(), calls=%async_computation.1 | async-start | bytes 6684672 | tf_op jit(solution)/shard_map/all_gather | solution.py:433
  52.3 35.8 %copy-start.6 = (bf16[4,64,512]{2,1,0:T(8,128)(2,1)S(1)}, bf16[4,64,512]{2,1,0:T(8,128)(2,1)}, u32[]{:S(2)}) copy-start(bf16[4,64,512]{2,1,0:T(8,128)(2,1)} %copy-done.5) | copy-start | bytes 786436
  52.3 35.8 %collective-permute-start.5 = (bf16[2,3,64,1024]{3,2,1,0:T(8,128)(2,1)}, bf16[2,3,64,1024]{3,2,1,0:T(8,128)(2,1)S(1)}, u32[]{:S(2)}, u32[]{:S(2)}) collective-permute-start(bf16[2,3,64,1024]{3,2,1,0:T(8,128)(2,1)} %collective-permute-done.1.refs_0_), channel_id=1, source_target_pairs={{1,0},{2,1},{3,2},{0,3},{5,4},{6,5},{7,6},{4,7},{9,8},{10,9},{11,1... | collective-permute-start | bytes 2359304 | tf_op jit(solution)/shard_map/ppermute | solution.py:31
  55.8 32.3 %collective-permute-start.6 = (bf16[2,3,64,1024]{3,2,1,0:T(8,128)(2,1)}, bf16[2,3,64,1024]{3,2,1,0:T(8,128)(2,1)S(1)}, u32[]{:S(2)}, u32[]{:S(2)}) collective-permute-start(bf16[2,3,64,1024]{3,2,1,0:T(8,128)(2,1)} %collective-permute-done.4.refs_3_), channel_id=1, source_target_pairs={{3,0},{0,1},{1,2},{2,3},{7,4},{4,5},{5,6},{6,7},{11,8},{8,9},{9,10... | collective-permute-start | bytes 2359304 | tf_op jit(solution)/shard_map/ppermute | solution.py:31
  57.8 15.3 %collective-permute-start.10 = (bf16[16,512]{1,0:T(8,128)(2,1)S(1)}, bf16[16,512]{1,0:T(8,128)(2,1)S(1)}, u32[]{:S(2)}, u32[]{:S(2)}) collective-permute-start(bf16[16,512]{1,0:T(8,128)(2,1)S(1)} %get-tuple-element.59), channel_id=1, source_target_pairs={{2,1},{4,65},{6,129},{8,193},{10,257},{12,321},{14,385},{66,3},{68... | collective-permute-start | bytes 49160 | tf_op jit(solution)/shard_map/ppermute | solution.py:380
  59.1 29.0 %collective-permute-start.9 = (bf16[16,512]{1,0:T(8,128)(2,1)S(1)}, bf16[16,512]{1,0:T(8,128)(2,1)S(1)}, u32[]{:S(2)}, u32[]{:S(2)}) collective-permute-start(bf16[16,512]{1,0:T(8,128)(2,1)S(1)} %get-tuple-element.60), channel_id=1, source_target_pairs={{2,0},{4,64},{6,128},{8,192},{10,256},{12,320},{14,384},{66,2},{68... | collective-permute-start | bytes 49160 | tf_op jit(solution)/shard_map/ppermute | solution.py:379
  59.8 28.3 %collective-permute-start.8 = (bf16[64,512]{1,0:T(8,128)(2,1)S(1)}, bf16[64,512]{1,0:T(8,128)(2,1)S(1)}, u32[]{:S(2)}, u32[]{:S(2)}) collective-permute-start(bf16[64,512]{1,0:T(8,128)(2,1)S(1)} %get-tuple-element.61), channel_id=1, source_target_pairs={{0,1},{1,0},{2,65},{3,64},{4,129},{5,128},{6,193},{7,192},{8,257},... | collective-permute-start | bytes 196616 | tf_op jit(solution)/shard_map/ppermute | solution.py:378
  73.1 15.0 %collective-permute-start.7 = (bf16[64,512]{1,0:T(8,128)(2,1)S(1)}, bf16[64,512]{1,0:T(8,128)(2,1)S(1)}, u32[]{:S(2)}, u32[]{:S(2)}) collective-permute-start(bf16[64,512]{1,0:T(8,128)(2,1)S(1)} %get-tuple-element.62), channel_id=1, source_target_pairs={{0,0},{1,1},{2,64},{3,65},{4,128},{5,129},{6,192},{7,193},{8,256},... | collective-permute-start | bytes 196616 | tf_op jit(solution)/shard_map/ppermute | solution.py:377
  82.5 31.3 %copy-start.11 = (s32[4]{0:T(128)S(1)}, s32[4]{0:T(128)}, u32[]{:S(2)}) copy-start(s32[4]{0:T(128)} %param.7) | copy-start | bytes 52
  82.5 41.3 %copy-start.9 = (f32[512]{0:T(512)S(1)}, f32[512]{0:T(512)}, u32[]{:S(2)}) copy-start(f32[512]{0:T(512)} %param.6) | copy-start | bytes 6148
  88.2 1.0 copy-start.4
  92.5 0.8 copy-start.7
  93.3 4.1 %collective-permute-start.13 = (bf16[4,144,512]{2,1,0:T(8,128)(2,1)}, bf16[4,144,512]{2,1,0:T(8,128)(2,1)S(1)}, u32[]{:S(2)}, u32[]{:S(2)}) collective-permute-start(bf16[4,144,512]{2,1,0:T(8,128)(2,1)} %get-tuple-element.36), channel_id=1, source_target_pairs={{64,0},{0,64},{192,128},{128,192},{320,256},{256,320},{448,384},{3... | collective-permute-start | bytes 1769480 | tf_op jit(solution)/shard_map/ppermute | solution.py:35
  100.1 1.1 copy-start.8
  101.4 16.6 %collective-permute-start.14 = (bf16[144,512]{1,0:T(8,128)(2,1)S(1)}, bf16[144,512]{1,0:T(8,128)(2,1)S(1)}, u32[]{:S(2)}, u32[]{:S(2)}) collective-permute-start(bf16[144,512]{1,0:T(8,128)(2,1)S(1)} %get-tuple-element.39), channel_id=1, source_target_pairs={{128,0},{192,64},{256,128},{320,192},{384,256},{448,320},{0,384},{... | collective-permute-start | bytes 442376 | tf_op jit(solution)/shard_map/ppermute | solution.py:40
  103.3 17.4 %collective-permute-start.15 = (bf16[144,512]{1,0:T(8,128)(2,1)S(1)}, bf16[144,512]{1,0:T(8,128)(2,1)S(1)}, u32[]{:S(2)}, u32[]{:S(2)}) collective-permute-start(bf16[144,512]{1,0:T(8,128)(2,1)S(1)} %get-tuple-element.40), channel_id=1, source_target_pairs={{256,0},{320,64},{384,128},{448,192},{0,256},{64,320},{128,384},{1... | collective-permute-start | bytes 442376 | tf_op jit(solution)/shard_map/ppermute | solution.py:40
  111.9 11.9 %collective-permute-start.16 = (bf16[144,512]{1,0:T(8,128)(2,1)S(1)}, bf16[144,512]{1,0:T(8,128)(2,1)S(1)}, u32[]{:S(2)}, u32[]{:S(2)}) collective-permute-start(bf16[144,512]{1,0:T(8,128)(2,1)S(1)} %get-tuple-element.41), channel_id=1, source_target_pairs={{384,0},{448,64},{0,128},{64,192},{128,256},{192,320},{256,384},{3... | collective-permute-start | bytes 442376 | tf_op jit(solution)/shard_map/ppermute | solution.py:40
  156.1 38.3 %collective-permute-start.19 = (bf16[4,144,512]{2,1,0:T(8,128)(2,1)S(1)}, bf16[4,144,512]{2,1,0:T(8,128)(2,1)S(1)}, u32[]{:S(2)}, u32[]{:S(2)}) collective-permute-start(bf16[4,144,512]{2,1,0:T(8,128)(2,1)S(1)} %bitcast.36), channel_id=1, source_target_pairs={{64,0},{0,64},{192,128},{128,192},{320,256},{256,320},{448,384},{3... | collective-permute-start | bytes 1769480 | tf_op jit(solution)/shard_map/ppermute | solution.py:35
  158.9 35.5 %collective-permute-start.18 = (bf16[4,144,512]{2,1,0:T(8,128)(2,1)S(1)}, bf16[4,144,512]{2,1,0:T(8,128)(2,1)S(1)}, u32[]{:S(2)}, u32[]{:S(2)}) collective-permute-start(bf16[4,144,512]{2,1,0:T(8,128)(2,1)S(1)} %bitcast.37), channel_id=1, source_target_pairs={{432,0},{384,16},{400,32},{416,48},{496,64},{448,80},{464,96},{480... | collective-permute-start | bytes 1769480 | tf_op jit(solution)/shard_map/ppermute | solution.py:53
  160.8 33.6 %collective-permute-start.17 = (bf16[4,144,512]{2,1,0:T(8,128)(2,1)S(1)}, bf16[4,144,512]{2,1,0:T(8,128)(2,1)S(1)}, u32[]{:S(2)}, u32[]{:S(2)}) collective-permute-start(bf16[4,144,512]{2,1,0:T(8,128)(2,1)S(1)} %bitcast.38), channel_id=1, source_target_pairs={{128,0},{144,16},{160,32},{176,48},{192,64},{208,80},{224,96},{240... | collective-permute-start | bytes 1769480 | tf_op jit(solution)/shard_map/ppermute | solution.py:53
  164.2 19.4 %collective-permute-start.21 = (bf16[2,144,512]{2,1,0:T(8,128)(2,1)S(1)}, bf16[2,144,512]{2,1,0:T(8,128)(2,1)S(1)}, u32[]{:S(2)}, u32[]{:S(2)}) collective-permute-start(bf16[2,144,512]{2,1,0:T(8,128)(2,1)S(1)} %bitcast.50), channel_id=1, source_target_pairs={{304,0},{256,16},{272,32},{288,48},{368,64},{320,80},{336,96},{352... | collective-permute-start | bytes 884744 | tf_op jit(solution)/shard_map/ppermute | solution.py:53
  170.6 23.8 %collective-permute-start.20 = (bf16[2,144,512]{2,1,0:T(8,128)(2,1)S(1)}, bf16[2,144,512]{2,1,0:T(8,128)(2,1)S(1)}, u32[]{:S(2)}, u32[]{:S(2)}) collective-permute-start(bf16[2,144,512]{2,1,0:T(8,128)(2,1)S(1)} %bitcast.49), channel_id=1, source_target_pairs={{256,0},{272,16},{288,32},{304,48},{320,64},{336,80},{352,96},{368... | collective-permute-start | bytes 884744 | tf_op jit(solution)/shard_map/ppermute | solution.py:53
  194.5 7.5 %collective-permute-start.22 = (bf16[4,144,512]{2,1,0:T(8,128)(2,1)S(1)}, bf16[4,144,512]{2,1,0:T(8,128)(2,1)S(1)}, u32[]{:S(2)}, u32[]{:S(2)}) collective-permute-start(bf16[4,144,512]{2,1,0:T(8,128)(2,1)S(1)} %collective-permute-done.17.refs_2_), channel_id=1, source_target_pairs={{64,0},{0,64},{192,128},{128,192},{320,256},{256,320},{448,384},{3... | collective-permute-start | bytes 1769480 | tf_op jit(solution)/shard_map/ppermute | solution.py:35
  197.5 4.5 %collective-permute-start.23 = (bf16[4,144,512]{2,1,0:T(8,128)(2,1)S(1)}, bf16[4,144,512]{2,1,0:T(8,128)(2,1)}, u32[]{:S(2)}, u32[]{:S(2)}) collective-permute-start(bf16[4,144,512]{2,1,0:T(8,128)(2,1)S(1)} %collective-permute-done.18.refs_3_), channel_id=1, source_target_pairs={{64,0},{0,64},{192,128},{128,192},{320,256},{256,320},{448,384},{3... | collective-permute-start | bytes 1769480 | tf_op jit(solution)/shard_map/ppermute | solution.py:35
  199.4 4.2 %collective-permute-start.24 = (bf16[4,144,512]{2,1,0:T(8,128)(2,1)S(1)}, bf16[4,144,512]{2,1,0:T(8,128)(2,1)}, u32[]{:S(2)}, u32[]{:S(2)}) collective-permute-start(bf16[4,144,512]{2,1,0:T(8,128)(2,1)S(1)} %pad_maximum_fusion.refs_4_), channel_id=1, source_target_pairs={{64,0},{0,64},{192,128},{128,192},{320,256},{256,320},{448,384},{3... | collective-permute-start | bytes 1769480 | tf_op jit(solution)/shard_map/ppermute | solution.py:35
  203.6 2.8 %copy-start.10 = (bf16[48,256,256]{2,1,0:T(8,128)(2,1)S(1)}, bf16[48,256,256]{2,1,0:T(8,128)(2,1)}, u32[]{:S(2)}) copy-start(bf16[48,256,256]{2,1,0:T(8,128)(2,1)} %all-gather.4.cloned.1.call-done) | copy-start | bytes 18874372
Sparse Core Ops, SparseCore 0:
  100.3 79.3 all-gather.3

commit v11 on v10

--- a/solution.py
+++ b/solution.py
@@ -418,6 +418,8 @@
     weight = fc_weight.transpose(1, 0, 2)
 
     next_, last, across = (plane_move(step, True)(own) for step in (1, 3, 2))
+    halves = send_high(own[LEVELS - 1], draft_index)
+    last, across, halves = lax.optimization_barrier((last, across, halves))
     low, high = pair(own, next_), pair(across, last)
     up_low, down_high = plane_move(1, False)(low), plane_move(-1, False)(high)
     up_high, down_low = plane_move(1, False)(high), plane_move(-1, False)(low)
@@ -425,9 +427,8 @@
     up_low, down_high, zero, later = lax.optimization_barrier((up_low, down_high, zero, own))
     traded = trade_columns(later)
     far_low, far_high = plane_move(1, False)(up_low), plane_move(-1, False)(down_high)
-    halves = send_high(later[LEVELS - 1], draft_index)
     sides = project([up_low, up_high, down_low, down_high], weight, 58)
-    far_low, far_high, halves, sides = lax.optimization_barrier((far_low, far_high, halves, sides))
+    far_low, far_high, sides = lax.optimization_barrier((far_low, far_high, sides))
     keep, send = project_place([far_low, far_high], weight, zero, sides, core, x, y)
     got, traded = lax.optimization_barrier((from_other_core(send), traded))
     every = lax.all_gather(turn(traded), "draft", axis=0, tiled=False)

time: 220 us -> 229 us (1.041)
  the two profiles are of different devices: /device:TPU:75 before, /device:TPU:1 now
where the time goes in v11:
time: 229 us; the launch traced here: 228 us
  starting transfers between devices  107 us (47%)
  blocking collectives  35.1 us (15%)
  waiting for transfers between devices  27.8 us (12%)
  Pallas kernels  24.2 us (11%)
  between operations  16.5 us (7%)
  local copies, waits for them, and re-layouts  15.4 us (7%)
    ppermute x9, starting transfers between devices, plane_move(): return lambda block: lax.ppermute(block, ('tp', 'draft'), pairs)  44.1 us
    all_gather x1, blocking collectives, gather_grads(): stack = lax.all_gather(grad, 'dp', axis=0, tiled=False)  35.1 us
    ppermute x4, waiting for transfers between devices, from_z(): return lax.ppermute(block, ('tp', 'dp'), pairs)  18.4 us
    ppermute x4, starting transfers between devices, from_z(): return lax.ppermute(block, ('tp', 'dp'), pairs)  13.9 us
    ppermute x5, starting transfers between devices, from_other_core(): return lax.ppermute(block, 'tp', [(t ^ 1, t) for t in range(ZL * CORES)])  13 us
    unnamed x34, local copies, waits for them, and re-layouts  12.3 us
    all_to_all x1, starting transfers between devices, trade_columns(): lax.all_to_all(quarters, 'dp', split_axis=0, concat_axis=0, tiled=True)  12 us
    ppermute x1, starting transfers between devices, send_high(): lax.ppermute(jnp.where(even, right, left), axes, crossed)  8.9 us
  transfers between devices with their start and end apart: 27, of which 7 were waited for; matrix products, arithmetic and copies ran while one was open for 2% of the time, Pallas kernels for 7%

profile of v11, /device:TPU:1, one launch (start us, length us, event | category | flops | bytes accessed | tf_op | source)
XLA Modules:
  0.0 228.0 jit_solution(4285006886733752398)
XLA Ops:
  7.2 5.8 %collective-permute-start.3 = (bf16[3,64,1024]{2,1,0:T(8,128)(2,1)}, bf16[3,64,1024]{2,1,0:T(8,128)(2,1)S(1)}, u32[]{:S(2)}, u32[]{:S(2)}) collective-permute-start(bf16[3,64,1024]{2,1,0:T(8,128)(2,1)} %bitcast.40), channel_id=1, source_target_pairs={{8,0},{9,1},{10,2},{11,3},{12,4},{13,5},{14,6},{15,7},{0,8},{1,9},... | collective-permute-start | bytes 1179656 | tf_op jit(solution)/shard_map/ppermute | solution.py:31
  13.0 2.3 %collective-permute-start.2 = (bf16[3,64,1024]{2,1,0:T(8,128)(2,1)}, bf16[3,64,1024]{2,1,0:T(8,128)(2,1)S(1)}, u32[]{:S(2)}, u32[]{:S(2)}) collective-permute-start(bf16[3,64,1024]{2,1,0:T(8,128)(2,1)} %bitcast.41), channel_id=1, source_target_pairs={{12,0},{13,1},{14,2},{15,3},{0,4},{1,5},{2,6},{3,7},{4,8},{5,9},{6... | collective-permute-start | bytes 1179656 | tf_op jit(solution)/shard_map/ppermute | solution.py:31
  15.3 4.2 %collective-permute-start = (bf16[3,64,1024]{2,1,0:T(8,128)(2,1)}, bf16[3,64,1024]{2,1,0:T(8,128)(2,1)S(1)}, u32[]{:S(2)}, u32[]{:S(2)}) collective-permute-start(bf16[3,64,1024]{2,1,0:T(8,128)(2,1)} %bitcast.42), channel_id=1, source_target_pairs={{4,0},{5,1},{6,2},{7,3},{8,4},{9,5},{10,6},{11,7},{12,8},{13,9},{1... | collective-permute-start | bytes 1179656 | tf_op jit(solution)/shard_map/ppermute | solution.py:31
  19.5 0.9 slice_bitcast_fusion
  20.4 0.7 collective-permute-start.7
  21.1 1.3 collective-permute-start.6
  22.4 8.9 %collective-permute-start.5 = (bf16[64,512]{1,0:T(8,128)(2,1)S(1)}, bf16[64,512]{1,0:T(8,128)(2,1)S(1)}, u32[]{:S(2)}, u32[]{:S(2)}) collective-permute-start(bf16[64,512]{1,0:T(8,128)(2,1)S(1)} %get-tuple-element.65), channel_id=1, source_target_pairs={{0,1},{1,0},{2,65},{3,64},{4,129},{5,128},{6,193},{7,192},{8,257},... | collective-permute-start | bytes 196616 | tf_op jit(solution)/shard_map/ppermute | solution.py:378
  31.4 0.6 copy-done.13
  32.0 5.1 %collective-permute-start.4 = (bf16[64,512]{1,0:T(8,128)(2,1)S(1)}, bf16[64,512]{1,0:T(8,128)(2,1)S(1)}, u32[]{:S(2)}, u32[]{:S(2)}) collective-permute-start(bf16[64,512]{1,0:T(8,128)(2,1)S(1)} %get-tuple-element.66), channel_id=1, source_target_pairs={{0,0},{1,1},{2,64},{3,65},{4,128},{5,129},{6,192},{7,193},{8,256},... | collective-permute-start | bytes 196616 | tf_op jit(solution)/shard_map/ppermute | solution.py:377
  37.1 2.0 collective-permute-done.4.refs_4_
  39.1 1.0 copy-done.2
  40.1 0.9 pair.2.refs_0_
  41.0 18.1 %collective-permute-start.1 = (bf16[2,3,64,1024]{3,2,1,0:T(8,128)(2,1)}, bf16[2,3,64,1024]{3,2,1,0:T(8,128)(2,1)}, u32[]{:S(2)}, u32[]{:S(2)}) collective-permute-start(bf16[2,3,64,1024]{3,2,1,0:T(8,128)(2,1)} %pair.2.refs_0_), channel_id=1, source_target_pairs={{1,0},{2,1},{3,2},{0,3},{5,4},{6,5},{7,6},{4,7},{9,8},{10,9},{11,1... | collective-permute-start | bytes 2359304 | tf_op jit(solution)/shard_map/ppermute | solution.py:31
  59.1 0.9 pair.3.refs_1_
  60.1 1.9 collective-permute-start.8
  62.0 1.9 collective-permute-start.12
  63.9 4.6 %collective-permute-start.11 = (bf16[2,3,64,1024]{3,2,1,0:T(8,128)(2,1)}, bf16[2,3,64,1024]{3,2,1,0:T(8,128)(2,1)}, u32[]{:S(2)}, u32[]{:S(2)}) collective-permute-start(bf16[2,3,64,1024]{3,2,1,0:T(8,128)(2,1)} %pair.3.refs_1_), channel_id=1, source_target_pairs={{1,0},{2,1},{3,2},{0,3},{5,4},{6,5},{7,6},{4,7},{9,8},{10,9},{11,1... | collective-permute-start | bytes 2359304 | tf_op jit(solution)/shard_map/ppermute | solution.py:31
  68.5 1.9 copy-done
  70.4 3.2 %project.2.refs_3_ = bf16[4,64,512]{2,1,0:T(8,128)(2,1)S(1)} custom-call(bf16[2,3,64,1024]{3,2,1,0:T(8,128)(2,1)} %pair.2.refs_0_, bf16[2,3,64,1024]{3,2,1,0:T(8,128)(2,1)} %pair.3.refs_1_, bf16[3,1024,512]{2,1,0:T(8,128)(2,1)S(1)} %bitcast.34), custom_call_target="tpu_custom_call" | custom-call | bytes 1572864 | tf_op jit(solution)/shard_map/project/pallas_call | solution.py:114
  73.6 1.0 collective-permute-done.8.refs_3_
  74.6 2.4 %collective-permute-start.9 = (bf16[2,3,64,1024]{3,2,1,0:T(8,128)(2,1)}, bf16[2,3,64,1024]{3,2,1,0:T(8,128)(2,1)}, u32[]{:S(2)}, u32[]{:S(2)}) collective-permute-start(bf16[2,3,64,1024]{3,2,1,0:T(8,128)(2,1)} %collective-permute-done.1.refs_0_), channel_id=1, source_target_pairs={{1,0},{2,1},{3,2},{0,3},{5,4},{6,5},{7,6},{4,7},{9,8},{10,9},{11,1... | collective-permute-start | bytes 2359304 | tf_op jit(solution)/shard_map/ppermute | solution.py:31
  77.0 2.9 %collective-permute-start.10 = (bf16[2,3,64,1024]{3,2,1,0:T(8,128)(2,1)}, bf16[2,3,64,1024]{3,2,1,0:T(8,128)(2,1)}, u32[]{:S(2)}, u32[]{:S(2)}) collective-permute-start(bf16[2,3,64,1024]{3,2,1,0:T(8,128)(2,1)} %collective-permute-done.8.refs_3_), channel_id=1, source_target_pairs={{3,0},{0,1},{1,2},{2,3},{7,4},{4,5},{5,6},{6,7},{11,8},{8,9},{9,10... | collective-permute-start | bytes 2359304 | tf_op jit(solution)/shard_map/ppermute | solution.py:31
  79.9 0.8 copy.10
  80.7 12.0 %all-to-all-start = ((bf16[4,3,64,256]{3,2,1,0:T(8,128)(2,1)}), bf16[4,3,64,256]{3,2,1,0:T(8,128)(2,1)S(1)}, u32[]{:S(2)}, u32[]{:S(2)}) async-start(bf16[4,3,64,256]{3,2,1,0:T(8,128)(2,1)} %bitcast.48), calls=%async_computation | async-start | bytes 786432 | tf_op jit(solution)/shard_map/all_to_all | solution.py:387
  92.7 0.1 pad_add_fusion.1.meta_ref
  92.8 5.5 %project.3.refs_4_ = bf16[8,64,512]{2,1,0:T(8,128)(2,1)} custom-call(bf16[2,3,64,1024]{3,2,1,0:T(8,128)(2,1)} %collective-permute-done.1.refs_0_, bf16[2,3,64,1024]{3,2,1,0:T(8,128)(2,1)} %collective-permute-done.11.refs_1_, bf16[2,3,64,1024]{3,2,1,0:T(8,128)(2,1)} %collective-permute-done.12.refs_2_, ...), custom_call_target="tpu_custom_call" | custom-call | bytes 3145728 | tf_op jit(solution)/shard_map/project/pallas_call | solution.py:114
  98.4 1.0 copy-done.4
  99.4 4.7 %project_place.1 = (bf16[4,144,512]{2,1,0:T(8,128)(2,1)S(1)}, bf16[4,144,512]{2,1,0:T(8,128)(2,1)}) custom-call(s32[3]{0:T(128)S(1)} %pad_add_fusion.1.meta_ref, bf16[2,3,64,1024]{3,2,1,0:T(8,128)(2,1)} %collective-permute-done.9.refs_0_, bf16[2,3,64,1024]{3,2,1,0:T(8,128)(2,1)} %collective-permute-done.10.refs_1_, bf16[3,1024,512]{2,1,0:T(8,128)(2,1)S(1)} %bitcast.35, ...), custom_call_target="tpu_custom_call" | custom-call | bytes 1572864 | tf_op jit(solution)/shard_map/project_place/pallas_call | solution.py:167
  104.1 0.8 copy-done.7
  104.9 1.9 collective-permute-start.13
  106.8 4.4 %all-to-all-done.traded_ref = bf16[4,3,64,256]{3,2,1,0:T(8,128)(2,1)S(1)} async-done(((bf16[4,3,64,256]{3,2,1,0:T(8,128)(2,1)}), bf16[4,3,64,256]{3,2,1,0:T(8,128)(2,1)S(1)}, u32[]{:S(2)}, u32[]{:S(2)}) %all-to-all-start) | async-done | bytes 393248 | tf_op jit(solution)/shard_map/all_to_all | solution.py:387
  111.2 1.6 turn.1
  112.8 0.0 all-gather.4.cloned.1.call-update
  112.8 1.1 copy-done.8
  113.9 0.1 join.1
  114.0 1.9 collective-permute-start.14
  115.9 4.0 %collective-permute-start.15 = (bf16[144,512]{1,0:T(8,128)(2,1)S(1)}, bf16[144,512]{1,0:T(8,128)(2,1)S(1)}, u32[]{:S(2)}, u32[]{:S(2)}) collective-permute-start(bf16[144,512]{1,0:T(8,128)(2,1)S(1)} %get-tuple-element.44), channel_id=1, source_target_pairs={{256,0},{320,64},{384,128},{448,192},{0,256},{64,320},{128,384},{1... | collective-permute-start | bytes 442376 | tf_op jit(solution)/shard_map/ppermute | solution.py:40
  119.9 1.9 collective-permute-start.16
  121.9 1.4 maximum_reduce_fusion
  123.3 1.3 dynamic_slice.3
  126.5 0.7 pad_add_fusion.meta_ref
  127.2 0.5 collective-permute-done.16.refs_3_
  127.7 0.8 copy-done.10
  128.5 0.8 copy-done.12
  129.4 0.7 copy-done.14
  130.1 0.7 copy-done.15
  130.8 1.4 chain.1
  132.2 35.1 %all-gather = bf16[576,512]{1,0:T(8,128)(2,1)S(1)} all-gather(bf16[144,512]{1,0:T(8,128)(2,1)S(1)} %chain.1), channel_id=2, replica_groups=mesh['tp'=8,'dp'=4,'draft'=16] {'dp'}, dimensions={0}, use_global_device_ids=true | all-gather | bytes 737280 | tf_op jit(solution)/shard_map/all_gather | solution.py:391
  167.3 3.7 %collective-permute-start.19 = (bf16[4,144,512]{2,1,0:T(8,128)(2,1)S(1)}, bf16[4,144,512]{2,1,0:T(8,128)(2,1)S(1)}, u32[]{:S(2)}, u32[]{:S(2)}) collective-permute-start(bf16[4,144,512]{2,1,0:T(8,128)(2,1)S(1)} %bitcast.36), channel_id=1, source_target_pairs={{64,0},{0,64},{192,128},{128,192},{320,256},{256,320},{448,384},{3... | collective-permute-start | bytes 1769480 | tf_op jit(solution)/shard_map/ppermute | solution.py:35
  171.0 1.9 collective-permute-start.18
  172.9 4.6 %collective-permute-start.17 = (bf16[4,144,512]{2,1,0:T(8,128)(2,1)S(1)}, bf16[4,144,512]{2,1,0:T(8,128)(2,1)S(1)}, u32[]{:S(2)}, u32[]{:S(2)}) collective-permute-start(bf16[4,144,512]{2,1,0:T(8,128)(2,1)S(1)} %bitcast.38), channel_id=1, source_target_pairs={{128,0},{144,16},{160,32},{176,48},{192,64},{208,80},{224,96},{240... | collective-permute-start | bytes 1769480 | tf_op jit(solution)/shard_map/ppermute | solution.py:53
  177.6 1.9 collective-permute-start.21
  179.5 5.5 %collective-permute-start.20 = (bf16[2,144,512]{2,1,0:T(8,128)(2,1)S(1)}, bf16[2,144,512]{2,1,0:T(8,128)(2,1)S(1)}, u32[]{:S(2)}, u32[]{:S(2)}) collective-permute-start(bf16[2,144,512]{2,1,0:T(8,128)(2,1)S(1)} %bitcast.49), channel_id=1, source_target_pairs={{256,0},{272,16},{288,32},{304,48},{320,64},{336,80},{352,96},{368... | collective-permute-start | bytes 884744 | tf_op jit(solution)/shard_map/ppermute | solution.py:53
  185.0 8.8 %collective-permute-done.21 = bf16[2,144,512]{2,1,0:T(8,128)(2,1)S(1)} collective-permute-done((bf16[2,144,512]{2,1,0:T(8,128)(2,1)S(1)}, bf16[2,144,512]{2,1,0:T(8,128)(2,1)S(1)}, u32[]{:S(2)}, u32[]{:S(2)}) %collective-permute-start.21) | collective-permute-done | bytes 294944 | tf_op jit(solution)/shard_map/ppermute | solution.py:53
  193.7 9.6 %collective-permute-done.20 = bf16[2,144,512]{2,1,0:T(8,128)(2,1)S(1)} collective-permute-done((bf16[2,144,512]{2,1,0:T(8,128)(2,1)S(1)}, bf16[2,144,512]{2,1,0:T(8,128)(2,1)S(1)}, u32[]{:S(2)}, u32[]{:S(2)}) %collective-permute-start.20) | collective-permute-done | bytes 294944 | tf_op jit(solution)/shard_map/ppermute | solution.py:53
  203.3 0.1 pad_maximum_fusion.refs_4_
  203.4 0.0 all-gather.4.cloned.1.call-done
  203.4 3.0 %collective-permute-start.22 = (bf16[4,144,512]{2,1,0:T(8,128)(2,1)S(1)}, bf16[4,144,512]{2,1,0:T(8,128)(2,1)S(1)}, u32[]{:S(2)}, u32[]{:S(2)}) collective-permute-start(bf16[4,144,512]{2,1,0:T(8,128)(2,1)S(1)} %collective-permute-done.17.refs_2_), channel_id=1, source_target_pairs={{64,0},{0,64},{192,128},{128,192},{320,256},{256,320},{448,384},{3... | collective-permute-start | bytes 1769480 | tf_op jit(solution)/shard_map/ppermute | solution.py:35
  206.5 1.9 collective-permute-start.23
  208.4 2.4 %collective-permute-start.24 = (bf16[4,144,512]{2,1,0:T(8,128)(2,1)S(1)}, bf16[4,144,512]{2,1,0:T(8,128)(2,1)}, u32[]{:S(2)}, u32[]{:S(2)}) collective-permute-start(bf16[4,144,512]{2,1,0:T(8,128)(2,1)S(1)} %pad_maximum_fusion.refs_4_), channel_id=1, source_target_pairs={{64,0},{0,64},{192,128},{128,192},{320,256},{256,320},{448,384},{3... | collective-permute-start | bytes 1769480 | tf_op jit(solution)/shard_map/ppermute | solution.py:35
  210.9 0.1 stack.56.meta_ref
  211.0 1.6 collective-permute-done.24.refs_7_
  212.6 2.8 %copy-done.16 = bf16[48,256,256]{2,1,0:T(8,128)(2,1)S(1)} copy-done((bf16[48,256,256]{2,1,0:T(8,128)(2,1)S(1)}, bf16[48,256,256]{2,1,0:T(8,128)(2,1)}, u32[]{:S(2)}) %copy-start.16) | copy-done | bytes 6291480
  215.3 5.8 %weight_grad.1 = (bf16[3,256,512]{2,1,0:T(8,128)(2,1)}, f32[1,512]{1,0:T(1,128)}) custom-call(s32[8]{0:T(128)S(1)} %stack.56.meta_ref, bf16[16,3,256,256]{3,2,1,0:T(8,128)(2,1)S(1)} %bitcast.47, bf16[4,144,512]{2,1,0:T(8,128)(2,1)S(1)} %bitcast.39, bf16[4,144,512]{2,1,0:T(8,128)(2,1)S(1)} %collective-permute-done.19.refs_1_, ...), custom_call_target="tpu_custom_call" | custom-call | flops 3221225472 | bytes 10485760 | tf_op jit(solution)/shard_map/weight_grad/pallas_call | solution.py:315
  (46 shorter events, 0.2 us)
Async XLA Ops:
  7.2 72.7 %copy-start.3 = (bf16[64,3,1024]{2,0,1:T(8,128)(2,1)S(1)}, bf16[64,3,1024]{2,0,1:T(8,128)(2,1)}, u32[]{:S(2)}) copy-start(bf16[64,3,1024]{2,0,1:T(8,128)(2,1)} %param.4) | copy-start | bytes 1179652
  7.2 31.9 %collective-permute-start.3 = (bf16[3,64,1024]{2,1,0:T(8,128)(2,1)}, bf16[3,64,1024]{2,1,0:T(8,128)(2,1)S(1)}, u32[]{:S(2)}, u32[]{:S(2)}) collective-permute-start(bf16[3,64,1024]{2,1,0:T(8,128)(2,1)} %bitcast.40), channel_id=1, source_target_pairs={{8,0},{9,1},{10,2},{11,3},{12,4},{13,5},{14,6},{15,7},{0,8},{1,9},... | collective-permute-start | bytes 1179656 | tf_op jit(solution)/shard_map/ppermute | solution.py:31
  13.0 26.1 %collective-permute-start.2 = (bf16[3,64,1024]{2,1,0:T(8,128)(2,1)}, bf16[3,64,1024]{2,1,0:T(8,128)(2,1)S(1)}, u32[]{:S(2)}, u32[]{:S(2)}) collective-permute-start(bf16[3,64,1024]{2,1,0:T(8,128)(2,1)} %bitcast.41), channel_id=1, source_target_pairs={{12,0},{13,1},{14,2},{15,3},{0,4},{1,5},{2,6},{3,7},{4,8},{5,9},{6... | collective-permute-start | bytes 1179656 | tf_op jit(solution)/shard_map/ppermute | solution.py:31
  15.3 23.8 %collective-permute-start = (bf16[3,64,1024]{2,1,0:T(8,128)(2,1)}, bf16[3,64,1024]{2,1,0:T(8,128)(2,1)S(1)}, u32[]{:S(2)}, u32[]{:S(2)}) collective-permute-start(bf16[3,64,1024]{2,1,0:T(8,128)(2,1)} %bitcast.42), channel_id=1, source_target_pairs={{4,0},{5,1},{6,2},{7,3},{8,4},{9,5},{10,6},{11,7},{12,8},{13,9},{1... | collective-permute-start | bytes 1179656 | tf_op jit(solution)/shard_map/ppermute | solution.py:31
  20.4 2.0 collective-permute-start.7
  21.1 10.3 %collective-permute-start.6 = (bf16[16,512]{1,0:T(8,128)(2,1)S(1)}, bf16[16,512]{1,0:T(8,128)(2,1)S(1)}, u32[]{:S(2)}, u32[]{:S(2)}) collective-permute-start(bf16[16,512]{1,0:T(8,128)(2,1)S(1)} %get-tuple-element.64), channel_id=1, source_target_pairs={{2,0},{4,64},{6,128},{8,192},{10,256},{12,320},{14,384},{66,2},{68... | collective-permute-start | bytes 49160 | tf_op jit(solution)/shard_map/ppermute | solution.py:379
  22.4 14.6 %collective-permute-start.5 = (bf16[64,512]{1,0:T(8,128)(2,1)S(1)}, bf16[64,512]{1,0:T(8,128)(2,1)S(1)}, u32[]{:S(2)}, u32[]{:S(2)}) collective-permute-start(bf16[64,512]{1,0:T(8,128)(2,1)S(1)} %get-tuple-element.65), channel_id=1, source_target_pairs={{0,1},{1,0},{2,65},{3,64},{4,129},{5,128},{6,193},{7,192},{8,257},... | collective-permute-start | bytes 196616 | tf_op jit(solution)/shard_map/ppermute | solution.py:378
  31.4 0.6 copy-start.13
  32.0 7.1 %collective-permute-start.4 = (bf16[64,512]{1,0:T(8,128)(2,1)S(1)}, bf16[64,512]{1,0:T(8,128)(2,1)S(1)}, u32[]{:S(2)}, u32[]{:S(2)}) collective-permute-start(bf16[64,512]{1,0:T(8,128)(2,1)S(1)} %get-tuple-element.66), channel_id=1, source_target_pairs={{0,0},{1,1},{2,64},{3,65},{4,128},{5,129},{6,192},{7,193},{8,256},... | collective-permute-start | bytes 196616 | tf_op jit(solution)/shard_map/ppermute | solution.py:377
  37.1 31.4 %copy-start.9 = (bf16[64,512]{1,0:T(8,128)(2,1)}, bf16[64,512]{1,0:T(8,128)(2,1)S(1)}, u32[]{:S(2)}) copy-start(bf16[64,512]{1,0:T(8,128)(2,1)S(1)} %collective-permute-done.5.refs_5_) | copy-start | bytes 196612
  39.0 29.5 %copy-start.11 = (bf16[64,512]{1,0:T(8,128)(2,1)}, bf16[64,512]{1,0:T(8,128)(2,1)S(1)}, u32[]{:S(2)}) copy-start(bf16[64,512]{1,0:T(8,128)(2,1)S(1)} %collective-permute-done.4.refs_4_) | copy-start | bytes 196612
  39.1 1.0 copy-start.2
  41.0 32.6 %collective-permute-start.1 = (bf16[2,3,64,1024]{3,2,1,0:T(8,128)(2,1)}, bf16[2,3,64,1024]{3,2,1,0:T(8,128)(2,1)}, u32[]{:S(2)}, u32[]{:S(2)}) collective-permute-start(bf16[2,3,64,1024]{3,2,1,0:T(8,128)(2,1)} %pair.2.refs_0_), channel_id=1, source_target_pairs={{1,0},{2,1},{3,2},{0,3},{5,4},{6,5},{7,6},{4,7},{9,8},{10,9},{11,1... | collective-permute-start | bytes 2359304 | tf_op jit(solution)/shard_map/ppermute | solution.py:31
  60.1 14.5 %collective-permute-start.8 = (bf16[2,3,64,1024]{3,2,1,0:T(8,128)(2,1)}, bf16[2,3,64,1024]{3,2,1,0:T(8,128)(2,1)}, u32[]{:S(2)}, u32[]{:S(2)}) collective-permute-start(bf16[2,3,64,1024]{3,2,1,0:T(8,128)(2,1)} %pair.3.refs_1_), channel_id=1, source_target_pairs={{3,0},{0,1},{1,2},{2,3},{7,4},{4,5},{5,6},{6,7},{11,8},{8,9},{9,10... | collective-permute-start | bytes 2359304 | tf_op jit(solution)/shard_map/ppermute | solution.py:31
  62.0 30.8 %collective-permute-start.12 = (bf16[2,3,64,1024]{3,2,1,0:T(8,128)(2,1)}, bf16[2,3,64,1024]{3,2,1,0:T(8,128)(2,1)}, u32[]{:S(2)}, u32[]{:S(2)}) collective-permute-start(bf16[2,3,64,1024]{3,2,1,0:T(8,128)(2,1)} %pair.2.refs_0_), channel_id=1, source_target_pairs={{3,0},{0,1},{1,2},{2,3},{7,4},{4,5},{5,6},{6,7},{11,8},{8,9},{9,10... | collective-permute-start | bytes 2359304 | tf_op jit(solution)/shard_map/ppermute | solution.py:31
  63.9 28.9 %collective-permute-start.11 = (bf16[2,3,64,1024]{3,2,1,0:T(8,128)(2,1)}, bf16[2,3,64,1024]{3,2,1,0:T(8,128)(2,1)}, u32[]{:S(2)}, u32[]{:S(2)}) collective-permute-start(bf16[2,3,64,1024]{3,2,1,0:T(8,128)(2,1)} %pair.3.refs_1_), channel_id=1, source_target_pairs={{1,0},{2,1},{3,2},{0,3},{5,4},{6,5},{7,6},{4,7},{9,8},{10,9},{11,1... | collective-permute-start | bytes 2359304 | tf_op jit(solution)/shard_map/ppermute | solution.py:31
  68.5 1.9 copy-start
  70.4 27.9 %copy-start.1 = (bf16[1024,3,512]{2,0,1:T(8,128)(2,1)S(1)}, bf16[1024,3,512]{2,0,1:T(8,128)(2,1)}, u32[]{:S(2)}) copy-start(bf16[1024,3,512]{2,0,1:T(8,128)(2,1)} %param.5) | copy-start | bytes 9437188
  73.6 7.1 %copy-start.5 = (bf16[4,64,512]{2,1,0:T(8,128)(2,1)}, bf16[4,64,512]{2,1,0:T(8,128)(2,1)S(1)}, u32[]{:S(2)}) copy-start(bf16[4,64,512]{2,1,0:T(8,128)(2,1)S(1)} %project.2.refs_3_) | copy-start | bytes 786436
  74.6 23.7 %collective-permute-start.9 = (bf16[2,3,64,1024]{3,2,1,0:T(8,128)(2,1)}, bf16[2,3,64,1024]{3,2,1,0:T(8,128)(2,1)}, u32[]{:S(2)}, u32[]{:S(2)}) collective-permute-start(bf16[2,3,64,1024]{3,2,1,0:T(8,128)(2,1)} %collective-permute-done.1.refs_0_), channel_id=1, source_target_pairs={{1,0},{2,1},{3,2},{0,3},{5,4},{6,5},{7,6},{4,7},{9,8},{10,9},{11,1... | collective-permute-start | bytes 2359304 | tf_op jit(solution)/shard_map/ppermute | solution.py:31
  77.0 21.3 %collective-permute-start.10 = (bf16[2,3,64,1024]{3,2,1,0:T(8,128)(2,1)}, bf16[2,3,64,1024]{3,2,1,0:T(8,128)(2,1)}, u32[]{:S(2)}, u32[]{:S(2)}) collective-permute-start(bf16[2,3,64,1024]{3,2,1,0:T(8,128)(2,1)} %collective-permute-done.8.refs_3_), channel_id=1, source_target_pairs={{3,0},{0,1},{1,2},{2,3},{7,4},{4,5},{5,6},{6,7},{11,8},{8,9},{9,10... | collective-permute-start | bytes 2359304 | tf_op jit(solution)/shard_map/ppermute | solution.py:31
  80.7 30.5 %all-to-all-start = ((bf16[4,3,64,256]{3,2,1,0:T(8,128)(2,1)}), bf16[4,3,64,256]{3,2,1,0:T(8,128)(2,1)S(1)}, u32[]{:S(2)}, u32[]{:S(2)}) async-start(bf16[4,3,64,256]{3,2,1,0:T(8,128)(2,1)} %bitcast.48), calls=%async_computation | async-start | bytes 786432 | tf_op jit(solution)/shard_map/all_to_all | solution.py:387
  92.7 110.7 %all-gather.4.cloned.1.call-start = ((), (), s32[]{:S(2)}) async-start(), calls=%async_computation.1 | async-start | bytes 6684672 | tf_op jit(solution)/shard_map/all_gather | solution.py:434
  92.7 5.6 %copy-start.6 = (bf16[4,64,512]{2,1,0:T(8,128)(2,1)S(1)}, bf16[4,64,512]{2,1,0:T(8,128)(2,1)}, u32[]{:S(2)}) copy-start(bf16[4,64,512]{2,1,0:T(8,128)(2,1)} %copy-done.5) | copy-start | bytes 786436
  98.4 1.0 copy-start.4
  104.1 0.8 copy-start.7
  104.9 6.3 %collective-permute-start.13 = (bf16[4,144,512]{2,1,0:T(8,128)(2,1)}, bf16[4,144,512]{2,1,0:T(8,128)(2,1)S(1)}, u32[]{:S(2)}, u32[]{:S(2)}) collective-permute-start(bf16[4,144,512]{2,1,0:T(8,128)(2,1)} %get-tuple-element.39), channel_id=1, source_target_pairs={{64,0},{0,64},{192,128},{128,192},{320,256},{256,320},{448,384},{3... | collective-permute-start | bytes 1769480 | tf_op jit(solution)/shard_map/ppermute | solution.py:35
  112.8 1.1 copy-start.8
  114.0 13.2 %collective-permute-start.14 = (bf16[144,512]{1,0:T(8,128)(2,1)S(1)}, bf16[144,512]{1,0:T(8,128)(2,1)S(1)}, u32[]{:S(2)}, u32[]{:S(2)}) collective-permute-start(bf16[144,512]{1,0:T(8,128)(2,1)S(1)} %get-tuple-element.43), channel_id=1, source_target_pairs={{128,0},{192,64},{256,128},{320,192},{384,256},{448,320},{0,384},{... | collective-permute-start | bytes 442376 | tf_op jit(solution)/shard_map/ppermute | solution.py:40
  115.9 11.3 %collective-permute-start.15 = (bf16[144,512]{1,0:T(8,128)(2,1)S(1)}, bf16[144,512]{1,0:T(8,128)(2,1)S(1)}, u32[]{:S(2)}, u32[]{:S(2)}) collective-permute-start(bf16[144,512]{1,0:T(8,128)(2,1)S(1)} %get-tuple-element.44), channel_id=1, source_target_pairs={{256,0},{320,64},{384,128},{448,192},{0,256},{64,320},{128,384},{1... | collective-permute-start | bytes 442376 | tf_op jit(solution)/shard_map/ppermute | solution.py:40
  119.9 7.8 %collective-permute-start.16 = (bf16[144,512]{1,0:T(8,128)(2,1)S(1)}, bf16[144,512]{1,0:T(8,128)(2,1)S(1)}, u32[]{:S(2)}, u32[]{:S(2)}) collective-permute-start(bf16[144,512]{1,0:T(8,128)(2,1)S(1)} %get-tuple-element.45), channel_id=1, source_target_pairs={{384,0},{448,64},{0,128},{64,192},{128,256},{192,320},{256,384},{3... | collective-permute-start | bytes 442376 | tf_op jit(solution)/shard_map/ppermute | solution.py:40
  127.7 0.8 copy-start.10
  128.5 0.8 copy-start.12
  129.4 0.7 copy-start.14
  130.1 0.7 copy-start.15
  167.3 36.1 %collective-permute-start.19 = (bf16[4,144,512]{2,1,0:T(8,128)(2,1)S(1)}, bf16[4,144,512]{2,1,0:T(8,128)(2,1)S(1)}, u32[]{:S(2)}, u32[]{:S(2)}) collective-permute-start(bf16[4,144,512]{2,1,0:T(8,128)(2,1)S(1)} %bitcast.36), channel_id=1, source_target_pairs={{64,0},{0,64},{192,128},{128,192},{320,256},{256,320},{448,384},{3... | collective-permute-start | bytes 1769480 | tf_op jit(solution)/shard_map/ppermute | solution.py:35
  171.0 32.4 %collective-permute-start.18 = (bf16[4,144,512]{2,1,0:T(8,128)(2,1)S(1)}, bf16[4,144,512]{2,1,0:T(8,128)(2,1)S(1)}, u32[]{:S(2)}, u32[]{:S(2)}) collective-permute-start(bf16[4,144,512]{2,1,0:T(8,128)(2,1)S(1)} %bitcast.37), channel_id=1, source_target_pairs={{432,0},{384,16},{400,32},{416,48},{496,64},{448,80},{464,96},{480... | collective-permute-start | bytes 1769480 | tf_op jit(solution)/shard_map/ppermute | solution.py:53
  172.9 30.5 %collective-permute-start.17 = (bf16[4,144,512]{2,1,0:T(8,128)(2,1)S(1)}, bf16[4,144,512]{2,1,0:T(8,128)(2,1)S(1)}, u32[]{:S(2)}, u32[]{:S(2)}) collective-permute-start(bf16[4,144,512]{2,1,0:T(8,128)(2,1)S(1)} %bitcast.38), channel_id=1, source_target_pairs={{128,0},{144,16},{160,32},{176,48},{192,64},{208,80},{224,96},{240... | collective-permute-start | bytes 1769480 | tf_op jit(solution)/shard_map/ppermute | solution.py:53
  177.6 16.2 %collective-permute-start.21 = (bf16[2,144,512]{2,1,0:T(8,128)(2,1)S(1)}, bf16[2,144,512]{2,1,0:T(8,128)(2,1)S(1)}, u32[]{:S(2)}, u32[]{:S(2)}) collective-permute-start(bf16[2,144,512]{2,1,0:T(8,128)(2,1)S(1)} %bitcast.50), channel_id=1, source_target_pairs={{304,0},{256,16},{272,32},{288,48},{368,64},{320,80},{336,96},{352... | collective-permute-start | bytes 884744 | tf_op jit(solution)/shard_map/ppermute | solution.py:53
  179.5 23.8 %collective-permute-start.20 = (bf16[2,144,512]{2,1,0:T(8,128)(2,1)S(1)}, bf16[2,144,512]{2,1,0:T(8,128)(2,1)S(1)}, u32[]{:S(2)}, u32[]{:S(2)}) collective-permute-start(bf16[2,144,512]{2,1,0:T(8,128)(2,1)S(1)} %bitcast.49), channel_id=1, source_target_pairs={{256,0},{272,16},{288,32},{304,48},{320,64},{336,80},{352,96},{368... | collective-permute-start | bytes 884744 | tf_op jit(solution)/shard_map/ppermute | solution.py:53
  203.4 7.5 %collective-permute-start.22 = (bf16[4,144,512]{2,1,0:T(8,128)(2,1)S(1)}, bf16[4,144,512]{2,1,0:T(8,128)(2,1)S(1)}, u32[]{:S(2)}, u32[]{:S(2)}) collective-permute-start(bf16[4,144,512]{2,1,0:T(8,128)(2,1)S(1)} %collective-permute-done.17.refs_2_), channel_id=1, source_target_pairs={{64,0},{0,64},{192,128},{128,192},{320,256},{256,320},{448,384},{3... | collective-permute-start | bytes 1769480 | tf_op jit(solution)/shard_map/ppermute | solution.py:35
  206.5 4.5 %collective-permute-start.23 = (bf16[4,144,512]{2,1,0:T(8,128)(2,1)S(1)}, bf16[4,144,512]{2,1,0:T(8,128)(2,1)}, u32[]{:S(2)}, u32[]{:S(2)}) collective-permute-start(bf16[4,144,512]{2,1,0:T(8,128)(2,1)S(1)} %collective-permute-done.18.refs_3_), channel_id=1, source_target_pairs={{64,0},{0,64},{192,128},{128,192},{320,256},{256,320},{448,384},{3... | collective-permute-start | bytes 1769480 | tf_op jit(solution)/shard_map/ppermute | solution.py:35
  208.4 4.2 %collective-permute-start.24 = (bf16[4,144,512]{2,1,0:T(8,128)(2,1)S(1)}, bf16[4,144,512]{2,1,0:T(8,128)(2,1)}, u32[]{:S(2)}, u32[]{:S(2)}) collective-permute-start(bf16[4,144,512]{2,1,0:T(8,128)(2,1)S(1)} %pad_maximum_fusion.refs_4_), channel_id=1, source_target_pairs={{64,0},{0,64},{192,128},{128,192},{320,256},{256,320},{448,384},{3... | collective-permute-start | bytes 1769480 | tf_op jit(solution)/shard_map/ppermute | solution.py:35
  212.6 2.8 %copy-start.16 = (bf16[48,256,256]{2,1,0:T(8,128)(2,1)S(1)}, bf16[48,256,256]{2,1,0:T(8,128)(2,1)}, u32[]{:S(2)}) copy-start(bf16[48,256,256]{2,1,0:T(8,128)(2,1)} %all-gather.4.cloned.1.call-done) | copy-start | bytes 18874372
Sparse Core Ops, SparseCore 0:
  112.9 75.0 all-gather.3

commit v12 on v11

--- a/solution.py
+++ b/solution.py
@@ -418,8 +418,6 @@
     weight = fc_weight.transpose(1, 0, 2)
 
     next_, last, across = (plane_move(step, True)(own) for step in (1, 3, 2))
-    halves = send_high(own[LEVELS - 1], draft_index)
-    last, across, halves = lax.optimization_barrier((last, across, halves))
     low, high = pair(own, next_), pair(across, last)
     up_low, down_high = plane_move(1, False)(low), plane_move(-1, False)(high)
     up_high, down_low = plane_move(1, False)(high), plane_move(-1, False)(low)
@@ -430,9 +428,10 @@
     sides = project([up_low, up_high, down_low, down_high], weight, 58)
     far_low, far_high, sides = lax.optimization_barrier((far_low, far_high, sides))
     keep, send = project_place([far_low, far_high], weight, zero, sides, core, x, y)
-    got, traded = lax.optimization_barrier((from_other_core(send), traded))
+    mine, *away = join(keep, from_other_core(send), zl)
+    top, mine, traded = lax.optimization_barrier((own[LEVELS - 1], mine, traded))
+    halves = send_high(top, draft_index)
     every = lax.all_gather(turn(traded), "draft", axis=0, tiled=False)
-    mine, *away = join(keep, got, zl)
     parts = [mine] + [from_zl(block, step) for step, block in zip((1, 2, 3), away)]
     scale = LOSS_SCALE / valid_total(lengths)
     odd = draft_index % 2

time: 229 us -> 218 us (0.952)
  the two profiles are of different devices: /device:TPU:1 before, /device:TPU:5 now
where the time goes in v12:
time: 218 us; the launch traced here: 216 us
  starting transfers between devices  98.3 us (45%)
  waiting for transfers between devices  37 us (17%)
  blocking collectives  26.7 us (12%)
  Pallas kernels  25.4 us (12%)
  between operations  16.4 us (8%)
  local copies, waits for them, and re-layouts  10.9 us (5%)
    all_gather x1, blocking collectives, gather_grads(): stack = lax.all_gather(grad, 'dp', axis=0, tiled=False)  26.7 us
    ppermute x9, starting transfers between devices, plane_move(): return lambda block: lax.ppermute(block, ('tp', 'draft'), pairs)  25.8 us
    ppermute x4, waiting for transfers between devices, from_z(): return lax.ppermute(block, ('tp', 'dp'), pairs)  19.9 us
    ppermute x4, starting transfers between devices, from_z(): return lax.ppermute(block, ('tp', 'dp'), pairs)  16.4 us
    all_to_all x1, starting transfers between devices, trade_columns(): lax.all_to_all(quarters, 'dp', split_axis=0, concat_axis=0, tiled=True)  14.8 us
    ppermute x5, starting transfers between devices, from_other_core(): return lax.ppermute(block, 'tp', [(t ^ 1, t) for t in range(ZL * CORES)])  13 us
    ppermute x3, starting transfers between devices, from_zl(): return lax.ppermute(block, 'tp', pairs)  11.3 us
    unnamed x24, local copies, waits for them, and re-layouts  9.31 us
  transfers between devices with their start and end apart: 27, of which 7 were waited for; matrix products, arithmetic and copies ran while one was open for 1% of the time, Pallas kernels for 8%

profile of v12, /device:TPU:5, one launch (start us, length us, event | category | flops | bytes accessed | tf_op | source)
XLA Modules:
  0.0 216.3 jit_solution(16318522124337175200)
XLA Ops:
  7.2 4.6 %collective-permute-start = (bf16[3,64,1024]{2,1,0:T(8,128)(2,1)}, bf16[3,64,1024]{2,1,0:T(8,128)(2,1)S(1)}, u32[]{:S(2)}, u32[]{:S(2)}) collective-permute-start(bf16[3,64,1024]{2,1,0:T(8,128)(2,1)} %bitcast.40), channel_id=1, source_target_pairs={{4,0},{5,1},{6,2},{7,3},{8,4},{9,5},{10,6},{11,7},{12,8},{13,9},{1... | collective-permute-start | bytes 1179656 | tf_op jit(solution)/shard_map/ppermute | solution.py:31
  11.8 1.9 collective-permute-start.3
  13.7 3.5 %collective-permute-start.2 = (bf16[3,64,1024]{2,1,0:T(8,128)(2,1)}, bf16[3,64,1024]{2,1,0:T(8,128)(2,1)S(1)}, u32[]{:S(2)}, u32[]{:S(2)}) collective-permute-start(bf16[3,64,1024]{2,1,0:T(8,128)(2,1)} %bitcast.42), channel_id=1, source_target_pairs={{8,0},{9,1},{10,2},{11,3},{12,4},{13,5},{14,6},{15,7},{0,8},{1,9},... | collective-permute-start | bytes 1179656 | tf_op jit(solution)/shard_map/ppermute | solution.py:31
  17.3 1.0 copy-done.2
  18.3 0.9 pair.2.refs_0_
  19.2 2.2 collective-permute-start.1
  21.4 4.7 %collective-permute-done.3.second_ref = bf16[3,64,1024]{2,1,0:T(8,128)(2,1)S(1)} collective-permute-done((bf16[3,64,1024]{2,1,0:T(8,128)(2,1)}, bf16[3,64,1024]{2,1,0:T(8,128)(2,1)S(1)}, u32[]{:S(2)}, u32[]{:S(2)}) %collective-permute-start.3) | collective-permute-done | bytes 393248 | tf_op jit(solution)/shard_map/ppermute | solution.py:31
  26.1 0.0 collective-permute-done.2.first_ref
  26.1 0.9 pair.3.refs_1_
  27.0 3.0 %collective-permute-start.4 = (bf16[2,3,64,1024]{3,2,1,0:T(8,128)(2,1)}, bf16[2,3,64,1024]{3,2,1,0:T(8,128)(2,1)}, u32[]{:S(2)}, u32[]{:S(2)}) collective-permute-start(bf16[2,3,64,1024]{3,2,1,0:T(8,128)(2,1)} %pair.3.refs_1_), channel_id=1, source_target_pairs={{3,0},{0,1},{1,2},{2,3},{7,4},{4,5},{5,6},{6,7},{11,8},{8,9},{9,10... | collective-permute-start | bytes 2359304 | tf_op jit(solution)/shard_map/ppermute | solution.py:31
  30.0 2.1 collective-permute-start.8
  32.1 3.2 %collective-permute-start.7 = (bf16[2,3,64,1024]{3,2,1,0:T(8,128)(2,1)}, bf16[2,3,64,1024]{3,2,1,0:T(8,128)(2,1)}, u32[]{:S(2)}, u32[]{:S(2)}) collective-permute-start(bf16[2,3,64,1024]{3,2,1,0:T(8,128)(2,1)} %pair.3.refs_1_), channel_id=1, source_target_pairs={{1,0},{2,1},{3,2},{0,3},{5,4},{6,5},{7,6},{4,7},{9,8},{10,9},{11,1... | collective-permute-start | bytes 2359304 | tf_op jit(solution)/shard_map/ppermute | solution.py:31
  35.3 0.0 copy-start
  35.3 1.9 copy-done
  37.2 3.2 %project.2.refs_3_ = bf16[4,64,512]{2,1,0:T(8,128)(2,1)S(1)} custom-call(bf16[2,3,64,1024]{3,2,1,0:T(8,128)(2,1)} %pair.2.refs_0_, bf16[2,3,64,1024]{3,2,1,0:T(8,128)(2,1)} %pair.3.refs_1_, bf16[3,1024,512]{2,1,0:T(8,128)(2,1)S(1)} %bitcast.34), custom_call_target="tpu_custom_call" | custom-call | bytes 1572864 | tf_op jit(solution)/shard_map/project/pallas_call | solution.py:114
  40.5 0.7 copy-done.5
  41.2 2.3 %collective-permute-start.5 = (bf16[2,3,64,1024]{3,2,1,0:T(8,128)(2,1)}, bf16[2,3,64,1024]{3,2,1,0:T(8,128)(2,1)}, u32[]{:S(2)}, u32[]{:S(2)}) collective-permute-start(bf16[2,3,64,1024]{3,2,1,0:T(8,128)(2,1)} %collective-permute-done.1.refs_0_), channel_id=1, source_target_pairs={{1,0},{2,1},{3,2},{0,3},{5,4},{6,5},{7,6},{4,7},{9,8},{10,9},{11,1... | collective-permute-start | bytes 2359304 | tf_op jit(solution)/shard_map/ppermute | solution.py:31
  43.5 3.0 %collective-permute-start.6 = (bf16[2,3,64,1024]{3,2,1,0:T(8,128)(2,1)}, bf16[2,3,64,1024]{3,2,1,0:T(8,128)(2,1)}, u32[]{:S(2)}, u32[]{:S(2)}) collective-permute-start(bf16[2,3,64,1024]{3,2,1,0:T(8,128)(2,1)} %collective-permute-done.4.refs_3_), channel_id=1, source_target_pairs={{3,0},{0,1},{1,2},{2,3},{7,4},{4,5},{5,6},{6,7},{11,8},{8,9},{9,10... | collective-permute-start | bytes 2359304 | tf_op jit(solution)/shard_map/ppermute | solution.py:31
  46.5 0.8 copy.10
  47.3 14.8 %all-to-all-start = ((bf16[4,3,64,256]{3,2,1,0:T(8,128)(2,1)}), bf16[4,3,64,256]{3,2,1,0:T(8,128)(2,1)}, u32[]{:S(2)}, u32[]{:S(2)}) async-start(bf16[4,3,64,256]{3,2,1,0:T(8,128)(2,1)} %bitcast.48), calls=%async_computation | async-start | bytes 786432 | tf_op jit(solution)/shard_map/all_to_all | solution.py:387
  62.1 0.1 pad_add_fusion.1.meta_ref
  62.1 0.0 collective-permute-done.7.refs_1_
  62.2 5.5 %project.3.refs_4_ = bf16[8,64,512]{2,1,0:T(8,128)(2,1)} custom-call(bf16[2,3,64,1024]{3,2,1,0:T(8,128)(2,1)} %collective-permute-done.1.refs_0_, bf16[2,3,64,1024]{3,2,1,0:T(8,128)(2,1)} %collective-permute-done.7.refs_1_, bf16[2,3,64,1024]{3,2,1,0:T(8,128)(2,1)} %collective-permute-done.8.refs_2_, bf16[2,3,64,1024]{3,2,1,0:T(8,128)(2,1)} %collective-permute-done.4.refs_3_, ...), custom_call_target="tpu_custom_call" | custom-call | bytes 3145728 | tf_op jit(solution)/shard_map/project/pallas_call | solution.py:114
  67.7 0.0 collective-permute-done.5.refs_0_
  67.7 0.0 copy-start.4
  67.7 1.0 copy-done.4
  68.8 4.7 %project_place.1 = (bf16[4,144,512]{2,1,0:T(8,128)(2,1)S(1)}, bf16[4,144,512]{2,1,0:T(8,128)(2,1)}) custom-call(s32[3]{0:T(128)S(1)} %pad_add_fusion.1.meta_ref, bf16[2,3,64,1024]{3,2,1,0:T(8,128)(2,1)} %collective-permute-done.5.refs_0_, bf16[2,3,64,1024]{3,2,1,0:T(8,128)(2,1)} %collective-permute-done.6.refs_1_, bf16[3,1024,512]{2,1,0:T(8,128)(2,1)S(1)} %bitcast.35, ...), custom_call_target="tpu_custom_call" | custom-call | bytes 1572864 | tf_op jit(solution)/shard_map/project_place/pallas_call | solution.py:167
  73.5 0.8 copy-done.7
  74.3 4.0 %collective-permute-start.9 = (bf16[4,144,512]{2,1,0:T(8,128)(2,1)}, bf16[4,144,512]{2,1,0:T(8,128)(2,1)S(1)}, u32[]{:S(2)}, u32[]{:S(2)}) collective-permute-start(bf16[4,144,512]{2,1,0:T(8,128)(2,1)} %get-tuple-element.32), channel_id=1, source_target_pairs={{64,0},{0,64},{192,128},{128,192},{320,256},{256,320},{448,384},{3... | collective-permute-start | bytes 1769480 | tf_op jit(solution)/shard_map/ppermute | solution.py:35
  78.3 1.8 collective-permute-done.9.got_ref
  80.1 1.1 copy-done.8
  81.2 0.2 join.1
  81.3 2.7 %turn.1 = bf16[3,256,256]{2,1,0:T(8,128)(2,1)} custom-call(bf16[4,3,64,256]{3,2,1,0:T(8,128)(2,1)} %all-to-all-done.traded_ref), custom_call_target="tpu_custom_call" | custom-call | bytes 786432 | tf_op jit(solution)/shard_map/turn/pallas_call | solution.py:341
  84.1 0.0 all-gather.4.cloned.1.call-update
  84.1 0.6 dynamic_slice.3
  84.8 0.7 maximum_reduce_fusion
  87.3 6.8 %collective-permute-start.16 = (bf16[16,512]{1,0:T(8,128)(2,1)S(1)}, bf16[16,512]{1,0:T(8,128)(2,1)S(1)}, u32[]{:S(2)}, u32[]{:S(2)}) collective-permute-start(bf16[16,512]{1,0:T(8,128)(2,1)S(1)} %get-tuple-element.53), channel_id=1, source_target_pairs={{2,1},{4,65},{6,129},{8,193},{10,257},{12,321},{14,385},{66,3},{68... | collective-permute-start | bytes 49160 | tf_op jit(solution)/shard_map/ppermute | solution.py:380
  94.1 4.9 %collective-permute-start.15 = (bf16[16,512]{1,0:T(8,128)(2,1)S(1)}, bf16[16,512]{1,0:T(8,128)(2,1)S(1)}, u32[]{:S(2)}, u32[]{:S(2)}) collective-permute-start(bf16[16,512]{1,0:T(8,128)(2,1)S(1)} %get-tuple-element.54), channel_id=1, source_target_pairs={{2,0},{4,64},{6,128},{8,192},{10,256},{12,320},{14,384},{66,2},{68... | collective-permute-start | bytes 49160 | tf_op jit(solution)/shard_map/ppermute | solution.py:379
  99.0 5.1 %collective-permute-start.10 = (bf16[144,512]{1,0:T(8,128)(2,1)S(1)}, bf16[144,512]{1,0:T(8,128)(2,1)S(1)}, u32[]{:S(2)}, u32[]{:S(2)}) collective-permute-start(bf16[144,512]{1,0:T(8,128)(2,1)S(1)} %get-tuple-element.36), channel_id=1, source_target_pairs={{128,0},{192,64},{256,128},{320,192},{384,256},{448,320},{0,384},{... | collective-permute-start | bytes 442376 | tf_op jit(solution)/shard_map/ppermute | solution.py:40
  104.1 2.9 %collective-permute-start.11 = (bf16[144,512]{1,0:T(8,128)(2,1)S(1)}, bf16[144,512]{1,0:T(8,128)(2,1)S(1)}, u32[]{:S(2)}, u32[]{:S(2)}) collective-permute-start(bf16[144,512]{1,0:T(8,128)(2,1)S(1)} %get-tuple-element.37), channel_id=1, source_target_pairs={{256,0},{320,64},{384,128},{448,192},{0,256},{64,320},{128,384},{1... | collective-permute-start | bytes 442376 | tf_op jit(solution)/shard_map/ppermute | solution.py:40
  106.9 3.4 %collective-permute-start.12 = (bf16[144,512]{1,0:T(8,128)(2,1)S(1)}, bf16[144,512]{1,0:T(8,128)(2,1)S(1)}, u32[]{:S(2)}, u32[]{:S(2)}) collective-permute-start(bf16[144,512]{1,0:T(8,128)(2,1)S(1)} %get-tuple-element.38), channel_id=1, source_target_pairs={{384,0},{448,64},{0,128},{64,192},{128,256},{192,320},{256,384},{3... | collective-permute-start | bytes 442376 | tf_op jit(solution)/shard_map/ppermute | solution.py:40
  110.4 1.9 collective-permute-start.14
  112.3 3.4 %collective-permute-start.13 = (bf16[64,512]{1,0:T(8,128)(2,1)S(1)}, bf16[64,512]{1,0:T(8,128)(2,1)S(1)}, u32[]{:S(2)}, u32[]{:S(2)}) collective-permute-start(bf16[64,512]{1,0:T(8,128)(2,1)S(1)} %get-tuple-element.56), channel_id=1, source_target_pairs={{0,0},{1,1},{2,64},{3,65},{4,128},{5,129},{6,192},{7,193},{8,256},... | collective-permute-start | bytes 196616 | tf_op jit(solution)/shard_map/ppermute | solution.py:377
  115.7 0.7 pad_add_fusion.meta_ref
  116.4 6.4 %collective-permute-done.14.refs_5_ = bf16[64,512]{1,0:T(8,128)(2,1)S(1)} collective-permute-done((bf16[64,512]{1,0:T(8,128)(2,1)S(1)}, bf16[64,512]{1,0:T(8,128)(2,1)S(1)}, u32[]{:S(2)}, u32[]{:S(2)}) %collective-permute-start.14) | collective-permute-done | bytes 65568 | tf_op jit(solution)/shard_map/ppermute | solution.py:378
  122.9 2.6 %collective-permute-done.13.refs_4_ = bf16[64,512]{1,0:T(8,128)(2,1)S(1)} collective-permute-done((bf16[64,512]{1,0:T(8,128)(2,1)S(1)}, bf16[64,512]{1,0:T(8,128)(2,1)S(1)}, u32[]{:S(2)}, u32[]{:S(2)}) %collective-permute-start.13) | collective-permute-done | bytes 65568 | tf_op jit(solution)/shard_map/ppermute | solution.py:377
  125.4 1.4 chain.1
  126.8 26.7 %all-gather = bf16[576,512]{1,0:T(8,128)(2,1)S(1)} all-gather(bf16[144,512]{1,0:T(8,128)(2,1)S(1)} %chain.1), channel_id=2, replica_groups=mesh['tp'=8,'dp'=4,'draft'=16] {'dp'}, dimensions={0}, use_global_device_ids=true | all-gather | bytes 737280 | tf_op jit(solution)/shard_map/all_gather | solution.py:391
  153.6 1.9 collective-permute-start.19
  155.5 7.1 %collective-permute-start.18 = (bf16[4,144,512]{2,1,0:T(8,128)(2,1)S(1)}, bf16[4,144,512]{2,1,0:T(8,128)(2,1)S(1)}, u32[]{:S(2)}, u32[]{:S(2)}) collective-permute-start(bf16[4,144,512]{2,1,0:T(8,128)(2,1)S(1)} %bitcast.37), channel_id=1, source_target_pairs={{432,0},{384,16},{400,32},{416,48},{496,64},{448,80},{464,96},{480... | collective-permute-start | bytes 1769480 | tf_op jit(solution)/shard_map/ppermute | solution.py:53
  162.6 1.9 collective-permute-start.17
  164.6 3.1 %collective-permute-start.21 = (bf16[2,144,512]{2,1,0:T(8,128)(2,1)S(1)}, bf16[2,144,512]{2,1,0:T(8,128)(2,1)S(1)}, u32[]{:S(2)}, u32[]{:S(2)}) collective-permute-start(bf16[2,144,512]{2,1,0:T(8,128)(2,1)S(1)} %bitcast.50), channel_id=1, source_target_pairs={{304,0},{256,16},{272,32},{288,48},{368,64},{320,80},{336,96},{352... | collective-permute-start | bytes 884744 | tf_op jit(solution)/shard_map/ppermute | solution.py:53
  167.7 4.3 %collective-permute-start.20 = (bf16[2,144,512]{2,1,0:T(8,128)(2,1)S(1)}, bf16[2,144,512]{2,1,0:T(8,128)(2,1)S(1)}, u32[]{:S(2)}, u32[]{:S(2)}) collective-permute-start(bf16[2,144,512]{2,1,0:T(8,128)(2,1)S(1)} %bitcast.49), channel_id=1, source_target_pairs={{256,0},{272,16},{288,32},{304,48},{320,64},{336,80},{352,96},{368... | collective-permute-start | bytes 884744 | tf_op jit(solution)/shard_map/ppermute | solution.py:53
  172.0 16.0 %collective-permute-done.21 = bf16[2,144,512]{2,1,0:T(8,128)(2,1)S(1)} collective-permute-done((bf16[2,144,512]{2,1,0:T(8,128)(2,1)S(1)}, bf16[2,144,512]{2,1,0:T(8,128)(2,1)S(1)}, u32[]{:S(2)}, u32[]{:S(2)}) %collective-permute-start.21) | collective-permute-done | bytes 294944 | tf_op jit(solution)/shard_map/ppermute | solution.py:53
  188.0 3.9 %collective-permute-done.20 = bf16[2,144,512]{2,1,0:T(8,128)(2,1)S(1)} collective-permute-done((bf16[2,144,512]{2,1,0:T(8,128)(2,1)S(1)}, bf16[2,144,512]{2,1,0:T(8,128)(2,1)S(1)}, u32[]{:S(2)}, u32[]{:S(2)}) %collective-permute-start.20) | collective-permute-done | bytes 294944 | tf_op jit(solution)/shard_map/ppermute | solution.py:53
  191.9 0.1 pad_maximum_fusion.refs_4_
  192.0 0.0 all-gather.4.cloned.1.call-done
  192.0 2.8 %collective-permute-start.22 = (bf16[4,144,512]{2,1,0:T(8,128)(2,1)S(1)}, bf16[4,144,512]{2,1,0:T(8,128)(2,1)S(1)}, u32[]{:S(2)}, u32[]{:S(2)}) collective-permute-start(bf16[4,144,512]{2,1,0:T(8,128)(2,1)S(1)} %collective-permute-done.17.refs_2_), channel_id=1, source_target_pairs={{64,0},{0,64},{192,128},{128,192},{320,256},{256,320},{448,384},{3... | collective-permute-start | bytes 1769480 | tf_op jit(solution)/shard_map/ppermute | solution.py:35
  194.8 1.9 collective-permute-start.23
  196.7 2.4 %collective-permute-start.24 = (bf16[4,144,512]{2,1,0:T(8,128)(2,1)S(1)}, bf16[4,144,512]{2,1,0:T(8,128)(2,1)}, u32[]{:S(2)}, u32[]{:S(2)}) collective-permute-start(bf16[4,144,512]{2,1,0:T(8,128)(2,1)S(1)} %pad_maximum_fusion.refs_4_), channel_id=1, source_target_pairs={{64,0},{0,64},{192,128},{128,192},{320,256},{256,320},{448,384},{3... | collective-permute-start | bytes 1769480 | tf_op jit(solution)/shard_map/ppermute | solution.py:35
  199.2 0.1 stack.56.meta_ref
  199.3 1.6 collective-permute-done.24.refs_7_
  200.8 2.8 %copy-done.10 = bf16[48,256,256]{2,1,0:T(8,128)(2,1)S(1)} copy-done((bf16[48,256,256]{2,1,0:T(8,128)(2,1)S(1)}, bf16[48,256,256]{2,1,0:T(8,128)(2,1)}, u32[]{:S(2)}) %copy-start.10) | copy-done | bytes 6291480
  203.6 5.8 %weight_grad.1 = (bf16[3,256,512]{2,1,0:T(8,128)(2,1)}, f32[1,512]{1,0:T(1,128)}) custom-call(s32[8]{0:T(128)S(1)} %stack.56.meta_ref, bf16[16,3,256,256]{3,2,1,0:T(8,128)(2,1)S(1)} %bitcast.47, bf16[4,144,512]{2,1,0:T(8,128)(2,1)S(1)} %bitcast.39, bf16[4,144,512]{2,1,0:T(8,128)(2,1)S(1)} %collective-permute-done.19.refs_1_, ...), custom_call_target="tpu_custom_call" | custom-call | flops 3221225472 | bytes 10485760 | tf_op jit(solution)/shard_map/weight_grad/pallas_call | solution.py:315
  (36 shorter events, 0.1 us)
Async XLA Ops:
  7.2 10.1 %collective-permute-start = (bf16[3,64,1024]{2,1,0:T(8,128)(2,1)}, bf16[3,64,1024]{2,1,0:T(8,128)(2,1)S(1)}, u32[]{:S(2)}, u32[]{:S(2)}) collective-permute-start(bf16[3,64,1024]{2,1,0:T(8,128)(2,1)} %bitcast.40), channel_id=1, source_target_pairs={{4,0},{5,1},{6,2},{7,3},{8,4},{9,5},{10,6},{11,7},{12,8},{13,9},{1... | collective-permute-start | bytes 1179656 | tf_op jit(solution)/shard_map/ppermute | solution.py:31
  11.8 14.3 %collective-permute-start.3 = (bf16[3,64,1024]{2,1,0:T(8,128)(2,1)}, bf16[3,64,1024]{2,1,0:T(8,128)(2,1)S(1)}, u32[]{:S(2)}, u32[]{:S(2)}) collective-permute-start(bf16[3,64,1024]{2,1,0:T(8,128)(2,1)} %bitcast.41), channel_id=1, source_target_pairs={{12,0},{13,1},{14,2},{15,3},{0,4},{1,5},{2,6},{3,7},{4,8},{5,9},{6... | collective-permute-start | bytes 1179656 | tf_op jit(solution)/shard_map/ppermute | solution.py:31
  13.7 12.4 %collective-permute-start.2 = (bf16[3,64,1024]{2,1,0:T(8,128)(2,1)}, bf16[3,64,1024]{2,1,0:T(8,128)(2,1)S(1)}, u32[]{:S(2)}, u32[]{:S(2)}) collective-permute-start(bf16[3,64,1024]{2,1,0:T(8,128)(2,1)} %bitcast.42), channel_id=1, source_target_pairs={{8,0},{9,1},{10,2},{11,3},{12,4},{13,5},{14,6},{15,7},{0,8},{1,9},... | collective-permute-start | bytes 1179656 | tf_op jit(solution)/shard_map/ppermute | solution.py:31
  17.3 1.0 copy-start.2
  18.3 28.2 %copy-start.3 = (bf16[64,3,1024]{2,0,1:T(8,128)(2,1)S(1)}, bf16[64,3,1024]{2,0,1:T(8,128)(2,1)}, u32[]{:S(2)}) copy-start(bf16[64,3,1024]{2,0,1:T(8,128)(2,1)} %param.4) | copy-start | bytes 1179652
  19.2 21.9 %collective-permute-start.1 = (bf16[2,3,64,1024]{3,2,1,0:T(8,128)(2,1)}, bf16[2,3,64,1024]{3,2,1,0:T(8,128)(2,1)}, u32[]{:S(2)}, u32[]{:S(2)}) collective-permute-start(bf16[2,3,64,1024]{3,2,1,0:T(8,128)(2,1)} %pair.2.refs_0_), channel_id=1, source_target_pairs={{1,0},{2,1},{3,2},{0,3},{5,4},{6,5},{7,6},{4,7},{9,8},{10,9},{11,1... | collective-permute-start | bytes 2359304 | tf_op jit(solution)/shard_map/ppermute | solution.py:31
  27.0 14.1 %collective-permute-start.4 = (bf16[2,3,64,1024]{3,2,1,0:T(8,128)(2,1)}, bf16[2,3,64,1024]{3,2,1,0:T(8,128)(2,1)}, u32[]{:S(2)}, u32[]{:S(2)}) collective-permute-start(bf16[2,3,64,1024]{3,2,1,0:T(8,128)(2,1)} %pair.3.refs_1_), channel_id=1, source_target_pairs={{3,0},{0,1},{1,2},{2,3},{7,4},{4,5},{5,6},{6,7},{11,8},{8,9},{9,10... | collective-permute-start | bytes 2359304 | tf_op jit(solution)/shard_map/ppermute | solution.py:31
  30.0 32.1 %collective-permute-start.8 = (bf16[2,3,64,1024]{3,2,1,0:T(8,128)(2,1)}, bf16[2,3,64,1024]{3,2,1,0:T(8,128)(2,1)}, u32[]{:S(2)}, u32[]{:S(2)}) collective-permute-start(bf16[2,3,64,1024]{3,2,1,0:T(8,128)(2,1)} %pair.2.refs_0_), channel_id=1, source_target_pairs={{3,0},{0,1},{1,2},{2,3},{7,4},{4,5},{5,6},{6,7},{11,8},{8,9},{9,10... | collective-permute-start | bytes 2359304 | tf_op jit(solution)/shard_map/ppermute | solution.py:31
  32.1 30.0 %collective-permute-start.7 = (bf16[2,3,64,1024]{3,2,1,0:T(8,128)(2,1)}, bf16[2,3,64,1024]{3,2,1,0:T(8,128)(2,1)}, u32[]{:S(2)}, u32[]{:S(2)}) collective-permute-start(bf16[2,3,64,1024]{3,2,1,0:T(8,128)(2,1)} %pair.3.refs_1_), channel_id=1, source_target_pairs={{1,0},{2,1},{3,2},{0,3},{5,4},{6,5},{7,6},{4,7},{9,8},{10,9},{11,1... | collective-permute-start | bytes 2359304 | tf_op jit(solution)/shard_map/ppermute | solution.py:31
  35.3 1.9 copy-start
  37.2 30.5 %copy-start.1 = (bf16[1024,3,512]{2,0,1:T(8,128)(2,1)S(1)}, bf16[1024,3,512]{2,0,1:T(8,128)(2,1)}, u32[]{:S(2)}) copy-start(bf16[1024,3,512]{2,0,1:T(8,128)(2,1)} %param.5) | copy-start | bytes 9437188
  40.4 0.7 copy-start.5
  41.2 26.6 %collective-permute-start.5 = (bf16[2,3,64,1024]{3,2,1,0:T(8,128)(2,1)}, bf16[2,3,64,1024]{3,2,1,0:T(8,128)(2,1)}, u32[]{:S(2)}, u32[]{:S(2)}) collective-permute-start(bf16[2,3,64,1024]{3,2,1,0:T(8,128)(2,1)} %collective-permute-done.1.refs_0_), channel_id=1, source_target_pairs={{1,0},{2,1},{3,2},{0,3},{5,4},{6,5},{7,6},{4,7},{9,8},{10,9},{11,1... | collective-permute-start | bytes 2359304 | tf_op jit(solution)/shard_map/ppermute | solution.py:31
  43.5 24.3 %collective-permute-start.6 = (bf16[2,3,64,1024]{3,2,1,0:T(8,128)(2,1)}, bf16[2,3,64,1024]{3,2,1,0:T(8,128)(2,1)}, u32[]{:S(2)}, u32[]{:S(2)}) collective-permute-start(bf16[2,3,64,1024]{3,2,1,0:T(8,128)(2,1)} %collective-permute-done.4.refs_3_), channel_id=1, source_target_pairs={{3,0},{0,1},{1,2},{2,3},{7,4},{4,5},{5,6},{6,7},{11,8},{8,9},{9,10... | collective-permute-start | bytes 2359304 | tf_op jit(solution)/shard_map/ppermute | solution.py:31
  47.3 34.1 %all-to-all-start = ((bf16[4,3,64,256]{3,2,1,0:T(8,128)(2,1)}), bf16[4,3,64,256]{3,2,1,0:T(8,128)(2,1)}, u32[]{:S(2)}, u32[]{:S(2)}) async-start(bf16[4,3,64,256]{3,2,1,0:T(8,128)(2,1)} %bitcast.48), calls=%async_computation | async-start | bytes 786432 | tf_op jit(solution)/shard_map/all_to_all | solution.py:387
  62.1 129.9 %all-gather.4.cloned.1.call-start = ((), (), s32[]{:S(2)}) async-start(), calls=%async_computation.1 | async-start | bytes 6684672 | tf_op jit(solution)/shard_map/all_gather | solution.py:434
  62.1 5.7 %copy-start.6 = (bf16[4,64,512]{2,1,0:T(8,128)(2,1)S(1)}, bf16[4,64,512]{2,1,0:T(8,128)(2,1)}, u32[]{:S(2)}) copy-start(bf16[4,64,512]{2,1,0:T(8,128)(2,1)} %copy-done.5) | copy-start | bytes 786436
  62.1 22.0 %copy-start.11 = (s32[4]{0:T(128)S(1)}, s32[4]{0:T(128)}, u32[]{:S(2)}) copy-start(s32[4]{0:T(128)} %param.7) | copy-start | bytes 52
  62.1 63.3 %copy-start.9 = (f32[512]{0:T(512)S(1)}, f32[512]{0:T(512)}, u32[]{:S(2)}) copy-start(f32[512]{0:T(512)} %param.6) | copy-start | bytes 6148
  67.7 1.0 copy-start.4
  73.5 0.8 copy-start.7
  74.3 5.8 %collective-permute-start.9 = (bf16[4,144,512]{2,1,0:T(8,128)(2,1)}, bf16[4,144,512]{2,1,0:T(8,128)(2,1)S(1)}, u32[]{:S(2)}, u32[]{:S(2)}) collective-permute-start(bf16[4,144,512]{2,1,0:T(8,128)(2,1)} %get-tuple-element.32), channel_id=1, source_target_pairs={{64,0},{0,64},{192,128},{128,192},{320,256},{256,320},{448,384},{3... | collective-permute-start | bytes 1769480 | tf_op jit(solution)/shard_map/ppermute | solution.py:35
  80.1 1.1 copy-start.8
  87.3 23.0 %collective-permute-start.16 = (bf16[16,512]{1,0:T(8,128)(2,1)S(1)}, bf16[16,512]{1,0:T(8,128)(2,1)S(1)}, u32[]{:S(2)}, u32[]{:S(2)}) collective-permute-start(bf16[16,512]{1,0:T(8,128)(2,1)S(1)} %get-tuple-element.53), channel_id=1, source_target_pairs={{2,1},{4,65},{6,129},{8,193},{10,257},{12,321},{14,385},{66,3},{68... | collective-permute-start | bytes 49160 | tf_op jit(solution)/shard_map/ppermute | solution.py:380
  94.1 18.2 %collective-permute-start.15 = (bf16[16,512]{1,0:T(8,128)(2,1)S(1)}, bf16[16,512]{1,0:T(8,128)(2,1)S(1)}, u32[]{:S(2)}, u32[]{:S(2)}) collective-permute-start(bf16[16,512]{1,0:T(8,128)(2,1)S(1)} %get-tuple-element.54), channel_id=1, source_target_pairs={{2,0},{4,64},{6,128},{8,192},{10,256},{12,320},{14,384},{66,2},{68... | collective-permute-start | bytes 49160 | tf_op jit(solution)/shard_map/ppermute | solution.py:379
  99.0 26.4 %collective-permute-start.10 = (bf16[144,512]{1,0:T(8,128)(2,1)S(1)}, bf16[144,512]{1,0:T(8,128)(2,1)S(1)}, u32[]{:S(2)}, u32[]{:S(2)}) collective-permute-start(bf16[144,512]{1,0:T(8,128)(2,1)S(1)} %get-tuple-element.36), channel_id=1, source_target_pairs={{128,0},{192,64},{256,128},{320,192},{384,256},{448,320},{0,384},{... | collective-permute-start | bytes 442376 | tf_op jit(solution)/shard_map/ppermute | solution.py:40
  104.1 21.3 %collective-permute-start.11 = (bf16[144,512]{1,0:T(8,128)(2,1)S(1)}, bf16[144,512]{1,0:T(8,128)(2,1)S(1)}, u32[]{:S(2)}, u32[]{:S(2)}) collective-permute-start(bf16[144,512]{1,0:T(8,128)(2,1)S(1)} %get-tuple-element.37), channel_id=1, source_target_pairs={{256,0},{320,64},{384,128},{448,192},{0,256},{64,320},{128,384},{1... | collective-permute-start | bytes 442376 | tf_op jit(solution)/shard_map/ppermute | solution.py:40
  106.9 18.5 %collective-permute-start.12 = (bf16[144,512]{1,0:T(8,128)(2,1)S(1)}, bf16[144,512]{1,0:T(8,128)(2,1)S(1)}, u32[]{:S(2)}, u32[]{:S(2)}) collective-permute-start(bf16[144,512]{1,0:T(8,128)(2,1)S(1)} %get-tuple-element.38), channel_id=1, source_target_pairs={{384,0},{448,64},{0,128},{64,192},{128,256},{192,320},{256,384},{3... | collective-permute-start | bytes 442376 | tf_op jit(solution)/shard_map/ppermute | solution.py:40
  110.4 12.5 %collective-permute-start.14 = (bf16[64,512]{1,0:T(8,128)(2,1)S(1)}, bf16[64,512]{1,0:T(8,128)(2,1)S(1)}, u32[]{:S(2)}, u32[]{:S(2)}) collective-permute-start(bf16[64,512]{1,0:T(8,128)(2,1)S(1)} %get-tuple-element.55), channel_id=1, source_target_pairs={{0,1},{1,0},{2,65},{3,64},{4,129},{5,128},{6,193},{7,192},{8,257},... | collective-permute-start | bytes 196616 | tf_op jit(solution)/shard_map/ppermute | solution.py:378
  112.3 13.1 %collective-permute-start.13 = (bf16[64,512]{1,0:T(8,128)(2,1)S(1)}, bf16[64,512]{1,0:T(8,128)(2,1)S(1)}, u32[]{:S(2)}, u32[]{:S(2)}) collective-permute-start(bf16[64,512]{1,0:T(8,128)(2,1)S(1)} %get-tuple-element.56), channel_id=1, source_target_pairs={{0,0},{1,1},{2,64},{3,65},{4,128},{5,129},{6,192},{7,193},{8,256},... | collective-permute-start | bytes 196616 | tf_op jit(solution)/shard_map/ppermute | solution.py:377
  153.6 38.4 %collective-permute-start.19 = (bf16[4,144,512]{2,1,0:T(8,128)(2,1)S(1)}, bf16[4,144,512]{2,1,0:T(8,128)(2,1)S(1)}, u32[]{:S(2)}, u32[]{:S(2)}) collective-permute-start(bf16[4,144,512]{2,1,0:T(8,128)(2,1)S(1)} %bitcast.36), channel_id=1, source_target_pairs={{64,0},{0,64},{192,128},{128,192},{320,256},{256,320},{448,384},{3... | collective-permute-start | bytes 1769480 | tf_op jit(solution)/shard_map/ppermute | solution.py:35
  155.5 36.5 %collective-permute-start.18 = (bf16[4,144,512]{2,1,0:T(8,128)(2,1)S(1)}, bf16[4,144,512]{2,1,0:T(8,128)(2,1)S(1)}, u32[]{:S(2)}, u32[]{:S(2)}) collective-permute-start(bf16[4,144,512]{2,1,0:T(8,128)(2,1)S(1)} %bitcast.37), channel_id=1, source_target_pairs={{432,0},{384,16},{400,32},{416,48},{496,64},{448,80},{464,96},{480... | collective-permute-start | bytes 1769480 | tf_op jit(solution)/shard_map/ppermute | solution.py:53
  162.6 29.3 %collective-permute-start.17 = (bf16[4,144,512]{2,1,0:T(8,128)(2,1)S(1)}, bf16[4,144,512]{2,1,0:T(8,128)(2,1)S(1)}, u32[]{:S(2)}, u32[]{:S(2)}) collective-permute-start(bf16[4,144,512]{2,1,0:T(8,128)(2,1)S(1)} %bitcast.38), channel_id=1, source_target_pairs={{128,0},{144,16},{160,32},{176,48},{192,64},{208,80},{224,96},{240... | collective-permute-start | bytes 1769480 | tf_op jit(solution)/shard_map/ppermute | solution.py:53
  164.6 23.4 %collective-permute-start.21 = (bf16[2,144,512]{2,1,0:T(8,128)(2,1)S(1)}, bf16[2,144,512]{2,1,0:T(8,128)(2,1)S(1)}, u32[]{:S(2)}, u32[]{:S(2)}) collective-permute-start(bf16[2,144,512]{2,1,0:T(8,128)(2,1)S(1)} %bitcast.50), channel_id=1, source_target_pairs={{304,0},{256,16},{272,32},{288,48},{368,64},{320,80},{336,96},{352... | collective-permute-start | bytes 884744 | tf_op jit(solution)/shard_map/ppermute | solution.py:53
  167.7 24.2 %collective-permute-start.20 = (bf16[2,144,512]{2,1,0:T(8,128)(2,1)S(1)}, bf16[2,144,512]{2,1,0:T(8,128)(2,1)S(1)}, u32[]{:S(2)}, u32[]{:S(2)}) collective-permute-start(bf16[2,144,512]{2,1,0:T(8,128)(2,1)S(1)} %bitcast.49), channel_id=1, source_target_pairs={{256,0},{272,16},{288,32},{304,48},{320,64},{336,80},{352,96},{368... | collective-permute-start | bytes 884744 | tf_op jit(solution)/shard_map/ppermute | solution.py:53
  192.0 7.3 %collective-permute-start.22 = (bf16[4,144,512]{2,1,0:T(8,128)(2,1)S(1)}, bf16[4,144,512]{2,1,0:T(8,128)(2,1)S(1)}, u32[]{:S(2)}, u32[]{:S(2)}) collective-permute-start(bf16[4,144,512]{2,1,0:T(8,128)(2,1)S(1)} %collective-permute-done.17.refs_2_), channel_id=1, source_target_pairs={{64,0},{0,64},{192,128},{128,192},{320,256},{256,320},{448,384},{3... | collective-permute-start | bytes 1769480 | tf_op jit(solution)/shard_map/ppermute | solution.py:35
  194.8 4.5 %collective-permute-start.23 = (bf16[4,144,512]{2,1,0:T(8,128)(2,1)S(1)}, bf16[4,144,512]{2,1,0:T(8,128)(2,1)}, u32[]{:S(2)}, u32[]{:S(2)}) collective-permute-start(bf16[4,144,512]{2,1,0:T(8,128)(2,1)S(1)} %collective-permute-done.18.refs_3_), channel_id=1, source_target_pairs={{64,0},{0,64},{192,128},{128,192},{320,256},{256,320},{448,384},{3... | collective-permute-start | bytes 1769480 | tf_op jit(solution)/shard_map/ppermute | solution.py:35
  196.7 4.2 %collective-permute-start.24 = (bf16[4,144,512]{2,1,0:T(8,128)(2,1)S(1)}, bf16[4,144,512]{2,1,0:T(8,128)(2,1)}, u32[]{:S(2)}, u32[]{:S(2)}) collective-permute-start(bf16[4,144,512]{2,1,0:T(8,128)(2,1)S(1)} %pad_maximum_fusion.refs_4_), channel_id=1, source_target_pairs={{64,0},{0,64},{192,128},{128,192},{320,256},{256,320},{448,384},{3... | collective-permute-start | bytes 1769480 | tf_op jit(solution)/shard_map/ppermute | solution.py:35
  200.8 2.8 %copy-start.10 = (bf16[48,256,256]{2,1,0:T(8,128)(2,1)S(1)}, bf16[48,256,256]{2,1,0:T(8,128)(2,1)}, u32[]{:S(2)}) copy-start(bf16[48,256,256]{2,1,0:T(8,128)(2,1)} %all-gather.4.cloned.1.call-done) | copy-start | bytes 18874372
Sparse Core Ops, SparseCore 0:
  84.2 83.1 all-gather.3

commit v13 on v12

--- a/solution.py
+++ b/solution.py
@@ -125,7 +125,7 @@
 
 
 def project_place_kernel(meta_ref, *refs):
-    *block_refs, weight_ref, zero_ref, sides_ref, keep_ref, send_ref, total_ref, token_ref = refs
+    *block_refs, weight_ref, near_ref, keep_ref, send_ref, total_ref, token_ref = refs
     accumulate(
         total_ref, jnp.dot(rows_of(block_refs), weight_ref[0], preferred_element_type=jnp.float32)
     )
@@ -133,7 +133,7 @@
     @pl.when(pl.program_id(0) == LEVELS - 1)
     def _():
         core, x, y = meta_ref[0], meta_ref[1], meta_ref[2]
-        rows = zero_ref.shape[1]
+        rows = near_ref.shape[1]
         total = rows * X * Y
         edge = jnp.zeros((HALO, token_ref.shape[1]), jnp.float32)
         token_ref[pl.ds(0, HALO), :] = edge
@@ -144,12 +144,10 @@
                 dy = jnp.where(core == 0, second, first)
                 e = lax.rem(x + dx, X) * Y + lax.rem(y + dy, Y)
                 at = pl.multiple_of(e * rows + HALO, 8)
-                if second == 0:
-                    block = zero_ref[first].astype(jnp.float32)
-                elif second == 2:
+                if second == 2:
                     block = total_ref[pl.ds(first * rows, rows), :]
                 else:
-                    block = sides_ref[second // 2 * 4 + first].astype(jnp.float32)
+                    block = near_ref[(0, 4, 0, 8)[second] + first].astype(jnp.float32)
                 token_ref[pl.ds(at, rows), :] = block
         piece = total // (ZL * CORES)
         for zl in range(ZL):
@@ -158,8 +156,8 @@
                 out_ref[zl] = token_ref[pl.ds(at, piece + 2 * HALO), :].astype(jnp.bfloat16)
 
 
-def project_place(blocks, weight, zero, sides, core, x, y):
-    _, rows, width = zero.shape
+def project_place(blocks, weight, near, core, x, y):
+    _, rows, width = near.shape
     count = sum(b.shape[0] for b in blocks)
     total = rows * X * Y
     pieces = (ZL, total // (ZL * CORES) + 2 * HALO, width)
@@ -170,7 +168,7 @@
         grid_spec=pltpu.PrefetchScalarGridSpec(
             num_scalar_prefetch=1,
             grid=(LEVELS,),
-            in_specs=product_specs(blocks, weight) + [whole(zero.shape), whole(sides.shape)],
+            in_specs=product_specs(blocks, weight) + [whole(near.shape)],
             out_specs=(whole(pieces),) * 2,
             scratch_shapes=[
                 pltpu.VMEM((count * rows, width), jnp.float32),
@@ -180,7 +178,7 @@
         compiler_params=params(18),
         cost_estimate=product_cost(blocks, weight),
         name="project_place",
-    )(jnp.stack([core, x, y]), *blocks, weight, zero, sides)
+    )(jnp.stack([core, x, y]), *blocks, weight, near)
 
 
 def join_kernel(meta_ref, keep_ref, got_ref, own_ref, *away_refs):
@@ -288,9 +286,15 @@
 
 
 def weight_grad_kernel(meta_ref, features_ref, *refs):
-    *group_refs, out_ref, mix_ref, grads_ref = refs
+    *group_refs, out_ref, mix_ref, grads_ref, held_ref, sem = refs
     half = grads_ref.shape[1] // ZH
     width = grads_ref.shape[2]
+    held = [
+        pltpu.make_async_copy(features_ref.at[:, at], held_ref.at[at], sem.at[at])
+        for at in range(LEVELS)
+    ]
+    for copy in held:
+        copy.start()
     mix = jnp.zeros((TAIL, width), jnp.float32)
     for at, group_ref in enumerate(group_refs):
         for part in range(2):
@@ -301,9 +305,10 @@
         for sequence in range(ZH):
             mix = mix + group_ref[sequence, pl.ds(2 * half, TAIL), :].astype(jnp.float32)
     mix_ref[...] = jnp.sum(mix, axis=0, keepdims=True)
-    blocks = features_ref.shape[0]
-    for level in range(LEVELS):
-        left = jnp.concatenate([features_ref[e, level] for e in range(blocks)], axis=1)
+    blocks = held_ref.shape[1]
+    for level, copy in enumerate(held):
+        copy.wait()
+        left = jnp.concatenate([held_ref[level, e] for e in range(blocks)], axis=1)
         right = grads_ref[...].reshape(-1, width)
         term = jnp.dot(left, right, preferred_element_type=jnp.float32)
         out_ref[level] = term.astype(jnp.bfloat16)
@@ -318,10 +323,14 @@
             jax.ShapeDtypeStruct((LEVELS, columns, width), jnp.bfloat16),
             jax.ShapeDtypeStruct((1, width), jnp.float32),
         ),
-        in_specs=[SMEM] + [VMEM] * (count + 1),
+        in_specs=[SMEM, pl.BlockSpec(memory_space=pltpu.HBM)] + [VMEM] * count,
         out_specs=(VMEM, VMEM),
-        scratch_shapes=[pltpu.VMEM((draft, tokens, width), jnp.bfloat16)],
-        compiler_params=params(28),
+        scratch_shapes=[
+            pltpu.VMEM((draft, tokens, width), jnp.bfloat16),
+            pltpu.VMEM((LEVELS, draft, columns, tokens), jnp.bfloat16),
+            pltpu.SemaphoreType.DMA((LEVELS,)),
+        ],
+        compiler_params=params(46),
         cost_estimate=pl.CostEstimate(
             flops=2 * draft * LEVELS * columns * tokens * width,
             bytes_accessed=2 * features.size + 2 * draft * tokens * width,
@@ -421,13 +430,12 @@
     low, high = pair(own, next_), pair(across, last)
     up_low, down_high = plane_move(1, False)(low), plane_move(-1, False)(high)
     up_high, down_low = plane_move(1, False)(high), plane_move(-1, False)(low)
-    zero = project([low, high], weight, 14)
-    up_low, down_high, zero, later = lax.optimization_barrier((up_low, down_high, zero, own))
+    up_low, down_high, later = lax.optimization_barrier((up_low, down_high, own))
     traded = trade_columns(later)
     far_low, far_high = plane_move(1, False)(up_low), plane_move(-1, False)(down_high)
-    sides = project([up_low, up_high, down_low, down_high], weight, 58)
-    far_low, far_high, sides = lax.optimization_barrier((far_low, far_high, sides))
-    keep, send = project_place([far_low, far_high], weight, zero, sides, core, x, y)
+    near = project([low, high, up_low, up_high, down_low, down_high], weight, 58)
+    far_low, far_high, near = lax.optimization_barrier((far_low, far_high, near))
+    keep, send = project_place([far_low, far_high], weight, near, core, x, y)
     mine, *away = join(keep, from_other_core(send), zl)
     top, mine, traded = lax.optimization_barrier((own[LEVELS - 1], mine, traded))
     halves = send_high(top, draft_index)

time: 218 us -> 217 us (level)
  waiting for transfers between devices: 37 us -> 41 us
  local copies, waits for them, and re-layouts: 10.9 us -> 7.47 us
    ppermute x1, waiting for transfers between devices: 6.4 us -> 0.92 us  [send_high(): lax.ppermute(jnp.where(even, right, left), axes, crossed)]
    unnamed x24 -> x14, local copies, waits for them, and re-layouts: 9.31 us -> 4.04 us
    ppermute x1, waiting for transfers between devices: 2.57 us -> 7.57 us  [send_high(): lax.ppermute(jnp.where(even, left, right), axes, straight)]
    ppermute x9, waiting for transfers between devices: 4.74 us -> 9.48 us  [plane_move(): return lambda block: lax.ppermute(block, ('tp', 'draft'), pairs)]
    ppermute x1, starting transfers between devices: 3.44 us -> 7.69 us  [send_high(): lax.ppermute(jnp.where(even, left, right), axes, straight)]
    ppermute x3, starting transfers between devices: 11.3 us -> 8.97 us  [from_zl(): return lax.ppermute(block, 'tp', pairs)]
    pallas_call x2 -> x1, Pallas kernels: 8.76 us -> 6.62 us  [project(): pl.pallas_call(project_kernel, grid=(LEVELS,), out_shape=jax.ShapeDtypeSt...]
  transfers between devices with their start and end apart: 27 -> 27, of which waited for: 7 -> 9; matrix products, arithmetic and copies ran while one was open for 1% -> 2% of each run, Pallas kernels for 8% -> 7%
where the time goes in v13:
time: 217 us; the launch traced here: 216 us
  starting transfers between devices  100 us (46%)
  waiting for transfers between devices  41 us (19%)
  blocking collectives  25.3 us (12%)
  Pallas kernels  23.9 us (11%)
  between operations  16.4 us (8%)
  local copies, waits for them, and re-layouts  7.47 us (3%)
    ppermute x9, starting transfers between devices, plane_move(): return lambda block: lax.ppermute(block, ('tp', 'draft'), pairs)  26.1 us
    all_gather x1, blocking collectives, gather_grads(): stack = lax.all_gather(grad, 'dp', axis=0, tiled=False)  25.3 us
    ppermute x4, waiting for transfers between devices, from_z(): return lax.ppermute(block, ('tp', 'dp'), pairs)  20.5 us
    ppermute x4, starting transfers between devices, from_z(): return lax.ppermute(block, ('tp', 'dp'), pairs)  16.1 us
    all_to_all x1, starting transfers between devices, trade_columns(): lax.all_to_all(quarters, 'dp', split_axis=0, concat_axis=0, tiled=True)  14.7 us
    ppermute x5, starting transfers between devices, from_other_core(): return lax.ppermute(block, 'tp', [(t ^ 1, t) for t in range(ZL * CORES)])  13.2 us
    ppermute x9, waiting for transfers between devices, plane_move(): return lambda block: lax.ppermute(block, ('tp', 'draft'), pairs)  9.48 us
    ppermute x3, starting transfers between devices, from_zl(): return lax.ppermute(block, 'tp', pairs)  8.97 us
  transfers between devices with their start and end apart: 27, of which 9 were waited for; matrix products, arithmetic and copies ran while one was open for 2% of the time, Pallas kernels for 7%

profile of v13, /device:TPU:5, one launch (start us, length us, event | category | flops | bytes accessed | tf_op | source)
XLA Modules:
  0.0 215.8 jit_solution(7920515388989569555)
XLA Ops:
  7.2 4.6 %collective-permute-start = (bf16[3,64,1024]{2,1,0:T(8,128)(2,1)}, bf16[3,64,1024]{2,1,0:T(8,128)(2,1)S(1)}, u32[]{:S(2)}, u32[]{:S(2)}) collective-permute-start(bf16[3,64,1024]{2,1,0:T(8,128)(2,1)} %bitcast.39), channel_id=1, source_target_pairs={{4,0},{5,1},{6,2},{7,3},{8,4},{9,5},{10,6},{11,7},{12,8},{13,9},{1... | collective-permute-start | bytes 1179656 | tf_op jit(solution)/shard_map/ppermute | solution.py:31
  11.8 1.9 collective-permute-start.3
  13.7 3.5 %collective-permute-start.2 = (bf16[3,64,1024]{2,1,0:T(8,128)(2,1)}, bf16[3,64,1024]{2,1,0:T(8,128)(2,1)S(1)}, u32[]{:S(2)}, u32[]{:S(2)}) collective-permute-start(bf16[3,64,1024]{2,1,0:T(8,128)(2,1)} %bitcast.41), channel_id=1, source_target_pairs={{8,0},{9,1},{10,2},{11,3},{12,4},{13,5},{14,6},{15,7},{0,8},{1,9},... | collective-permute-start | bytes 1179656 | tf_op jit(solution)/shard_map/ppermute | solution.py:31
  17.3 0.0 copy-start.2
  17.3 1.0 copy-done.2
  18.3 0.9 pair.2.refs_0_
  19.3 2.4 %collective-permute-start.1 = (bf16[2,3,64,1024]{3,2,1,0:T(8,128)(2,1)}, bf16[2,3,64,1024]{3,2,1,0:T(8,128)(2,1)}, u32[]{:S(2)}, u32[]{:S(2)}) collective-permute-start(bf16[2,3,64,1024]{3,2,1,0:T(8,128)(2,1)} %pair.2.refs_0_), channel_id=1, source_target_pairs={{1,0},{2,1},{3,2},{0,3},{5,4},{6,5},{7,6},{4,7},{9,8},{10,9},{11,1... | collective-permute-start | bytes 2359304 | tf_op jit(solution)/shard_map/ppermute | solution.py:31
  21.7 4.4 %collective-permute-done.3.second_ref = bf16[3,64,1024]{2,1,0:T(8,128)(2,1)S(1)} collective-permute-done((bf16[3,64,1024]{2,1,0:T(8,128)(2,1)}, bf16[3,64,1024]{2,1,0:T(8,128)(2,1)S(1)}, u32[]{:S(2)}, u32[]{:S(2)}) %collective-permute-start.3) | collective-permute-done | bytes 393248 | tf_op jit(solution)/shard_map/ppermute | solution.py:31
  26.1 0.0 collective-permute-done.2.first_ref
  26.1 0.9 pair.3.refs_1_
  27.0 3.0 %collective-permute-start.4 = (bf16[2,3,64,1024]{3,2,1,0:T(8,128)(2,1)}, bf16[2,3,64,1024]{3,2,1,0:T(8,128)(2,1)}, u32[]{:S(2)}, u32[]{:S(2)}) collective-permute-start(bf16[2,3,64,1024]{3,2,1,0:T(8,128)(2,1)} %pair.3.refs_1_), channel_id=1, source_target_pairs={{3,0},{0,1},{1,2},{2,3},{7,4},{4,5},{5,6},{6,7},{11,8},{8,9},{9,10... | collective-permute-start | bytes 2359304 | tf_op jit(solution)/shard_map/ppermute | solution.py:31
  30.0 2.1 collective-permute-start.8
  32.1 3.2 %collective-permute-start.7 = (bf16[2,3,64,1024]{3,2,1,0:T(8,128)(2,1)}, bf16[2,3,64,1024]{3,2,1,0:T(8,128)(2,1)}, u32[]{:S(2)}, u32[]{:S(2)}) collective-permute-start(bf16[2,3,64,1024]{3,2,1,0:T(8,128)(2,1)} %pair.3.refs_1_), channel_id=1, source_target_pairs={{1,0},{2,1},{3,2},{0,3},{5,4},{6,5},{7,6},{4,7},{9,8},{10,9},{11,1... | collective-permute-start | bytes 2359304 | tf_op jit(solution)/shard_map/ppermute | solution.py:31
  35.3 0.9 collective-permute-done.1.refs_2_
  36.2 4.2 %collective-permute-done.4.refs_5_ = bf16[2,3,64,1024]{3,2,1,0:T(8,128)(2,1)} collective-permute-done((bf16[2,3,64,1024]{3,2,1,0:T(8,128)(2,1)}, bf16[2,3,64,1024]{3,2,1,0:T(8,128)(2,1)}, u32[]{:S(2)}, u32[]{:S(2)}) %collective-permute-start.4) | collective-permute-done | bytes 786464 | tf_op jit(solution)/shard_map/ppermute | solution.py:31
  40.4 2.2 collective-permute-start.5
  42.5 3.1 %collective-permute-start.6 = (bf16[2,3,64,1024]{3,2,1,0:T(8,128)(2,1)}, bf16[2,3,64,1024]{3,2,1,0:T(8,128)(2,1)}, u32[]{:S(2)}, u32[]{:S(2)}) collective-permute-start(bf16[2,3,64,1024]{3,2,1,0:T(8,128)(2,1)} %collective-permute-done.4.refs_5_), channel_id=1, source_target_pairs={{3,0},{0,1},{1,2},{2,3},{7,4},{4,5},{5,6},{6,7},{11,8},{8,9},{9,10... | collective-permute-start | bytes 2359304 | tf_op jit(solution)/shard_map/ppermute | solution.py:31
  45.7 1.8 copy.10
  47.5 14.7 %all-to-all-start = ((bf16[4,3,64,256]{3,2,1,0:T(8,128)(2,1)}), bf16[4,3,64,256]{3,2,1,0:T(8,128)(2,1)S(1)}, u32[]{:S(2)}, u32[]{:S(2)}) async-start(bf16[4,3,64,256]{3,2,1,0:T(8,128)(2,1)} %bitcast.46), calls=%async_computation | async-start | bytes 786432 | tf_op jit(solution)/shard_map/all_to_all | solution.py:396
  62.1 0.1 pad_add_fusion.1.meta_ref
  62.2 0.0 collective-permute-done.8.refs_4_
  62.2 0.0 collective-permute-done.7.refs_3_
  62.2 0.0 copy-start.5
  62.2 6.6 %project.1.refs_3_ = bf16[12,64,512]{2,1,0:T(8,128)(2,1)} custom-call(bf16[2,3,64,1024]{3,2,1,0:T(8,128)(2,1)} %pair.2.refs_0_, bf16[2,3,64,1024]{3,2,1,0:T(8,128)(2,1)} %pair.3.refs_1_, bf16[2,3,64,1024]{3,2,1,0:T(8,128)(2,1)} %collective-permute-done.1.refs_2_, bf16[2,3,64,1024]{3,2,1,0:T(8,128)(2,1)} %collective-permute-done.7.refs_3_, ...), custom_call_target="tpu_custom_call" | custom-call | bytes 4718592 | tf_op jit(solution)/shard_map/project/pallas_call | solution.py:114
  68.9 0.0 collective-permute-done.5.refs_0_
  68.9 1.1 copy-done.1
  70.0 4.7 %project_place.1 = (bf16[4,144,512]{2,1,0:T(8,128)(2,1)S(1)}, bf16[4,144,512]{2,1,0:T(8,128)(2,1)}) custom-call(s32[3]{0:T(128)S(1)} %pad_add_fusion.1.meta_ref, bf16[2,3,64,1024]{3,2,1,0:T(8,128)(2,1)} %collective-permute-done.5.refs_0_, bf16[2,3,64,1024]{3,2,1,0:T(8,128)(2,1)} %collective-permute-done.6.refs_1_, bf16[3,1024,512]{2,1,0:T(8,128)(2,1)S(1)} %bitcast.34, ...), custom_call_target="tpu_custom_call" | custom-call | bytes 1572864 | tf_op jit(solution)/shard_map/project_place/pallas_call | solution.py:165
  74.7 0.8 copy-done.3
  75.5 3.9 %collective-permute-start.9 = (bf16[4,144,512]{2,1,0:T(8,128)(2,1)}, bf16[4,144,512]{2,1,0:T(8,128)(2,1)S(1)}, u32[]{:S(2)}, u32[]{:S(2)}) collective-permute-start(bf16[4,144,512]{2,1,0:T(8,128)(2,1)} %get-tuple-element.30), channel_id=1, source_target_pairs={{64,0},{0,64},{192,128},{128,192},{320,256},{256,320},{448,384},{3... | collective-permute-start | bytes 1769480 | tf_op jit(solution)/shard_map/ppermute | solution.py:35
  79.4 0.9 slice_bitcast_fusion
  80.4 0.9 collective-permute-done.9.got_ref
  81.3 1.1 copy-done.4
  82.3 0.1 join.1
  82.5 1.6 turn.1
  84.0 0.0 all-gather.4.cloned.1.call-update
  84.1 0.6 dynamic_slice.3
  84.7 0.7 maximum_reduce_fusion
  87.3 7.8 %collective-permute-start.16 = (bf16[16,512]{1,0:T(8,128)(2,1)S(1)}, bf16[16,512]{1,0:T(8,128)(2,1)S(1)}, u32[]{:S(2)}, u32[]{:S(2)}) collective-permute-start(bf16[16,512]{1,0:T(8,128)(2,1)S(1)} %get-tuple-element.51), channel_id=1, source_target_pairs={{2,1},{4,65},{6,129},{8,193},{10,257},{12,321},{14,385},{66,3},{68... | collective-permute-start | bytes 49160 | tf_op jit(solution)/shard_map/ppermute | solution.py:389
  95.1 3.8 %collective-permute-start.15 = (bf16[16,512]{1,0:T(8,128)(2,1)S(1)}, bf16[16,512]{1,0:T(8,128)(2,1)S(1)}, u32[]{:S(2)}, u32[]{:S(2)}) collective-permute-start(bf16[16,512]{1,0:T(8,128)(2,1)S(1)} %get-tuple-element.52), channel_id=1, source_target_pairs={{2,0},{4,64},{6,128},{8,192},{10,256},{12,320},{14,384},{66,2},{68... | collective-permute-start | bytes 49160 | tf_op jit(solution)/shard_map/ppermute | solution.py:388
  98.8 4.9 %collective-permute-start.10 = (bf16[144,512]{1,0:T(8,128)(2,1)S(1)}, bf16[144,512]{1,0:T(8,128)(2,1)S(1)}, u32[]{:S(2)}, u32[]{:S(2)}) collective-permute-start(bf16[144,512]{1,0:T(8,128)(2,1)S(1)} %get-tuple-element.34), channel_id=1, source_target_pairs={{128,0},{192,64},{256,128},{320,192},{384,256},{448,320},{0,384},{... | collective-permute-start | bytes 442376 | tf_op jit(solution)/shard_map/ppermute | solution.py:40
  103.7 1.9 collective-permute-start.11
  105.6 2.2 %collective-permute-start.12 = (bf16[144,512]{1,0:T(8,128)(2,1)S(1)}, bf16[144,512]{1,0:T(8,128)(2,1)S(1)}, u32[]{:S(2)}, u32[]{:S(2)}) collective-permute-start(bf16[144,512]{1,0:T(8,128)(2,1)S(1)} %get-tuple-element.36), channel_id=1, source_target_pairs={{384,0},{448,64},{0,128},{64,192},{128,256},{192,320},{256,384},{3... | collective-permute-start | bytes 442376 | tf_op jit(solution)/shard_map/ppermute | solution.py:40
  107.9 1.9 collective-permute-start.14
  109.8 7.7 %collective-permute-start.13 = (bf16[64,512]{1,0:T(8,128)(2,1)S(1)}, bf16[64,512]{1,0:T(8,128)(2,1)S(1)}, u32[]{:S(2)}, u32[]{:S(2)}) collective-permute-start(bf16[64,512]{1,0:T(8,128)(2,1)S(1)} %get-tuple-element.54), channel_id=1, source_target_pairs={{0,0},{1,1},{2,64},{3,65},{4,128},{5,129},{6,192},{7,193},{8,256},... | collective-permute-start | bytes 196616 | tf_op jit(solution)/shard_map/ppermute | solution.py:386
  117.5 0.7 pad_add_fusion.meta_ref
  118.2 0.9 collective-permute-done.14.refs_5_
  119.1 7.6 %collective-permute-done.13.refs_4_ = bf16[64,512]{1,0:T(8,128)(2,1)S(1)} collective-permute-done((bf16[64,512]{1,0:T(8,128)(2,1)S(1)}, bf16[64,512]{1,0:T(8,128)(2,1)S(1)}, u32[]{:S(2)}, u32[]{:S(2)}) %collective-permute-start.13) | collective-permute-done | bytes 65568 | tf_op jit(solution)/shard_map/ppermute | solution.py:386
  126.7 1.4 chain.1
  128.1 25.3 %all-gather = bf16[576,512]{1,0:T(8,128)(2,1)S(1)} all-gather(bf16[144,512]{1,0:T(8,128)(2,1)S(1)} %chain.1), channel_id=2, replica_groups=mesh['tp'=8,'dp'=4,'draft'=16] {'dp'}, dimensions={0}, use_global_device_ids=true | all-gather | bytes 737280 | tf_op jit(solution)/shard_map/all_gather | solution.py:400
  153.4 1.9 collective-permute-start.19
  155.3 6.8 %collective-permute-start.18 = (bf16[4,144,512]{2,1,0:T(8,128)(2,1)S(1)}, bf16[4,144,512]{2,1,0:T(8,128)(2,1)S(1)}, u32[]{:S(2)}, u32[]{:S(2)}) collective-permute-start(bf16[4,144,512]{2,1,0:T(8,128)(2,1)S(1)} %bitcast.36), channel_id=1, source_target_pairs={{432,0},{384,16},{400,32},{416,48},{496,64},{448,80},{464,96},{480... | collective-permute-start | bytes 1769480 | tf_op jit(solution)/shard_map/ppermute | solution.py:53
  162.1 1.9 collective-permute-start.17
  164.1 4.1 %collective-permute-start.21 = (bf16[2,144,512]{2,1,0:T(8,128)(2,1)S(1)}, bf16[2,144,512]{2,1,0:T(8,128)(2,1)S(1)}, u32[]{:S(2)}, u32[]{:S(2)}) collective-permute-start(bf16[2,144,512]{2,1,0:T(8,128)(2,1)S(1)} %bitcast.48), channel_id=1, source_target_pairs={{304,0},{256,16},{272,32},{288,48},{368,64},{320,80},{336,96},{352... | collective-permute-start | bytes 884744 | tf_op jit(solution)/shard_map/ppermute | solution.py:53
  168.2 3.3 %collective-permute-start.20 = (bf16[2,144,512]{2,1,0:T(8,128)(2,1)S(1)}, bf16[2,144,512]{2,1,0:T(8,128)(2,1)S(1)}, u32[]{:S(2)}, u32[]{:S(2)}) collective-permute-start(bf16[2,144,512]{2,1,0:T(8,128)(2,1)S(1)} %bitcast.47), channel_id=1, source_target_pairs={{256,0},{272,16},{288,32},{304,48},{320,64},{336,80},{352,96},{368... | collective-permute-start | bytes 884744 | tf_op jit(solution)/shard_map/ppermute | solution.py:53
  171.5 16.0 %collective-permute-done.21 = bf16[2,144,512]{2,1,0:T(8,128)(2,1)S(1)} collective-permute-done((bf16[2,144,512]{2,1,0:T(8,128)(2,1)S(1)}, bf16[2,144,512]{2,1,0:T(8,128)(2,1)S(1)}, u32[]{:S(2)}, u32[]{:S(2)}) %collective-permute-start.21) | collective-permute-done | bytes 294944 | tf_op jit(solution)/shard_map/ppermute | solution.py:53
  187.5 4.5 %collective-permute-done.20 = bf16[2,144,512]{2,1,0:T(8,128)(2,1)S(1)} collective-permute-done((bf16[2,144,512]{2,1,0:T(8,128)(2,1)S(1)}, bf16[2,144,512]{2,1,0:T(8,128)(2,1)S(1)}, u32[]{:S(2)}, u32[]{:S(2)}) %collective-permute-start.20) | collective-permute-done | bytes 294944 | tf_op jit(solution)/shard_map/ppermute | solution.py:53
  192.0 0.1 pad_maximum_fusion.refs_4_
  192.1 0.0 all-gather.4.cloned.1.call-done
  192.1 3.0 %collective-permute-start.22 = (bf16[4,144,512]{2,1,0:T(8,128)(2,1)S(1)}, bf16[4,144,512]{2,1,0:T(8,128)(2,1)S(1)}, u32[]{:S(2)}, u32[]{:S(2)}) collective-permute-start(bf16[4,144,512]{2,1,0:T(8,128)(2,1)S(1)} %collective-permute-done.17.refs_2_), channel_id=1, source_target_pairs={{64,0},{0,64},{192,128},{128,192},{320,256},{256,320},{448,384},{3... | collective-permute-start | bytes 1769480 | tf_op jit(solution)/shard_map/ppermute | solution.py:35
  195.2 1.9 collective-permute-start.23
  197.1 2.4 %collective-permute-start.24 = (bf16[4,144,512]{2,1,0:T(8,128)(2,1)S(1)}, bf16[4,144,512]{2,1,0:T(8,128)(2,1)}, u32[]{:S(2)}, u32[]{:S(2)}) collective-permute-start(bf16[4,144,512]{2,1,0:T(8,128)(2,1)S(1)} %pad_maximum_fusion.refs_4_), channel_id=1, source_target_pairs={{64,0},{0,64},{192,128},{128,192},{320,256},{256,320},{448,384},{3... | collective-permute-start | bytes 1769480 | tf_op jit(solution)/shard_map/ppermute | solution.py:35
  199.6 0.1 stack.56.meta_ref
  199.7 1.6 collective-permute-done.24.refs_7_
  201.2 7.7 %weight_grad.1 = (bf16[3,256,512]{2,1,0:T(8,128)(2,1)}, f32[1,512]{1,0:T(1,128)}) custom-call(s32[8]{0:T(128)S(1)} %stack.56.meta_ref, bf16[16,3,256,256]{3,2,1,0:T(8,128)(2,1)} %bitcast.49, bf16[4,144,512]{2,1,0:T(8,128)(2,1)S(1)} %bitcast.38, bf16[4,144,512]{2,1,0:T(8,128)(2,1)S(1)} %collective-permute-done.19.refs_1_, ...), custom_call_target="tpu_custom_call" | custom-call | flops 3221225472 | bytes 10485760 | tf_op jit(solution)/shard_map/weight_grad/pallas_call | solution.py:320
  (25 shorter events, 0.1 us)
Async XLA Ops:
  7.2 10.1 %collective-permute-start = (bf16[3,64,1024]{2,1,0:T(8,128)(2,1)}, bf16[3,64,1024]{2,1,0:T(8,128)(2,1)S(1)}, u32[]{:S(2)}, u32[]{:S(2)}) collective-permute-start(bf16[3,64,1024]{2,1,0:T(8,128)(2,1)} %bitcast.39), channel_id=1, source_target_pairs={{4,0},{5,1},{6,2},{7,3},{8,4},{9,5},{10,6},{11,7},{12,8},{13,9},{1... | collective-permute-start | bytes 1179656 | tf_op jit(solution)/shard_map/ppermute | solution.py:31
  11.8 14.3 %collective-permute-start.3 = (bf16[3,64,1024]{2,1,0:T(8,128)(2,1)}, bf16[3,64,1024]{2,1,0:T(8,128)(2,1)S(1)}, u32[]{:S(2)}, u32[]{:S(2)}) collective-permute-start(bf16[3,64,1024]{2,1,0:T(8,128)(2,1)} %bitcast.40), channel_id=1, source_target_pairs={{12,0},{13,1},{14,2},{15,3},{0,4},{1,5},{2,6},{3,7},{4,8},{5,9},{6... | collective-permute-start | bytes 1179656 | tf_op jit(solution)/shard_map/ppermute | solution.py:31
  13.7 12.4 %collective-permute-start.2 = (bf16[3,64,1024]{2,1,0:T(8,128)(2,1)}, bf16[3,64,1024]{2,1,0:T(8,128)(2,1)S(1)}, u32[]{:S(2)}, u32[]{:S(2)}) collective-permute-start(bf16[3,64,1024]{2,1,0:T(8,128)(2,1)} %bitcast.41), channel_id=1, source_target_pairs={{8,0},{9,1},{10,2},{11,3},{12,4},{13,5},{14,6},{15,7},{0,8},{1,9},... | collective-permute-start | bytes 1179656 | tf_op jit(solution)/shard_map/ppermute | solution.py:31
  17.3 1.0 copy-start.2
  19.3 49.6 %copy-start = (bf16[1024,3,512]{2,0,1:T(8,128)(2,1)S(1)}, bf16[1024,3,512]{2,0,1:T(8,128)(2,1)}, u32[]{:S(2)}) copy-start(bf16[1024,3,512]{2,0,1:T(8,128)(2,1)} %param.5) | copy-start | bytes 9437188
  19.3 16.9 %collective-permute-start.1 = (bf16[2,3,64,1024]{3,2,1,0:T(8,128)(2,1)}, bf16[2,3,64,1024]{3,2,1,0:T(8,128)(2,1)}, u32[]{:S(2)}, u32[]{:S(2)}) collective-permute-start(bf16[2,3,64,1024]{3,2,1,0:T(8,128)(2,1)} %pair.2.refs_0_), channel_id=1, source_target_pairs={{1,0},{2,1},{3,2},{0,3},{5,4},{6,5},{7,6},{4,7},{9,8},{10,9},{11,1... | collective-permute-start | bytes 2359304 | tf_op jit(solution)/shard_map/ppermute | solution.py:31
  27.0 13.3 %collective-permute-start.4 = (bf16[2,3,64,1024]{3,2,1,0:T(8,128)(2,1)}, bf16[2,3,64,1024]{3,2,1,0:T(8,128)(2,1)}, u32[]{:S(2)}, u32[]{:S(2)}) collective-permute-start(bf16[2,3,64,1024]{3,2,1,0:T(8,128)(2,1)} %pair.3.refs_1_), channel_id=1, source_target_pairs={{3,0},{0,1},{1,2},{2,3},{7,4},{4,5},{5,6},{6,7},{11,8},{8,9},{9,10... | collective-permute-start | bytes 2359304 | tf_op jit(solution)/shard_map/ppermute | solution.py:31
  30.0 32.2 %collective-permute-start.8 = (bf16[2,3,64,1024]{3,2,1,0:T(8,128)(2,1)}, bf16[2,3,64,1024]{3,2,1,0:T(8,128)(2,1)}, u32[]{:S(2)}, u32[]{:S(2)}) collective-permute-start(bf16[2,3,64,1024]{3,2,1,0:T(8,128)(2,1)} %pair.2.refs_0_), channel_id=1, source_target_pairs={{3,0},{0,1},{1,2},{2,3},{7,4},{4,5},{5,6},{6,7},{11,8},{8,9},{9,10... | collective-permute-start | bytes 2359304 | tf_op jit(solution)/shard_map/ppermute | solution.py:31
  32.1 30.1 %collective-permute-start.7 = (bf16[2,3,64,1024]{3,2,1,0:T(8,128)(2,1)}, bf16[2,3,64,1024]{3,2,1,0:T(8,128)(2,1)}, u32[]{:S(2)}, u32[]{:S(2)}) collective-permute-start(bf16[2,3,64,1024]{3,2,1,0:T(8,128)(2,1)} %pair.3.refs_1_), channel_id=1, source_target_pairs={{1,0},{2,1},{3,2},{0,3},{5,4},{6,5},{7,6},{4,7},{9,8},{10,9},{11,1... | collective-permute-start | bytes 2359304 | tf_op jit(solution)/shard_map/ppermute | solution.py:31
  40.4 28.5 %collective-permute-start.5 = (bf16[2,3,64,1024]{3,2,1,0:T(8,128)(2,1)}, bf16[2,3,64,1024]{3,2,1,0:T(8,128)(2,1)}, u32[]{:S(2)}, u32[]{:S(2)}) collective-permute-start(bf16[2,3,64,1024]{3,2,1,0:T(8,128)(2,1)} %collective-permute-done.1.refs_2_), channel_id=1, source_target_pairs={{1,0},{2,1},{3,2},{0,3},{5,4},{6,5},{7,6},{4,7},{9,8},{10,9},{11,1... | collective-permute-start | bytes 2359304 | tf_op jit(solution)/shard_map/ppermute | solution.py:31
  42.5 26.3 %collective-permute-start.6 = (bf16[2,3,64,1024]{3,2,1,0:T(8,128)(2,1)}, bf16[2,3,64,1024]{3,2,1,0:T(8,128)(2,1)}, u32[]{:S(2)}, u32[]{:S(2)}) collective-permute-start(bf16[2,3,64,1024]{3,2,1,0:T(8,128)(2,1)} %collective-permute-done.4.refs_5_), channel_id=1, source_target_pairs={{3,0},{0,1},{1,2},{2,3},{7,4},{4,5},{5,6},{6,7},{11,8},{8,9},{9,10... | collective-permute-start | bytes 2359304 | tf_op jit(solution)/shard_map/ppermute | solution.py:31
  47.5 35.0 %all-to-all-start = ((bf16[4,3,64,256]{3,2,1,0:T(8,128)(2,1)}), bf16[4,3,64,256]{3,2,1,0:T(8,128)(2,1)S(1)}, u32[]{:S(2)}, u32[]{:S(2)}) async-start(bf16[4,3,64,256]{3,2,1,0:T(8,128)(2,1)} %bitcast.46), calls=%async_computation | async-start | bytes 786432 | tf_op jit(solution)/shard_map/all_to_all | solution.py:396
  62.1 130.0 %all-gather.4.cloned.1.call-start = ((), (), s32[]{:S(2)}) async-start(), calls=%async_computation.1 | async-start | bytes 6684672 | tf_op jit(solution)/shard_map/all_gather | solution.py:442
  62.2 21.9 %copy-start.6 = (s32[4]{0:T(128)S(1)}, s32[4]{0:T(128)}, u32[]{:S(2)}) copy-start(s32[4]{0:T(128)} %param.7) | copy-start | bytes 52
  62.2 64.5 %copy-start.5 = (f32[512]{0:T(512)S(1)}, f32[512]{0:T(512)}, u32[]{:S(2)}) copy-start(f32[512]{0:T(512)} %param.6) | copy-start | bytes 6148
  68.9 1.1 copy-start.1
  74.7 0.8 copy-start.3
  75.5 5.8 %collective-permute-start.9 = (bf16[4,144,512]{2,1,0:T(8,128)(2,1)}, bf16[4,144,512]{2,1,0:T(8,128)(2,1)S(1)}, u32[]{:S(2)}, u32[]{:S(2)}) collective-permute-start(bf16[4,144,512]{2,1,0:T(8,128)(2,1)} %get-tuple-element.30), channel_id=1, source_target_pairs={{64,0},{0,64},{192,128},{128,192},{320,256},{256,320},{448,384},{3... | collective-permute-start | bytes 1769480 | tf_op jit(solution)/shard_map/ppermute | solution.py:35
  81.2 1.1 copy-start.4
  87.3 20.6 %collective-permute-start.16 = (bf16[16,512]{1,0:T(8,128)(2,1)S(1)}, bf16[16,512]{1,0:T(8,128)(2,1)S(1)}, u32[]{:S(2)}, u32[]{:S(2)}) collective-permute-start(bf16[16,512]{1,0:T(8,128)(2,1)S(1)} %get-tuple-element.51), channel_id=1, source_target_pairs={{2,1},{4,65},{6,129},{8,193},{10,257},{12,321},{14,385},{66,3},{68... | collective-permute-start | bytes 49160 | tf_op jit(solution)/shard_map/ppermute | solution.py:389
  95.1 14.7 %collective-permute-start.15 = (bf16[16,512]{1,0:T(8,128)(2,1)S(1)}, bf16[16,512]{1,0:T(8,128)(2,1)S(1)}, u32[]{:S(2)}, u32[]{:S(2)}) collective-permute-start(bf16[16,512]{1,0:T(8,128)(2,1)S(1)} %get-tuple-element.52), channel_id=1, source_target_pairs={{2,0},{4,64},{6,128},{8,192},{10,256},{12,320},{14,384},{66,2},{68... | collective-permute-start | bytes 49160 | tf_op jit(solution)/shard_map/ppermute | solution.py:388
  98.8 27.8 %collective-permute-start.10 = (bf16[144,512]{1,0:T(8,128)(2,1)S(1)}, bf16[144,512]{1,0:T(8,128)(2,1)S(1)}, u32[]{:S(2)}, u32[]{:S(2)}) collective-permute-start(bf16[144,512]{1,0:T(8,128)(2,1)S(1)} %get-tuple-element.34), channel_id=1, source_target_pairs={{128,0},{192,64},{256,128},{320,192},{384,256},{448,320},{0,384},{... | collective-permute-start | bytes 442376 | tf_op jit(solution)/shard_map/ppermute | solution.py:40
  103.7 23.0 %collective-permute-start.11 = (bf16[144,512]{1,0:T(8,128)(2,1)S(1)}, bf16[144,512]{1,0:T(8,128)(2,1)S(1)}, u32[]{:S(2)}, u32[]{:S(2)}) collective-permute-start(bf16[144,512]{1,0:T(8,128)(2,1)S(1)} %get-tuple-element.35), channel_id=1, source_target_pairs={{256,0},{320,64},{384,128},{448,192},{0,256},{64,320},{128,384},{1... | collective-permute-start | bytes 442376 | tf_op jit(solution)/shard_map/ppermute | solution.py:40
  105.6 21.1 %collective-permute-start.12 = (bf16[144,512]{1,0:T(8,128)(2,1)S(1)}, bf16[144,512]{1,0:T(8,128)(2,1)S(1)}, u32[]{:S(2)}, u32[]{:S(2)}) collective-permute-start(bf16[144,512]{1,0:T(8,128)(2,1)S(1)} %get-tuple-element.36), channel_id=1, source_target_pairs={{384,0},{448,64},{0,128},{64,192},{128,256},{192,320},{256,384},{3... | collective-permute-start | bytes 442376 | tf_op jit(solution)/shard_map/ppermute | solution.py:40
  107.9 11.2 %collective-permute-start.14 = (bf16[64,512]{1,0:T(8,128)(2,1)S(1)}, bf16[64,512]{1,0:T(8,128)(2,1)S(1)}, u32[]{:S(2)}, u32[]{:S(2)}) collective-permute-start(bf16[64,512]{1,0:T(8,128)(2,1)S(1)} %get-tuple-element.53), channel_id=1, source_target_pairs={{0,1},{1,0},{2,65},{3,64},{4,129},{5,128},{6,193},{7,192},{8,257},... | collective-permute-start | bytes 196616 | tf_op jit(solution)/shard_map/ppermute | solution.py:387
  109.8 16.9 %collective-permute-start.13 = (bf16[64,512]{1,0:T(8,128)(2,1)S(1)}, bf16[64,512]{1,0:T(8,128)(2,1)S(1)}, u32[]{:S(2)}, u32[]{:S(2)}) collective-permute-start(bf16[64,512]{1,0:T(8,128)(2,1)S(1)} %get-tuple-element.54), channel_id=1, source_target_pairs={{0,0},{1,1},{2,64},{3,65},{4,128},{5,129},{6,192},{7,193},{8,256},... | collective-permute-start | bytes 196616 | tf_op jit(solution)/shard_map/ppermute | solution.py:386
  153.4 38.7 %collective-permute-start.19 = (bf16[4,144,512]{2,1,0:T(8,128)(2,1)S(1)}, bf16[4,144,512]{2,1,0:T(8,128)(2,1)S(1)}, u32[]{:S(2)}, u32[]{:S(2)}) collective-permute-start(bf16[4,144,512]{2,1,0:T(8,128)(2,1)S(1)} %bitcast.35), channel_id=1, source_target_pairs={{64,0},{0,64},{192,128},{128,192},{320,256},{256,320},{448,384},{3... | collective-permute-start | bytes 1769480 | tf_op jit(solution)/shard_map/ppermute | solution.py:35
  155.3 36.8 %collective-permute-start.18 = (bf16[4,144,512]{2,1,0:T(8,128)(2,1)S(1)}, bf16[4,144,512]{2,1,0:T(8,128)(2,1)S(1)}, u32[]{:S(2)}, u32[]{:S(2)}) collective-permute-start(bf16[4,144,512]{2,1,0:T(8,128)(2,1)S(1)} %bitcast.36), channel_id=1, source_target_pairs={{432,0},{384,16},{400,32},{416,48},{496,64},{448,80},{464,96},{480... | collective-permute-start | bytes 1769480 | tf_op jit(solution)/shard_map/ppermute | solution.py:53
  162.1 30.0 %collective-permute-start.17 = (bf16[4,144,512]{2,1,0:T(8,128)(2,1)S(1)}, bf16[4,144,512]{2,1,0:T(8,128)(2,1)S(1)}, u32[]{:S(2)}, u32[]{:S(2)}) collective-permute-start(bf16[4,144,512]{2,1,0:T(8,128)(2,1)S(1)} %bitcast.37), channel_id=1, source_target_pairs={{128,0},{144,16},{160,32},{176,48},{192,64},{208,80},{224,96},{240... | collective-permute-start | bytes 1769480 | tf_op jit(solution)/shard_map/ppermute | solution.py:53
  164.1 23.4 %collective-permute-start.21 = (bf16[2,144,512]{2,1,0:T(8,128)(2,1)S(1)}, bf16[2,144,512]{2,1,0:T(8,128)(2,1)S(1)}, u32[]{:S(2)}, u32[]{:S(2)}) collective-permute-start(bf16[2,144,512]{2,1,0:T(8,128)(2,1)S(1)} %bitcast.48), channel_id=1, source_target_pairs={{304,0},{256,16},{272,32},{288,48},{368,64},{320,80},{336,96},{352... | collective-permute-start | bytes 884744 | tf_op jit(solution)/shard_map/ppermute | solution.py:53
  168.2 23.8 %collective-permute-start.20 = (bf16[2,144,512]{2,1,0:T(8,128)(2,1)S(1)}, bf16[2,144,512]{2,1,0:T(8,128)(2,1)S(1)}, u32[]{:S(2)}, u32[]{:S(2)}) collective-permute-start(bf16[2,144,512]{2,1,0:T(8,128)(2,1)S(1)} %bitcast.47), channel_id=1, source_target_pairs={{256,0},{272,16},{288,32},{304,48},{320,64},{336,80},{352,96},{368... | collective-permute-start | bytes 884744 | tf_op jit(solution)/shard_map/ppermute | solution.py:53
  192.1 7.5 %collective-permute-start.22 = (bf16[4,144,512]{2,1,0:T(8,128)(2,1)S(1)}, bf16[4,144,512]{2,1,0:T(8,128)(2,1)S(1)}, u32[]{:S(2)}, u32[]{:S(2)}) collective-permute-start(bf16[4,144,512]{2,1,0:T(8,128)(2,1)S(1)} %collective-permute-done.17.refs_2_), channel_id=1, source_target_pairs={{64,0},{0,64},{192,128},{128,192},{320,256},{256,320},{448,384},{3... | collective-permute-start | bytes 1769480 | tf_op jit(solution)/shard_map/ppermute | solution.py:35
  195.2 4.5 %collective-permute-start.23 = (bf16[4,144,512]{2,1,0:T(8,128)(2,1)S(1)}, bf16[4,144,512]{2,1,0:T(8,128)(2,1)}, u32[]{:S(2)}, u32[]{:S(2)}) collective-permute-start(bf16[4,144,512]{2,1,0:T(8,128)(2,1)S(1)} %collective-permute-done.18.refs_3_), channel_id=1, source_target_pairs={{64,0},{0,64},{192,128},{128,192},{320,256},{256,320},{448,384},{3... | collective-permute-start | bytes 1769480 | tf_op jit(solution)/shard_map/ppermute | solution.py:35
  197.1 4.2 %collective-permute-start.24 = (bf16[4,144,512]{2,1,0:T(8,128)(2,1)S(1)}, bf16[4,144,512]{2,1,0:T(8,128)(2,1)}, u32[]{:S(2)}, u32[]{:S(2)}) collective-permute-start(bf16[4,144,512]{2,1,0:T(8,128)(2,1)S(1)} %pad_maximum_fusion.refs_4_), channel_id=1, source_target_pairs={{64,0},{0,64},{192,128},{128,192},{320,256},{256,320},{448,384},{3... | collective-permute-start | bytes 1769480 | tf_op jit(solution)/shard_map/ppermute | solution.py:35
Sparse Core Ops, SparseCore 0:
  84.2 83.6 all-gather.3

commit v14 on v13

--- a/solution.py
+++ b/solution.py
@@ -428,13 +428,13 @@
 
     next_, last, across = (plane_move(step, True)(own) for step in (1, 3, 2))
     low, high = pair(own, next_), pair(across, last)
+    high, later = lax.optimization_barrier((high, own))
+    traded = trade_columns(later)
     up_low, down_high = plane_move(1, False)(low), plane_move(-1, False)(high)
     up_high, down_low = plane_move(1, False)(high), plane_move(-1, False)(low)
-    up_low, down_high, later = lax.optimization_barrier((up_low, down_high, own))
-    traded = trade_columns(later)
     far_low, far_high = plane_move(1, False)(up_low), plane_move(-1, False)(down_high)
     near = project([low, high, up_low, up_high, down_low, down_high], weight, 58)
-    far_low, far_high, near = lax.optimization_barrier((far_low, far_high, near))
+    far_low, far_high, near, traded = lax.optimization_barrier((far_low, far_high, near, traded))
     keep, send = project_place([far_low, far_high], weight, near, core, x, y)
     mine, *away = join(keep, from_other_core(send), zl)
     top, mine, traded = lax.optimization_barrier((own[LEVELS - 1], mine, traded))

time: 217 us -> 224 us (1.032)
  blocking collectives: 25.3 us -> 31.4 us
    all_gather x1, blocking collectives: 25.3 us -> 31.4 us  [gather_grads(): stack = lax.all_gather(grad, 'dp', axis=0, tiled=False)]
    ppermute x5, starting transfers between devices: 13.2 us -> 19.2 us  [from_other_core(): return lax.ppermute(block, 'tp', [(t ^ 1, t) for t in range(ZL * CORES)])]
    ppermute x1, waiting for transfers between devices: 7.57 us -> 2.74 us  [send_high(): lax.ppermute(jnp.where(even, left, right), axes, straight)]
    ppermute x1, waiting for transfers between devices: 0.92 us -> 4.82 us  [send_high(): lax.ppermute(jnp.where(even, right, left), axes, crossed)]
    ppermute x9, waiting for transfers between devices: 9.48 us -> 13.1 us  [plane_move(): return lambda block: lax.ppermute(block, ('tp', 'draft'), pairs)]
    ppermute x1, starting transfers between devices: 7.76 us -> 4.63 us  [send_high(): lax.ppermute(right[:TAIL], axes, after_right)]
    ppermute x4, waiting for transfers between devices: 20.5 us -> 17.5 us  [from_z(): return lax.ppermute(block, ('tp', 'dp'), pairs)]
    ppermute x1, starting transfers between devices: 7.69 us -> 4.72 us  [send_high(): lax.ppermute(jnp.where(even, left, right), axes, straight)]
  transfers between devices with their start and end apart: 27 -> 27, of which waited for: 9 -> 11; matrix products, arithmetic and copies ran while one was open for 2% -> 2% of each run, Pallas kernels for 7% -> 4%
where the time goes in v14:
time: 224 us; the launch traced here: 223 us
  starting transfers between devices  101 us (45%)
  waiting for transfers between devices  40.7 us (18%)
  blocking collectives  31.4 us (14%)
  Pallas kernels  24 us (11%)
  between operations  16.4 us (7%)
  local copies, waits for them, and re-layouts  7.7 us (3%)
    all_gather x1, blocking collectives, gather_grads(): stack = lax.all_gather(grad, 'dp', axis=0, tiled=False)  31.4 us
    ppermute x9, starting transfers between devices, plane_move(): return lambda block: lax.ppermute(block, ('tp', 'draft'), pairs)  27.2 us
    ppermute x5, starting transfers between devices, from_other_core(): return lax.ppermute(block, 'tp', [(t ^ 1, t) for t in range(ZL * CORES)])  19.2 us
    ppermute x4, waiting for transfers between devices, from_z(): return lax.ppermute(block, ('tp', 'dp'), pairs)  17.5 us
    all_to_all x1, starting transfers between devices, trade_columns(): lax.all_to_all(quarters, 'dp', split_axis=0, concat_axis=0, tiled=True)  14.8 us
    ppermute x4, starting transfers between devices, from_z(): return lax.ppermute(block, ('tp', 'dp'), pairs)  13.9 us
    ppermute x9, waiting for transfers between devices, plane_move(): return lambda block: lax.ppermute(block, ('tp', 'draft'), pairs)  13.1 us
    ppermute x3, starting transfers between devices, from_zl(): return lax.ppermute(block, 'tp', pairs)  9.17 us
  transfers between devices with their start and end apart: 27, of which 11 were waited for; matrix products, arithmetic and copies ran while one was open for 2% of the time, Pallas kernels for 4%

profile of v14, /device:TPU:5, one launch (start us, length us, event | category | flops | bytes accessed | tf_op | source)
XLA Modules:
  0.0 222.9 jit_solution(13572166874342486808)
XLA Ops:
  7.2 3.2 %collective-permute-start.4 = (bf16[3,64,1024]{2,1,0:T(8,128)(2,1)}, bf16[3,64,1024]{2,1,0:T(8,128)(2,1)S(1)}, u32[]{:S(2)}, u32[]{:S(2)}) collective-permute-start(bf16[3,64,1024]{2,1,0:T(8,128)(2,1)} %bitcast.39), channel_id=1, source_target_pairs={{12,0},{13,1},{14,2},{15,3},{0,4},{1,5},{2,6},{3,7},{4,8},{5,9},{6... | collective-permute-start | bytes 1179656 | tf_op jit(solution)/shard_map/ppermute | solution.py:31
  10.4 4.5 %collective-permute-start.3 = (bf16[3,64,1024]{2,1,0:T(8,128)(2,1)}, bf16[3,64,1024]{2,1,0:T(8,128)(2,1)S(1)}, u32[]{:S(2)}, u32[]{:S(2)}) collective-permute-start(bf16[3,64,1024]{2,1,0:T(8,128)(2,1)} %bitcast.40), channel_id=1, source_target_pairs={{8,0},{9,1},{10,2},{11,3},{12,4},{13,5},{14,6},{15,7},{0,8},{1,9},... | collective-permute-start | bytes 1179656 | tf_op jit(solution)/shard_map/ppermute | solution.py:31
  14.9 3.0 %collective-permute-start = (bf16[3,64,1024]{2,1,0:T(8,128)(2,1)}, bf16[3,64,1024]{2,1,0:T(8,128)(2,1)S(1)}, u32[]{:S(2)}, u32[]{:S(2)}) collective-permute-start(bf16[3,64,1024]{2,1,0:T(8,128)(2,1)} %bitcast.41), channel_id=1, source_target_pairs={{4,0},{5,1},{6,2},{7,3},{8,4},{9,5},{10,6},{11,7},{12,8},{13,9},{1... | collective-permute-start | bytes 1179656 | tf_op jit(solution)/shard_map/ppermute | solution.py:31
  17.9 4.6 %collective-permute-done.3.first_ref = bf16[3,64,1024]{2,1,0:T(8,128)(2,1)S(1)} collective-permute-done((bf16[3,64,1024]{2,1,0:T(8,128)(2,1)}, bf16[3,64,1024]{2,1,0:T(8,128)(2,1)S(1)}, u32[]{:S(2)}, u32[]{:S(2)}) %collective-permute-start.3) | collective-permute-done | bytes 393248 | tf_op jit(solution)/shard_map/ppermute | solution.py:31
  22.6 0.9 pair.3.refs_1_
  23.5 0.7 collective-permute-done.second_ref
  24.2 1.2 copy-done.2
  25.4 0.9 pair.2.refs_0_
  26.4 2.2 collective-permute-start.1
  28.5 3.1 %collective-permute-start.5 = (bf16[2,3,64,1024]{3,2,1,0:T(8,128)(2,1)}, bf16[2,3,64,1024]{3,2,1,0:T(8,128)(2,1)}, u32[]{:S(2)}, u32[]{:S(2)}) collective-permute-start(bf16[2,3,64,1024]{3,2,1,0:T(8,128)(2,1)} %pair.3.refs_1_), channel_id=1, source_target_pairs={{3,0},{0,1},{1,2},{2,3},{7,4},{4,5},{5,6},{6,7},{11,8},{8,9},{9,10... | collective-permute-start | bytes 2359304 | tf_op jit(solution)/shard_map/ppermute | solution.py:31
  31.7 1.8 copy.10
  33.4 14.8 %all-to-all-start = ((bf16[4,3,64,256]{3,2,1,0:T(8,128)(2,1)}), bf16[4,3,64,256]{3,2,1,0:T(8,128)(2,1)S(1)}, u32[]{:S(2)}, u32[]{:S(2)}) async-start(bf16[4,3,64,256]{3,2,1,0:T(8,128)(2,1)} %bitcast.46), calls=%async_computation | async-start | bytes 786432 | tf_op jit(solution)/shard_map/all_to_all | solution.py:396
  48.3 4.0 %collective-permute-start.8 = (bf16[2,3,64,1024]{3,2,1,0:T(8,128)(2,1)}, bf16[2,3,64,1024]{3,2,1,0:T(8,128)(2,1)}, u32[]{:S(2)}, u32[]{:S(2)}) collective-permute-start(bf16[2,3,64,1024]{3,2,1,0:T(8,128)(2,1)} %pair.2.refs_0_), channel_id=1, source_target_pairs={{3,0},{0,1},{1,2},{2,3},{7,4},{4,5},{5,6},{6,7},{11,8},{8,9},{9,10... | collective-permute-start | bytes 2359304 | tf_op jit(solution)/shard_map/ppermute | solution.py:31
  52.3 1.9 collective-permute-start.7
  54.2 0.0 collective-permute-done.1.refs_2_
  54.2 1.9 collective-permute-start.2
  56.2 0.0 collective-permute-done.5.refs_5_
  56.2 3.4 %collective-permute-start.6 = (bf16[2,3,64,1024]{3,2,1,0:T(8,128)(2,1)}, bf16[2,3,64,1024]{3,2,1,0:T(8,128)(2,1)}, u32[]{:S(2)}, u32[]{:S(2)}) collective-permute-start(bf16[2,3,64,1024]{3,2,1,0:T(8,128)(2,1)} %collective-permute-done.5.refs_5_), channel_id=1, source_target_pairs={{3,0},{0,1},{1,2},{2,3},{7,4},{4,5},{5,6},{6,7},{11,8},{8,9},{9,10... | collective-permute-start | bytes 2359304 | tf_op jit(solution)/shard_map/ppermute | solution.py:31
  59.6 0.1 pad_add_fusion.1.meta_ref
  59.6 1.9 collective-permute-done.8.refs_4_
  61.6 4.0 %collective-permute-done.7.refs_3_ = bf16[2,3,64,1024]{3,2,1,0:T(8,128)(2,1)} collective-permute-done((bf16[2,3,64,1024]{3,2,1,0:T(8,128)(2,1)}, bf16[2,3,64,1024]{3,2,1,0:T(8,128)(2,1)}, u32[]{:S(2)}, u32[]{:S(2)}) %collective-permute-start.7) | collective-permute-done | bytes 786464 | tf_op jit(solution)/shard_map/ppermute | solution.py:31
  65.6 6.6 %project.1.refs_3_ = bf16[12,64,512]{2,1,0:T(8,128)(2,1)} custom-call(bf16[2,3,64,1024]{3,2,1,0:T(8,128)(2,1)} %pair.2.refs_0_, bf16[2,3,64,1024]{3,2,1,0:T(8,128)(2,1)} %pair.3.refs_1_, bf16[2,3,64,1024]{3,2,1,0:T(8,128)(2,1)} %collective-permute-done.1.refs_2_, bf16[2,3,64,1024]{3,2,1,0:T(8,128)(2,1)} %collective-permute-done.7.refs_3_, ...), custom_call_target="tpu_custom_call" | custom-call | bytes 4718592 | tf_op jit(solution)/shard_map/project/pallas_call | solution.py:114
  72.3 1.8 collective-permute-done.2.refs_0_
  74.1 1.1 copy-done.1
  75.2 4.7 %project_place.1 = (bf16[4,144,512]{2,1,0:T(8,128)(2,1)S(1)}, bf16[4,144,512]{2,1,0:T(8,128)(2,1)}) custom-call(s32[3]{0:T(128)S(1)} %pad_add_fusion.1.meta_ref, bf16[2,3,64,1024]{3,2,1,0:T(8,128)(2,1)} %collective-permute-done.2.refs_0_, bf16[2,3,64,1024]{3,2,1,0:T(8,128)(2,1)} %collective-permute-done.6.refs_1_, bf16[3,1024,512]{2,1,0:T(8,128)(2,1)S(1)} %bitcast.34, ...), custom_call_target="tpu_custom_call" | custom-call | bytes 1572864 | tf_op jit(solution)/shard_map/project_place/pallas_call | solution.py:165
  79.9 0.8 copy-done.3
  80.7 5.9 %collective-permute-start.9 = (bf16[4,144,512]{2,1,0:T(8,128)(2,1)}, bf16[4,144,512]{2,1,0:T(8,128)(2,1)S(1)}, u32[]{:S(2)}, u32[]{:S(2)}) collective-permute-start(bf16[4,144,512]{2,1,0:T(8,128)(2,1)} %get-tuple-element.30), channel_id=1, source_target_pairs={{64,0},{0,64},{192,128},{128,192},{320,256},{256,320},{448,384},{3... | collective-permute-start | bytes 1769480 | tf_op jit(solution)/shard_map/ppermute | solution.py:35
  86.6 0.9 slice_bitcast_fusion
  87.5 0.9 collective-permute-done.9.got_ref
  88.4 1.1 copy-done.4
  89.5 0.2 join.1
  89.6 1.6 turn.1
  91.2 0.0 all-gather.4.cloned.1.call-update
  91.2 0.6 dynamic_slice.3
  91.8 0.7 maximum_reduce_fusion
  94.5 4.6 %collective-permute-start.16 = (bf16[16,512]{1,0:T(8,128)(2,1)S(1)}, bf16[16,512]{1,0:T(8,128)(2,1)S(1)}, u32[]{:S(2)}, u32[]{:S(2)}) collective-permute-start(bf16[16,512]{1,0:T(8,128)(2,1)S(1)} %get-tuple-element.51), channel_id=1, source_target_pairs={{2,1},{4,65},{6,129},{8,193},{10,257},{12,321},{14,385},{66,3},{68... | collective-permute-start | bytes 49160 | tf_op jit(solution)/shard_map/ppermute | solution.py:389
  99.1 5.6 %collective-permute-start.15 = (bf16[16,512]{1,0:T(8,128)(2,1)S(1)}, bf16[16,512]{1,0:T(8,128)(2,1)S(1)}, u32[]{:S(2)}, u32[]{:S(2)}) collective-permute-start(bf16[16,512]{1,0:T(8,128)(2,1)S(1)} %get-tuple-element.52), channel_id=1, source_target_pairs={{2,0},{4,64},{6,128},{8,192},{10,256},{12,320},{14,384},{66,2},{68... | collective-permute-start | bytes 49160 | tf_op jit(solution)/shard_map/ppermute | solution.py:388
  104.7 5.1 %collective-permute-start.10 = (bf16[144,512]{1,0:T(8,128)(2,1)S(1)}, bf16[144,512]{1,0:T(8,128)(2,1)S(1)}, u32[]{:S(2)}, u32[]{:S(2)}) collective-permute-start(bf16[144,512]{1,0:T(8,128)(2,1)S(1)} %get-tuple-element.34), channel_id=1, source_target_pairs={{128,0},{192,64},{256,128},{320,192},{384,256},{448,320},{0,384},{... | collective-permute-start | bytes 442376 | tf_op jit(solution)/shard_map/ppermute | solution.py:40
  109.7 1.9 collective-permute-start.11
  111.7 2.2 collective-permute-start.12
  113.9 1.9 collective-permute-start.14
  115.8 0.0 collective-permute-done.15.refs_6_
  115.8 4.7 %collective-permute-start.13 = (bf16[64,512]{1,0:T(8,128)(2,1)S(1)}, bf16[64,512]{1,0:T(8,128)(2,1)S(1)}, u32[]{:S(2)}, u32[]{:S(2)}) collective-permute-start(bf16[64,512]{1,0:T(8,128)(2,1)S(1)} %get-tuple-element.54), channel_id=1, source_target_pairs={{0,0},{1,1},{2,64},{3,65},{4,128},{5,129},{6,192},{7,193},{8,256},... | collective-permute-start | bytes 196616 | tf_op jit(solution)/shard_map/ppermute | solution.py:386
  120.6 0.7 pad_add_fusion.meta_ref
  121.2 4.8 %collective-permute-done.14.refs_5_ = bf16[64,512]{1,0:T(8,128)(2,1)S(1)} collective-permute-done((bf16[64,512]{1,0:T(8,128)(2,1)S(1)}, bf16[64,512]{1,0:T(8,128)(2,1)S(1)}, u32[]{:S(2)}, u32[]{:S(2)}) %collective-permute-start.14) | collective-permute-done | bytes 65568 | tf_op jit(solution)/shard_map/ppermute | solution.py:387
  126.1 2.7 %collective-permute-done.13.refs_4_ = bf16[64,512]{1,0:T(8,128)(2,1)S(1)} collective-permute-done((bf16[64,512]{1,0:T(8,128)(2,1)S(1)}, bf16[64,512]{1,0:T(8,128)(2,1)S(1)}, u32[]{:S(2)}, u32[]{:S(2)}) %collective-permute-start.13) | collective-permute-done | bytes 65568 | tf_op jit(solution)/shard_map/ppermute | solution.py:386
  128.8 0.0 collective-permute-done.10.refs_1_
  128.8 1.4 chain.1
  130.2 31.4 %all-gather = bf16[576,512]{1,0:T(8,128)(2,1)S(1)} all-gather(bf16[144,512]{1,0:T(8,128)(2,1)S(1)} %chain.1), channel_id=2, replica_groups=mesh['tp'=8,'dp'=4,'draft'=16] {'dp'}, dimensions={0}, use_global_device_ids=true | all-gather | bytes 737280 | tf_op jit(solution)/shard_map/all_gather | solution.py:400
  161.6 5.9 %collective-permute-start.19 = (bf16[4,144,512]{2,1,0:T(8,128)(2,1)S(1)}, bf16[4,144,512]{2,1,0:T(8,128)(2,1)S(1)}, u32[]{:S(2)}, u32[]{:S(2)}) collective-permute-start(bf16[4,144,512]{2,1,0:T(8,128)(2,1)S(1)} %bitcast.35), channel_id=1, source_target_pairs={{64,0},{0,64},{192,128},{128,192},{320,256},{256,320},{448,384},{3... | collective-permute-start | bytes 1769480 | tf_op jit(solution)/shard_map/ppermute | solution.py:35
  167.5 1.9 collective-permute-start.18
  169.4 4.6 %collective-permute-start.17 = (bf16[4,144,512]{2,1,0:T(8,128)(2,1)S(1)}, bf16[4,144,512]{2,1,0:T(8,128)(2,1)S(1)}, u32[]{:S(2)}, u32[]{:S(2)}) collective-permute-start(bf16[4,144,512]{2,1,0:T(8,128)(2,1)S(1)} %bitcast.37), channel_id=1, source_target_pairs={{128,0},{144,16},{160,32},{176,48},{192,64},{208,80},{224,96},{240... | collective-permute-start | bytes 1769480 | tf_op jit(solution)/shard_map/ppermute | solution.py:53
  174.1 1.9 collective-permute-start.21
  176.0 5.5 %collective-permute-start.20 = (bf16[2,144,512]{2,1,0:T(8,128)(2,1)S(1)}, bf16[2,144,512]{2,1,0:T(8,128)(2,1)S(1)}, u32[]{:S(2)}, u32[]{:S(2)}) collective-permute-start(bf16[2,144,512]{2,1,0:T(8,128)(2,1)S(1)} %bitcast.47), channel_id=1, source_target_pairs={{256,0},{272,16},{288,32},{304,48},{320,64},{336,80},{352,96},{368... | collective-permute-start | bytes 884744 | tf_op jit(solution)/shard_map/ppermute | solution.py:53
  181.5 11.6 %collective-permute-done.21 = bf16[2,144,512]{2,1,0:T(8,128)(2,1)S(1)} collective-permute-done((bf16[2,144,512]{2,1,0:T(8,128)(2,1)S(1)}, bf16[2,144,512]{2,1,0:T(8,128)(2,1)S(1)}, u32[]{:S(2)}, u32[]{:S(2)}) %collective-permute-start.21) | collective-permute-done | bytes 294944 | tf_op jit(solution)/shard_map/ppermute | solution.py:53
  193.0 5.9 %collective-permute-done.20 = bf16[2,144,512]{2,1,0:T(8,128)(2,1)S(1)} collective-permute-done((bf16[2,144,512]{2,1,0:T(8,128)(2,1)S(1)}, bf16[2,144,512]{2,1,0:T(8,128)(2,1)S(1)}, u32[]{:S(2)}, u32[]{:S(2)}) %collective-permute-start.20) | collective-permute-done | bytes 294944 | tf_op jit(solution)/shard_map/ppermute | solution.py:53
  199.0 0.1 pad_maximum_fusion.refs_4_
  199.0 0.0 all-gather.4.cloned.1.call-done
  199.1 3.2 %collective-permute-start.22 = (bf16[4,144,512]{2,1,0:T(8,128)(2,1)S(1)}, bf16[4,144,512]{2,1,0:T(8,128)(2,1)S(1)}, u32[]{:S(2)}, u32[]{:S(2)}) collective-permute-start(bf16[4,144,512]{2,1,0:T(8,128)(2,1)S(1)} %collective-permute-done.17.refs_2_), channel_id=1, source_target_pairs={{64,0},{0,64},{192,128},{128,192},{320,256},{256,320},{448,384},{3... | collective-permute-start | bytes 1769480 | tf_op jit(solution)/shard_map/ppermute | solution.py:35
  202.2 1.9 collective-permute-start.23
  204.2 2.4 %collective-permute-start.24 = (bf16[4,144,512]{2,1,0:T(8,128)(2,1)S(1)}, bf16[4,144,512]{2,1,0:T(8,128)(2,1)}, u32[]{:S(2)}, u32[]{:S(2)}) collective-permute-start(bf16[4,144,512]{2,1,0:T(8,128)(2,1)S(1)} %pad_maximum_fusion.refs_4_), channel_id=1, source_target_pairs={{64,0},{0,64},{192,128},{128,192},{320,256},{256,320},{448,384},{3... | collective-permute-start | bytes 1769480 | tf_op jit(solution)/shard_map/ppermute | solution.py:35
  206.7 0.1 stack.56.meta_ref
  206.8 1.6 collective-permute-done.24.refs_7_
  208.3 7.7 %weight_grad.1 = (bf16[3,256,512]{2,1,0:T(8,128)(2,1)}, f32[1,512]{1,0:T(1,128)}) custom-call(s32[8]{0:T(128)S(1)} %stack.56.meta_ref, bf16[16,3,256,256]{3,2,1,0:T(8,128)(2,1)} %bitcast.49, bf16[4,144,512]{2,1,0:T(8,128)(2,1)S(1)} %bitcast.38, bf16[4,144,512]{2,1,0:T(8,128)(2,1)S(1)} %collective-permute-done.19.refs_1_, ...), custom_call_target="tpu_custom_call" | custom-call | flops 3221225472 | bytes 10485760 | tf_op jit(solution)/shard_map/weight_grad/pallas_call | solution.py:320
  (25 shorter events, 0.1 us)
Async XLA Ops:
  7.2 10.7 %collective-permute-start.4 = (bf16[3,64,1024]{2,1,0:T(8,128)(2,1)}, bf16[3,64,1024]{2,1,0:T(8,128)(2,1)S(1)}, u32[]{:S(2)}, u32[]{:S(2)}) collective-permute-start(bf16[3,64,1024]{2,1,0:T(8,128)(2,1)} %bitcast.39), channel_id=1, source_target_pairs={{12,0},{13,1},{14,2},{15,3},{0,4},{1,5},{2,6},{3,7},{4,8},{5,9},{6... | collective-permute-start | bytes 1179656 | tf_op jit(solution)/shard_map/ppermute | solution.py:31
  10.4 12.2 %collective-permute-start.3 = (bf16[3,64,1024]{2,1,0:T(8,128)(2,1)}, bf16[3,64,1024]{2,1,0:T(8,128)(2,1)S(1)}, u32[]{:S(2)}, u32[]{:S(2)}) collective-permute-start(bf16[3,64,1024]{2,1,0:T(8,128)(2,1)} %bitcast.40), channel_id=1, source_target_pairs={{8,0},{9,1},{10,2},{11,3},{12,4},{13,5},{14,6},{15,7},{0,8},{1,9},... | collective-permute-start | bytes 1179656 | tf_op jit(solution)/shard_map/ppermute | solution.py:31
  14.9 9.3 %collective-permute-start = (bf16[3,64,1024]{2,1,0:T(8,128)(2,1)}, bf16[3,64,1024]{2,1,0:T(8,128)(2,1)S(1)}, u32[]{:S(2)}, u32[]{:S(2)}) collective-permute-start(bf16[3,64,1024]{2,1,0:T(8,128)(2,1)} %bitcast.41), channel_id=1, source_target_pairs={{4,0},{5,1},{6,2},{7,3},{8,4},{9,5},{10,6},{11,7},{12,8},{13,9},{1... | collective-permute-start | bytes 1179656 | tf_op jit(solution)/shard_map/ppermute | solution.py:31
  23.5 50.6 %copy-start = (bf16[1024,3,512]{2,0,1:T(8,128)(2,1)S(1)}, bf16[1024,3,512]{2,0,1:T(8,128)(2,1)}, u32[]{:S(2)}) copy-start(bf16[1024,3,512]{2,0,1:T(8,128)(2,1)} %param.5) | copy-start | bytes 9437188
  24.2 1.3 copy-start.2
  26.4 27.9 %collective-permute-start.1 = (bf16[2,3,64,1024]{3,2,1,0:T(8,128)(2,1)}, bf16[2,3,64,1024]{3,2,1,0:T(8,128)(2,1)}, u32[]{:S(2)}, u32[]{:S(2)}) collective-permute-start(bf16[2,3,64,1024]{3,2,1,0:T(8,128)(2,1)} %pair.2.refs_0_), channel_id=1, source_target_pairs={{1,0},{2,1},{3,2},{0,3},{5,4},{6,5},{7,6},{4,7},{9,8},{10,9},{11,1... | collective-permute-start | bytes 2359304 | tf_op jit(solution)/shard_map/ppermute | solution.py:31
  28.5 27.6 %collective-permute-start.5 = (bf16[2,3,64,1024]{3,2,1,0:T(8,128)(2,1)}, bf16[2,3,64,1024]{3,2,1,0:T(8,128)(2,1)}, u32[]{:S(2)}, u32[]{:S(2)}) collective-permute-start(bf16[2,3,64,1024]{3,2,1,0:T(8,128)(2,1)} %pair.3.refs_1_), channel_id=1, source_target_pairs={{3,0},{0,1},{1,2},{2,3},{7,4},{4,5},{5,6},{6,7},{11,8},{8,9},{9,10... | collective-permute-start | bytes 2359304 | tf_op jit(solution)/shard_map/ppermute | solution.py:31
  33.4 38.8 %all-to-all-start = ((bf16[4,3,64,256]{3,2,1,0:T(8,128)(2,1)}), bf16[4,3,64,256]{3,2,1,0:T(8,128)(2,1)S(1)}, u32[]{:S(2)}, u32[]{:S(2)}) async-start(bf16[4,3,64,256]{3,2,1,0:T(8,128)(2,1)} %bitcast.46), calls=%async_computation | async-start | bytes 786432 | tf_op jit(solution)/shard_map/all_to_all | solution.py:396
  48.2 150.8 %all-gather.4.cloned.1.call-start = ((), (), s32[]{:S(2)}) async-start(), calls=%async_computation.1 | async-start | bytes 6684672 | tf_op jit(solution)/shard_map/all_gather | solution.py:442
  48.3 13.3 %collective-permute-start.8 = (bf16[2,3,64,1024]{3,2,1,0:T(8,128)(2,1)}, bf16[2,3,64,1024]{3,2,1,0:T(8,128)(2,1)}, u32[]{:S(2)}, u32[]{:S(2)}) collective-permute-start(bf16[2,3,64,1024]{3,2,1,0:T(8,128)(2,1)} %pair.2.refs_0_), channel_id=1, source_target_pairs={{3,0},{0,1},{1,2},{2,3},{7,4},{4,5},{5,6},{6,7},{11,8},{8,9},{9,10... | collective-permute-start | bytes 2359304 | tf_op jit(solution)/shard_map/ppermute | solution.py:31
  52.3 13.3 %collective-permute-start.7 = (bf16[2,3,64,1024]{3,2,1,0:T(8,128)(2,1)}, bf16[2,3,64,1024]{3,2,1,0:T(8,128)(2,1)}, u32[]{:S(2)}, u32[]{:S(2)}) collective-permute-start(bf16[2,3,64,1024]{3,2,1,0:T(8,128)(2,1)} %pair.3.refs_1_), channel_id=1, source_target_pairs={{1,0},{2,1},{3,2},{0,3},{5,4},{6,5},{7,6},{4,7},{9,8},{10,9},{11,1... | collective-permute-start | bytes 2359304 | tf_op jit(solution)/shard_map/ppermute | solution.py:31
  54.2 19.8 %collective-permute-start.2 = (bf16[2,3,64,1024]{3,2,1,0:T(8,128)(2,1)}, bf16[2,3,64,1024]{3,2,1,0:T(8,128)(2,1)}, u32[]{:S(2)}, u32[]{:S(2)}) collective-permute-start(bf16[2,3,64,1024]{3,2,1,0:T(8,128)(2,1)} %collective-permute-done.1.refs_2_), channel_id=1, source_target_pairs={{1,0},{2,1},{3,2},{0,3},{5,4},{6,5},{7,6},{4,7},{9,8},{10,9},{11,1... | collective-permute-start | bytes 2359304 | tf_op jit(solution)/shard_map/ppermute | solution.py:31
  56.2 17.9 %collective-permute-start.6 = (bf16[2,3,64,1024]{3,2,1,0:T(8,128)(2,1)}, bf16[2,3,64,1024]{3,2,1,0:T(8,128)(2,1)}, u32[]{:S(2)}, u32[]{:S(2)}) collective-permute-start(bf16[2,3,64,1024]{3,2,1,0:T(8,128)(2,1)} %collective-permute-done.5.refs_5_), channel_id=1, source_target_pairs={{3,0},{0,1},{1,2},{2,3},{7,4},{4,5},{5,6},{6,7},{11,8},{8,9},{9,10... | collective-permute-start | bytes 2359304 | tf_op jit(solution)/shard_map/ppermute | solution.py:31
  65.6 25.6 %copy-start.6 = (s32[4]{0:T(128)S(1)}, s32[4]{0:T(128)}, u32[]{:S(2)}) copy-start(s32[4]{0:T(128)} %param.7) | copy-start | bytes 52
  65.6 63.2 %copy-start.5 = (f32[512]{0:T(512)S(1)}, f32[512]{0:T(512)}, u32[]{:S(2)}) copy-start(f32[512]{0:T(512)} %param.6) | copy-start | bytes 6148
  74.1 1.1 copy-start.1
  79.9 0.8 copy-start.3
  80.7 7.7 %collective-permute-start.9 = (bf16[4,144,512]{2,1,0:T(8,128)(2,1)}, bf16[4,144,512]{2,1,0:T(8,128)(2,1)S(1)}, u32[]{:S(2)}, u32[]{:S(2)}) collective-permute-start(bf16[4,144,512]{2,1,0:T(8,128)(2,1)} %get-tuple-element.30), channel_id=1, source_target_pairs={{64,0},{0,64},{192,128},{128,192},{320,256},{256,320},{448,384},{3... | collective-permute-start | bytes 1769480 | tf_op jit(solution)/shard_map/ppermute | solution.py:35
  88.4 1.1 copy-start.4
  94.5 19.4 %collective-permute-start.16 = (bf16[16,512]{1,0:T(8,128)(2,1)S(1)}, bf16[16,512]{1,0:T(8,128)(2,1)S(1)}, u32[]{:S(2)}, u32[]{:S(2)}) collective-permute-start(bf16[16,512]{1,0:T(8,128)(2,1)S(1)} %get-tuple-element.51), channel_id=1, source_target_pairs={{2,1},{4,65},{6,129},{8,193},{10,257},{12,321},{14,385},{66,3},{68... | collective-permute-start | bytes 49160 | tf_op jit(solution)/shard_map/ppermute | solution.py:389
  99.1 16.7 %collective-permute-start.15 = (bf16[16,512]{1,0:T(8,128)(2,1)S(1)}, bf16[16,512]{1,0:T(8,128)(2,1)S(1)}, u32[]{:S(2)}, u32[]{:S(2)}) collective-permute-start(bf16[16,512]{1,0:T(8,128)(2,1)S(1)} %get-tuple-element.52), channel_id=1, source_target_pairs={{2,0},{4,64},{6,128},{8,192},{10,256},{12,320},{14,384},{66,2},{68... | collective-permute-start | bytes 49160 | tf_op jit(solution)/shard_map/ppermute | solution.py:388
  104.7 24.1 %collective-permute-start.10 = (bf16[144,512]{1,0:T(8,128)(2,1)S(1)}, bf16[144,512]{1,0:T(8,128)(2,1)S(1)}, u32[]{:S(2)}, u32[]{:S(2)}) collective-permute-start(bf16[144,512]{1,0:T(8,128)(2,1)S(1)} %get-tuple-element.34), channel_id=1, source_target_pairs={{128,0},{192,64},{256,128},{320,192},{384,256},{448,320},{0,384},{... | collective-permute-start | bytes 442376 | tf_op jit(solution)/shard_map/ppermute | solution.py:40
  109.7 19.1 %collective-permute-start.11 = (bf16[144,512]{1,0:T(8,128)(2,1)S(1)}, bf16[144,512]{1,0:T(8,128)(2,1)S(1)}, u32[]{:S(2)}, u32[]{:S(2)}) collective-permute-start(bf16[144,512]{1,0:T(8,128)(2,1)S(1)} %get-tuple-element.35), channel_id=1, source_target_pairs={{256,0},{320,64},{384,128},{448,192},{0,256},{64,320},{128,384},{1... | collective-permute-start | bytes 442376 | tf_op jit(solution)/shard_map/ppermute | solution.py:40
  111.7 17.2 %collective-permute-start.12 = (bf16[144,512]{1,0:T(8,128)(2,1)S(1)}, bf16[144,512]{1,0:T(8,128)(2,1)S(1)}, u32[]{:S(2)}, u32[]{:S(2)}) collective-permute-start(bf16[144,512]{1,0:T(8,128)(2,1)S(1)} %get-tuple-element.36), channel_id=1, source_target_pairs={{384,0},{448,64},{0,128},{64,192},{128,256},{192,320},{256,384},{3... | collective-permute-start | bytes 442376 | tf_op jit(solution)/shard_map/ppermute | solution.py:40
  113.9 12.2 %collective-permute-start.14 = (bf16[64,512]{1,0:T(8,128)(2,1)S(1)}, bf16[64,512]{1,0:T(8,128)(2,1)S(1)}, u32[]{:S(2)}, u32[]{:S(2)}) collective-permute-start(bf16[64,512]{1,0:T(8,128)(2,1)S(1)} %get-tuple-element.53), channel_id=1, source_target_pairs={{0,1},{1,0},{2,65},{3,64},{4,129},{5,128},{6,193},{7,192},{8,257},... | collective-permute-start | bytes 196616 | tf_op jit(solution)/shard_map/ppermute | solution.py:387
  115.8 13.0 %collective-permute-start.13 = (bf16[64,512]{1,0:T(8,128)(2,1)S(1)}, bf16[64,512]{1,0:T(8,128)(2,1)S(1)}, u32[]{:S(2)}, u32[]{:S(2)}) collective-permute-start(bf16[64,512]{1,0:T(8,128)(2,1)S(1)} %get-tuple-element.54), channel_id=1, source_target_pairs={{0,0},{1,1},{2,64},{3,65},{4,128},{5,129},{6,192},{7,193},{8,256},... | collective-permute-start | bytes 196616 | tf_op jit(solution)/shard_map/ppermute | solution.py:386
  161.6 37.4 %collective-permute-start.19 = (bf16[4,144,512]{2,1,0:T(8,128)(2,1)S(1)}, bf16[4,144,512]{2,1,0:T(8,128)(2,1)S(1)}, u32[]{:S(2)}, u32[]{:S(2)}) collective-permute-start(bf16[4,144,512]{2,1,0:T(8,128)(2,1)S(1)} %bitcast.35), channel_id=1, source_target_pairs={{64,0},{0,64},{192,128},{128,192},{320,256},{256,320},{448,384},{3... | collective-permute-start | bytes 1769480 | tf_op jit(solution)/shard_map/ppermute | solution.py:35
  167.5 31.5 %collective-permute-start.18 = (bf16[4,144,512]{2,1,0:T(8,128)(2,1)S(1)}, bf16[4,144,512]{2,1,0:T(8,128)(2,1)S(1)}, u32[]{:S(2)}, u32[]{:S(2)}) collective-permute-start(bf16[4,144,512]{2,1,0:T(8,128)(2,1)S(1)} %bitcast.36), channel_id=1, source_target_pairs={{432,0},{384,16},{400,32},{416,48},{496,64},{448,80},{464,96},{480... | collective-permute-start | bytes 1769480 | tf_op jit(solution)/shard_map/ppermute | solution.py:53
  169.4 29.6 %collective-permute-start.17 = (bf16[4,144,512]{2,1,0:T(8,128)(2,1)S(1)}, bf16[4,144,512]{2,1,0:T(8,128)(2,1)S(1)}, u32[]{:S(2)}, u32[]{:S(2)}) collective-permute-start(bf16[4,144,512]{2,1,0:T(8,128)(2,1)S(1)} %bitcast.37), channel_id=1, source_target_pairs={{128,0},{144,16},{160,32},{176,48},{192,64},{208,80},{224,96},{240... | collective-permute-start | bytes 1769480 | tf_op jit(solution)/shard_map/ppermute | solution.py:53
  174.1 19.0 %collective-permute-start.21 = (bf16[2,144,512]{2,1,0:T(8,128)(2,1)S(1)}, bf16[2,144,512]{2,1,0:T(8,128)(2,1)S(1)}, u32[]{:S(2)}, u32[]{:S(2)}) collective-permute-start(bf16[2,144,512]{2,1,0:T(8,128)(2,1)S(1)} %bitcast.48), channel_id=1, source_target_pairs={{304,0},{256,16},{272,32},{288,48},{368,64},{320,80},{336,96},{352... | collective-permute-start | bytes 884744 | tf_op jit(solution)/shard_map/ppermute | solution.py:53
  176.0 23.0 %collective-permute-start.20 = (bf16[2,144,512]{2,1,0:T(8,128)(2,1)S(1)}, bf16[2,144,512]{2,1,0:T(8,128)(2,1)S(1)}, u32[]{:S(2)}, u32[]{:S(2)}) collective-permute-start(bf16[2,144,512]{2,1,0:T(8,128)(2,1)S(1)} %bitcast.47), channel_id=1, source_target_pairs={{256,0},{272,16},{288,32},{304,48},{320,64},{336,80},{352,96},{368... | collective-permute-start | bytes 884744 | tf_op jit(solution)/shard_map/ppermute | solution.py:53
  199.1 7.7 %collective-permute-start.22 = (bf16[4,144,512]{2,1,0:T(8,128)(2,1)S(1)}, bf16[4,144,512]{2,1,0:T(8,128)(2,1)S(1)}, u32[]{:S(2)}, u32[]{:S(2)}) collective-permute-start(bf16[4,144,512]{2,1,0:T(8,128)(2,1)S(1)} %collective-permute-done.17.refs_2_), channel_id=1, source_target_pairs={{64,0},{0,64},{192,128},{128,192},{320,256},{256,320},{448,384},{3... | collective-permute-start | bytes 1769480 | tf_op jit(solution)/shard_map/ppermute | solution.py:35
  202.2 4.5 %collective-permute-start.23 = (bf16[4,144,512]{2,1,0:T(8,128)(2,1)S(1)}, bf16[4,144,512]{2,1,0:T(8,128)(2,1)}, u32[]{:S(2)}, u32[]{:S(2)}) collective-permute-start(bf16[4,144,512]{2,1,0:T(8,128)(2,1)S(1)} %collective-permute-done.18.refs_3_), channel_id=1, source_target_pairs={{64,0},{0,64},{192,128},{128,192},{320,256},{256,320},{448,384},{3... | collective-permute-start | bytes 1769480 | tf_op jit(solution)/shard_map/ppermute | solution.py:35
  204.2 4.2 %collective-permute-start.24 = (bf16[4,144,512]{2,1,0:T(8,128)(2,1)S(1)}, bf16[4,144,512]{2,1,0:T(8,128)(2,1)}, u32[]{:S(2)}, u32[]{:S(2)}) collective-permute-start(bf16[4,144,512]{2,1,0:T(8,128)(2,1)S(1)} %pad_maximum_fusion.refs_4_), channel_id=1, source_target_pairs={{64,0},{0,64},{192,128},{128,192},{320,256},{256,320},{448,384},{3... | collective-permute-start | bytes 1769480 | tf_op jit(solution)/shard_map/ppermute | solution.py:35
Sparse Core Ops, SparseCore 0:
  91.3 79.3 all-gather.3

commit v15 on v13

--- a/solution.py
+++ b/solution.py
@@ -430,7 +430,7 @@
     low, high = pair(own, next_), pair(across, last)
     up_low, down_high = plane_move(1, False)(low), plane_move(-1, False)(high)
     up_high, down_low = plane_move(1, False)(high), plane_move(-1, False)(low)
-    up_low, down_high, later = lax.optimization_barrier((up_low, down_high, own))
+    up_low, later = lax.optimization_barrier((up_low, own))
     traded = trade_columns(later)
     far_low, far_high = plane_move(1, False)(up_low), plane_move(-1, False)(down_high)
     near = project([low, high, up_low, up_high, down_low, down_high], weight, 58)

time: 217 us -> 214 us (0.986)
  waiting for transfers between devices: 41 us -> 37.1 us
    ppermute x9, waiting for transfers between devices: 9.48 us -> 6.42 us  [plane_move(): return lambda block: lax.ppermute(block, ('tp', 'draft'), pairs)]
    ppermute x1, waiting for transfers between devices: 7.57 us -> 5.04 us  [send_high(): lax.ppermute(jnp.where(even, left, right), axes, straight)]
  transfers between devices with their start and end apart: 27 -> 27, of which waited for: 9 -> 10; matrix products, arithmetic and copies ran while one was open for 2% -> 2% of each run, Pallas kernels for 7% -> 7%
where the time goes in v15:
time: 214 us; the launch traced here: 213 us
  starting transfers between devices  99.4 us (46%)
  waiting for transfers between devices  37.1 us (17%)
  blocking collectives  26.6 us (12%)
  Pallas kernels  23.9 us (11%)
  between operations  16.4 us (8%)
  local copies, waits for them, and re-layouts  7.47 us (3%)
    all_gather x1, blocking collectives, gather_grads(): stack = lax.all_gather(grad, 'dp', axis=0, tiled=False)  26.6 us
    ppermute x9, starting transfers between devices, plane_move(): return lambda block: lax.ppermute(block, ('tp', 'draft'), pairs)  26.5 us
    ppermute x4, waiting for transfers between devices, from_z(): return lax.ppermute(block, ('tp', 'dp'), pairs)  19.9 us
    ppermute x4, starting transfers between devices, from_z(): return lax.ppermute(block, ('tp', 'dp'), pairs)  16.7 us
    all_to_all x1, starting transfers between devices, trade_columns(): lax.all_to_all(quarters, 'dp', split_axis=0, concat_axis=0, tiled=True)  15.1 us
    ppermute x5, starting transfers between devices, from_other_core(): return lax.ppermute(block, 'tp', [(t ^ 1, t) for t in range(ZL * CORES)])  11.5 us
    ppermute x3, starting transfers between devices, from_zl(): return lax.ppermute(block, 'tp', pairs)  10.9 us
    pallas_call x1, Pallas kernels, weight_grad(): pl.pallas_call(weight_grad_kernel, out_shape=(jax.ShapeDtypeStruct((LEVEL...  7.69 us
  transfers between devices with their start and end apart: 27, of which 10 were waited for; matrix products, arithmetic and copies ran while one was open for 2% of the time, Pallas kernels for 7%

profile of v15, /device:TPU:5, one launch (start us, length us, event | category | flops | bytes accessed | tf_op | source)
XLA Modules:
  0.0 212.5 jit_solution(10238733206314146582)
XLA Ops:
  7.2 4.6 %collective-permute-start = (bf16[3,64,1024]{2,1,0:T(8,128)(2,1)}, bf16[3,64,1024]{2,1,0:T(8,128)(2,1)S(1)}, u32[]{:S(2)}, u32[]{:S(2)}) collective-permute-start(bf16[3,64,1024]{2,1,0:T(8,128)(2,1)} %bitcast.39), channel_id=1, source_target_pairs={{4,0},{5,1},{6,2},{7,3},{8,4},{9,5},{10,6},{11,7},{12,8},{13,9},{1... | collective-permute-start | bytes 1179656 | tf_op jit(solution)/shard_map/ppermute | solution.py:31
  11.8 1.9 collective-permute-start.4
  13.7 3.5 %collective-permute-start.3 = (bf16[3,64,1024]{2,1,0:T(8,128)(2,1)}, bf16[3,64,1024]{2,1,0:T(8,128)(2,1)S(1)}, u32[]{:S(2)}, u32[]{:S(2)}) collective-permute-start(bf16[3,64,1024]{2,1,0:T(8,128)(2,1)} %bitcast.41), channel_id=1, source_target_pairs={{8,0},{9,1},{10,2},{11,3},{12,4},{13,5},{14,6},{15,7},{0,8},{1,9},... | collective-permute-start | bytes 1179656 | tf_op jit(solution)/shard_map/ppermute | solution.py:31
  17.3 0.0 copy-start.2
  17.3 1.0 copy-done.2
  18.3 0.9 pair.2.refs_0_
  19.3 2.4 %collective-permute-start.1 = (bf16[2,3,64,1024]{3,2,1,0:T(8,128)(2,1)}, bf16[2,3,64,1024]{3,2,1,0:T(8,128)(2,1)}, u32[]{:S(2)}, u32[]{:S(2)}) collective-permute-start(bf16[2,3,64,1024]{3,2,1,0:T(8,128)(2,1)} %pair.2.refs_0_), channel_id=1, source_target_pairs={{1,0},{2,1},{3,2},{0,3},{5,4},{6,5},{7,6},{4,7},{9,8},{10,9},{11,1... | collective-permute-start | bytes 2359304 | tf_op jit(solution)/shard_map/ppermute | solution.py:31
  21.7 4.4 %collective-permute-done.4.second_ref = bf16[3,64,1024]{2,1,0:T(8,128)(2,1)S(1)} collective-permute-done((bf16[3,64,1024]{2,1,0:T(8,128)(2,1)}, bf16[3,64,1024]{2,1,0:T(8,128)(2,1)S(1)}, u32[]{:S(2)}, u32[]{:S(2)}) %collective-permute-start.4) | collective-permute-done | bytes 393248 | tf_op jit(solution)/shard_map/ppermute | solution.py:31
  26.1 0.0 collective-permute-done.3.first_ref
  26.1 0.9 pair.3.refs_1_
  27.0 3.0 %collective-permute-start.5 = (bf16[2,3,64,1024]{3,2,1,0:T(8,128)(2,1)}, bf16[2,3,64,1024]{3,2,1,0:T(8,128)(2,1)}, u32[]{:S(2)}, u32[]{:S(2)}) collective-permute-start(bf16[2,3,64,1024]{3,2,1,0:T(8,128)(2,1)} %pair.3.refs_1_), channel_id=1, source_target_pairs={{3,0},{0,1},{1,2},{2,3},{7,4},{4,5},{5,6},{6,7},{11,8},{8,9},{9,10... | collective-permute-start | bytes 2359304 | tf_op jit(solution)/shard_map/ppermute | solution.py:31
  30.0 2.1 collective-permute-start.8
  32.1 3.2 %collective-permute-start.7 = (bf16[2,3,64,1024]{3,2,1,0:T(8,128)(2,1)}, bf16[2,3,64,1024]{3,2,1,0:T(8,128)(2,1)}, u32[]{:S(2)}, u32[]{:S(2)}) collective-permute-start(bf16[2,3,64,1024]{3,2,1,0:T(8,128)(2,1)} %pair.3.refs_1_), channel_id=1, source_target_pairs={{1,0},{2,1},{3,2},{0,3},{5,4},{6,5},{7,6},{4,7},{9,8},{10,9},{11,1... | collective-permute-start | bytes 2359304 | tf_op jit(solution)/shard_map/ppermute | solution.py:31
  35.3 0.9 collective-permute-done.1.refs_2_
  36.2 3.0 %collective-permute-start.2 = (bf16[2,3,64,1024]{3,2,1,0:T(8,128)(2,1)}, bf16[2,3,64,1024]{3,2,1,0:T(8,128)(2,1)}, u32[]{:S(2)}, u32[]{:S(2)}) collective-permute-start(bf16[2,3,64,1024]{3,2,1,0:T(8,128)(2,1)} %collective-permute-done.1.refs_2_), channel_id=1, source_target_pairs={{1,0},{2,1},{3,2},{0,3},{5,4},{6,5},{7,6},{4,7},{9,8},{10,9},{11,1... | collective-permute-start | bytes 2359304 | tf_op jit(solution)/shard_map/ppermute | solution.py:31
  39.2 1.1 collective-permute-done.5.refs_5_
  40.4 2.7 %collective-permute-start.6 = (bf16[2,3,64,1024]{3,2,1,0:T(8,128)(2,1)}, bf16[2,3,64,1024]{3,2,1,0:T(8,128)(2,1)}, u32[]{:S(2)}, u32[]{:S(2)}) collective-permute-start(bf16[2,3,64,1024]{3,2,1,0:T(8,128)(2,1)} %collective-permute-done.5.refs_5_), channel_id=1, source_target_pairs={{3,0},{0,1},{1,2},{2,3},{7,4},{4,5},{5,6},{6,7},{11,8},{8,9},{9,10... | collective-permute-start | bytes 2359304 | tf_op jit(solution)/shard_map/ppermute | solution.py:31
  43.1 1.8 copy.10
  44.9 15.1 %all-to-all-start = ((bf16[4,3,64,256]{3,2,1,0:T(8,128)(2,1)}), bf16[4,3,64,256]{3,2,1,0:T(8,128)(2,1)S(1)}, u32[]{:S(2)}, u32[]{:S(2)}) async-start(bf16[4,3,64,256]{3,2,1,0:T(8,128)(2,1)} %bitcast.46), calls=%async_computation | async-start | bytes 786432 | tf_op jit(solution)/shard_map/all_to_all | solution.py:396
  60.0 0.1 pad_add_fusion.1.meta_ref
  60.0 0.0 copy-start.5
  60.1 6.6 %project.1.refs_3_ = bf16[12,64,512]{2,1,0:T(8,128)(2,1)} custom-call(bf16[2,3,64,1024]{3,2,1,0:T(8,128)(2,1)} %pair.2.refs_0_, bf16[2,3,64,1024]{3,2,1,0:T(8,128)(2,1)} %pair.3.refs_1_, bf16[2,3,64,1024]{3,2,1,0:T(8,128)(2,1)} %collective-permute-done.1.refs_2_, bf16[2,3,64,1024]{3,2,1,0:T(8,128)(2,1)} %collective-permute-done.7.refs_3_, ...), custom_call_target="tpu_custom_call" | custom-call | bytes 4718592 | tf_op jit(solution)/shard_map/project/pallas_call | solution.py:114
  66.7 1.1 copy-done.1
  67.8 4.7 %project_place.1 = (bf16[4,144,512]{2,1,0:T(8,128)(2,1)S(1)}, bf16[4,144,512]{2,1,0:T(8,128)(2,1)}) custom-call(s32[3]{0:T(128)S(1)} %pad_add_fusion.1.meta_ref, bf16[2,3,64,1024]{3,2,1,0:T(8,128)(2,1)} %collective-permute-done.2.refs_0_, bf16[2,3,64,1024]{3,2,1,0:T(8,128)(2,1)} %collective-permute-done.6.refs_1_, bf16[3,1024,512]{2,1,0:T(8,128)(2,1)S(1)} %bitcast.34, ...), custom_call_target="tpu_custom_call" | custom-call | bytes 1572864 | tf_op jit(solution)/shard_map/project_place/pallas_call | solution.py:165
  72.5 0.8 copy-done.3
  73.3 2.5 %collective-permute-start.9 = (bf16[4,144,512]{2,1,0:T(8,128)(2,1)}, bf16[4,144,512]{2,1,0:T(8,128)(2,1)S(1)}, u32[]{:S(2)}, u32[]{:S(2)}) collective-permute-start(bf16[4,144,512]{2,1,0:T(8,128)(2,1)} %get-tuple-element.28), channel_id=1, source_target_pairs={{64,0},{0,64},{192,128},{128,192},{320,256},{256,320},{448,384},{3... | collective-permute-start | bytes 1769480 | tf_op jit(solution)/shard_map/ppermute | solution.py:35
  75.9 0.9 slice_bitcast_fusion
  76.8 0.9 collective-permute-done.9.got_ref
  77.7 1.1 copy-done.4
  78.7 0.1 join.1
  78.9 1.9 all-to-all-done.traded_ref
  80.8 1.6 turn.1
  82.4 0.0 all-gather.4.cloned.1.call-update
  82.4 0.6 dynamic_slice.3
  83.0 0.7 maximum_reduce_fusion
  85.6 5.7 %collective-permute-start.16 = (bf16[16,512]{1,0:T(8,128)(2,1)S(1)}, bf16[16,512]{1,0:T(8,128)(2,1)S(1)}, u32[]{:S(2)}, u32[]{:S(2)}) collective-permute-start(bf16[16,512]{1,0:T(8,128)(2,1)S(1)} %get-tuple-element.49), channel_id=1, source_target_pairs={{2,1},{4,65},{6,129},{8,193},{10,257},{12,321},{14,385},{66,3},{68... | collective-permute-start | bytes 49160 | tf_op jit(solution)/shard_map/ppermute | solution.py:389
  91.3 3.9 %collective-permute-start.15 = (bf16[16,512]{1,0:T(8,128)(2,1)S(1)}, bf16[16,512]{1,0:T(8,128)(2,1)S(1)}, u32[]{:S(2)}, u32[]{:S(2)}) collective-permute-start(bf16[16,512]{1,0:T(8,128)(2,1)S(1)} %get-tuple-element.50), channel_id=1, source_target_pairs={{2,0},{4,64},{6,128},{8,192},{10,256},{12,320},{14,384},{66,2},{68... | collective-permute-start | bytes 49160 | tf_op jit(solution)/shard_map/ppermute | solution.py:388
  95.3 5.1 %collective-permute-start.10 = (bf16[144,512]{1,0:T(8,128)(2,1)S(1)}, bf16[144,512]{1,0:T(8,128)(2,1)S(1)}, u32[]{:S(2)}, u32[]{:S(2)}) collective-permute-start(bf16[144,512]{1,0:T(8,128)(2,1)S(1)} %get-tuple-element.32), channel_id=1, source_target_pairs={{128,0},{192,64},{256,128},{320,192},{384,256},{448,320},{0,384},{... | collective-permute-start | bytes 442376 | tf_op jit(solution)/shard_map/ppermute | solution.py:40
  100.3 2.4 %collective-permute-start.11 = (bf16[144,512]{1,0:T(8,128)(2,1)S(1)}, bf16[144,512]{1,0:T(8,128)(2,1)S(1)}, u32[]{:S(2)}, u32[]{:S(2)}) collective-permute-start(bf16[144,512]{1,0:T(8,128)(2,1)S(1)} %get-tuple-element.33), channel_id=1, source_target_pairs={{256,0},{320,64},{384,128},{448,192},{0,256},{64,320},{128,384},{1... | collective-permute-start | bytes 442376 | tf_op jit(solution)/shard_map/ppermute | solution.py:40
  102.8 3.4 %collective-permute-start.12 = (bf16[144,512]{1,0:T(8,128)(2,1)S(1)}, bf16[144,512]{1,0:T(8,128)(2,1)S(1)}, u32[]{:S(2)}, u32[]{:S(2)}) collective-permute-start(bf16[144,512]{1,0:T(8,128)(2,1)S(1)} %get-tuple-element.34), channel_id=1, source_target_pairs={{384,0},{448,64},{0,128},{64,192},{128,256},{192,320},{256,384},{3... | collective-permute-start | bytes 442376 | tf_op jit(solution)/shard_map/ppermute | solution.py:40
  106.2 0.0 collective-permute-done.16.refs_7_
  106.2 1.9 collective-permute-start.14
  108.1 7.3 %collective-permute-start.13 = (bf16[64,512]{1,0:T(8,128)(2,1)S(1)}, bf16[64,512]{1,0:T(8,128)(2,1)S(1)}, u32[]{:S(2)}, u32[]{:S(2)}) collective-permute-start(bf16[64,512]{1,0:T(8,128)(2,1)S(1)} %get-tuple-element.52), channel_id=1, source_target_pairs={{0,0},{1,1},{2,64},{3,65},{4,128},{5,129},{6,192},{7,193},{8,256},... | collective-permute-start | bytes 196616 | tf_op jit(solution)/shard_map/ppermute | solution.py:386
  115.4 0.7 pad_add_fusion.meta_ref
  116.1 1.4 collective-permute-done.14.refs_5_
  117.4 5.0 %collective-permute-done.13.refs_4_ = bf16[64,512]{1,0:T(8,128)(2,1)S(1)} collective-permute-done((bf16[64,512]{1,0:T(8,128)(2,1)S(1)}, bf16[64,512]{1,0:T(8,128)(2,1)S(1)}, u32[]{:S(2)}, u32[]{:S(2)}) %collective-permute-start.13) | collective-permute-done | bytes 65568 | tf_op jit(solution)/shard_map/ppermute | solution.py:386
  122.5 0.0 collective-permute-done.12.refs_3_
  122.5 1.4 chain.1
  123.9 26.6 %all-gather = bf16[576,512]{1,0:T(8,128)(2,1)S(1)} all-gather(bf16[144,512]{1,0:T(8,128)(2,1)S(1)} %chain.1), channel_id=2, replica_groups=mesh['tp'=8,'dp'=4,'draft'=16] {'dp'}, dimensions={0}, use_global_device_ids=true | all-gather | bytes 737280 | tf_op jit(solution)/shard_map/all_gather | solution.py:400
  150.5 1.9 collective-permute-start.19
  152.4 7.4 %collective-permute-start.18 = (bf16[4,144,512]{2,1,0:T(8,128)(2,1)S(1)}, bf16[4,144,512]{2,1,0:T(8,128)(2,1)S(1)}, u32[]{:S(2)}, u32[]{:S(2)}) collective-permute-start(bf16[4,144,512]{2,1,0:T(8,128)(2,1)S(1)} %bitcast.36), channel_id=1, source_target_pairs={{432,0},{384,16},{400,32},{416,48},{496,64},{448,80},{464,96},{480... | collective-permute-start | bytes 1769480 | tf_op jit(solution)/shard_map/ppermute | solution.py:53
  159.8 1.9 collective-permute-start.17
  161.7 3.1 %collective-permute-start.21 = (bf16[2,144,512]{2,1,0:T(8,128)(2,1)S(1)}, bf16[2,144,512]{2,1,0:T(8,128)(2,1)S(1)}, u32[]{:S(2)}, u32[]{:S(2)}) collective-permute-start(bf16[2,144,512]{2,1,0:T(8,128)(2,1)S(1)} %bitcast.48), channel_id=1, source_target_pairs={{304,0},{256,16},{272,32},{288,48},{368,64},{320,80},{336,96},{352... | collective-permute-start | bytes 884744 | tf_op jit(solution)/shard_map/ppermute | solution.py:53
  164.8 4.3 %collective-permute-start.20 = (bf16[2,144,512]{2,1,0:T(8,128)(2,1)S(1)}, bf16[2,144,512]{2,1,0:T(8,128)(2,1)S(1)}, u32[]{:S(2)}, u32[]{:S(2)}) collective-permute-start(bf16[2,144,512]{2,1,0:T(8,128)(2,1)S(1)} %bitcast.47), channel_id=1, source_target_pairs={{256,0},{272,16},{288,32},{304,48},{320,64},{336,80},{352,96},{368... | collective-permute-start | bytes 884744 | tf_op jit(solution)/shard_map/ppermute | solution.py:53
  169.1 16.0 %collective-permute-done.21 = bf16[2,144,512]{2,1,0:T(8,128)(2,1)S(1)} collective-permute-done((bf16[2,144,512]{2,1,0:T(8,128)(2,1)S(1)}, bf16[2,144,512]{2,1,0:T(8,128)(2,1)S(1)}, u32[]{:S(2)}, u32[]{:S(2)}) %collective-permute-start.21) | collective-permute-done | bytes 294944 | tf_op jit(solution)/shard_map/ppermute | solution.py:53
  185.1 3.9 %collective-permute-done.20 = bf16[2,144,512]{2,1,0:T(8,128)(2,1)S(1)} collective-permute-done((bf16[2,144,512]{2,1,0:T(8,128)(2,1)S(1)}, bf16[2,144,512]{2,1,0:T(8,128)(2,1)S(1)}, u32[]{:S(2)}, u32[]{:S(2)}) %collective-permute-start.20) | collective-permute-done | bytes 294944 | tf_op jit(solution)/shard_map/ppermute | solution.py:53
  189.0 0.1 pad_maximum_fusion.refs_4_
  189.1 0.0 all-gather.4.cloned.1.call-done
  189.1 2.8 %collective-permute-start.22 = (bf16[4,144,512]{2,1,0:T(8,128)(2,1)S(1)}, bf16[4,144,512]{2,1,0:T(8,128)(2,1)S(1)}, u32[]{:S(2)}, u32[]{:S(2)}) collective-permute-start(bf16[4,144,512]{2,1,0:T(8,128)(2,1)S(1)} %collective-permute-done.17.refs_2_), channel_id=1, source_target_pairs={{64,0},{0,64},{192,128},{128,192},{320,256},{256,320},{448,384},{3... | collective-permute-start | bytes 1769480 | tf_op jit(solution)/shard_map/ppermute | solution.py:35
  191.9 1.9 collective-permute-start.23
  193.8 2.4 %collective-permute-start.24 = (bf16[4,144,512]{2,1,0:T(8,128)(2,1)S(1)}, bf16[4,144,512]{2,1,0:T(8,128)(2,1)}, u32[]{:S(2)}, u32[]{:S(2)}) collective-permute-start(bf16[4,144,512]{2,1,0:T(8,128)(2,1)S(1)} %pad_maximum_fusion.refs_4_), channel_id=1, source_target_pairs={{64,0},{0,64},{192,128},{128,192},{320,256},{256,320},{448,384},{3... | collective-permute-start | bytes 1769480 | tf_op jit(solution)/shard_map/ppermute | solution.py:35
  196.3 0.1 stack.56.meta_ref
  196.4 1.6 collective-permute-done.24.refs_7_
  198.0 7.7 %weight_grad.1 = (bf16[3,256,512]{2,1,0:T(8,128)(2,1)}, f32[1,512]{1,0:T(1,128)}) custom-call(s32[8]{0:T(128)S(1)} %stack.56.meta_ref, bf16[16,3,256,256]{3,2,1,0:T(8,128)(2,1)} %bitcast.49, bf16[4,144,512]{2,1,0:T(8,128)(2,1)S(1)} %bitcast.38, bf16[4,144,512]{2,1,0:T(8,128)(2,1)S(1)} %collective-permute-done.19.refs_1_, ...), custom_call_target="tpu_custom_call" | custom-call | flops 3221225472 | bytes 10485760 | tf_op jit(solution)/shard_map/weight_grad/pallas_call | solution.py:320
  (25 shorter events, 0.1 us)
Async XLA Ops:
  7.2 10.1 %collective-permute-start = (bf16[3,64,1024]{2,1,0:T(8,128)(2,1)}, bf16[3,64,1024]{2,1,0:T(8,128)(2,1)S(1)}, u32[]{:S(2)}, u32[]{:S(2)}) collective-permute-start(bf16[3,64,1024]{2,1,0:T(8,128)(2,1)} %bitcast.39), channel_id=1, source_target_pairs={{4,0},{5,1},{6,2},{7,3},{8,4},{9,5},{10,6},{11,7},{12,8},{13,9},{1... | collective-permute-start | bytes 1179656 | tf_op jit(solution)/shard_map/ppermute | solution.py:31
  11.8 14.3 %collective-permute-start.4 = (bf16[3,64,1024]{2,1,0:T(8,128)(2,1)}, bf16[3,64,1024]{2,1,0:T(8,128)(2,1)S(1)}, u32[]{:S(2)}, u32[]{:S(2)}) collective-permute-start(bf16[3,64,1024]{2,1,0:T(8,128)(2,1)} %bitcast.40), channel_id=1, source_target_pairs={{12,0},{13,1},{14,2},{15,3},{0,4},{1,5},{2,6},{3,7},{4,8},{5,9},{6... | collective-permute-start | bytes 1179656 | tf_op jit(solution)/shard_map/ppermute | solution.py:31
  13.7 12.4 %collective-permute-start.3 = (bf16[3,64,1024]{2,1,0:T(8,128)(2,1)}, bf16[3,64,1024]{2,1,0:T(8,128)(2,1)S(1)}, u32[]{:S(2)}, u32[]{:S(2)}) collective-permute-start(bf16[3,64,1024]{2,1,0:T(8,128)(2,1)} %bitcast.41), channel_id=1, source_target_pairs={{8,0},{9,1},{10,2},{11,3},{12,4},{13,5},{14,6},{15,7},{0,8},{1,9},... | collective-permute-start | bytes 1179656 | tf_op jit(solution)/shard_map/ppermute | solution.py:31
  17.3 1.0 copy-start.2
  19.3 47.4 %copy-start = (bf16[1024,3,512]{2,0,1:T(8,128)(2,1)S(1)}, bf16[1024,3,512]{2,0,1:T(8,128)(2,1)}, u32[]{:S(2)}) copy-start(bf16[1024,3,512]{2,0,1:T(8,128)(2,1)} %param.5) | copy-start | bytes 9437188
  19.3 16.9 %collective-permute-start.1 = (bf16[2,3,64,1024]{3,2,1,0:T(8,128)(2,1)}, bf16[2,3,64,1024]{3,2,1,0:T(8,128)(2,1)}, u32[]{:S(2)}, u32[]{:S(2)}) collective-permute-start(bf16[2,3,64,1024]{3,2,1,0:T(8,128)(2,1)} %pair.2.refs_0_), channel_id=1, source_target_pairs={{1,0},{2,1},{3,2},{0,3},{5,4},{6,5},{7,6},{4,7},{9,8},{10,9},{11,1... | collective-permute-start | bytes 2359304 | tf_op jit(solution)/shard_map/ppermute | solution.py:31
  27.0 13.3 %collective-permute-start.5 = (bf16[2,3,64,1024]{3,2,1,0:T(8,128)(2,1)}, bf16[2,3,64,1024]{3,2,1,0:T(8,128)(2,1)}, u32[]{:S(2)}, u32[]{:S(2)}) collective-permute-start(bf16[2,3,64,1024]{3,2,1,0:T(8,128)(2,1)} %pair.3.refs_1_), channel_id=1, source_target_pairs={{3,0},{0,1},{1,2},{2,3},{7,4},{4,5},{5,6},{6,7},{11,8},{8,9},{9,10... | collective-permute-start | bytes 2359304 | tf_op jit(solution)/shard_map/ppermute | solution.py:31
  30.0 30.0 %collective-permute-start.8 = (bf16[2,3,64,1024]{3,2,1,0:T(8,128)(2,1)}, bf16[2,3,64,1024]{3,2,1,0:T(8,128)(2,1)}, u32[]{:S(2)}, u32[]{:S(2)}) collective-permute-start(bf16[2,3,64,1024]{3,2,1,0:T(8,128)(2,1)} %pair.2.refs_0_), channel_id=1, source_target_pairs={{3,0},{0,1},{1,2},{2,3},{7,4},{4,5},{5,6},{6,7},{11,8},{8,9},{9,10... | collective-permute-start | bytes 2359304 | tf_op jit(solution)/shard_map/ppermute | solution.py:31
  32.1 27.9 %collective-permute-start.7 = (bf16[2,3,64,1024]{3,2,1,0:T(8,128)(2,1)}, bf16[2,3,64,1024]{3,2,1,0:T(8,128)(2,1)}, u32[]{:S(2)}, u32[]{:S(2)}) collective-permute-start(bf16[2,3,64,1024]{3,2,1,0:T(8,128)(2,1)} %pair.3.refs_1_), channel_id=1, source_target_pairs={{1,0},{2,1},{3,2},{0,3},{5,4},{6,5},{7,6},{4,7},{9,8},{10,9},{11,1... | collective-permute-start | bytes 2359304 | tf_op jit(solution)/shard_map/ppermute | solution.py:31
  36.2 30.5 %collective-permute-start.2 = (bf16[2,3,64,1024]{3,2,1,0:T(8,128)(2,1)}, bf16[2,3,64,1024]{3,2,1,0:T(8,128)(2,1)}, u32[]{:S(2)}, u32[]{:S(2)}) collective-permute-start(bf16[2,3,64,1024]{3,2,1,0:T(8,128)(2,1)} %collective-permute-done.1.refs_2_), channel_id=1, source_target_pairs={{1,0},{2,1},{3,2},{0,3},{5,4},{6,5},{7,6},{4,7},{9,8},{10,9},{11,1... | collective-permute-start | bytes 2359304 | tf_op jit(solution)/shard_map/ppermute | solution.py:31
  40.4 26.3 %collective-permute-start.6 = (bf16[2,3,64,1024]{3,2,1,0:T(8,128)(2,1)}, bf16[2,3,64,1024]{3,2,1,0:T(8,128)(2,1)}, u32[]{:S(2)}, u32[]{:S(2)}) collective-permute-start(bf16[2,3,64,1024]{3,2,1,0:T(8,128)(2,1)} %collective-permute-done.5.refs_5_), channel_id=1, source_target_pairs={{3,0},{0,1},{1,2},{2,3},{7,4},{4,5},{5,6},{6,7},{11,8},{8,9},{9,10... | collective-permute-start | bytes 2359304 | tf_op jit(solution)/shard_map/ppermute | solution.py:31
  44.9 35.9 %all-to-all-start = ((bf16[4,3,64,256]{3,2,1,0:T(8,128)(2,1)}), bf16[4,3,64,256]{3,2,1,0:T(8,128)(2,1)S(1)}, u32[]{:S(2)}, u32[]{:S(2)}) async-start(bf16[4,3,64,256]{3,2,1,0:T(8,128)(2,1)} %bitcast.46), calls=%async_computation | async-start | bytes 786432 | tf_op jit(solution)/shard_map/all_to_all | solution.py:396
  60.0 129.2 %all-gather.4.cloned.1.call-start = ((), (), s32[]{:S(2)}) async-start(), calls=%async_computation.1 | async-start | bytes 6684672 | tf_op jit(solution)/shard_map/all_gather | solution.py:442
  60.0 22.4 %copy-start.6 = (s32[4]{0:T(128)S(1)}, s32[4]{0:T(128)}, u32[]{:S(2)}) copy-start(s32[4]{0:T(128)} %param.7) | copy-start | bytes 52
  60.0 62.4 %copy-start.5 = (f32[512]{0:T(512)S(1)}, f32[512]{0:T(512)}, u32[]{:S(2)}) copy-start(f32[512]{0:T(512)} %param.6) | copy-start | bytes 6148
  66.7 1.1 copy-start.1
  72.5 0.8 copy-start.3
  73.3 4.3 %collective-permute-start.9 = (bf16[4,144,512]{2,1,0:T(8,128)(2,1)}, bf16[4,144,512]{2,1,0:T(8,128)(2,1)S(1)}, u32[]{:S(2)}, u32[]{:S(2)}) collective-permute-start(bf16[4,144,512]{2,1,0:T(8,128)(2,1)} %get-tuple-element.28), channel_id=1, source_target_pairs={{64,0},{0,64},{192,128},{128,192},{320,256},{256,320},{448,384},{3... | collective-permute-start | bytes 1769480 | tf_op jit(solution)/shard_map/ppermute | solution.py:35
  77.7 1.1 copy-start.4
  85.6 20.5 %collective-permute-start.16 = (bf16[16,512]{1,0:T(8,128)(2,1)S(1)}, bf16[16,512]{1,0:T(8,128)(2,1)S(1)}, u32[]{:S(2)}, u32[]{:S(2)}) collective-permute-start(bf16[16,512]{1,0:T(8,128)(2,1)S(1)} %get-tuple-element.49), channel_id=1, source_target_pairs={{2,1},{4,65},{6,129},{8,193},{10,257},{12,321},{14,385},{66,3},{68... | collective-permute-start | bytes 49160 | tf_op jit(solution)/shard_map/ppermute | solution.py:389
  91.3 16.8 %collective-permute-start.15 = (bf16[16,512]{1,0:T(8,128)(2,1)S(1)}, bf16[16,512]{1,0:T(8,128)(2,1)S(1)}, u32[]{:S(2)}, u32[]{:S(2)}) collective-permute-start(bf16[16,512]{1,0:T(8,128)(2,1)S(1)} %get-tuple-element.50), channel_id=1, source_target_pairs={{2,0},{4,64},{6,128},{8,192},{10,256},{12,320},{14,384},{66,2},{68... | collective-permute-start | bytes 49160 | tf_op jit(solution)/shard_map/ppermute | solution.py:388
  95.3 27.2 %collective-permute-start.10 = (bf16[144,512]{1,0:T(8,128)(2,1)S(1)}, bf16[144,512]{1,0:T(8,128)(2,1)S(1)}, u32[]{:S(2)}, u32[]{:S(2)}) collective-permute-start(bf16[144,512]{1,0:T(8,128)(2,1)S(1)} %get-tuple-element.32), channel_id=1, source_target_pairs={{128,0},{192,64},{256,128},{320,192},{384,256},{448,320},{0,384},{... | collective-permute-start | bytes 442376 | tf_op jit(solution)/shard_map/ppermute | solution.py:40
  100.3 22.2 %collective-permute-start.11 = (bf16[144,512]{1,0:T(8,128)(2,1)S(1)}, bf16[144,512]{1,0:T(8,128)(2,1)S(1)}, u32[]{:S(2)}, u32[]{:S(2)}) collective-permute-start(bf16[144,512]{1,0:T(8,128)(2,1)S(1)} %get-tuple-element.33), channel_id=1, source_target_pairs={{256,0},{320,64},{384,128},{448,192},{0,256},{64,320},{128,384},{1... | collective-permute-start | bytes 442376 | tf_op jit(solution)/shard_map/ppermute | solution.py:40
  102.8 19.7 %collective-permute-start.12 = (bf16[144,512]{1,0:T(8,128)(2,1)S(1)}, bf16[144,512]{1,0:T(8,128)(2,1)S(1)}, u32[]{:S(2)}, u32[]{:S(2)}) collective-permute-start(bf16[144,512]{1,0:T(8,128)(2,1)S(1)} %get-tuple-element.34), channel_id=1, source_target_pairs={{384,0},{448,64},{0,128},{64,192},{128,256},{192,320},{256,384},{3... | collective-permute-start | bytes 442376 | tf_op jit(solution)/shard_map/ppermute | solution.py:40
  106.2 11.3 %collective-permute-start.14 = (bf16[64,512]{1,0:T(8,128)(2,1)S(1)}, bf16[64,512]{1,0:T(8,128)(2,1)S(1)}, u32[]{:S(2)}, u32[]{:S(2)}) collective-permute-start(bf16[64,512]{1,0:T(8,128)(2,1)S(1)} %get-tuple-element.51), channel_id=1, source_target_pairs={{0,1},{1,0},{2,65},{3,64},{4,129},{5,128},{6,193},{7,192},{8,257},... | collective-permute-start | bytes 196616 | tf_op jit(solution)/shard_map/ppermute | solution.py:387
  108.1 14.4 %collective-permute-start.13 = (bf16[64,512]{1,0:T(8,128)(2,1)S(1)}, bf16[64,512]{1,0:T(8,128)(2,1)S(1)}, u32[]{:S(2)}, u32[]{:S(2)}) collective-permute-start(bf16[64,512]{1,0:T(8,128)(2,1)S(1)} %get-tuple-element.52), channel_id=1, source_target_pairs={{0,0},{1,1},{2,64},{3,65},{4,128},{5,129},{6,192},{7,193},{8,256},... | collective-permute-start | bytes 196616 | tf_op jit(solution)/shard_map/ppermute | solution.py:386
  150.5 38.6 %collective-permute-start.19 = (bf16[4,144,512]{2,1,0:T(8,128)(2,1)S(1)}, bf16[4,144,512]{2,1,0:T(8,128)(2,1)S(1)}, u32[]{:S(2)}, u32[]{:S(2)}) collective-permute-start(bf16[4,144,512]{2,1,0:T(8,128)(2,1)S(1)} %bitcast.35), channel_id=1, source_target_pairs={{64,0},{0,64},{192,128},{128,192},{320,256},{256,320},{448,384},{3... | collective-permute-start | bytes 1769480 | tf_op jit(solution)/shard_map/ppermute | solution.py:35
  152.4 36.7 %collective-permute-start.18 = (bf16[4,144,512]{2,1,0:T(8,128)(2,1)S(1)}, bf16[4,144,512]{2,1,0:T(8,128)(2,1)S(1)}, u32[]{:S(2)}, u32[]{:S(2)}) collective-permute-start(bf16[4,144,512]{2,1,0:T(8,128)(2,1)S(1)} %bitcast.36), channel_id=1, source_target_pairs={{432,0},{384,16},{400,32},{416,48},{496,64},{448,80},{464,96},{480... | collective-permute-start | bytes 1769480 | tf_op jit(solution)/shard_map/ppermute | solution.py:53
  159.8 29.3 %collective-permute-start.17 = (bf16[4,144,512]{2,1,0:T(8,128)(2,1)S(1)}, bf16[4,144,512]{2,1,0:T(8,128)(2,1)S(1)}, u32[]{:S(2)}, u32[]{:S(2)}) collective-permute-start(bf16[4,144,512]{2,1,0:T(8,128)(2,1)S(1)} %bitcast.37), channel_id=1, source_target_pairs={{128,0},{144,16},{160,32},{176,48},{192,64},{208,80},{224,96},{240... | collective-permute-start | bytes 1769480 | tf_op jit(solution)/shard_map/ppermute | solution.py:53
  161.7 23.4 %collective-permute-start.21 = (bf16[2,144,512]{2,1,0:T(8,128)(2,1)S(1)}, bf16[2,144,512]{2,1,0:T(8,128)(2,1)S(1)}, u32[]{:S(2)}, u32[]{:S(2)}) collective-permute-start(bf16[2,144,512]{2,1,0:T(8,128)(2,1)S(1)} %bitcast.48), channel_id=1, source_target_pairs={{304,0},{256,16},{272,32},{288,48},{368,64},{320,80},{336,96},{352... | collective-permute-start | bytes 884744 | tf_op jit(solution)/shard_map/ppermute | solution.py:53
  164.8 24.2 %collective-permute-start.20 = (bf16[2,144,512]{2,1,0:T(8,128)(2,1)S(1)}, bf16[2,144,512]{2,1,0:T(8,128)(2,1)S(1)}, u32[]{:S(2)}, u32[]{:S(2)}) collective-permute-start(bf16[2,144,512]{2,1,0:T(8,128)(2,1)S(1)} %bitcast.47), channel_id=1, source_target_pairs={{256,0},{272,16},{288,32},{304,48},{320,64},{336,80},{352,96},{368... | collective-permute-start | bytes 884744 | tf_op jit(solution)/shard_map/ppermute | solution.py:53
  189.1 7.3 %collective-permute-start.22 = (bf16[4,144,512]{2,1,0:T(8,128)(2,1)S(1)}, bf16[4,144,512]{2,1,0:T(8,128)(2,1)S(1)}, u32[]{:S(2)}, u32[]{:S(2)}) collective-permute-start(bf16[4,144,512]{2,1,0:T(8,128)(2,1)S(1)} %collective-permute-done.17.refs_2_), channel_id=1, source_target_pairs={{64,0},{0,64},{192,128},{128,192},{320,256},{256,320},{448,384},{3... | collective-permute-start | bytes 1769480 | tf_op jit(solution)/shard_map/ppermute | solution.py:35
  191.9 4.5 %collective-permute-start.23 = (bf16[4,144,512]{2,1,0:T(8,128)(2,1)S(1)}, bf16[4,144,512]{2,1,0:T(8,128)(2,1)}, u32[]{:S(2)}, u32[]{:S(2)}) collective-permute-start(bf16[4,144,512]{2,1,0:T(8,128)(2,1)S(1)} %collective-permute-done.18.refs_3_), channel_id=1, source_target_pairs={{64,0},{0,64},{192,128},{128,192},{320,256},{256,320},{448,384},{3... | collective-permute-start | bytes 1769480 | tf_op jit(solution)/shard_map/ppermute | solution.py:35
  193.8 4.2 %collective-permute-start.24 = (bf16[4,144,512]{2,1,0:T(8,128)(2,1)S(1)}, bf16[4,144,512]{2,1,0:T(8,128)(2,1)}, u32[]{:S(2)}, u32[]{:S(2)}) collective-permute-start(bf16[4,144,512]{2,1,0:T(8,128)(2,1)S(1)} %pad_maximum_fusion.refs_4_), channel_id=1, source_target_pairs={{64,0},{0,64},{192,128},{128,192},{320,256},{256,320},{448,384},{3... | collective-permute-start | bytes 1769480 | tf_op jit(solution)/shard_map/ppermute | solution.py:35
Sparse Core Ops, SparseCore 0:
  82.5 81.9 all-gather.3

commit v16 on v15

--- a/solution.py
+++ b/solution.py
@@ -214,7 +214,7 @@
     return 1.0 / (1.0 + jnp.exp(-v))
 
 
-def chain_kernel(meta_ref, scale_ref, *refs):
+def chain_kernel(meta_ref, lengths_ref, *refs):
     *part_refs, one_ref, two_ref, left_ref, right_ref, gain_ref, grad_ref = refs
     rows, width = part_refs[0].shape
     own = rows - 2 * HALO
@@ -227,8 +227,12 @@
         [pick(one_ref, two_ref), pick(two_ref, one_ref), pick(left_ref, right_ref)], axis=0
     )
     gain = gain_ref[...]
-    scale = scale_ref[0]
-    start, length = meta_ref[0], meta_ref[1]
+    start, length = meta_ref[0], lengths_ref[meta_ref[1]]
+    valid = jnp.int32(0)
+    for step in range(1, UNROLL + 1):
+        for sequence in range(lengths_ref.shape[0]):
+            valid = valid + jnp.maximum(lengths_ref[sequence] - step, 0)
+    scale = LOSS_SCALE / jnp.full((1, width), valid, jnp.int32).astype(jnp.float32)
     position = start - HALO + lax.broadcasted_iota(jnp.int32, (rows, width), 0)
 
     def down(values):
@@ -269,7 +273,7 @@
     grad_ref[pl.ds(own, TAIL), :] = jnp.concatenate(tail, axis=0).astype(jnp.bfloat16)
 
 
-def chain(parts, halves, gain, start, length, odd, scale):
+def chain(parts, halves, gain, start, zh, odd, lengths):
     rows, width = parts[0].shape
     own = rows - 2 * HALO
     return pl.pallas_call(
@@ -282,7 +286,7 @@
             flops=60 * rows * width, bytes_accessed=10 * rows * width, transcendentals=3 * rows * width
         ),
         name="chain",
-    )(jnp.stack([start, length, odd]), scale.reshape(1), *parts, *halves, gain.reshape(1, width))
+    )(jnp.stack([start, zh, odd]), lengths, *parts, *halves, gain.reshape(1, width))
 
 
 def weight_grad_kernel(meta_ref, features_ref, *refs):
@@ -359,13 +363,6 @@
     )(traded)
 
 
-def valid_total(lengths):
-    running = jnp.zeros((), jnp.float32)
-    for unroll in range(1, UNROLL + 1):
-        running = running + jnp.sum(jnp.maximum(lengths - unroll, 0)).astype(jnp.float32)
-    return running
-
-
 def send_high(top, draft_index):
     members, draft_count = ZL * CORES, X * Y
     width = top.shape[1] // 2
@@ -441,9 +438,8 @@
     halves = send_high(top, draft_index)
     every = lax.all_gather(turn(traded), "draft", axis=0, tiled=False)
     parts = [mine] + [from_zl(block, step) for step, block in zip((1, 2, 3), away)]
-    scale = LOSS_SCALE / valid_total(lengths)
     odd = draft_index % 2
-    grad = chain(parts, halves, mix_gain, tp_index * piece, lengths[zh], odd, scale)
+    grad = chain(parts, halves, mix_gain, tp_index * piece, zh, odd, lengths)
     fc_grad, mix_total = gather_grads(grad, every, zl, core)
     return (fc_grad.transpose(1, 0, 2), mix_total[0])
 

time: 214 us -> 210 us (0.981)
  the two profiles are of different devices: /device:TPU:5 before, /device:TPU:1 now
where the time goes in v16:
time: 210 us; the launch traced here: 206 us
  starting transfers between devices  106 us (50%)
  waiting for transfers between devices  28.2 us (13%)
  blocking collectives  26.3 us (13%)
  Pallas kernels  24 us (11%)
  between operations  14.5 us (7%)
  local copies, waits for them, and re-layouts  6.9 us (3%)
    ppermute x9, starting transfers between devices, plane_move(): return lambda block: lax.ppermute(block, ('tp', 'draft'), pairs)  31.6 us
    all_gather x1, blocking collectives, gather_grads(): stack = lax.all_gather(grad, 'dp', axis=0, tiled=False)  26.3 us
    ppermute x4, waiting for transfers between devices, from_z(): return lax.ppermute(block, ('tp', 'dp'), pairs)  19.8 us
    ppermute x4, starting transfers between devices, from_z(): return lax.ppermute(block, ('tp', 'dp'), pairs)  18.9 us
    all_to_all x1, starting transfers between devices, trade_columns(): lax.all_to_all(quarters, 'dp', split_axis=0, concat_axis=0, tiled=True)  14.7 us
    ppermute x5, starting transfers between devices, from_other_core(): return lax.ppermute(block, 'tp', [(t ^ 1, t) for t in range(ZL * CORES)])  13.9 us
    ppermute x3, starting transfers between devices, from_zl(): return lax.ppermute(block, 'tp', pairs)  10.7 us
    ppermute x1, starting transfers between devices, send_high(): lax.ppermute(jnp.where(even, left, right), axes, straight)  9.22 us
  transfers between devices with their start and end apart: 27, of which 7 were waited for; matrix products, arithmetic and copies ran while one was open for 1% of the time, Pallas kernels for 7%

profile of v16, /device:TPU:1, one launch (start us, length us, event | category | flops | bytes accessed | tf_op | source)
XLA Modules:
  0.0 206.4 jit_solution(13924768903167590944)
XLA Ops:
  7.2 5.5 %collective-permute-start = (bf16[3,64,1024]{2,1,0:T(8,128)(2,1)}, bf16[3,64,1024]{2,1,0:T(8,128)(2,1)S(1)}, u32[]{:S(2)}, u32[]{:S(2)}) collective-permute-start(bf16[3,64,1024]{2,1,0:T(8,128)(2,1)} %bitcast.39), channel_id=1, source_target_pairs={{4,0},{5,1},{6,2},{7,3},{8,4},{9,5},{10,6},{11,7},{12,8},{13,9},{1... | collective-permute-start | bytes 1179656 | tf_op jit(solution)/shard_map/ppermute | solution.py:31
  12.6 1.9 collective-permute-start.4
  14.6 3.5 %collective-permute-start.3 = (bf16[3,64,1024]{2,1,0:T(8,128)(2,1)}, bf16[3,64,1024]{2,1,0:T(8,128)(2,1)S(1)}, u32[]{:S(2)}, u32[]{:S(2)}) collective-permute-start(bf16[3,64,1024]{2,1,0:T(8,128)(2,1)} %bitcast.41), channel_id=1, source_target_pairs={{8,0},{9,1},{10,2},{11,3},{12,4},{13,5},{14,6},{15,7},{0,8},{1,9},... | collective-permute-start | bytes 1179656 | tf_op jit(solution)/shard_map/ppermute | solution.py:31
  18.1 0.0 collective-permute-done.second_ref
  18.1 0.0 copy-start.2
  18.1 1.0 copy-done.2
  19.2 0.9 pair.2.refs_0_
  20.1 4.6 %collective-permute-start.1 = (bf16[2,3,64,1024]{3,2,1,0:T(8,128)(2,1)}, bf16[2,3,64,1024]{3,2,1,0:T(8,128)(2,1)}, u32[]{:S(2)}, u32[]{:S(2)}) collective-permute-start(bf16[2,3,64,1024]{3,2,1,0:T(8,128)(2,1)} %pair.2.refs_0_), channel_id=1, source_target_pairs={{1,0},{2,1},{3,2},{0,3},{5,4},{6,5},{7,6},{4,7},{9,8},{10,9},{11,1... | collective-permute-start | bytes 2359304 | tf_op jit(solution)/shard_map/ppermute | solution.py:31
  24.8 2.3 %collective-permute-done.4.second_ref = bf16[3,64,1024]{2,1,0:T(8,128)(2,1)S(1)} collective-permute-done((bf16[3,64,1024]{2,1,0:T(8,128)(2,1)}, bf16[3,64,1024]{2,1,0:T(8,128)(2,1)S(1)}, u32[]{:S(2)}, u32[]{:S(2)}) %collective-permute-start.4) | collective-permute-done | bytes 393248 | tf_op jit(solution)/shard_map/ppermute | solution.py:31
  27.1 0.0 collective-permute-done.3.first_ref
  27.1 0.9 pair.3.refs_1_
  28.0 3.0 %collective-permute-start.5 = (bf16[2,3,64,1024]{3,2,1,0:T(8,128)(2,1)}, bf16[2,3,64,1024]{3,2,1,0:T(8,128)(2,1)}, u32[]{:S(2)}, u32[]{:S(2)}) collective-permute-start(bf16[2,3,64,1024]{3,2,1,0:T(8,128)(2,1)} %pair.3.refs_1_), channel_id=1, source_target_pairs={{3,0},{0,1},{1,2},{2,3},{7,4},{4,5},{5,6},{6,7},{11,8},{8,9},{9,10... | collective-permute-start | bytes 2359304 | tf_op jit(solution)/shard_map/ppermute | solution.py:31
  31.0 3.1 %collective-permute-start.8 = (bf16[2,3,64,1024]{3,2,1,0:T(8,128)(2,1)}, bf16[2,3,64,1024]{3,2,1,0:T(8,128)(2,1)}, u32[]{:S(2)}, u32[]{:S(2)}) collective-permute-start(bf16[2,3,64,1024]{3,2,1,0:T(8,128)(2,1)} %pair.2.refs_0_), channel_id=1, source_target_pairs={{3,0},{0,1},{1,2},{2,3},{7,4},{4,5},{5,6},{6,7},{11,8},{8,9},{9,10... | collective-permute-start | bytes 2359304 | tf_op jit(solution)/shard_map/ppermute | solution.py:31
  34.1 3.4 %collective-permute-start.7 = (bf16[2,3,64,1024]{3,2,1,0:T(8,128)(2,1)}, bf16[2,3,64,1024]{3,2,1,0:T(8,128)(2,1)}, u32[]{:S(2)}, u32[]{:S(2)}) collective-permute-start(bf16[2,3,64,1024]{3,2,1,0:T(8,128)(2,1)} %pair.3.refs_1_), channel_id=1, source_target_pairs={{1,0},{2,1},{3,2},{0,3},{5,4},{6,5},{7,6},{4,7},{9,8},{10,9},{11,1... | collective-permute-start | bytes 2359304 | tf_op jit(solution)/shard_map/ppermute | solution.py:31
  37.5 0.4 collective-permute-done.1.refs_2_
  37.9 4.7 %collective-permute-start.2 = (bf16[2,3,64,1024]{3,2,1,0:T(8,128)(2,1)}, bf16[2,3,64,1024]{3,2,1,0:T(8,128)(2,1)}, u32[]{:S(2)}, u32[]{:S(2)}) collective-permute-start(bf16[2,3,64,1024]{3,2,1,0:T(8,128)(2,1)} %collective-permute-done.1.refs_2_), channel_id=1, source_target_pairs={{1,0},{2,1},{3,2},{0,3},{5,4},{6,5},{7,6},{4,7},{9,8},{10,9},{11,1... | collective-permute-start | bytes 2359304 | tf_op jit(solution)/shard_map/ppermute | solution.py:31
  42.6 1.9 collective-permute-start.6
  44.5 1.8 copy.10
  46.3 14.7 %all-to-all-start = ((bf16[4,3,64,256]{3,2,1,0:T(8,128)(2,1)}), bf16[4,3,64,256]{3,2,1,0:T(8,128)(2,1)S(1)}, u32[]{:S(2)}, u32[]{:S(2)}) async-start(bf16[4,3,64,256]{3,2,1,0:T(8,128)(2,1)} %bitcast.46), calls=%async_computation | async-start | bytes 786432 | tf_op jit(solution)/shard_map/all_to_all | solution.py:393
  61.1 0.1 pad_add_fusion.1.meta_ref
  61.2 0.0 copy-start.6
  61.2 6.6 %project.1.refs_3_ = bf16[12,64,512]{2,1,0:T(8,128)(2,1)} custom-call(bf16[2,3,64,1024]{3,2,1,0:T(8,128)(2,1)} %pair.2.refs_0_, bf16[2,3,64,1024]{3,2,1,0:T(8,128)(2,1)} %pair.3.refs_1_, bf16[2,3,64,1024]{3,2,1,0:T(8,128)(2,1)} %collective-permute-done.1.refs_2_, bf16[2,3,64,1024]{3,2,1,0:T(8,128)(2,1)} %collective-permute-done.7.refs_3_, ...), custom_call_target="tpu_custom_call" | custom-call | bytes 4718592 | tf_op jit(solution)/shard_map/project/pallas_call | solution.py:114
  67.8 1.1 copy-done.1
  69.0 4.7 %project_place.1 = (bf16[4,144,512]{2,1,0:T(8,128)(2,1)S(1)}, bf16[4,144,512]{2,1,0:T(8,128)(2,1)}) custom-call(s32[3]{0:T(128)S(1)} %pad_add_fusion.1.meta_ref, bf16[2,3,64,1024]{3,2,1,0:T(8,128)(2,1)} %collective-permute-done.2.refs_0_, bf16[2,3,64,1024]{3,2,1,0:T(8,128)(2,1)} %collective-permute-done.6.refs_1_, bf16[3,1024,512]{2,1,0:T(8,128)(2,1)S(1)} %bitcast.34, ...), custom_call_target="tpu_custom_call" | custom-call | bytes 1572864 | tf_op jit(solution)/shard_map/project_place/pallas_call | solution.py:165
  73.6 0.8 copy-done.3
  74.5 4.9 %collective-permute-start.9 = (bf16[4,144,512]{2,1,0:T(8,128)(2,1)}, bf16[4,144,512]{2,1,0:T(8,128)(2,1)S(1)}, u32[]{:S(2)}, u32[]{:S(2)}) collective-permute-start(bf16[4,144,512]{2,1,0:T(8,128)(2,1)} %get-tuple-element.28), channel_id=1, source_target_pairs={{64,0},{0,64},{192,128},{128,192},{320,256},{256,320},{448,384},{3... | collective-permute-start | bytes 1769480 | tf_op jit(solution)/shard_map/ppermute | solution.py:35
  79.4 0.9 slice_bitcast_fusion
  80.4 0.9 collective-permute-done.9.got_ref
  81.2 1.1 copy-done.4
  82.3 0.1 join.1
  82.4 0.0 all-to-all-done.traded_ref
  82.4 1.6 turn.1
  84.0 0.0 all-gather.4.cloned.1.call-update
  84.1 0.7 collective-permute-start.16
  84.7 1.3 collective-permute-start.15
  86.0 2.9 %collective-permute-start.10 = (bf16[144,512]{1,0:T(8,128)(2,1)S(1)}, bf16[144,512]{1,0:T(8,128)(2,1)S(1)}, u32[]{:S(2)}, u32[]{:S(2)}) collective-permute-start(bf16[144,512]{1,0:T(8,128)(2,1)S(1)} %get-tuple-element.32), channel_id=1, source_target_pairs={{128,0},{192,64},{256,128},{320,192},{384,256},{448,320},{0,384},{... | collective-permute-start | bytes 442376 | tf_op jit(solution)/shard_map/ppermute | solution.py:40
  89.0 5.2 %collective-permute-start.11 = (bf16[144,512]{1,0:T(8,128)(2,1)S(1)}, bf16[144,512]{1,0:T(8,128)(2,1)S(1)}, u32[]{:S(2)}, u32[]{:S(2)}) collective-permute-start(bf16[144,512]{1,0:T(8,128)(2,1)S(1)} %get-tuple-element.33), channel_id=1, source_target_pairs={{256,0},{320,64},{384,128},{448,192},{0,256},{64,320},{128,384},{1... | collective-permute-start | bytes 442376 | tf_op jit(solution)/shard_map/ppermute | solution.py:40
  94.2 2.6 %collective-permute-start.12 = (bf16[144,512]{1,0:T(8,128)(2,1)S(1)}, bf16[144,512]{1,0:T(8,128)(2,1)S(1)}, u32[]{:S(2)}, u32[]{:S(2)}) collective-permute-start(bf16[144,512]{1,0:T(8,128)(2,1)S(1)} %get-tuple-element.34), channel_id=1, source_target_pairs={{384,0},{448,64},{0,128},{64,192},{128,256},{192,320},{256,384},{3... | collective-permute-start | bytes 442376 | tf_op jit(solution)/shard_map/ppermute | solution.py:40
  96.8 5.2 %collective-permute-start.14 = (bf16[64,512]{1,0:T(8,128)(2,1)S(1)}, bf16[64,512]{1,0:T(8,128)(2,1)S(1)}, u32[]{:S(2)}, u32[]{:S(2)}) collective-permute-start(bf16[64,512]{1,0:T(8,128)(2,1)S(1)} %get-tuple-element.48), channel_id=1, source_target_pairs={{0,1},{1,0},{2,65},{3,64},{4,129},{5,128},{6,193},{7,192},{8,257},... | collective-permute-start | bytes 196616 | tf_op jit(solution)/shard_map/ppermute | solution.py:384
  102.0 9.2 %collective-permute-start.13 = (bf16[64,512]{1,0:T(8,128)(2,1)S(1)}, bf16[64,512]{1,0:T(8,128)(2,1)S(1)}, u32[]{:S(2)}, u32[]{:S(2)}) collective-permute-start(bf16[64,512]{1,0:T(8,128)(2,1)S(1)} %get-tuple-element.49), channel_id=1, source_target_pairs={{0,0},{1,1},{2,64},{3,65},{4,128},{5,129},{6,192},{7,193},{8,256},... | collective-permute-start | bytes 196616 | tf_op jit(solution)/shard_map/ppermute | solution.py:383
  111.2 0.1 pad_add_fusion.meta_ref
  111.3 0.0 collective-permute-done.14.refs_5_
  111.3 3.1 %collective-permute-done.13.refs_4_ = bf16[64,512]{1,0:T(8,128)(2,1)S(1)} collective-permute-done((bf16[64,512]{1,0:T(8,128)(2,1)S(1)}, bf16[64,512]{1,0:T(8,128)(2,1)S(1)}, u32[]{:S(2)}, u32[]{:S(2)}) %collective-permute-start.13) | collective-permute-done | bytes 65568 | tf_op jit(solution)/shard_map/ppermute | solution.py:383
  114.4 0.0 collective-permute-done.10.refs_1_
  114.5 0.0 collective-permute-done.11.refs_2_
  114.5 0.0 collective-permute-done.12.refs_3_
  114.5 1.4 chain.1
  115.9 26.3 %all-gather = bf16[576,512]{1,0:T(8,128)(2,1)S(1)} all-gather(bf16[144,512]{1,0:T(8,128)(2,1)S(1)} %chain.1), channel_id=2, replica_groups=mesh['tp'=8,'dp'=4,'draft'=16] {'dp'}, dimensions={0}, use_global_device_ids=true | all-gather | bytes 737280 | tf_op jit(solution)/shard_map/all_gather | solution.py:397
  142.2 1.9 collective-permute-start.19
  144.1 9.6 %collective-permute-start.18 = (bf16[4,144,512]{2,1,0:T(8,128)(2,1)S(1)}, bf16[4,144,512]{2,1,0:T(8,128)(2,1)S(1)}, u32[]{:S(2)}, u32[]{:S(2)}) collective-permute-start(bf16[4,144,512]{2,1,0:T(8,128)(2,1)S(1)} %bitcast.36), channel_id=1, source_target_pairs={{432,0},{384,16},{400,32},{416,48},{496,64},{448,80},{464,96},{480... | collective-permute-start | bytes 1769480 | tf_op jit(solution)/shard_map/ppermute | solution.py:53
  153.7 1.9 collective-permute-start.17
  155.7 3.1 %collective-permute-start.21 = (bf16[2,144,512]{2,1,0:T(8,128)(2,1)S(1)}, bf16[2,144,512]{2,1,0:T(8,128)(2,1)S(1)}, u32[]{:S(2)}, u32[]{:S(2)}) collective-permute-start(bf16[2,144,512]{2,1,0:T(8,128)(2,1)S(1)} %bitcast.48), channel_id=1, source_target_pairs={{304,0},{256,16},{272,32},{288,48},{368,64},{320,80},{336,96},{352... | collective-permute-start | bytes 884744 | tf_op jit(solution)/shard_map/ppermute | solution.py:53
  158.8 4.3 %collective-permute-start.20 = (bf16[2,144,512]{2,1,0:T(8,128)(2,1)S(1)}, bf16[2,144,512]{2,1,0:T(8,128)(2,1)S(1)}, u32[]{:S(2)}, u32[]{:S(2)}) collective-permute-start(bf16[2,144,512]{2,1,0:T(8,128)(2,1)S(1)} %bitcast.47), channel_id=1, source_target_pairs={{256,0},{272,16},{288,32},{304,48},{320,64},{336,80},{352,96},{368... | collective-permute-start | bytes 884744 | tf_op jit(solution)/shard_map/ppermute | solution.py:53
  163.1 16.4 %collective-permute-done.21 = bf16[2,144,512]{2,1,0:T(8,128)(2,1)S(1)} collective-permute-done((bf16[2,144,512]{2,1,0:T(8,128)(2,1)S(1)}, bf16[2,144,512]{2,1,0:T(8,128)(2,1)S(1)}, u32[]{:S(2)}, u32[]{:S(2)}) %collective-permute-start.21) | collective-permute-done | bytes 294944 | tf_op jit(solution)/shard_map/ppermute | solution.py:53
  179.5 3.5 %collective-permute-done.20 = bf16[2,144,512]{2,1,0:T(8,128)(2,1)S(1)} collective-permute-done((bf16[2,144,512]{2,1,0:T(8,128)(2,1)S(1)}, bf16[2,144,512]{2,1,0:T(8,128)(2,1)S(1)}, u32[]{:S(2)}, u32[]{:S(2)}) %collective-permute-start.20) | collective-permute-done | bytes 294944 | tf_op jit(solution)/shard_map/ppermute | solution.py:53
  182.9 0.1 pad_maximum_fusion.refs_4_
  183.0 0.0 collective-permute-done.18.refs_3_
  183.0 0.0 all-gather.4.cloned.1.call-done
  183.1 2.7 %collective-permute-start.22 = (bf16[4,144,512]{2,1,0:T(8,128)(2,1)S(1)}, bf16[4,144,512]{2,1,0:T(8,128)(2,1)S(1)}, u32[]{:S(2)}, u32[]{:S(2)}) collective-permute-start(bf16[4,144,512]{2,1,0:T(8,128)(2,1)S(1)} %collective-permute-done.17.refs_2_), channel_id=1, source_target_pairs={{64,0},{0,64},{192,128},{128,192},{320,256},{256,320},{448,384},{3... | collective-permute-start | bytes 1769480 | tf_op jit(solution)/shard_map/ppermute | solution.py:35
  185.8 1.9 collective-permute-start.23
  187.7 2.4 %collective-permute-start.24 = (bf16[4,144,512]{2,1,0:T(8,128)(2,1)S(1)}, bf16[4,144,512]{2,1,0:T(8,128)(2,1)}, u32[]{:S(2)}, u32[]{:S(2)}) collective-permute-start(bf16[4,144,512]{2,1,0:T(8,128)(2,1)S(1)} %pad_maximum_fusion.refs_4_), channel_id=1, source_target_pairs={{64,0},{0,64},{192,128},{128,192},{320,256},{256,320},{448,384},{3... | collective-permute-start | bytes 1769480 | tf_op jit(solution)/shard_map/ppermute | solution.py:35
  190.2 0.1 stack.59.meta_ref
  190.3 1.6 collective-permute-done.24.refs_7_
  191.9 7.7 %weight_grad.1 = (bf16[3,256,512]{2,1,0:T(8,128)(2,1)}, f32[1,512]{1,0:T(1,128)}) custom-call(s32[8]{0:T(128)S(1)} %stack.59.meta_ref, bf16[16,3,256,256]{3,2,1,0:T(8,128)(2,1)} %bitcast.49, bf16[4,144,512]{2,1,0:T(8,128)(2,1)S(1)} %bitcast.38, bf16[4,144,512]{2,1,0:T(8,128)(2,1)S(1)} %collective-permute-done.19.refs_1_, ...), custom_call_target="tpu_custom_call" | custom-call | flops 3221225472 | bytes 10485760 | tf_op jit(solution)/shard_map/weight_grad/pallas_call | solution.py:324
  (23 shorter events, 0.1 us)
Async XLA Ops:
  7.2 11.0 %collective-permute-start = (bf16[3,64,1024]{2,1,0:T(8,128)(2,1)}, bf16[3,64,1024]{2,1,0:T(8,128)(2,1)S(1)}, u32[]{:S(2)}, u32[]{:S(2)}) collective-permute-start(bf16[3,64,1024]{2,1,0:T(8,128)(2,1)} %bitcast.39), channel_id=1, source_target_pairs={{4,0},{5,1},{6,2},{7,3},{8,4},{9,5},{10,6},{11,7},{12,8},{13,9},{1... | collective-permute-start | bytes 1179656 | tf_op jit(solution)/shard_map/ppermute | solution.py:31
  12.6 14.5 %collective-permute-start.4 = (bf16[3,64,1024]{2,1,0:T(8,128)(2,1)}, bf16[3,64,1024]{2,1,0:T(8,128)(2,1)S(1)}, u32[]{:S(2)}, u32[]{:S(2)}) collective-permute-start(bf16[3,64,1024]{2,1,0:T(8,128)(2,1)} %bitcast.40), channel_id=1, source_target_pairs={{12,0},{13,1},{14,2},{15,3},{0,4},{1,5},{2,6},{3,7},{4,8},{5,9},{6... | collective-permute-start | bytes 1179656 | tf_op jit(solution)/shard_map/ppermute | solution.py:31
  14.6 12.5 %collective-permute-start.3 = (bf16[3,64,1024]{2,1,0:T(8,128)(2,1)}, bf16[3,64,1024]{2,1,0:T(8,128)(2,1)S(1)}, u32[]{:S(2)}, u32[]{:S(2)}) collective-permute-start(bf16[3,64,1024]{2,1,0:T(8,128)(2,1)} %bitcast.41), channel_id=1, source_target_pairs={{8,0},{9,1},{10,2},{11,3},{12,4},{13,5},{14,6},{15,7},{0,8},{1,9},... | collective-permute-start | bytes 1179656 | tf_op jit(solution)/shard_map/ppermute | solution.py:31
  18.1 1.0 copy-start.2
  20.1 47.7 %copy-start = (bf16[1024,3,512]{2,0,1:T(8,128)(2,1)S(1)}, bf16[1024,3,512]{2,0,1:T(8,128)(2,1)}, u32[]{:S(2)}) copy-start(bf16[1024,3,512]{2,0,1:T(8,128)(2,1)} %param.5) | copy-start | bytes 9437188
  20.1 17.8 %collective-permute-start.1 = (bf16[2,3,64,1024]{3,2,1,0:T(8,128)(2,1)}, bf16[2,3,64,1024]{3,2,1,0:T(8,128)(2,1)}, u32[]{:S(2)}, u32[]{:S(2)}) collective-permute-start(bf16[2,3,64,1024]{3,2,1,0:T(8,128)(2,1)} %pair.2.refs_0_), channel_id=1, source_target_pairs={{1,0},{2,1},{3,2},{0,3},{5,4},{6,5},{7,6},{4,7},{9,8},{10,9},{11,1... | collective-permute-start | bytes 2359304 | tf_op jit(solution)/shard_map/ppermute | solution.py:31
  28.0 14.6 %collective-permute-start.5 = (bf16[2,3,64,1024]{3,2,1,0:T(8,128)(2,1)}, bf16[2,3,64,1024]{3,2,1,0:T(8,128)(2,1)}, u32[]{:S(2)}, u32[]{:S(2)}) collective-permute-start(bf16[2,3,64,1024]{3,2,1,0:T(8,128)(2,1)} %pair.3.refs_1_), channel_id=1, source_target_pairs={{3,0},{0,1},{1,2},{2,3},{7,4},{4,5},{5,6},{6,7},{11,8},{8,9},{9,10... | collective-permute-start | bytes 2359304 | tf_op jit(solution)/shard_map/ppermute | solution.py:31
  31.0 30.2 %collective-permute-start.8 = (bf16[2,3,64,1024]{3,2,1,0:T(8,128)(2,1)}, bf16[2,3,64,1024]{3,2,1,0:T(8,128)(2,1)}, u32[]{:S(2)}, u32[]{:S(2)}) collective-permute-start(bf16[2,3,64,1024]{3,2,1,0:T(8,128)(2,1)} %pair.2.refs_0_), channel_id=1, source_target_pairs={{3,0},{0,1},{1,2},{2,3},{7,4},{4,5},{5,6},{6,7},{11,8},{8,9},{9,10... | collective-permute-start | bytes 2359304 | tf_op jit(solution)/shard_map/ppermute | solution.py:31
  34.1 27.1 %collective-permute-start.7 = (bf16[2,3,64,1024]{3,2,1,0:T(8,128)(2,1)}, bf16[2,3,64,1024]{3,2,1,0:T(8,128)(2,1)}, u32[]{:S(2)}, u32[]{:S(2)}) collective-permute-start(bf16[2,3,64,1024]{3,2,1,0:T(8,128)(2,1)} %pair.3.refs_1_), channel_id=1, source_target_pairs={{1,0},{2,1},{3,2},{0,3},{5,4},{6,5},{7,6},{4,7},{9,8},{10,9},{11,1... | collective-permute-start | bytes 2359304 | tf_op jit(solution)/shard_map/ppermute | solution.py:31
  37.9 29.9 %collective-permute-start.2 = (bf16[2,3,64,1024]{3,2,1,0:T(8,128)(2,1)}, bf16[2,3,64,1024]{3,2,1,0:T(8,128)(2,1)}, u32[]{:S(2)}, u32[]{:S(2)}) collective-permute-start(bf16[2,3,64,1024]{3,2,1,0:T(8,128)(2,1)} %collective-permute-done.1.refs_2_), channel_id=1, source_target_pairs={{1,0},{2,1},{3,2},{0,3},{5,4},{6,5},{7,6},{4,7},{9,8},{10,9},{11,1... | collective-permute-start | bytes 2359304 | tf_op jit(solution)/shard_map/ppermute | solution.py:31
  42.6 25.2 %collective-permute-start.6 = (bf16[2,3,64,1024]{3,2,1,0:T(8,128)(2,1)}, bf16[2,3,64,1024]{3,2,1,0:T(8,128)(2,1)}, u32[]{:S(2)}, u32[]{:S(2)}) collective-permute-start(bf16[2,3,64,1024]{3,2,1,0:T(8,128)(2,1)} %collective-permute-done.5.refs_5_), channel_id=1, source_target_pairs={{3,0},{0,1},{1,2},{2,3},{7,4},{4,5},{5,6},{6,7},{11,8},{8,9},{9,10... | collective-permute-start | bytes 2359304 | tf_op jit(solution)/shard_map/ppermute | solution.py:31
  46.3 36.1 %all-to-all-start = ((bf16[4,3,64,256]{3,2,1,0:T(8,128)(2,1)}), bf16[4,3,64,256]{3,2,1,0:T(8,128)(2,1)S(1)}, u32[]{:S(2)}, u32[]{:S(2)}) async-start(bf16[4,3,64,256]{3,2,1,0:T(8,128)(2,1)} %bitcast.46), calls=%async_computation | async-start | bytes 786432 | tf_op jit(solution)/shard_map/all_to_all | solution.py:393
  61.1 122.0 %all-gather.4.cloned.1.call-start = ((), (), s32[]{:S(2)}) async-start(), calls=%async_computation.1 | async-start | bytes 6684672 | tf_op jit(solution)/shard_map/all_gather | solution.py:439
  61.2 53.3 %copy-start.5 = (f32[512]{0:T(512)S(1)}, f32[512]{0:T(512)}, u32[]{:S(2)}) copy-start(f32[512]{0:T(512)} %param.6) | copy-start | bytes 6148
  61.2 53.3 %copy-start.6 = (s32[4]{0:T(128)S(1)}, s32[4]{0:T(128)}, u32[]{:S(2)}) copy-start(s32[4]{0:T(128)} %lengths_ref.1) | copy-start | bytes 52
  67.8 1.1 copy-start.1
  73.6 0.8 copy-start.3
  74.5 6.8 %collective-permute-start.9 = (bf16[4,144,512]{2,1,0:T(8,128)(2,1)}, bf16[4,144,512]{2,1,0:T(8,128)(2,1)S(1)}, u32[]{:S(2)}, u32[]{:S(2)}) collective-permute-start(bf16[4,144,512]{2,1,0:T(8,128)(2,1)} %get-tuple-element.28), channel_id=1, source_target_pairs={{64,0},{0,64},{192,128},{128,192},{320,256},{256,320},{448,384},{3... | collective-permute-start | bytes 1769480 | tf_op jit(solution)/shard_map/ppermute | solution.py:35
  81.2 1.1 copy-start.4
  84.1 12.7 %collective-permute-start.16 = (bf16[16,512]{1,0:T(8,128)(2,1)S(1)}, bf16[16,512]{1,0:T(8,128)(2,1)S(1)}, u32[]{:S(2)}, u32[]{:S(2)}) collective-permute-start(bf16[16,512]{1,0:T(8,128)(2,1)S(1)} %get-tuple-element.46), channel_id=1, source_target_pairs={{2,1},{4,65},{6,129},{8,193},{10,257},{12,321},{14,385},{66,3},{68... | collective-permute-start | bytes 49160 | tf_op jit(solution)/shard_map/ppermute | solution.py:386
  84.7 17.3 %collective-permute-start.15 = (bf16[16,512]{1,0:T(8,128)(2,1)S(1)}, bf16[16,512]{1,0:T(8,128)(2,1)S(1)}, u32[]{:S(2)}, u32[]{:S(2)}) collective-permute-start(bf16[16,512]{1,0:T(8,128)(2,1)S(1)} %get-tuple-element.47), channel_id=1, source_target_pairs={{2,0},{4,64},{6,128},{8,192},{10,256},{12,320},{14,384},{66,2},{68... | collective-permute-start | bytes 49160 | tf_op jit(solution)/shard_map/ppermute | solution.py:385
  86.0 28.4 %collective-permute-start.10 = (bf16[144,512]{1,0:T(8,128)(2,1)S(1)}, bf16[144,512]{1,0:T(8,128)(2,1)S(1)}, u32[]{:S(2)}, u32[]{:S(2)}) collective-permute-start(bf16[144,512]{1,0:T(8,128)(2,1)S(1)} %get-tuple-element.32), channel_id=1, source_target_pairs={{128,0},{192,64},{256,128},{320,192},{384,256},{448,320},{0,384},{... | collective-permute-start | bytes 442376 | tf_op jit(solution)/shard_map/ppermute | solution.py:40
  89.0 25.5 %collective-permute-start.11 = (bf16[144,512]{1,0:T(8,128)(2,1)S(1)}, bf16[144,512]{1,0:T(8,128)(2,1)S(1)}, u32[]{:S(2)}, u32[]{:S(2)}) collective-permute-start(bf16[144,512]{1,0:T(8,128)(2,1)S(1)} %get-tuple-element.33), channel_id=1, source_target_pairs={{256,0},{320,64},{384,128},{448,192},{0,256},{64,320},{128,384},{1... | collective-permute-start | bytes 442376 | tf_op jit(solution)/shard_map/ppermute | solution.py:40
  94.2 20.3 %collective-permute-start.12 = (bf16[144,512]{1,0:T(8,128)(2,1)S(1)}, bf16[144,512]{1,0:T(8,128)(2,1)S(1)}, u32[]{:S(2)}, u32[]{:S(2)}) collective-permute-start(bf16[144,512]{1,0:T(8,128)(2,1)S(1)} %get-tuple-element.34), channel_id=1, source_target_pairs={{384,0},{448,64},{0,128},{64,192},{128,256},{192,320},{256,384},{3... | collective-permute-start | bytes 442376 | tf_op jit(solution)/shard_map/ppermute | solution.py:40
  96.8 14.5 %collective-permute-start.14 = (bf16[64,512]{1,0:T(8,128)(2,1)S(1)}, bf16[64,512]{1,0:T(8,128)(2,1)S(1)}, u32[]{:S(2)}, u32[]{:S(2)}) collective-permute-start(bf16[64,512]{1,0:T(8,128)(2,1)S(1)} %get-tuple-element.48), channel_id=1, source_target_pairs={{0,1},{1,0},{2,65},{3,64},{4,129},{5,128},{6,193},{7,192},{8,257},... | collective-permute-start | bytes 196616 | tf_op jit(solution)/shard_map/ppermute | solution.py:384
  102.0 12.4 %collective-permute-start.13 = (bf16[64,512]{1,0:T(8,128)(2,1)S(1)}, bf16[64,512]{1,0:T(8,128)(2,1)S(1)}, u32[]{:S(2)}, u32[]{:S(2)}) collective-permute-start(bf16[64,512]{1,0:T(8,128)(2,1)S(1)} %get-tuple-element.49), channel_id=1, source_target_pairs={{0,0},{1,1},{2,64},{3,65},{4,128},{5,129},{6,192},{7,193},{8,256},... | collective-permute-start | bytes 196616 | tf_op jit(solution)/shard_map/ppermute | solution.py:383
  142.2 40.8 %collective-permute-start.19 = (bf16[4,144,512]{2,1,0:T(8,128)(2,1)S(1)}, bf16[4,144,512]{2,1,0:T(8,128)(2,1)S(1)}, u32[]{:S(2)}, u32[]{:S(2)}) collective-permute-start(bf16[4,144,512]{2,1,0:T(8,128)(2,1)S(1)} %bitcast.35), channel_id=1, source_target_pairs={{64,0},{0,64},{192,128},{128,192},{320,256},{256,320},{448,384},{3... | collective-permute-start | bytes 1769480 | tf_op jit(solution)/shard_map/ppermute | solution.py:35
  144.1 38.9 %collective-permute-start.18 = (bf16[4,144,512]{2,1,0:T(8,128)(2,1)S(1)}, bf16[4,144,512]{2,1,0:T(8,128)(2,1)S(1)}, u32[]{:S(2)}, u32[]{:S(2)}) collective-permute-start(bf16[4,144,512]{2,1,0:T(8,128)(2,1)S(1)} %bitcast.36), channel_id=1, source_target_pairs={{432,0},{384,16},{400,32},{416,48},{496,64},{448,80},{464,96},{480... | collective-permute-start | bytes 1769480 | tf_op jit(solution)/shard_map/ppermute | solution.py:53
  153.7 29.3 %collective-permute-start.17 = (bf16[4,144,512]{2,1,0:T(8,128)(2,1)S(1)}, bf16[4,144,512]{2,1,0:T(8,128)(2,1)S(1)}, u32[]{:S(2)}, u32[]{:S(2)}) collective-permute-start(bf16[4,144,512]{2,1,0:T(8,128)(2,1)S(1)} %bitcast.37), channel_id=1, source_target_pairs={{128,0},{144,16},{160,32},{176,48},{192,64},{208,80},{224,96},{240... | collective-permute-start | bytes 1769480 | tf_op jit(solution)/shard_map/ppermute | solution.py:53
  155.7 23.8 %collective-permute-start.21 = (bf16[2,144,512]{2,1,0:T(8,128)(2,1)S(1)}, bf16[2,144,512]{2,1,0:T(8,128)(2,1)S(1)}, u32[]{:S(2)}, u32[]{:S(2)}) collective-permute-start(bf16[2,144,512]{2,1,0:T(8,128)(2,1)S(1)} %bitcast.48), channel_id=1, source_target_pairs={{304,0},{256,16},{272,32},{288,48},{368,64},{320,80},{336,96},{352... | collective-permute-start | bytes 884744 | tf_op jit(solution)/shard_map/ppermute | solution.py:53
  158.8 24.1 %collective-permute-start.20 = (bf16[2,144,512]{2,1,0:T(8,128)(2,1)S(1)}, bf16[2,144,512]{2,1,0:T(8,128)(2,1)S(1)}, u32[]{:S(2)}, u32[]{:S(2)}) collective-permute-start(bf16[2,144,512]{2,1,0:T(8,128)(2,1)S(1)} %bitcast.47), channel_id=1, source_target_pairs={{256,0},{272,16},{288,32},{304,48},{320,64},{336,80},{352,96},{368... | collective-permute-start | bytes 884744 | tf_op jit(solution)/shard_map/ppermute | solution.py:53
  183.1 7.2 %collective-permute-start.22 = (bf16[4,144,512]{2,1,0:T(8,128)(2,1)S(1)}, bf16[4,144,512]{2,1,0:T(8,128)(2,1)S(1)}, u32[]{:S(2)}, u32[]{:S(2)}) collective-permute-start(bf16[4,144,512]{2,1,0:T(8,128)(2,1)S(1)} %collective-permute-done.17.refs_2_), channel_id=1, source_target_pairs={{64,0},{0,64},{192,128},{128,192},{320,256},{256,320},{448,384},{3... | collective-permute-start | bytes 1769480 | tf_op jit(solution)/shard_map/ppermute | solution.py:35
  185.8 4.5 %collective-permute-start.23 = (bf16[4,144,512]{2,1,0:T(8,128)(2,1)S(1)}, bf16[4,144,512]{2,1,0:T(8,128)(2,1)}, u32[]{:S(2)}, u32[]{:S(2)}) collective-permute-start(bf16[4,144,512]{2,1,0:T(8,128)(2,1)S(1)} %collective-permute-done.18.refs_3_), channel_id=1, source_target_pairs={{64,0},{0,64},{192,128},{128,192},{320,256},{256,320},{448,384},{3... | collective-permute-start | bytes 1769480 | tf_op jit(solution)/shard_map/ppermute | solution.py:35
  187.7 4.2 %collective-permute-start.24 = (bf16[4,144,512]{2,1,0:T(8,128)(2,1)S(1)}, bf16[4,144,512]{2,1,0:T(8,128)(2,1)}, u32[]{:S(2)}, u32[]{:S(2)}) collective-permute-start(bf16[4,144,512]{2,1,0:T(8,128)(2,1)S(1)} %pad_maximum_fusion.refs_4_), channel_id=1, source_target_pairs={{64,0},{0,64},{192,128},{128,192},{320,256},{256,320},{448,384},{3... | collective-permute-start | bytes 1769480 | tf_op jit(solution)/shard_map/ppermute | solution.py:35
Sparse Core Ops, SparseCore 0:
  84.2 80.7 all-gather.3

commit v17 on v16

--- a/solution.py
+++ b/solution.py
@@ -434,10 +434,11 @@
     far_low, far_high, near = lax.optimization_barrier((far_low, far_high, near))
     keep, send = project_place([far_low, far_high], weight, near, core, x, y)
     mine, *away = join(keep, from_other_core(send), zl)
-    top, mine, traded = lax.optimization_barrier((own[LEVELS - 1], mine, traded))
+    top, mine = lax.optimization_barrier((own[LEVELS - 1], mine))
     halves = send_high(top, draft_index)
+    parts = [mine] + [from_zl(block, step) for step, block in zip((1, 2, 3), away)]
+    parts[1], traded = lax.optimization_barrier((parts[1], traded))
     every = lax.all_gather(turn(traded), "draft", axis=0, tiled=False)
-    parts = [mine] + [from_zl(block, step) for step, block in zip((1, 2, 3), away)]
     odd = draft_index % 2
     grad = chain(parts, halves, mix_gain, tp_index * piece, zh, odd, lengths)
     fc_grad, mix_total = gather_grads(grad, every, zl, core)

time: 210 us -> 217 us (1.033)
  the two profiles are of different devices: /device:TPU:1 before, /device:TPU:31 now
where the time goes in v17:
time: 217 us; the launch traced here: 216 us
  starting transfers between devices  99.1 us (46%)
  waiting for transfers between devices  41.1 us (19%)
  blocking collectives  30 us (14%)
  Pallas kernels  23.9 us (11%)
  between operations  14.5 us (7%)
  local copies, waits for them, and re-layouts  6.87 us (3%)
    all_gather x1, blocking collectives, gather_grads(): stack = lax.all_gather(grad, 'dp', axis=0, tiled=False)  30 us
    ppermute x9, starting transfers between devices, plane_move(): return lambda block: lax.ppermute(block, ('tp', 'draft'), pairs)  23.4 us
    ppermute x4, waiting for transfers between devices, from_z(): return lax.ppermute(block, ('tp', 'dp'), pairs)  19.9 us
    ppermute x4, starting transfers between devices, from_z(): return lax.ppermute(block, ('tp', 'dp'), pairs)  16.7 us
    ppermute x5, starting transfers between devices, from_other_core(): return lax.ppermute(block, 'tp', [(t ^ 1, t) for t in range(ZL * CORES)])  15.8 us
    all_to_all x1, starting transfers between devices, trade_columns(): lax.all_to_all(quarters, 'dp', split_axis=0, concat_axis=0, tiled=True)  14.8 us
    ppermute x1, starting transfers between devices, send_high(): lax.ppermute(jnp.where(even, right, left), axes, crossed)  13.3 us
    ppermute x3, starting transfers between devices, from_zl(): return lax.ppermute(block, 'tp', pairs)  10.5 us
  transfers between devices with their start and end apart: 27, of which 11 were waited for; matrix products, arithmetic and copies ran while one was open for 1% of the time, Pallas kernels for 7%

profile of v17, /device:TPU:31, one launch (start us, length us, event | category | flops | bytes accessed | tf_op | source)
XLA Modules:
  0.0 215.8 jit_solution(18400060028997799212)
XLA Ops:
  7.2 2.4 %collective-permute-start = (bf16[3,64,1024]{2,1,0:T(8,128)(2,1)}, bf16[3,64,1024]{2,1,0:T(8,128)(2,1)S(1)}, u32[]{:S(2)}, u32[]{:S(2)}) collective-permute-start(bf16[3,64,1024]{2,1,0:T(8,128)(2,1)} %bitcast.39), channel_id=1, source_target_pairs={{4,0},{5,1},{6,2},{7,3},{8,4},{9,5},{10,6},{11,7},{12,8},{13,9},{1... | collective-permute-start | bytes 1179656 | tf_op jit(solution)/shard_map/ppermute | solution.py:31
  9.5 4.1 %collective-permute-start.4 = (bf16[3,64,1024]{2,1,0:T(8,128)(2,1)}, bf16[3,64,1024]{2,1,0:T(8,128)(2,1)S(1)}, u32[]{:S(2)}, u32[]{:S(2)}) collective-permute-start(bf16[3,64,1024]{2,1,0:T(8,128)(2,1)} %bitcast.40), channel_id=1, source_target_pairs={{12,0},{13,1},{14,2},{15,3},{0,4},{1,5},{2,6},{3,7},{4,8},{5,9},{6... | collective-permute-start | bytes 1179656 | tf_op jit(solution)/shard_map/ppermute | solution.py:31
  13.7 1.9 collective-permute-start.3
  15.6 1.8 collective-permute-done.second_ref
  17.4 1.0 copy-done.2
  18.4 0.9 pair.2.refs_0_
  19.3 2.4 %collective-permute-start.1 = (bf16[2,3,64,1024]{3,2,1,0:T(8,128)(2,1)}, bf16[2,3,64,1024]{3,2,1,0:T(8,128)(2,1)}, u32[]{:S(2)}, u32[]{:S(2)}) collective-permute-start(bf16[2,3,64,1024]{3,2,1,0:T(8,128)(2,1)} %pair.2.refs_0_), channel_id=1, source_target_pairs={{1,0},{2,1},{3,2},{0,3},{5,4},{6,5},{7,6},{4,7},{9,8},{10,9},{11,1... | collective-permute-start | bytes 2359304 | tf_op jit(solution)/shard_map/ppermute | solution.py:31
  21.8 1.2 collective-permute-done.4.second_ref
  22.9 1.3 collective-permute-done.3.first_ref
  24.2 0.9 pair.3.refs_1_
  25.1 2.1 collective-permute-start.5
  27.2 2.8 %collective-permute-start.8 = (bf16[2,3,64,1024]{3,2,1,0:T(8,128)(2,1)}, bf16[2,3,64,1024]{3,2,1,0:T(8,128)(2,1)}, u32[]{:S(2)}, u32[]{:S(2)}) collective-permute-start(bf16[2,3,64,1024]{3,2,1,0:T(8,128)(2,1)} %pair.2.refs_0_), channel_id=1, source_target_pairs={{3,0},{0,1},{1,2},{2,3},{7,4},{4,5},{5,6},{6,7},{11,8},{8,9},{9,10... | collective-permute-start | bytes 2359304 | tf_op jit(solution)/shard_map/ppermute | solution.py:31
  30.1 2.5 %collective-permute-start.7 = (bf16[2,3,64,1024]{3,2,1,0:T(8,128)(2,1)}, bf16[2,3,64,1024]{3,2,1,0:T(8,128)(2,1)}, u32[]{:S(2)}, u32[]{:S(2)}) collective-permute-start(bf16[2,3,64,1024]{3,2,1,0:T(8,128)(2,1)} %pair.3.refs_1_), channel_id=1, source_target_pairs={{1,0},{2,1},{3,2},{0,3},{5,4},{6,5},{7,6},{4,7},{9,8},{10,9},{11,1... | collective-permute-start | bytes 2359304 | tf_op jit(solution)/shard_map/ppermute | solution.py:31
  32.5 2.7 %collective-permute-done.1.refs_2_ = bf16[2,3,64,1024]{3,2,1,0:T(8,128)(2,1)} collective-permute-done((bf16[2,3,64,1024]{3,2,1,0:T(8,128)(2,1)}, bf16[2,3,64,1024]{3,2,1,0:T(8,128)(2,1)}, u32[]{:S(2)}, u32[]{:S(2)}) %collective-permute-start.1) | collective-permute-done | bytes 786464 | tf_op jit(solution)/shard_map/ppermute | solution.py:31
  35.2 1.9 collective-permute-start.2
  37.1 1.3 collective-permute-done.5.refs_5_
  38.5 3.2 %collective-permute-start.6 = (bf16[2,3,64,1024]{3,2,1,0:T(8,128)(2,1)}, bf16[2,3,64,1024]{3,2,1,0:T(8,128)(2,1)}, u32[]{:S(2)}, u32[]{:S(2)}) collective-permute-start(bf16[2,3,64,1024]{3,2,1,0:T(8,128)(2,1)} %collective-permute-done.5.refs_5_), channel_id=1, source_target_pairs={{3,0},{0,1},{1,2},{2,3},{7,4},{4,5},{5,6},{6,7},{11,8},{8,9},{9,10... | collective-permute-start | bytes 2359304 | tf_op jit(solution)/shard_map/ppermute | solution.py:31
  41.7 1.8 copy.10
  43.5 14.8 %all-to-all-start = ((bf16[4,3,64,256]{3,2,1,0:T(8,128)(2,1)}), bf16[4,3,64,256]{3,2,1,0:T(8,128)(2,1)S(1)}, u32[]{:S(2)}, u32[]{:S(2)}) async-start(bf16[4,3,64,256]{3,2,1,0:T(8,128)(2,1)} %bitcast.46), calls=%async_computation | async-start | bytes 786432 | tf_op jit(solution)/shard_map/all_to_all | solution.py:393
  58.3 0.1 pad_add_fusion.1.meta_ref
  58.4 0.0 collective-permute-done.8.refs_4_
  58.4 0.0 collective-permute-done.7.refs_3_
  58.4 0.0 copy-start.6
  58.4 6.6 %project.1.refs_3_ = bf16[12,64,512]{2,1,0:T(8,128)(2,1)} custom-call(bf16[2,3,64,1024]{3,2,1,0:T(8,128)(2,1)} %pair.2.refs_0_, bf16[2,3,64,1024]{3,2,1,0:T(8,128)(2,1)} %pair.3.refs_1_, bf16[2,3,64,1024]{3,2,1,0:T(8,128)(2,1)} %collective-permute-done.1.refs_2_, bf16[2,3,64,1024]{3,2,1,0:T(8,128)(2,1)} %collective-permute-done.7.refs_3_, ...), custom_call_target="tpu_custom_call" | custom-call | bytes 4718592 | tf_op jit(solution)/shard_map/project/pallas_call | solution.py:114
  65.0 0.0 collective-permute-done.2.refs_0_
  65.0 0.0 collective-permute-done.6.refs_1_
  65.1 1.1 copy-done.1
  66.2 4.7 %project_place.1 = (bf16[4,144,512]{2,1,0:T(8,128)(2,1)S(1)}, bf16[4,144,512]{2,1,0:T(8,128)(2,1)}) custom-call(s32[3]{0:T(128)S(1)} %pad_add_fusion.1.meta_ref, bf16[2,3,64,1024]{3,2,1,0:T(8,128)(2,1)} %collective-permute-done.2.refs_0_, bf16[2,3,64,1024]{3,2,1,0:T(8,128)(2,1)} %collective-permute-done.6.refs_1_, bf16[3,1024,512]{2,1,0:T(8,128)(2,1)S(1)} %bitcast.34, ...), custom_call_target="tpu_custom_call" | custom-call | bytes 1572864 | tf_op jit(solution)/shard_map/project_place/pallas_call | solution.py:165
  70.9 0.8 copy-done.3
  71.7 6.8 %collective-permute-start.9 = (bf16[4,144,512]{2,1,0:T(8,128)(2,1)}, bf16[4,144,512]{2,1,0:T(8,128)(2,1)S(1)}, u32[]{:S(2)}, u32[]{:S(2)}) collective-permute-start(bf16[4,144,512]{2,1,0:T(8,128)(2,1)} %get-tuple-element.29), channel_id=1, source_target_pairs={{64,0},{0,64},{192,128},{128,192},{320,256},{256,320},{448,384},{3... | collective-permute-start | bytes 1769480 | tf_op jit(solution)/shard_map/ppermute | solution.py:35
  78.5 1.8 collective-permute-done.9.got_ref
  80.3 1.1 copy-done.4
  81.4 0.1 join.1
  81.5 3.6 %collective-permute-start.10 = (bf16[144,512]{1,0:T(8,128)(2,1)S(1)}, bf16[144,512]{1,0:T(8,128)(2,1)S(1)}, u32[]{:S(2)}, u32[]{:S(2)}) collective-permute-start(bf16[144,512]{1,0:T(8,128)(2,1)S(1)} %get-tuple-element.32), channel_id=1, source_target_pairs={{128,0},{192,64},{256,128},{320,192},{384,256},{448,320},{0,384},{... | collective-permute-start | bytes 442376 | tf_op jit(solution)/shard_map/ppermute | solution.py:40
  85.1 0.0 all-to-all-done.traded_ref
  85.1 3.4 %collective-permute-done.10.refs_1_ = bf16[144,512]{1,0:T(8,128)(2,1)S(1)} collective-permute-done((bf16[144,512]{1,0:T(8,128)(2,1)S(1)}, bf16[144,512]{1,0:T(8,128)(2,1)S(1)}, u32[]{:S(2)}, u32[]{:S(2)}) %collective-permute-start.10) | collective-permute-done | bytes 147488 | tf_op jit(solution)/shard_map/ppermute | solution.py:40
  88.5 1.6 turn.1
  90.1 0.0 all-gather.4.cloned.1.call-update
  90.1 0.9 slice_bitcast_fusion
  91.0 1.3 collective-permute-start.16
  92.3 3.1 %collective-permute-start.11 = (bf16[144,512]{1,0:T(8,128)(2,1)S(1)}, bf16[144,512]{1,0:T(8,128)(2,1)S(1)}, u32[]{:S(2)}, u32[]{:S(2)}) collective-permute-start(bf16[144,512]{1,0:T(8,128)(2,1)S(1)} %get-tuple-element.35), channel_id=1, source_target_pairs={{256,0},{320,64},{384,128},{448,192},{0,256},{64,320},{128,384},{1... | collective-permute-start | bytes 442376 | tf_op jit(solution)/shard_map/ppermute | solution.py:40
  95.4 3.8 %collective-permute-start.12 = (bf16[144,512]{1,0:T(8,128)(2,1)S(1)}, bf16[144,512]{1,0:T(8,128)(2,1)S(1)}, u32[]{:S(2)}, u32[]{:S(2)}) collective-permute-start(bf16[144,512]{1,0:T(8,128)(2,1)S(1)} %get-tuple-element.36), channel_id=1, source_target_pairs={{384,0},{448,64},{0,128},{64,192},{128,256},{192,320},{256,384},{3... | collective-permute-start | bytes 442376 | tf_op jit(solution)/shard_map/ppermute | solution.py:40
  99.3 0.7 collective-permute-start.15
  100.0 13.3 %collective-permute-start.14 = (bf16[64,512]{1,0:T(8,128)(2,1)S(1)}, bf16[64,512]{1,0:T(8,128)(2,1)S(1)}, u32[]{:S(2)}, u32[]{:S(2)}) collective-permute-start(bf16[64,512]{1,0:T(8,128)(2,1)S(1)} %get-tuple-element.50), channel_id=1, source_target_pairs={{0,1},{1,0},{2,65},{3,64},{4,129},{5,128},{6,193},{7,192},{8,257},... | collective-permute-start | bytes 196616 | tf_op jit(solution)/shard_map/ppermute | solution.py:384
  113.3 2.7 %collective-permute-start.13 = (bf16[64,512]{1,0:T(8,128)(2,1)S(1)}, bf16[64,512]{1,0:T(8,128)(2,1)S(1)}, u32[]{:S(2)}, u32[]{:S(2)}) collective-permute-start(bf16[64,512]{1,0:T(8,128)(2,1)S(1)} %get-tuple-element.51), channel_id=1, source_target_pairs={{0,0},{1,1},{2,64},{3,65},{4,128},{5,129},{6,192},{7,193},{8,256},... | collective-permute-start | bytes 196616 | tf_op jit(solution)/shard_map/ppermute | solution.py:383
  116.0 0.1 pad_add_fusion.meta_ref
  116.1 6.2 %collective-permute-done.13.refs_4_ = bf16[64,512]{1,0:T(8,128)(2,1)S(1)} collective-permute-done((bf16[64,512]{1,0:T(8,128)(2,1)S(1)}, bf16[64,512]{1,0:T(8,128)(2,1)S(1)}, u32[]{:S(2)}, u32[]{:S(2)}) %collective-permute-start.13) | collective-permute-done | bytes 65568 | tf_op jit(solution)/shard_map/ppermute | solution.py:383
  122.3 1.4 chain.1
  123.7 30.0 %all-gather = bf16[576,512]{1,0:T(8,128)(2,1)S(1)} all-gather(bf16[144,512]{1,0:T(8,128)(2,1)S(1)} %chain.1), channel_id=2, replica_groups=mesh['tp'=8,'dp'=4,'draft'=16] {'dp'}, dimensions={0}, use_global_device_ids=true | all-gather | bytes 737280 | tf_op jit(solution)/shard_map/all_gather | solution.py:397
  153.7 1.9 collective-permute-start.19
  155.7 7.3 %collective-permute-start.18 = (bf16[4,144,512]{2,1,0:T(8,128)(2,1)S(1)}, bf16[4,144,512]{2,1,0:T(8,128)(2,1)S(1)}, u32[]{:S(2)}, u32[]{:S(2)}) collective-permute-start(bf16[4,144,512]{2,1,0:T(8,128)(2,1)S(1)} %bitcast.36), channel_id=1, source_target_pairs={{432,0},{384,16},{400,32},{416,48},{496,64},{448,80},{464,96},{480... | collective-permute-start | bytes 1769480 | tf_op jit(solution)/shard_map/ppermute | solution.py:53
  163.0 1.9 collective-permute-start.17
  165.0 3.1 %collective-permute-start.21 = (bf16[2,144,512]{2,1,0:T(8,128)(2,1)S(1)}, bf16[2,144,512]{2,1,0:T(8,128)(2,1)S(1)}, u32[]{:S(2)}, u32[]{:S(2)}) collective-permute-start(bf16[2,144,512]{2,1,0:T(8,128)(2,1)S(1)} %bitcast.48), channel_id=1, source_target_pairs={{304,0},{256,16},{272,32},{288,48},{368,64},{320,80},{336,96},{352... | collective-permute-start | bytes 884744 | tf_op jit(solution)/shard_map/ppermute | solution.py:53
  168.1 4.3 %collective-permute-start.20 = (bf16[2,144,512]{2,1,0:T(8,128)(2,1)S(1)}, bf16[2,144,512]{2,1,0:T(8,128)(2,1)S(1)}, u32[]{:S(2)}, u32[]{:S(2)}) collective-permute-start(bf16[2,144,512]{2,1,0:T(8,128)(2,1)S(1)} %bitcast.47), channel_id=1, source_target_pairs={{256,0},{272,16},{288,32},{304,48},{320,64},{336,80},{352,96},{368... | collective-permute-start | bytes 884744 | tf_op jit(solution)/shard_map/ppermute | solution.py:53
  172.4 16.0 %collective-permute-done.21 = bf16[2,144,512]{2,1,0:T(8,128)(2,1)S(1)} collective-permute-done((bf16[2,144,512]{2,1,0:T(8,128)(2,1)S(1)}, bf16[2,144,512]{2,1,0:T(8,128)(2,1)S(1)}, u32[]{:S(2)}, u32[]{:S(2)}) %collective-permute-start.21) | collective-permute-done | bytes 294944 | tf_op jit(solution)/shard_map/ppermute | solution.py:53
  188.4 3.8 %collective-permute-done.20 = bf16[2,144,512]{2,1,0:T(8,128)(2,1)S(1)} collective-permute-done((bf16[2,144,512]{2,1,0:T(8,128)(2,1)S(1)}, bf16[2,144,512]{2,1,0:T(8,128)(2,1)S(1)}, u32[]{:S(2)}, u32[]{:S(2)}) %collective-permute-start.20) | collective-permute-done | bytes 294944 | tf_op jit(solution)/shard_map/ppermute | solution.py:53
  192.3 0.1 pad_maximum_fusion.refs_4_
  192.4 0.0 all-gather.4.cloned.1.call-done
  192.4 2.8 %collective-permute-start.22 = (bf16[4,144,512]{2,1,0:T(8,128)(2,1)S(1)}, bf16[4,144,512]{2,1,0:T(8,128)(2,1)S(1)}, u32[]{:S(2)}, u32[]{:S(2)}) collective-permute-start(bf16[4,144,512]{2,1,0:T(8,128)(2,1)S(1)} %collective-permute-done.17.refs_2_), channel_id=1, source_target_pairs={{64,0},{0,64},{192,128},{128,192},{320,256},{256,320},{448,384},{3... | collective-permute-start | bytes 1769480 | tf_op jit(solution)/shard_map/ppermute | solution.py:35
  195.2 1.9 collective-permute-start.23
  197.1 2.4 %collective-permute-start.24 = (bf16[4,144,512]{2,1,0:T(8,128)(2,1)S(1)}, bf16[4,144,512]{2,1,0:T(8,128)(2,1)}, u32[]{:S(2)}, u32[]{:S(2)}) collective-permute-start(bf16[4,144,512]{2,1,0:T(8,128)(2,1)S(1)} %pad_maximum_fusion.refs_4_), channel_id=1, source_target_pairs={{64,0},{0,64},{192,128},{128,192},{320,256},{256,320},{448,384},{3... | collective-permute-start | bytes 1769480 | tf_op jit(solution)/shard_map/ppermute | solution.py:35
  199.6 0.1 stack.59.meta_ref
  199.7 1.6 collective-permute-done.24.refs_7_
  201.2 7.7 %weight_grad.1 = (bf16[3,256,512]{2,1,0:T(8,128)(2,1)}, f32[1,512]{1,0:T(1,128)}) custom-call(s32[8]{0:T(128)S(1)} %stack.59.meta_ref, bf16[16,3,256,256]{3,2,1,0:T(8,128)(2,1)} %bitcast.49, bf16[4,144,512]{2,1,0:T(8,128)(2,1)S(1)} %bitcast.38, bf16[4,144,512]{2,1,0:T(8,128)(2,1)S(1)} %collective-permute-done.19.refs_1_, ...), custom_call_target="tpu_custom_call" | custom-call | flops 3221225472 | bytes 10485760 | tf_op jit(solution)/shard_map/weight_grad/pallas_call | solution.py:324
  (23 shorter events, 0.1 us)
Async XLA Ops:
  7.2 10.2 %collective-permute-start = (bf16[3,64,1024]{2,1,0:T(8,128)(2,1)}, bf16[3,64,1024]{2,1,0:T(8,128)(2,1)S(1)}, u32[]{:S(2)}, u32[]{:S(2)}) collective-permute-start(bf16[3,64,1024]{2,1,0:T(8,128)(2,1)} %bitcast.39), channel_id=1, source_target_pairs={{4,0},{5,1},{6,2},{7,3},{8,4},{9,5},{10,6},{11,7},{12,8},{13,9},{1... | collective-permute-start | bytes 1179656 | tf_op jit(solution)/shard_map/ppermute | solution.py:31
  9.5 13.4 %collective-permute-start.4 = (bf16[3,64,1024]{2,1,0:T(8,128)(2,1)}, bf16[3,64,1024]{2,1,0:T(8,128)(2,1)S(1)}, u32[]{:S(2)}, u32[]{:S(2)}) collective-permute-start(bf16[3,64,1024]{2,1,0:T(8,128)(2,1)} %bitcast.40), channel_id=1, source_target_pairs={{12,0},{13,1},{14,2},{15,3},{0,4},{1,5},{2,6},{3,7},{4,8},{5,9},{6... | collective-permute-start | bytes 1179656 | tf_op jit(solution)/shard_map/ppermute | solution.py:31
  13.7 10.5 %collective-permute-start.3 = (bf16[3,64,1024]{2,1,0:T(8,128)(2,1)}, bf16[3,64,1024]{2,1,0:T(8,128)(2,1)S(1)}, u32[]{:S(2)}, u32[]{:S(2)}) collective-permute-start(bf16[3,64,1024]{2,1,0:T(8,128)(2,1)} %bitcast.41), channel_id=1, source_target_pairs={{8,0},{9,1},{10,2},{11,3},{12,4},{13,5},{14,6},{15,7},{0,8},{1,9},... | collective-permute-start | bytes 1179656 | tf_op jit(solution)/shard_map/ppermute | solution.py:31
  17.4 1.0 copy-start.2
  19.3 45.7 %copy-start = (bf16[1024,3,512]{2,0,1:T(8,128)(2,1)S(1)}, bf16[1024,3,512]{2,0,1:T(8,128)(2,1)}, u32[]{:S(2)}) copy-start(bf16[1024,3,512]{2,0,1:T(8,128)(2,1)} %param.5) | copy-start | bytes 9437188
  19.3 15.9 %collective-permute-start.1 = (bf16[2,3,64,1024]{3,2,1,0:T(8,128)(2,1)}, bf16[2,3,64,1024]{3,2,1,0:T(8,128)(2,1)}, u32[]{:S(2)}, u32[]{:S(2)}) collective-permute-start(bf16[2,3,64,1024]{3,2,1,0:T(8,128)(2,1)} %pair.2.refs_0_), channel_id=1, source_target_pairs={{1,0},{2,1},{3,2},{0,3},{5,4},{6,5},{7,6},{4,7},{9,8},{10,9},{11,1... | collective-permute-start | bytes 2359304 | tf_op jit(solution)/shard_map/ppermute | solution.py:31
  25.1 13.3 %collective-permute-start.5 = (bf16[2,3,64,1024]{3,2,1,0:T(8,128)(2,1)}, bf16[2,3,64,1024]{3,2,1,0:T(8,128)(2,1)}, u32[]{:S(2)}, u32[]{:S(2)}) collective-permute-start(bf16[2,3,64,1024]{3,2,1,0:T(8,128)(2,1)} %pair.3.refs_1_), channel_id=1, source_target_pairs={{3,0},{0,1},{1,2},{2,3},{7,4},{4,5},{5,6},{6,7},{11,8},{8,9},{9,10... | collective-permute-start | bytes 2359304 | tf_op jit(solution)/shard_map/ppermute | solution.py:31
  27.2 31.2 %collective-permute-start.8 = (bf16[2,3,64,1024]{3,2,1,0:T(8,128)(2,1)}, bf16[2,3,64,1024]{3,2,1,0:T(8,128)(2,1)}, u32[]{:S(2)}, u32[]{:S(2)}) collective-permute-start(bf16[2,3,64,1024]{3,2,1,0:T(8,128)(2,1)} %pair.2.refs_0_), channel_id=1, source_target_pairs={{3,0},{0,1},{1,2},{2,3},{7,4},{4,5},{5,6},{6,7},{11,8},{8,9},{9,10... | collective-permute-start | bytes 2359304 | tf_op jit(solution)/shard_map/ppermute | solution.py:31
  30.1 28.3 %collective-permute-start.7 = (bf16[2,3,64,1024]{3,2,1,0:T(8,128)(2,1)}, bf16[2,3,64,1024]{3,2,1,0:T(8,128)(2,1)}, u32[]{:S(2)}, u32[]{:S(2)}) collective-permute-start(bf16[2,3,64,1024]{3,2,1,0:T(8,128)(2,1)} %pair.3.refs_1_), channel_id=1, source_target_pairs={{1,0},{2,1},{3,2},{0,3},{5,4},{6,5},{7,6},{4,7},{9,8},{10,9},{11,1... | collective-permute-start | bytes 2359304 | tf_op jit(solution)/shard_map/ppermute | solution.py:31
  35.2 29.8 %collective-permute-start.2 = (bf16[2,3,64,1024]{3,2,1,0:T(8,128)(2,1)}, bf16[2,3,64,1024]{3,2,1,0:T(8,128)(2,1)}, u32[]{:S(2)}, u32[]{:S(2)}) collective-permute-start(bf16[2,3,64,1024]{3,2,1,0:T(8,128)(2,1)} %collective-permute-done.1.refs_2_), channel_id=1, source_target_pairs={{1,0},{2,1},{3,2},{0,3},{5,4},{6,5},{7,6},{4,7},{9,8},{10,9},{11,1... | collective-permute-start | bytes 2359304 | tf_op jit(solution)/shard_map/ppermute | solution.py:31
  38.5 26.6 %collective-permute-start.6 = (bf16[2,3,64,1024]{3,2,1,0:T(8,128)(2,1)}, bf16[2,3,64,1024]{3,2,1,0:T(8,128)(2,1)}, u32[]{:S(2)}, u32[]{:S(2)}) collective-permute-start(bf16[2,3,64,1024]{3,2,1,0:T(8,128)(2,1)} %collective-permute-done.5.refs_5_), channel_id=1, source_target_pairs={{3,0},{0,1},{1,2},{2,3},{7,4},{4,5},{5,6},{6,7},{11,8},{8,9},{9,10... | collective-permute-start | bytes 2359304 | tf_op jit(solution)/shard_map/ppermute | solution.py:31
  43.5 41.6 %all-to-all-start = ((bf16[4,3,64,256]{3,2,1,0:T(8,128)(2,1)}), bf16[4,3,64,256]{3,2,1,0:T(8,128)(2,1)S(1)}, u32[]{:S(2)}, u32[]{:S(2)}) async-start(bf16[4,3,64,256]{3,2,1,0:T(8,128)(2,1)} %bitcast.46), calls=%async_computation | async-start | bytes 786432 | tf_op jit(solution)/shard_map/all_to_all | solution.py:393
  58.3 134.1 %all-gather.4.cloned.1.call-start = ((), (), s32[]{:S(2)}) async-start(), calls=%async_computation.1 | async-start | bytes 6684672 | tf_op jit(solution)/shard_map/all_gather | solution.py:441
  58.4 63.9 %copy-start.5 = (f32[512]{0:T(512)S(1)}, f32[512]{0:T(512)}, u32[]{:S(2)}) copy-start(f32[512]{0:T(512)} %param.6) | copy-start | bytes 6148
  58.4 63.9 %copy-start.6 = (s32[4]{0:T(128)S(1)}, s32[4]{0:T(128)}, u32[]{:S(2)}) copy-start(s32[4]{0:T(128)} %lengths_ref.1) | copy-start | bytes 52
  65.1 1.1 copy-start.1
  70.9 0.8 copy-start.3
  71.7 8.6 %collective-permute-start.9 = (bf16[4,144,512]{2,1,0:T(8,128)(2,1)}, bf16[4,144,512]{2,1,0:T(8,128)(2,1)S(1)}, u32[]{:S(2)}, u32[]{:S(2)}) collective-permute-start(bf16[4,144,512]{2,1,0:T(8,128)(2,1)} %get-tuple-element.29), channel_id=1, source_target_pairs={{64,0},{0,64},{192,128},{128,192},{320,256},{256,320},{448,384},{3... | collective-permute-start | bytes 1769480 | tf_op jit(solution)/shard_map/ppermute | solution.py:35
  80.3 1.1 copy-start.4
  81.5 7.0 %collective-permute-start.10 = (bf16[144,512]{1,0:T(8,128)(2,1)S(1)}, bf16[144,512]{1,0:T(8,128)(2,1)S(1)}, u32[]{:S(2)}, u32[]{:S(2)}) collective-permute-start(bf16[144,512]{1,0:T(8,128)(2,1)S(1)} %get-tuple-element.32), channel_id=1, source_target_pairs={{128,0},{192,64},{256,128},{320,192},{384,256},{448,320},{0,384},{... | collective-permute-start | bytes 442376 | tf_op jit(solution)/shard_map/ppermute | solution.py:40
  91.0 22.3 %collective-permute-start.16 = (bf16[16,512]{1,0:T(8,128)(2,1)S(1)}, bf16[16,512]{1,0:T(8,128)(2,1)S(1)}, u32[]{:S(2)}, u32[]{:S(2)}) collective-permute-start(bf16[16,512]{1,0:T(8,128)(2,1)S(1)} %get-tuple-element.48), channel_id=1, source_target_pairs={{2,1},{4,65},{6,129},{8,193},{10,257},{12,321},{14,385},{66,3},{68... | collective-permute-start | bytes 49160 | tf_op jit(solution)/shard_map/ppermute | solution.py:386
  92.3 30.0 %collective-permute-start.11 = (bf16[144,512]{1,0:T(8,128)(2,1)S(1)}, bf16[144,512]{1,0:T(8,128)(2,1)S(1)}, u32[]{:S(2)}, u32[]{:S(2)}) collective-permute-start(bf16[144,512]{1,0:T(8,128)(2,1)S(1)} %get-tuple-element.35), channel_id=1, source_target_pairs={{256,0},{320,64},{384,128},{448,192},{0,256},{64,320},{128,384},{1... | collective-permute-start | bytes 442376 | tf_op jit(solution)/shard_map/ppermute | solution.py:40
  95.4 26.9 %collective-permute-start.12 = (bf16[144,512]{1,0:T(8,128)(2,1)S(1)}, bf16[144,512]{1,0:T(8,128)(2,1)S(1)}, u32[]{:S(2)}, u32[]{:S(2)}) collective-permute-start(bf16[144,512]{1,0:T(8,128)(2,1)S(1)} %get-tuple-element.36), channel_id=1, source_target_pairs={{384,0},{448,64},{0,128},{64,192},{128,256},{192,320},{256,384},{3... | collective-permute-start | bytes 442376 | tf_op jit(solution)/shard_map/ppermute | solution.py:40
  99.3 16.8 %collective-permute-start.15 = (bf16[16,512]{1,0:T(8,128)(2,1)S(1)}, bf16[16,512]{1,0:T(8,128)(2,1)S(1)}, u32[]{:S(2)}, u32[]{:S(2)}) collective-permute-start(bf16[16,512]{1,0:T(8,128)(2,1)S(1)} %get-tuple-element.49), channel_id=1, source_target_pairs={{2,0},{4,64},{6,128},{8,192},{10,256},{12,320},{14,384},{66,2},{68... | collective-permute-start | bytes 49160 | tf_op jit(solution)/shard_map/ppermute | solution.py:385
  100.0 16.2 %collective-permute-start.14 = (bf16[64,512]{1,0:T(8,128)(2,1)S(1)}, bf16[64,512]{1,0:T(8,128)(2,1)S(1)}, u32[]{:S(2)}, u32[]{:S(2)}) collective-permute-start(bf16[64,512]{1,0:T(8,128)(2,1)S(1)} %get-tuple-element.50), channel_id=1, source_target_pairs={{0,1},{1,0},{2,65},{3,64},{4,129},{5,128},{6,193},{7,192},{8,257},... | collective-permute-start | bytes 196616 | tf_op jit(solution)/shard_map/ppermute | solution.py:384
  113.3 9.0 %collective-permute-start.13 = (bf16[64,512]{1,0:T(8,128)(2,1)S(1)}, bf16[64,512]{1,0:T(8,128)(2,1)S(1)}, u32[]{:S(2)}, u32[]{:S(2)}) collective-permute-start(bf16[64,512]{1,0:T(8,128)(2,1)S(1)} %get-tuple-element.51), channel_id=1, source_target_pairs={{0,0},{1,1},{2,64},{3,65},{4,128},{5,129},{6,192},{7,193},{8,256},... | collective-permute-start | bytes 196616 | tf_op jit(solution)/shard_map/ppermute | solution.py:383
  153.7 38.6 %collective-permute-start.19 = (bf16[4,144,512]{2,1,0:T(8,128)(2,1)S(1)}, bf16[4,144,512]{2,1,0:T(8,128)(2,1)S(1)}, u32[]{:S(2)}, u32[]{:S(2)}) collective-permute-start(bf16[4,144,512]{2,1,0:T(8,128)(2,1)S(1)} %bitcast.35), channel_id=1, source_target_pairs={{64,0},{0,64},{192,128},{128,192},{320,256},{256,320},{448,384},{3... | collective-permute-start | bytes 1769480 | tf_op jit(solution)/shard_map/ppermute | solution.py:35
  155.7 36.7 %collective-permute-start.18 = (bf16[4,144,512]{2,1,0:T(8,128)(2,1)S(1)}, bf16[4,144,512]{2,1,0:T(8,128)(2,1)S(1)}, u32[]{:S(2)}, u32[]{:S(2)}) collective-permute-start(bf16[4,144,512]{2,1,0:T(8,128)(2,1)S(1)} %bitcast.36), channel_id=1, source_target_pairs={{432,0},{384,16},{400,32},{416,48},{496,64},{448,80},{464,96},{480... | collective-permute-start | bytes 1769480 | tf_op jit(solution)/shard_map/ppermute | solution.py:53
  163.0 29.3 %collective-permute-start.17 = (bf16[4,144,512]{2,1,0:T(8,128)(2,1)S(1)}, bf16[4,144,512]{2,1,0:T(8,128)(2,1)S(1)}, u32[]{:S(2)}, u32[]{:S(2)}) collective-permute-start(bf16[4,144,512]{2,1,0:T(8,128)(2,1)S(1)} %bitcast.37), channel_id=1, source_target_pairs={{128,0},{144,16},{160,32},{176,48},{192,64},{208,80},{224,96},{240... | collective-permute-start | bytes 1769480 | tf_op jit(solution)/shard_map/ppermute | solution.py:53
  165.0 23.4 %collective-permute-start.21 = (bf16[2,144,512]{2,1,0:T(8,128)(2,1)S(1)}, bf16[2,144,512]{2,1,0:T(8,128)(2,1)S(1)}, u32[]{:S(2)}, u32[]{:S(2)}) collective-permute-start(bf16[2,144,512]{2,1,0:T(8,128)(2,1)S(1)} %bitcast.48), channel_id=1, source_target_pairs={{304,0},{256,16},{272,32},{288,48},{368,64},{320,80},{336,96},{352... | collective-permute-start | bytes 884744 | tf_op jit(solution)/shard_map/ppermute | solution.py:53
  168.1 24.2 %collective-permute-start.20 = (bf16[2,144,512]{2,1,0:T(8,128)(2,1)S(1)}, bf16[2,144,512]{2,1,0:T(8,128)(2,1)S(1)}, u32[]{:S(2)}, u32[]{:S(2)}) collective-permute-start(bf16[2,144,512]{2,1,0:T(8,128)(2,1)S(1)} %bitcast.47), channel_id=1, source_target_pairs={{256,0},{272,16},{288,32},{304,48},{320,64},{336,80},{352,96},{368... | collective-permute-start | bytes 884744 | tf_op jit(solution)/shard_map/ppermute | solution.py:53
  192.4 7.3 %collective-permute-start.22 = (bf16[4,144,512]{2,1,0:T(8,128)(2,1)S(1)}, bf16[4,144,512]{2,1,0:T(8,128)(2,1)S(1)}, u32[]{:S(2)}, u32[]{:S(2)}) collective-permute-start(bf16[4,144,512]{2,1,0:T(8,128)(2,1)S(1)} %collective-permute-done.17.refs_2_), channel_id=1, source_target_pairs={{64,0},{0,64},{192,128},{128,192},{320,256},{256,320},{448,384},{3... | collective-permute-start | bytes 1769480 | tf_op jit(solution)/shard_map/ppermute | solution.py:35
  195.2 4.5 %collective-permute-start.23 = (bf16[4,144,512]{2,1,0:T(8,128)(2,1)S(1)}, bf16[4,144,512]{2,1,0:T(8,128)(2,1)}, u32[]{:S(2)}, u32[]{:S(2)}) collective-permute-start(bf16[4,144,512]{2,1,0:T(8,128)(2,1)S(1)} %collective-permute-done.18.refs_3_), channel_id=1, source_target_pairs={{64,0},{0,64},{192,128},{128,192},{320,256},{256,320},{448,384},{3... | collective-permute-start | bytes 1769480 | tf_op jit(solution)/shard_map/ppermute | solution.py:35
  197.1 4.2 %collective-permute-start.24 = (bf16[4,144,512]{2,1,0:T(8,128)(2,1)S(1)}, bf16[4,144,512]{2,1,0:T(8,128)(2,1)}, u32[]{:S(2)}, u32[]{:S(2)}) collective-permute-start(bf16[4,144,512]{2,1,0:T(8,128)(2,1)S(1)} %pad_maximum_fusion.refs_4_), channel_id=1, source_target_pairs={{64,0},{0,64},{192,128},{128,192},{320,256},{256,320},{448,384},{3... | collective-permute-start | bytes 1769480 | tf_op jit(solution)/shard_map/ppermute | solution.py:35
Sparse Core Ops, SparseCore 0:
  90.2 78.9 all-gather.3
